TPU v7x, 32 devices: a whole 2x2x4 slice. The times are simulated.
32 devices in a mesh: inst: 4 (over y, x), space: 8 (over z, core).
Axes of the slice: x: 2, y: 2, z: 4, core: 2. Of those that a mesh axis runs over, the one named last changes fastest.
Arguments:
- field_start: float32 [32, 128, 64, 128], P('inst', 'space'), may hold values from -6 to 6
- source: float32 [32, 128, 64, 128], P('inst', 'space'), may hold values from -6 to 6
- material: int32 [128, 64, 128], P('space'), may hold values from 0 to 7
- face_flags: int32 [32, 3, 128, 64, 128], P('inst', None, 'space'), may hold values from 0 to 1
- disp_table: float32 [8], replicated, may hold values from 0.3 to 3
- perm_table: float32 [8], replicated, may hold values from 0.2 to 2
Outputs:
- residual: float32 [32, 128, 64, 128], P('inst', 'space')
- field: float32 [32, 128, 64, 128], P('inst', 'space')
All inputs are finite; a program needn't handle non-finite values.
Results may differ from a plain program's by a relative error of at most 0.00005.
Values sent between devices are 32-bit elements; how exact they have to be, the bound alone decides.
No kernel may reach another device: no remote copies, remote signals or barrier semaphores. Data moves between devices by JAX's collectives and lax.ppermute only.
A program may use at most 192 MiB of HBM per device.

v0:
```python
import jax
import jax.numpy as jnp
from jax import lax
from jax.sharding import PartitionSpec as P

NT = 32


omega_scale = 0.25
decay_rate = 0.3
relax_weight = 0.8


def shifted(shard, axis, by):
    count = lax.axis_size(axis)
    pairs = [(i, i + by) for i in range(count) if 0 <= i + by < count]
    return lax.ppermute(shard, axis, pairs)


def with_halo(block, sides, width):
    for axis, dim in sides:
        count = lax.axis_size(axis)
        forward = [(i, i + 1) for i in range(count - 1)]
        backward = [(target, source) for source, target in forward]
        low = lax.ppermute(
            lax.slice_in_dim(block, block.shape[dim] - width, None, axis=dim), axis, forward
        )
        high = lax.ppermute(lax.slice_in_dim(block, 0, width, axis=dim), axis, backward)
        block = jnp.concatenate([low, block, high], axis=dim)
    return block


def spectral_matrix(first, count):
    rows = first + jnp.arange(count)
    cols = jnp.arange(NT)
    diff = rows[:, None] - cols[None, :]
    angle = jnp.pi * diff.astype(jnp.float32) / NT
    parity = 1.0 - 2.0 * (diff % 2).astype(jnp.float32)
    safe = jnp.where(diff == 0, 1.0, jnp.sin(angle))
    return jnp.where(diff == 0, 0.0, 0.5 * parity * jnp.cos(angle) / safe)


def lookup(material, table):
    total = jnp.zeros(material.shape, jnp.float32)
    for klass in range(table.shape[0]):
        total = total + jnp.where(material == klass, table[klass], 0.0)
    return total


def next_along(field, axis):
    count = field.shape[axis]
    zeros = jnp.zeros_like(lax.slice_in_dim(field, 0, 1, axis=axis))
    return jnp.concatenate([lax.slice_in_dim(field, 1, count, axis=axis), zeros], axis)


def prev_along(field, axis):
    count = field.shape[axis]
    zeros = jnp.zeros_like(lax.slice_in_dim(field, 0, 1, axis=axis))
    return jnp.concatenate([zeros, lax.slice_in_dim(field, 0, count - 1, axis=axis)], axis)


def face_terms(field, up_val, lo_val, kappa, lo_kappa, flow, lo_flow):
    return (
        kappa * (field - up_val)
        + lo_kappa * (field - lo_val)
        + jnp.maximum(flow, 0.0) * field
        + jnp.minimum(flow, 0.0) * up_val
        - jnp.maximum(lo_flow, 0.0) * lo_val
        - jnp.minimum(lo_flow, 0.0) * field
    )


def diag_terms(kappa, lo_kappa, flow, lo_flow):
    return kappa + lo_kappa + jnp.maximum(flow, 0.0) - jnp.minimum(lo_flow, 0.0)


def body(field_start, source, material, face_flags, disp_table, perm_table):
    count = field_start.shape[0]
    first = lax.axis_index("inst") * count
    kappa = lookup(material, disp_table)
    speed = lookup(material, perm_table)
    moments = (first + jnp.arange(count)).astype(jnp.float32)
    tide = 1.0 + 0.5 * jnp.cos(2.0 * jnp.pi * moments / NT)
    velocity = (
        speed[None, None]
        * tide[:, None, None, None, None]
        * (1.0 - 2.0 * face_flags.astype(jnp.float32))
    )
    top_plane = jnp.concatenate([kappa[-1:], velocity[:, 0, -1]], 0)
    below = shifted(top_plane, "space", 1)
    low_kappa_z = jnp.concatenate([below[:1], kappa[:-1]], 0)
    low_flow_z = jnp.concatenate([below[1:, None], velocity[:, 0, :-1]], 1)
    kappa_wide = kappa[None]
    diag = decay_rate + jnp.zeros_like(field_start)
    diag = diag + diag_terms(kappa_wide, low_kappa_z[None], velocity[:, 0], low_flow_z)
    for axis in (1, 2):
        flow = velocity[:, axis]
        diag = diag + diag_terms(
            kappa_wide, prev_along(kappa, axis)[None], flow, prev_along(flow, axis + 1)
        )
    dmat_rows = spectral_matrix(first, count)

    def coupled(field):
        piece = lax.all_gather(field, "inst", axis=0, tiled=True)
        flat = piece.reshape(piece.shape[0], -1)
        product = jnp.dot(
            dmat_rows, flat, precision=lax.Precision.HIGHEST, preferred_element_type=jnp.float32
        )
        return product.reshape(jnp.zeros(field.shape, jnp.float32).shape)

    def residual_of(field):
        padded = with_halo(field, (("space", 1),), 1)
        total = decay_rate * field
        total = total + face_terms(
            field,
            padded[:, 2:],
            padded[:, :-2],
            kappa_wide,
            low_kappa_z[None],
            velocity[:, 0],
            low_flow_z,
        )
        for axis in (1, 2):
            flow = velocity[:, axis]
            total = total + face_terms(
                field,
                next_along(field, axis + 1),
                prev_along(field, axis + 1),
                kappa_wide,
                prev_along(kappa, axis)[None],
                flow,
                prev_along(flow, axis + 1),
            )
        return omega_scale * coupled(field) + total - source

    residual = residual_of(field_start)
    middle = field_start - relax_weight * residual / diag
    second = residual_of(middle)
    field = middle - relax_weight * second / diag
    return (residual, field)


def solution(mesh):
    return jax.shard_map(
        body,
        mesh=mesh,
        in_specs=(
            P("inst", "space", None, None),
            P("inst", "space", None, None),
            P("space", None, None),
            P("inst", None, "space", None, None),
            P(),
            P(),
        ),
        out_specs=(P("inst", "space", None, None), P("inst", "space", None, None)),
        check_vma=False,
    )
```

profile of v0, /device:TPU:9, one launch (start us, length us, event | category | flops | bytes accessed | tf_op | source)
XLA Modules:
  0.0 481.8 jit_solution(833712866773597889)
XLA Ops:
  7.2 0.0 all-gather.3.cloned.1.call-start
  7.2 0.7 all-gather.3.cloned.1.call-update
  7.9 0.0 copy-start.5
  7.9 0.0 copy-start.6
  7.9 0.0 copy-start.4
  7.9 0.0 all-gather.5.cloned.1.call-start
  8.0 5.5 %copy.98 = f32[8,16,64,128]{3,0,2,1:T(8,128)S(1)} copy(f32[8,16,64,128]{3,2,1,0:T(8,128)} %param.6) | data formatting | bytes 8388608 | tf_op args[0]
  13.5 0.0 copy-start
  13.5 2.0 copy-done
  15.5 0.9 fusion.105
  16.4 2.6 collective-permute-start
  19.0 3.1 collective-permute-start.2
  22.1 0.0 copy-done.5
  22.1 0.7 fusion.107
  22.8 0.0 copy-done.6
  22.8 0.7 fusion.106
  23.5 0.0 copy-done.4
  23.5 8.3 %select_add_fusion.1 = (f32[16,64,128]{2,0,1:T(8,128)S(1)}, pred[16,64,128]{2,0,1:T(8,128)(4,1)S(1)}, pred[16,64,128]{2,0,1:T(8,128)(4,1)S(1)}, pred[16,64,128]{...) fusion(f32[]{:T(128)} %bitcast.10, f32[]{:T(128)} %bitcast.9, ...), kind=kLoop, calls=%fused_computation.69 | loop fusion | flops 3014656 | bytes 2097184 | tf_op jit(solution)/shard_map/add | solution.py:46
  31.8 5.4 %select_add_fusion = f32[16,64,128]{2,0,1:T(8,128)S(1)} fusion(pred[16,64,128]{2,0,1:T(8,128)(4,1)S(1)} %get-tuple-element.18, pred[16,64,128]{2,0,1:T(8,128)(4,1)S(1)} %get-tuple-element.17, pred[16,64,128]{2,0,1:T(8,128)(4,1)S(1)} %get-tuple-element.16, pred[16,64,128]{2,0,1:T(8,128)(4,1)S(1)} %get-tuple-element.15, ...), kind=kLoop, calls=%fused_computation.68 | loop fusion | flops 1966080 | bytes 1572896 | tf_op jit(solution)/shard_map/add | solution.py:46
  37.2 0.2 copy.111
  37.5 2.5 broadcast_multiply_fusion
  40.0 23.0 %fusion.6 = f32[8,3,16,64,128]{4,0,3,2,1:T(8,128)} fusion(s32[8,3,16,64,128]{4,3,2,1,0:T(8,128)} %param.9, f32[8,16,64,128]{3,0,2,1:T(8,128)} %broadcast_multiply_fusion), kind=kLoop, calls=%fused_computation.9 | loop fusion | flops 12582912 | bytes 29360128 | tf_op jit(solution)/shard_map/mul | solution.py:85
  63.0 1.0 slice_bitcast_fusion.4
  64.0 0.1 pad_maximum_fusion.6
  64.1 2.4 collective-permute-start.1
  66.5 0.2 copy.107
  66.7 0.2 copy.177
  66.9 0.2 copy.176
  67.1 1.0 concatenate.77.clone
  68.1 6.2 %slice_bitcast_fusion = (f32[8,16,64,128]{3,0,2,1:T(8,128)}, f32[8,16,64,128]{3,0,2,1:T(8,128)S(1)}) fusion(f32[8,3,16,64,128]{4,0,3,2,1:T(8,128)} %fusion.6), kind=kLoop, calls=%fused_computation.31 | loop fusion | bytes 16777216 | tf_op jit(solution)/shard_map/squeeze | solution.py:124
  74.3 2.4 slice.211
  76.8 1.6 copy-done.1
  78.4 4.7 fusion.103
  83.1 4.7 fusion.104
  87.8 4.3 slice_bitcast_fusion.2
  92.1 0.0 collective-permute-done.1
  92.1 0.3 pad_add_fusion
  92.4 0.2 copy.135
  92.5 0.2 copy.136
  92.7 0.2 copy.134
  92.9 0.2 copy.113
  93.1 75.3 %all-gather.3.cloned.1.call-done = f32[32,16,64,128]{3,2,1,0:T(8,128)} async-done(((f32[8,16,64,128]{3,2,1,0:T(8,128)}), f32[32,16,64,128]{3,2,1,0:T(8,128)}) %all-gather.3.cloned.1.call-update) | async-done | bytes 16777232 | tf_op jit(solution)/shard_map/all_gather | solution.py:104
  168.5 15.2 %copy.189 = f32[4,8,1024,128]{3,1,2,0:T(8,128)S(1)} copy(f32[4,8,1024,128]{3,2,1,0:T(8,128)} %bitcast.102) | data formatting | bytes 33554432
  183.7 6.9 %copy.145 = f32[4,8,1024,128]{3,2,1,0:T(8,128)} copy(f32[4,8,1024,128]{3,1,2,0:T(8,128)S(1)} %copy.189) | data formatting | bytes 33554432
  190.5 0.0 collective-permute-done
  190.5 0.0 collective-permute-done.2
  190.5 43.2 %divide_subtract_fusion = (f32[8,16,64,128]{3,0,2,1:T(8,128)}, f32[8,16,64,128]{3,0,2,1:T(8,128)}) fusion(f32[8,16,64,127]{3,0,2,1:T(8,128)} %bitcast.105, f32[8,16,63,128]{3,0,2,1:T(8,128)} %slice.211, f32[8,3,16,64,128]{4,0,3,2,1:T(8,128)} %fusion.6, f32[8,15,64,128]{3,0,2,1:T(8,128)} %slice_bitcast_fusion.2, ...), kind=kOutput, calls=%fused_computation.59 | convolution fusion | flops 479205120 | bytes 83591200 | tf_op jit(solution)/shard_map/dot_general | solution.py:106
  233.8 0.0 all-gather.5.cloned.1.call-update
  233.8 1.9 fusion.102
  235.7 2.6 collective-permute-start.3
  238.2 3.0 collective-permute-start.4
  241.3 0.0 copy-start.2
  241.3 9.9 %fusion.101 = (f32[8,16,64,127]{3,0,2,1:T(8,128)}, f32[8,16,64,127]{3,0,2,1:T(8,128)}) fusion(f32[8,16,64,128]{3,0,2,1:T(8,128)} %get-tuple-element.53), kind=kLoop, calls=%fused_computation.137 | loop fusion | bytes 16646144 | tf_op jit(solution)/shard_map/slice | solution.py:53
  251.2 0.0 copy-done.2
  251.2 4.4 fusion.100
  255.6 2.8 copy.141
  258.4 132.9 %all-gather.5.cloned.1.call-done = f32[32,16,64,128]{3,0,2,1:T(8,128)} async-done(((f32[8,16,64,128]{3,0,2,1:T(8,128)}), f32[32,16,64,128]{3,0,2,1:T(8,128)}) %all-gather.5.cloned.1.call-update) | async-done | bytes 16777232 | tf_op jit(solution)/shard_map/all_gather | solution.py:104
  391.2 9.6 %copy.138 = f32[32,16,64,128]{3,2,1,0:T(8,128)S(1)} copy(f32[32,16,64,128]{3,0,2,1:T(8,128)} %all-gather.5.cloned.1.call-done) | data formatting | bytes 33554432 | tf_op jit(solution)/shard_map/all_gather | solution.py:104
  400.8 22.4 %copy.188 = f32[4,8,1024,128]{3,1,2,0:T(8,128)S(1)} copy(f32[4,8,1024,128]{3,2,1,0:T(8,128)S(1)} %bitcast.98) | data formatting | bytes 33554432
  423.2 6.9 %copy.147 = f32[4,8,1024,128]{3,2,1,0:T(8,128)} copy(f32[4,8,1024,128]{3,1,2,0:T(8,128)S(1)} %copy.188) | data formatting | bytes 33554432
  430.0 0.0 collective-permute-done.3
  430.0 0.0 collective-permute-done.4
  430.0 39.8 %fusion.18 = f32[8,16,64,128]{3,0,2,1:T(8,128)} fusion(f32[8,16,64,128]{3,0,2,1:T(8,128)} %get-tuple-element.53, f32[8,1,64,128]{3,0,2,1:T(8,128)} %collective-permute-done.4, f32[8,1,64,128]{3,0,2,1:T(8,128)} %collective-permute-done.3, f32[8,16,64,127]{3,0,2,1:T(8,128)} %get-tuple-element.24, f32[8,16,64,127]{3,0,2,1:T(8,128)} %get-tuple-element.23, ...), kind=kOutput, calls=%fused_computation.22 | convolution fusion | flops 479205120 | bytes 75202592 | tf_op jit(solution)/shard_map/dot_general | solution.py:106
  469.8 5.0 %copy.142 = f32[8,16,64,128]{3,2,1,0:T(8,128)} copy(f32[8,16,64,128]{3,0,2,1:T(8,128)} %fusion.18) | data formatting | bytes 8388608
  (10 shorter events, 0.2 us)
Async XLA Ops:
  7.2 161.3 %all-gather.3.cloned.1.call-start = ((), (), s32[]{:S(2)}) async-start(), calls=%async_computation | async-start | bytes 20971520 | tf_op jit(solution)/shard_map/all_gather | solution.py:104
  7.9 14.2 %copy-start.5 = (f32[8]{0:T(128)S(1)}, f32[8]{0:T(128)}, u32[]{:S(2)}) copy-start(f32[8]{0:T(128)} %param.10) | copy-start | bytes 100
  7.9 14.9 %copy-start.6 = (f32[8]{0:T(128)S(1)}, f32[8]{0:T(128)}, u32[]{:S(2)}) copy-start(f32[8]{0:T(128)} %param.11) | copy-start | bytes 100
  7.9 15.6 %copy-start.4 = (s32[16,64,128]{2,1,0:T(8,128)S(1)}, s32[16,64,128]{2,1,0:T(8,128)}, u32[]{:S(2)}) copy-start(s32[16,64,128]{2,1,0:T(8,128)} %param.8) | copy-start | bytes 1572868
  7.9 383.3 %all-gather.5.cloned.1.call-start = ((), (), s32[]{:S(2)}) async-start(), calls=%async_computation.1 | async-start | bytes 20971520 | tf_op jit(solution)/shard_map/all_gather | solution.py:104
  13.5 2.0 copy-start
  16.4 174.1 %collective-permute-start = (f32[8,1,64,128]{3,0,2,1:T(8,128)}, f32[8,1,64,128]{3,0,2,1:T(8,128)}, u32[]{:S(2)}, u32[]{:S(2)}) collective-permute-start(f32[8,1,64,128]{3,0,2,1:T(8,128)} %get-tuple-element.31), channel_id=1, source_target_pairs={{1,0},{2,1},{3,2},{4,3},{5,4},{6,5},{7,6},{9,8},{10,9},{11,10},{12... | collective-permute-start | bytes 786440 | tf_op jit(solution)/shard_map/ppermute | solution.py:28
  19.0 171.5 %collective-permute-start.2 = (f32[8,1,64,128]{3,0,2,1:T(8,128)}, f32[8,1,64,128]{3,0,2,1:T(8,128)}, u32[]{:S(2)}, u32[]{:S(2)}) collective-permute-start(f32[8,1,64,128]{3,0,2,1:T(8,128)} %get-tuple-element.32), channel_id=1, source_target_pairs={{0,1},{1,2},{2,3},{3,4},{4,5},{5,6},{6,7},{8,9},{9,10},{10,11},{11... | collective-permute-start | bytes 786440 | tf_op jit(solution)/shard_map/ppermute | solution.py:25
  64.1 28.0 %collective-permute-start.1 = (f32[9,64,128]{2,0,1:T(8,128)S(1)}, f32[9,64,128]{2,0,1:T(8,128)S(1)}, u32[]{:S(2)}, u32[]{:S(2)}) collective-permute-start(f32[9,64,128]{2,0,1:T(8,128)S(1)} %pad_maximum_fusion.6), channel_id=1, source_target_pairs={{0,1},{1,2},{2,3},{3,4},{4,5},{5,6},{6,7},{8,9},{9,10},{10,11},{11... | collective-permute-start | bytes 884744 | tf_op jit(solution)/shard_map/ppermute | solution.py:17
  74.3 4.1 copy-start.1
  235.7 194.4 %collective-permute-start.3 = (f32[8,1,64,128]{3,0,2,1:T(8,128)}, f32[8,1,64,128]{3,0,2,1:T(8,128)}, u32[]{:S(2)}, u32[]{:S(2)}) collective-permute-start(f32[8,1,64,128]{3,0,2,1:T(8,128)} %get-tuple-element.25), channel_id=1, source_target_pairs={{1,0},{2,1},{3,2},{4,3},{5,4},{6,5},{7,6},{9,8},{10,9},{11,10},{12... | collective-permute-start | bytes 786440 | tf_op jit(solution)/shard_map/ppermute | solution.py:28
  238.2 191.8 %collective-permute-start.4 = (f32[8,1,64,128]{3,0,2,1:T(8,128)}, f32[8,1,64,128]{3,0,2,1:T(8,128)}, u32[]{:S(2)}, u32[]{:S(2)}) collective-permute-start(f32[8,1,64,128]{3,0,2,1:T(8,128)} %get-tuple-element.26), channel_id=1, source_target_pairs={{0,1},{1,2},{2,3},{3,4},{4,5},{5,6},{6,7},{8,9},{9,10},{10,11},{11... | collective-permute-start | bytes 786440 | tf_op jit(solution)/shard_map/ppermute | solution.py:25
  241.3 9.9 %copy-start.2 = (f32[8,16,64,128]{3,0,2,1:T(8,128)S(1)}, f32[8,16,64,128]{3,0,2,1:T(8,128)}, u32[]{:S(2)}) copy-start(f32[8,16,64,128]{3,0,2,1:T(8,128)} %get-tuple-element.53) | copy-start | bytes 12582916
  251.2 4.4 copy-start.3
Sparse Core Ops, SparseCore 0:
  9.8 158.5 all-gather.2
  233.9 157.2 all-gather.4
where the time goes:
time: 487 us; the launch traced here: 482 us
  waiting for transfers between devices  209 us (43%)
  local copies, waits for them, and re-layouts  122 us (25%)
  matrix products  83 us (17%)
  other arithmetic  39.7 us (8%)
  between operations  14.5 us (3%)
  starting transfers between devices  13.7 us (3%)
    all_gather x2, waiting for transfers between devices, coupled(): piece = lax.all_gather(field, 'inst', axis=0, tiled=True)  208 us
    dot_general x2, matrix products, coupled(): jnp.dot(dmat_rows, flat, precision=lax.Precision.HIGHEST, preferred_eleme...  83 us
    unnamed x23, local copies, waits for them, and re-layouts  68.6 us
    mul x2, other arithmetic, body(): speed[None, None] * tide[:, None, None, None, None]  25.6 us
    slice x4, local copies, waits for them, and re-layouts, next_along(): lax.slice_in_dim(field, 1, count, axis=axis)  23.6 us
    add x2, other arithmetic, lookup(): total = total + jnp.where(material == klass, table[klass], 0.0)  13.7 us
  transfers between devices with their start and end apart: 7, of which 2 were waited for; matrix products, arithmetic and copies ran while one was open for 32% of the time, Pallas kernels for 0%

commit v1 on v0

v1 whole, which is shorter than its diff:
```python
import functools

import jax
import jax.numpy as jnp
from jax import lax
from jax.experimental import pallas as pl
from jax.experimental.pallas import tpu as pltpu
from jax.sharding import PartitionSpec as P

NT = 32


omega_scale = 0.25
decay_rate = 0.3
relax_weight = 0.8

CHUNKS = 2
SUB = 8
MIB = 1 << 20


def spectral_blocks(me, n, count):
    spots = jnp.arange(NT)
    moments = (me ^ (spots // count)) * count + spots % count
    diff = moments[:, None] - moments[None, :]
    angle = jnp.pi * diff.astype(jnp.float32) / NT
    parity = 1.0 - 2.0 * (diff % 2).astype(jnp.float32)
    safe = jnp.where(diff == 0, 1.0, jnp.sin(angle))
    dmat = omega_scale * jnp.where(diff == 0, 0.0, 0.5 * parity * jnp.cos(angle) / safe)
    rows = jnp.repeat(jnp.repeat(dmat, SUB, 0), SUB, 1)
    lane = jnp.arange(NT * SUB) % SUB
    return jnp.where(lane[:, None] == lane[None, :], rows, 0.0)


def prep_kernel(disp_ref, perm_ref, tide_ref, material_ref, flags_ref, kappa_ref, speed_ref, top_ref):
    depth = material_ref.shape[0]

    def layer(z, carry):
        material = material_ref[z]
        kappa = jnp.zeros(material.shape, jnp.float32)
        speed = jnp.zeros(material.shape, jnp.float32)
        for klass in range(disp_ref.shape[0]):
            here = material == klass
            kappa = jnp.where(here, disp_ref[klass], kappa)
            speed = jnp.where(here, perm_ref[klass], speed)
        kappa_ref[z] = kappa
        speed_ref[z] = speed
        return carry

    lax.fori_loop(0, depth, layer, 0)
    top_ref[0] = kappa_ref[depth - 1]
    for t in range(flags_ref.shape[0]):
        flow = speed_ref[depth - 1] * tide_ref[t]
        top_ref[t + 1] = jnp.where(flags_ref[t, 0, 0] != 0, -flow, flow)


def prep(disp_table, perm_table, tide, material, face_flags):
    count, _, depth, width, length = face_flags.shape
    smem = pl.BlockSpec(memory_space=pltpu.SMEM)
    cells = pl.BlockSpec((depth, width, length), lambda i: (0, 0, 0))
    return pl.pallas_call(
        prep_kernel,
        grid=(1,),
        in_specs=[
            smem,
            smem,
            smem,
            cells,
            pl.BlockSpec((count, 1, 1, width, length), lambda i: (0, 0, depth - 1, 0, 0)),
        ],
        out_specs=[cells, cells, pl.BlockSpec((count + 1, width, length), lambda i: (0, 0, 0))],
        out_shape=[
            jax.ShapeDtypeStruct(material.shape, jnp.float32),
            jax.ShapeDtypeStruct(material.shape, jnp.float32),
            jax.ShapeDtypeStruct((count + 1, width, length), jnp.float32),
        ],
        compiler_params=pltpu.CompilerParams(vmem_limit_bytes=16 * MIB),
        cost_estimate=pl.CostEstimate(flops=material.size * 30, bytes_accessed=material.size * 12, transcendentals=0),
        name="prep",
    )(disp_table, perm_table, tide, material, face_flags)


def stencil_kernel(second, tide_ref, u_ref, low_ref, high_ref, flags_ref, src_ref, kappa_ref, speed_ref, below_k_ref, below_f_ref, *rest):
    if second:
        winv_ref, out_ref = rest
    else:
        out_ref, winv_ref = rest
    depth, width, length = u_ref.shape[1:]
    tide = tide_ref[pl.program_id(0)]
    row = lax.broadcasted_iota(jnp.int32, (width, length), 0)
    col = lax.broadcasted_iota(jnp.int32, (width, length), 1)
    last_row, last_col = row == width - 1, col == length - 1

    below_k, below_f = below_k_ref[0], below_f_ref[0]
    au_low = (below_k + jnp.maximum(below_f, 0.0)) * low_ref[0, 0]
    b_low = below_k - jnp.minimum(below_f, 0.0)

    def layer(z, carry, u_up):
        au_low, b_low = carry
        u = u_ref[0, z]
        kappa = kappa_ref[z]
        full = kappa + speed_ref[z] * tide

        def coefs(dim):
            back = flags_ref[0, dim, z] != 0
            return jnp.where(back, kappa, full), jnp.where(back, full, kappa)

        a, b = coefs(0)
        total = b * u_up + au_low
        diag = (decay_rate + a) + b_low
        next_carry = (a * u, b)
        for dim, last in ((1, last_row), (2, last_col)):
            a, b = coefs(dim)
            size = u.shape[dim - 1]
            b = jnp.where(last, 0.0, b)
            au = jnp.where(last, 0.0, a * u)
            total = total + b * pltpu.roll(u, size - 1, dim - 1) + pltpu.roll(au, 1, dim - 1)
            if not second:
                diag = diag + (a + pltpu.roll(b, 1, dim - 1))
        if second:
            out_ref[0, z] = (1.0 - relax_weight) * u + winv_ref[0, z] * (total + src_ref[0, z])
        else:
            out_ref[0, z] = diag * u - total - src_ref[0, z]
            winv_ref[0, z] = relax_weight / diag
        return next_carry

    carry = lax.fori_loop(0, depth - 1, lambda z, c: layer(z, c, u_ref[0, z + 1]), (au_low, b_low))
    layer(depth - 1, carry, high_ref[0, 0])


def stencil(second, tide, u, low, high, flags, src, kappa, speed, below, winv=None):
    count, depth, width, length = u.shape
    field = pl.BlockSpec((1, depth, width, length), lambda t: (t, 0, 0, 0))
    plane = pl.BlockSpec((1, 1, width, length), lambda t: (t, 0, 0, 0))
    cells = pl.BlockSpec((depth, width, length), lambda t: (0, 0, 0))
    in_specs = [
        pl.BlockSpec(memory_space=pltpu.SMEM),
        field,
        plane,
        plane,
        pl.BlockSpec((1, 3, depth, width, length), lambda t: (t, 0, 0, 0, 0)),
        field,
        cells,
        cells,
        pl.BlockSpec((1, width, length), lambda t: (0, 0, 0)),
        pl.BlockSpec((1, width, length), lambda t: (t + 1, 0, 0)),
    ]
    args = [tide, u, low, high, flags, src, kappa, speed, below, below]
    if second:
        in_specs.append(field)
        args.append(winv)
    shape = jax.ShapeDtypeStruct(u.shape, jnp.float32)
    return pl.pallas_call(
        functools.partial(stencil_kernel, second),
        grid=(count,),
        in_specs=in_specs,
        out_specs=field if second else [field, field],
        out_shape=shape if second else [shape, shape],
        compiler_params=pltpu.CompilerParams(vmem_limit_bytes=24 * MIB),
        cost_estimate=pl.CostEstimate(flops=u.size * 60, bytes_accessed=u.size * 28, transcendentals=0),
        name="stencil_two" if second else "stencil_one",
    )(*args)


def apply_kernel(n, me_ref, own_ref, *refs):
    received, mat_ref, outs = refs[: n - 1], refs[n - 1], refs[n:]
    parts = [own_ref, *received]
    count, _, width, length = own_ref.shape
    groups = width // SUB
    blocks = jnp.concatenate([part[:, 0] for part in parts], 0)
    wide = jnp.concatenate(
        [blocks[:, g * SUB : (g + 1) * SUB].reshape(NT * SUB, length) for g in range(groups)], 1
    )
    product = lax.dot_general(
        mat_ref[...],
        wide,
        (((1,), (0,)), ((), ())),
        precision=lax.Precision.HIGHEST,
        preferred_element_type=jnp.float32,
    )
    for g in range(groups):
        piece = product[:, g * length : (g + 1) * length].reshape(NT, SUB, length)
        for m, out in enumerate(outs):
            out[:, 0, g * SUB : (g + 1) * SUB] = piece[m * count : (m + 1) * count]


def apply_time(me, field, received, mat, chunk):
    n = len(received) + 1
    count, depth, width, length = field.shape
    part = received[0].shape[1]
    piece = pl.BlockSpec((count, 1, width, length), lambda i, me: (0, i, 0, 0))
    shape = jax.ShapeDtypeStruct(received[0].shape, jnp.float32)
    size = n * received[0].size
    return pl.pallas_call(
        functools.partial(apply_kernel, n),
        grid_spec=pltpu.PrefetchScalarGridSpec(
            num_scalar_prefetch=1,
            grid=(part,),
            in_specs=[
                pl.BlockSpec((count, 1, width, length), lambda i, me: (0, (chunk * n + me[0]) * part + i, 0, 0)),
                *([piece] * (n - 1)),
                pl.BlockSpec(mat.shape, lambda i, me: (0, 0)),
            ],
            out_specs=[piece] * n,
        ),
        out_shape=[shape] * n,
        compiler_params=pltpu.CompilerParams(vmem_limit_bytes=24 * MIB),
        cost_estimate=pl.CostEstimate(flops=size * 2 * NT * SUB * 6, bytes_accessed=size * 8, transcendentals=0),
        name="apply_time",
    )(me, field, *received, mat)


ROWS = 16


def first_kernel(n, aliased, me_ref, *refs):
    pieces, (s_ref, winv_ref, u_ref) = refs[:n], refs[n : n + 3]
    res_ref, mid_ref, *sends = refs[n + 3 + aliased :]
    part = pieces[0].shape[1]
    for m, piece in enumerate(pieces):
        for i in range(part):
            z = (me_ref[0] ^ m) * part + i
            res = s_ref[:, z] + piece[:, i]
            mid = u_ref[:, z] - winv_ref[:, z] * res
            res_ref[:, z] = res
            mid_ref[:, z] = mid
            if m:
                sends[m - 1][:, i] = mid


def first_update(me, pieces, s, winv, u, chunk, before):
    n = len(pieces)
    count, depth, width, length = u.shape
    part = pieces[0].shape[1]
    piece = pl.BlockSpec((count, part, ROWS, length), lambda i, me: (0, 0, i, 0))
    layers = pl.BlockSpec((count, n * part, ROWS, length), lambda i, me: (0, chunk, i, 0))
    whole = jax.ShapeDtypeStruct(u.shape, jnp.float32)
    aliased = len(before)
    size = n * pieces[0].size
    return pl.pallas_call(
        functools.partial(first_kernel, n, aliased),
        grid_spec=pltpu.PrefetchScalarGridSpec(
            num_scalar_prefetch=1,
            grid=(width // ROWS,),
            in_specs=[piece] * n + [layers] * 3 + [pl.BlockSpec(memory_space=pl.ANY)] * aliased,
            out_specs=[layers] * 2 + [piece] * (n - 1),
        ),
        out_shape=[whole] * 2 + [jax.ShapeDtypeStruct(pieces[0].shape, jnp.float32)] * (n - 1),
        input_output_aliases={n + 4 + i: i for i in range(aliased)},
        compiler_params=pltpu.CompilerParams(vmem_limit_bytes=24 * MIB),
        cost_estimate=pl.CostEstimate(flops=size * 3, bytes_accessed=size * 28, transcendentals=0),
        name="first_update",
    )(me, *pieces, s, winv, u, *before)


def last_kernel(n, aliased, me_ref, *refs):
    pieces, (f_ref, winv_ref) = refs[:n], refs[n : n + 2]
    out_ref = refs[n + 2 + aliased]
    part = pieces[0].shape[1]
    for m, piece in enumerate(pieces):
        for i in range(part):
            z = (me_ref[0] ^ m) * part + i
            out_ref[:, z] = f_ref[:, z] - winv_ref[:, z] * piece[:, i]


def last_update(me, pieces, f, winv, chunk, before):
    n = len(pieces)
    count, depth, width, length = f.shape
    part = pieces[0].shape[1]
    piece = pl.BlockSpec((count, part, ROWS, length), lambda i, me: (0, 0, i, 0))
    layers = pl.BlockSpec((count, n * part, ROWS, length), lambda i, me: (0, chunk, i, 0))
    aliased = len(before)
    size = n * pieces[0].size
    return pl.pallas_call(
        functools.partial(last_kernel, n, aliased),
        grid_spec=pltpu.PrefetchScalarGridSpec(
            num_scalar_prefetch=1,
            grid=(width // ROWS,),
            in_specs=[piece] * n + [layers] * 2 + [pl.BlockSpec(memory_space=pl.ANY)] * aliased,
            out_specs=layers,
        ),
        out_shape=jax.ShapeDtypeStruct(f.shape, jnp.float32),
        input_output_aliases={n + 3: 0} if aliased else {},
        compiler_params=pltpu.CompilerParams(vmem_limit_bytes=24 * MIB),
        cost_estimate=pl.CostEstimate(flops=size * 2, bytes_accessed=size * 16, transcendentals=0),
        name="last_update",
    )(me, *pieces, f, winv, *before)


def exchange(pieces):
    n = len(pieces) + 1
    return [
        lax.ppermute(piece, "inst", [(i, i ^ m) for i in range(n)]) for m, piece in enumerate(pieces, 1)
    ]


def halos(field):
    slabs = lax.axis_size("space")
    upward = [(i, i + 1) for i in range(slabs - 1)]
    downward = [(i + 1, i) for i in range(slabs - 1)]
    return lax.ppermute(field[:, -1:], "space", upward), lax.ppermute(field[:, :1], "space", downward)


def body(field_start, source, material, face_flags, disp_table, perm_table):
    count, depth, width, length = field_start.shape
    n = lax.axis_size("inst")
    slabs = lax.axis_size("space")
    chunks = min(CHUNKS, depth // n)
    part = depth // (chunks * n)
    me = lax.axis_index("inst")
    me_array = me.reshape(1).astype(jnp.int32)

    going = [
        [
            lax.dynamic_slice_in_dim(field_start, (chunk * n + (me ^ m)) * part, part, axis=1)
            for m in range(1, n)
        ]
        for chunk in range(chunks)
    ]
    there = [exchange(pieces) for pieces in going]

    moments = (me * count + jnp.arange(count)).astype(jnp.float32)
    tide = 1.0 + 0.5 * jnp.cos(2.0 * jnp.pi * moments / NT)
    mat = spectral_blocks(me, n, count)
    kappa, speed, top = prep(disp_table, perm_table, tide, material, face_flags)
    below = lax.ppermute(top, "space", [(i, i + 1) for i in range(slabs - 1)])
    low, high = halos(field_start)
    plain, winv = stencil(False, tide, field_start, low, high, face_flags, source, kappa, speed, below)

    back = []
    for chunk in range(chunks):
        own, *rest = apply_time(me_array, field_start, there[chunk], mat, chunk)
        back.append([own] + exchange(rest))

    whole = []
    there = []
    for chunk in range(chunks):
        *whole, = first_update(me_array, back[chunk], plain, winv, field_start, chunk, whole)
        whole, sends = whole[:2], whole[2:]
        there.append(exchange(sends))
    residual, middle = whole

    low, high = halos(middle)
    base = stencil(True, tide, middle, low, high, face_flags, source, kappa, speed, below, winv)

    back = []
    for chunk in range(chunks):
        own, *rest = apply_time(me_array, middle, there[chunk], mat, chunk)
        back.append([own] + exchange(rest))

    field = []
    for chunk in range(chunks):
        field = [last_update(me_array, back[chunk], base, winv, chunk, field)]
    return (residual, field[0])


def solution(mesh):
    return jax.shard_map(
        body,
        mesh=mesh,
        in_specs=(
            P("inst", "space", None, None),
            P("inst", "space", None, None),
            P("space", None, None),
            P("inst", None, "space", None, None),
            P(),
            P(),
        ),
        out_specs=(P("inst", "space", None, None), P("inst", "space", None, None)),
        check_vma=False,
    )
```

time: 487 us -> 197 us (0.40)
  waiting for transfers between devices: 209 us -> 62.2 us
  local copies, waits for them, and re-layouts: 122 us -> 27.3 us
  matrix products: 83 us -> 0 us
  Pallas kernels: 0 us -> 50.9 us
  other arithmetic: 39.7 us -> 0.31 us
  starting transfers between devices: 13.7 us -> 52.5 us
  between operations: 14.5 us -> 0.98 us
    all_gather x2 -> x0, waiting for transfers between devices: 208 us -> none  [coupled(): piece = lax.all_gather(field, 'inst', axis=0, tiled=True)]
    dot_general x2 -> x0, matrix products: 83 us -> none  [coupled(): jnp.dot(dmat_rows, flat, precision=lax.Precision.HIGHEST, preferred_eleme...]
    ppermute x5 -> x29, waiting for transfers between devices: 0.01 us -> 62.2 us  [the longest x24 58.6 us: exchange(): lax.ppermute(piece, 'inst', [(i, i ^ m) for i in range(n)])]
    pallas_call x0 -> x11, Pallas kernels: none -> 50.9 us  [the longest x2 26 us: stencil(): pl.pallas_call(functools.partial(stencil_kernel, second), grid=(count,),...]
    unnamed x23 -> x34, local copies, waits for them, and re-layouts: 68.6 us -> 22.4 us
    ppermute x5 -> x29, starting transfers between devices: 13.7 us -> 52.5 us  [the longest x24 28.4 us: exchange(): lax.ppermute(piece, 'inst', [(i, i ^ m) for i in range(n)])]
    slice x12 -> x2, local copies, waits for them, and re-layouts: 30.3 us -> 1.11 us  [halos(): field[:, :1]]
    mul x2 -> x1, other arithmetic: 25.6 us -> 0.16 us  [spectral_blocks(): omega_scale * jnp.where(diff == 0, 0.0, 0.5 * parity * jnp.cos(angle) / s...]
  transfers between devices with their start and end apart: 7 -> 29, of which waited for: 2 -> 10; matrix products, arithmetic and copies ran while one was open for 32% -> 1% of each run, Pallas kernels for 0% -> 25%
where the time goes in v1:
time: 197 us; the launch traced here: 194 us
  waiting for transfers between devices  62.2 us (32%)
  starting transfers between devices  52.5 us (27%)
  Pallas kernels  50.9 us (26%)
  local copies, waits for them, and re-layouts  27.3 us (14%)
    ppermute x24, waiting for transfers between devices, exchange(): lax.ppermute(piece, 'inst', [(i, i ^ m) for i in range(n)])  58.6 us
    ppermute x24, starting transfers between devices, exchange(): lax.ppermute(piece, 'inst', [(i, i ^ m) for i in range(n)])  28.4 us
    pallas_call x2, Pallas kernels, stencil(): pl.pallas_call(functools.partial(stencil_kernel, second), grid=(count,),...  26 us
    unnamed x34, local copies, waits for them, and re-layouts  22.4 us
    pallas_call x4, Pallas kernels, apply_time(): pl.pallas_call(functools.partial(apply_kernel, n), grid_spec=pltpu.Prefet...  11.1 us
    ppermute x2, starting transfers between devices, halos(): lax.ppermute(field[:, -1:], 'space', upward)  10.6 us
    ppermute x2, starting transfers between devices, halos(): lax.ppermute(field[:, :1], 'space', downward)  9.99 us
    pallas_call x2, Pallas kernels, first_update(): pl.pallas_call(functools.partial(first_kernel, n, aliased), grid_spec=plt...  7.77 us
  transfers between devices with their start and end apart: 29, of which 10 were waited for; matrix products, arithmetic and copies ran while one was open for 1% of the time, Pallas kernels for 25%

profile of v1, /device:TPU:9, one launch (start us, length us, event | category | flops | bytes accessed | tf_op | source)
XLA Modules:
  0.0 194.2 jit_solution(6254772884360853035)
XLA Ops:
  0.7 3.6 %constant_dynamic-slice_fusion = (f32[8,2,64,128]{3,2,1,0:T(8,128)}, f32[8,2,64,128]{3,2,1,0:T(8,128)}, f32[8,2,64,128]{3,2,1,0:T(8,128)}, f32[8,2,64,128]{3,2,1...) fusion(f32[8,16,64,128]{3,2,1,0:T(8,128)} %refs_6_.3, s32[]{:T(128)S(6)} %select_n.89, ...), kind=kLoop, calls=%fused_computation.26 | loop fusion | bytes 6291480 | tf_op jit(solution)/shard_map/dynamic_slice | solution.py:315
  4.2 2.2 %collective-permute-start.11 = (f32[8,2,64,128]{3,2,1,0:T(8,128)}, f32[8,2,64,128]{3,2,1,0:T(8,128)S(1)}, u32[]{:S(2)}, u32[]{:S(2)}) collective-permute-start(f32[8,2,64,128]{3,2,1,0:T(8,128)} %get-tuple-element.66), channel_id=1, source_target_pairs={{0,24},{8,16},{16,8},{24,0},{1,25},{9,17},{17,9},{25,1},{2,26},{10... | collective-permute-start | bytes 1572872 | tf_op jit(solution)/shard_map/ppermute | solution.py:293
  6.4 0.2 collective-permute-start.10
  6.6 0.3 collective-permute-start.9
  6.9 2.2 %collective-permute-start.2 = (f32[8,2,64,128]{3,2,1,0:T(8,128)}, f32[8,2,64,128]{3,2,1,0:T(8,128)S(1)}, u32[]{:S(2)}, u32[]{:S(2)}) collective-permute-start(f32[8,2,64,128]{3,2,1,0:T(8,128)} %get-tuple-element.69), channel_id=1, source_target_pairs={{0,24},{8,16},{16,8},{24,0},{1,25},{9,17},{17,9},{25,1},{2,26},{10... | collective-permute-start | bytes 1572872 | tf_op jit(solution)/shard_map/ppermute | solution.py:293
  9.1 0.2 collective-permute-start.1
  9.3 0.2 fusion.3
  9.6 0.1 copy.13
  9.7 8.5 %collective-permute-done.11.refs_2_ = f32[8,2,64,128]{3,2,1,0:T(8,128)S(1)} collective-permute-done((f32[8,2,64,128]{3,2,1,0:T(8,128)}, f32[8,2,64,128]{3,2,1,0:T(8,128)S(1)}, u32[]{:S(2)}, u32[]{:S(2)}) %collective-permute-start.11) | collective-permute-done | bytes 524320 | tf_op jit(solution)/shard_map/ppermute | solution.py:293
  18.2 1.2 collective-permute-start
  19.5 1.1 fusion.17
  20.6 10.9 %collective-permute-done.10.refs_1_ = f32[8,2,64,128]{3,2,1,0:T(8,128)S(1)} collective-permute-done((f32[8,2,64,128]{3,2,1,0:T(8,128)}, f32[8,2,64,128]{3,2,1,0:T(8,128)S(1)}, u32[]{:S(2)}, u32[]{:S(2)}) %collective-permute-start.10) | collective-permute-done | bytes 524320 | tf_op jit(solution)/shard_map/ppermute | solution.py:293
  31.4 2.6 %collective-permute-start.7 = (f32[8,1,64,128]{3,2,1,0:T(8,128)S(1)}, f32[8,1,64,128]{3,2,1,0:T(8,128)S(1)}, u32[]{:S(2)}, u32[]{:S(2)}) collective-permute-start(f32[8,1,64,128]{3,2,1,0:T(8,128)S(1)} %get-tuple-element.72), channel_id=1, source_target_pairs={{1,0},{2,1},{3,2},{4,3},{5,4},{6,5},{7,6},{9,8},{10,9},{11,10},{12... | collective-permute-start | bytes 786440 | tf_op jit(solution)/shard_map/ppermute | solution.py:301
  34.1 0.8 copy-done.10
  34.9 3.1 %collective-permute-start.6 = (f32[8,1,64,128]{3,2,1,0:T(8,128)S(1)}, f32[8,1,64,128]{3,2,1,0:T(8,128)}, u32[]{:S(2)}, u32[]{:S(2)}) collective-permute-start(f32[8,1,64,128]{3,2,1,0:T(8,128)S(1)} %get-tuple-element.73), channel_id=1, source_target_pairs={{0,1},{1,2},{2,3},{3,4},{4,5},{5,6},{6,7},{8,9},{9,10},{10,11},{11... | collective-permute-start | bytes 786440 | tf_op jit(solution)/shard_map/ppermute | solution.py:301
  38.0 2.2 %copy-done = f32[8,16,64,128]{3,2,1,0:T(8,128)S(1)} copy-done((f32[8,16,64,128]{3,2,1,0:T(8,128)S(1)}, f32[8,16,64,128]{3,2,1,0:T(8,128)}, u32[]{:S(2)}) %copy-start) | copy-done | bytes 4194328
  40.2 1.0 copy-done.11
  41.2 3.2 %apply_time.5 = (f32[8,2,64,128]{3,2,1,0:T(8,128)S(1)}, f32[8,2,64,128]{3,2,1,0:T(8,128)}, f32[8,2,64,128]{3,2,1,0:T(8,128)}, f32[8,2,64,128]{3,2,1,0:T(8,128)}) custom-call(s32[1]{0:T(128)} %bitcast.me_ref, f32[8,16,64,128]{3,2,1,0:T(8,128)S(1)} %copy-done, f32[8,2,64,128]{3,2,1,0:T(8,128)S(1)} %copy-done.11, ...), custom_call_target="tpu_custom_call" | custom-call | flops 1610612736 | bytes 4194304 | tf_op jit(solution)/shard_map/apply_time/pallas_call | solution.py:194
  44.4 1.3 collective-permute-start.12
  45.7 7.2 %collective-permute-done.1.refs_1_ = f32[8,2,64,128]{3,2,1,0:T(8,128)S(1)} collective-permute-done((f32[8,2,64,128]{3,2,1,0:T(8,128)}, f32[8,2,64,128]{3,2,1,0:T(8,128)S(1)}, u32[]{:S(2)}, u32[]{:S(2)}) %collective-permute-start.1) | collective-permute-done | bytes 524320 | tf_op jit(solution)/shard_map/ppermute | solution.py:293
  52.9 3.1 %collective-permute-start.13 = (f32[8,2,64,128]{3,2,1,0:T(8,128)}, f32[8,2,64,128]{3,2,1,0:T(8,128)}, u32[]{:S(2)}, u32[]{:S(2)}) collective-permute-start(f32[8,2,64,128]{3,2,1,0:T(8,128)} %get-tuple-element.44), channel_id=1, source_target_pairs={{0,16},{8,24},{16,0},{24,8},{1,17},{9,25},{17,1},{25,9},{2,18},{10... | collective-permute-start | bytes 1572872 | tf_op jit(solution)/shard_map/ppermute | solution.py:293
  56.0 3.2 %apply_time.4 = (f32[8,2,64,128]{3,2,1,0:T(8,128)S(1)}, f32[8,2,64,128]{3,2,1,0:T(8,128)}, f32[8,2,64,128]{3,2,1,0:T(8,128)}, f32[8,2,64,128]{3,2,1,0:T(8,128)}) custom-call(s32[1]{0:T(128)} %bitcast.me_ref, f32[8,16,64,128]{3,2,1,0:T(8,128)S(1)} %copy-done, f32[8,2,64,128]{3,2,1,0:T(8,128)S(1)} %collective-permute-done.refs_0_, ...), custom_call_target="tpu_custom_call" | custom-call | flops 1610612736 | bytes 4194304 | tf_op jit(solution)/shard_map/apply_time/pallas_call | solution.py:194
  59.1 0.7 copy-done.13
  59.9 1.2 collective-permute-start.3
  61.2 4.6 %copy-done.2 = s32[8,3,16,64,128]{4,3,2,1,0:T(8,128)S(1)} copy-done((s32[8,3,16,64,128]{4,3,2,1,0:T(8,128)S(1)}, s32[8,3,16,64,128]{4,3,2,1,0:T(8,128)}, u32[]{:S(2)}) %copy-start.2) | copy-done | bytes 12582936
  65.7 1.0 copy-done.12
  66.8 1.2 prep.1
  68.0 3.5 %collective-permute-start.8 = (f32[9,64,128]{2,1,0:T(8,128)S(1)}, f32[9,64,128]{2,1,0:T(8,128)S(1)}, u32[]{:S(2)}, u32[]{:S(2)}) collective-permute-start(f32[9,64,128]{2,1,0:T(8,128)S(1)} %get-tuple-element.39), channel_id=1, source_target_pairs={{0,1},{1,2},{2,3},{3,4},{4,5},{5,6},{6,7},{8,9},{9,10},{10,11},{11... | collective-permute-start | bytes 884744 | tf_op jit(solution)/shard_map/ppermute | solution.py:326
  71.5 3.6 %collective-permute-done.8.below_k_ref.below_f_ref = f32[9,64,128]{2,1,0:T(8,128)S(1)} collective-permute-done((f32[9,64,128]{2,1,0:T(8,128)S(1)}, f32[9,64,128]{2,1,0:T(8,128)S(1)}, u32[]{:S(2)}, u32[]{:S(2)}) %collective-permute-start.8) | collective-permute-done | bytes 294944 | tf_op jit(solution)/shard_map/ppermute | solution.py:326
  75.2 1.7 collective-permute-start.4
  76.8 0.2 collective-permute-start.5
  77.1 4.6 %copy-done.3 = s32[8,3,16,64,128]{4,3,2,1,0:T(8,128)S(1)} copy-done((s32[8,3,16,64,128]{4,3,2,1,0:T(8,128)S(1)}, s32[8,3,16,64,128]{4,3,2,1,0:T(8,128)}, u32[]{:S(2)}) %copy-start.3) | copy-done | bytes 12582936
  81.7 14.0 %stencil_one.1 = (f32[8,16,64,128]{3,2,1,0:T(8,128)S(1)}, f32[8,16,64,128]{3,2,1,0:T(8,128)S(1)}) custom-call(f32[8]{0:T(128)S(1)} %multiply_add_fusion.tide_ref, f32[8,16,64,128]{3,2,1,0:T(8,128)S(1)} %copy-done.1, f32[8,1,64,128]{3,2,1,0:T(8,128)} %collective-permute-done.6.low_ref, f32[8,1,64,128]{3,2,1,0:T(8,128)S(1)} %copy-done.14, ...), custom_call_target="tpu_custom_call" | custom-call | flops 62914560 | bytes 29360128 | tf_op jit(solution)/shard_map/stencil_one/pallas_call | solution.py:153
  95.7 1.0 copy-done.7
  96.7 4.0 %first_update.2 = (f32[8,16,64,128]{3,2,1,0:T(8,128)}, f32[8,16,64,128]{3,2,1,0:T(8,128)S(1)}, f32[8,2,64,128]{3,2,1,0:T(8,128)S(1)}, f32[8,2,64,128]{3,2,1,0:T(8,128)S(1)}, f32[8,2,64,128]{3,2,1,0:T(8,128)S(1)}) custom-call(s32[1]{0:T(128)} %bitcast.me_ref, f32[8,2,64,128]{3,2,1,0:T(8,128)S(1)} %get-tuple-element.42.refs_0_, ...), custom_call_target="tpu_custom_call" | custom-call | flops 1572864 | bytes 14680064 | tf_op jit(solution)/shard_map/first_update/pallas_call | solution.py:240
  100.7 1.0 collective-permute-start.23
  101.7 1.4 collective-permute-start.24
  103.1 0.2 collective-permute-start.25
  103.3 0.8 copy-done.8
  104.1 1.0 copy-done.9
  105.2 3.8 %first_update.3 = (f32[8,16,64,128]{3,2,1,0:T(8,128)}, f32[8,16,64,128]{3,2,1,0:T(8,128)S(1)}, f32[8,2,64,128]{3,2,1,0:T(8,128)S(1)}, f32[8,2,64,128]{3,2,1,0:T(8,128)S(1)}, f32[8,2,64,128]{3,2,1,0:T(8,128)S(1)}) custom-call(s32[1]{0:T(128)} %bitcast.me_ref, ...), custom_call_target="tpu_custom_call", output_to_operand_aliasing={{0}: (8, {}), {1}: (9, {})} | custom-call | flops 1572864 | bytes 14680064 | tf_op jit(solution)/shard_map/first_update/pallas_call | solution.py:240
  109.0 1.0 collective-permute-start.15
  110.0 1.4 collective-permute-start.16
  111.4 0.8 collective-permute-done.23.refs_0_
  112.2 2.1 %collective-permute-start.17 = (f32[8,2,64,128]{3,2,1,0:T(8,128)S(1)}, f32[8,2,64,128]{3,2,1,0:T(8,128)S(1)}, u32[]{:S(2)}, u32[]{:S(2)}) collective-permute-start(f32[8,2,64,128]{3,2,1,0:T(8,128)S(1)} %get-tuple-element.52), channel_id=1, source_target_pairs={{0,24},{8,16},{16,8},{24,0},{1,25},{9,17},{17,9},{25,1},{2,26},{10... | collective-permute-start | bytes 1572872 | tf_op jit(solution)/shard_map/ppermute | solution.py:293
  114.4 9.8 %collective-permute-done.25.refs_2_ = f32[8,2,64,128]{3,2,1,0:T(8,128)S(1)} collective-permute-done((f32[8,2,64,128]{3,2,1,0:T(8,128)S(1)}, f32[8,2,64,128]{3,2,1,0:T(8,128)S(1)}, u32[]{:S(2)}, u32[]{:S(2)}) %collective-permute-start.25) | collective-permute-done | bytes 524320 | tf_op jit(solution)/shard_map/ppermute | solution.py:293
  124.2 2.4 %apply_time.7 = (f32[8,2,64,128]{3,2,1,0:T(8,128)S(1)}, f32[8,2,64,128]{3,2,1,0:T(8,128)S(1)}, f32[8,2,64,128]{3,2,1,0:T(8,128)S(1)}, f32[8,2,64,128]{3,2,1,0:T(8,128)S(1)}) custom-call(s32[1]{0:T(128)} %bitcast.me_ref, f32[8,16,64,128]{3,2,1,0:T(8,128)S(1)} %get-tuple-element.49.own_ref.u_ref, f32[8,2,64,128]{3,2,1,0:T(8,128)S(1)} %collective-permute-done.23.refs_0_, ...), custom_call_target="tpu_custom_call" | custom-call | flops 1610612736 | bytes 4194304 | tf_op jit(solution)/shard_map/apply_time/pallas_call | solution.py:194
  126.6 1.5 collective-permute-start.26
  128.1 7.4 %collective-permute-start.22 = (f32[8,1,64,128]{3,2,1,0:T(8,128)S(1)}, f32[8,1,64,128]{3,2,1,0:T(8,128)S(1)}, u32[]{:S(2)}, u32[]{:S(2)}) collective-permute-start(f32[8,1,64,128]{3,2,1,0:T(8,128)S(1)} %get-tuple-element.64), channel_id=1, source_target_pairs={{1,0},{2,1},{3,2},{4,3},{5,4},{6,5},{7,6},{9,8},{10,9},{11,10},{12... | collective-permute-start | bytes 786440 | tf_op jit(solution)/shard_map/ppermute | solution.py:301
  135.5 7.5 %collective-permute-start.21 = (f32[8,1,64,128]{3,2,1,0:T(8,128)S(1)}, f32[8,1,64,128]{3,2,1,0:T(8,128)S(1)}, u32[]{:S(2)}, u32[]{:S(2)}) collective-permute-start(f32[8,1,64,128]{3,2,1,0:T(8,128)S(1)} %get-tuple-element.65), channel_id=1, source_target_pairs={{0,1},{1,2},{2,3},{3,4},{4,5},{5,6},{6,7},{8,9},{9,10},{10,11},{11... | collective-permute-start | bytes 786440 | tf_op jit(solution)/shard_map/ppermute | solution.py:301
  143.0 1.0 collective-permute-start.27
  144.0 2.7 %collective-permute-done.17.refs_2_ = f32[8,2,64,128]{3,2,1,0:T(8,128)S(1)} collective-permute-done((f32[8,2,64,128]{3,2,1,0:T(8,128)S(1)}, f32[8,2,64,128]{3,2,1,0:T(8,128)S(1)}, u32[]{:S(2)}, u32[]{:S(2)}) %collective-permute-start.17) | collective-permute-done | bytes 524320 | tf_op jit(solution)/shard_map/ppermute | solution.py:293
  146.7 1.5 collective-permute-start.28
  148.2 2.4 %apply_time.6 = (f32[8,2,64,128]{3,2,1,0:T(8,128)S(1)}, f32[8,2,64,128]{3,2,1,0:T(8,128)S(1)}, f32[8,2,64,128]{3,2,1,0:T(8,128)S(1)}, f32[8,2,64,128]{3,2,1,0:T(8,128)S(1)}) custom-call(s32[1]{0:T(128)} %bitcast.me_ref, f32[8,16,64,128]{3,2,1,0:T(8,128)S(1)} %get-tuple-element.49.own_ref.u_ref, f32[8,2,64,128]{3,2,1,0:T(8,128)S(1)} %collective-permute-done.15.refs_0_, ...), custom_call_target="tpu_custom_call" | custom-call | flops 1610612736 | bytes 4194304 | tf_op jit(solution)/shard_map/apply_time/pallas_call | solution.py:194
  150.6 0.2 collective-permute-start.18
  150.8 1.0 collective-permute-start.19
  151.9 5.4 %collective-permute-done.26.refs_1_ = f32[8,2,64,128]{3,2,1,0:T(8,128)S(1)} collective-permute-done((f32[8,2,64,128]{3,2,1,0:T(8,128)S(1)}, f32[8,2,64,128]{3,2,1,0:T(8,128)S(1)}, u32[]{:S(2)}, u32[]{:S(2)}) %collective-permute-start.26) | collective-permute-done | bytes 524320 | tf_op jit(solution)/shard_map/ppermute | solution.py:293
  157.3 2.1 %collective-permute-start.20 = (f32[8,2,64,128]{3,2,1,0:T(8,128)S(1)}, f32[8,2,64,128]{3,2,1,0:T(8,128)S(1)}, u32[]{:S(2)}, u32[]{:S(2)}) collective-permute-start(f32[8,2,64,128]{3,2,1,0:T(8,128)S(1)} %get-tuple-element.56), channel_id=1, source_target_pairs={{0,24},{8,16},{16,8},{24,0},{1,25},{9,17},{17,9},{25,1},{2,26},{10... | collective-permute-start | bytes 1572872 | tf_op jit(solution)/shard_map/ppermute | solution.py:293
  159.4 4.6 %copy-done.4 = s32[8,3,16,64,128]{4,3,2,1,0:T(8,128)S(1)} copy-done((s32[8,3,16,64,128]{4,3,2,1,0:T(8,128)S(1)}, s32[8,3,16,64,128]{4,3,2,1,0:T(8,128)}, u32[]{:S(2)}) %copy-start.4) | copy-done | bytes 12582936
  163.9 12.0 %stencil_two.1.refs_4_ = f32[8,16,64,128]{3,2,1,0:T(8,128)S(1)} custom-call(f32[8]{0:T(128)S(1)} %multiply_add_fusion.tide_ref, f32[8,16,64,128]{3,2,1,0:T(8,128)S(1)} %get-tuple-element.49.own_ref.u_ref, f32[8,1,64,128]{3,2,1,0:T(8,128)S(1)} %collective-permute-done.21.low_ref, f32[8,1,64,128]{3,2,1,0:T(8,128)S(1)} %collective-permute-done.22.high_ref, ...), custom_call_target="tpu_custom_call" | custom-call | flops 62914560 | bytes 29360128 | tf_op jit(solution)/shard_map/stencil_two/pallas_call | solution.py:153
  175.9 2.5 %last_update.2.refs_6_ = f32[8,16,64,128]{3,2,1,0:T(8,128)} custom-call(s32[1]{0:T(128)} %bitcast.me_ref, f32[8,2,64,128]{3,2,1,0:T(8,128)S(1)} %get-tuple-element.60.refs_0_, f32[8,2,64,128]{3,2,1,0:T(8,128)S(1)} %collective-permute-done.26.refs_1_, f32[8,2,64,128]{3,2,1,0:T(8,128)S(1)} %collective-permute-done.27.refs_2_, ...), custom_call_target="tpu_custom_call" | custom-call | flops 1048576 | bytes 8388608 | tf_op jit(solution)/shard_map/last_update/pallas_call | solution.py:274
  178.4 1.4 collective-permute-done.18.refs_1_
  179.8 12.0 %collective-permute-done.20.refs_3_ = f32[8,2,64,128]{3,2,1,0:T(8,128)S(1)} collective-permute-done((f32[8,2,64,128]{3,2,1,0:T(8,128)S(1)}, f32[8,2,64,128]{3,2,1,0:T(8,128)S(1)}, u32[]{:S(2)}, u32[]{:S(2)}) %collective-permute-start.20) | collective-permute-done | bytes 524320 | tf_op jit(solution)/shard_map/ppermute | solution.py:293
  191.7 2.4 %last_update.3 = f32[8,16,64,128]{3,2,1,0:T(8,128)} custom-call(s32[1]{0:T(128)} %bitcast.me_ref, f32[8,2,64,128]{3,2,1,0:T(8,128)S(1)} %get-tuple-element.53.refs_0_, f32[8,2,64,128]{3,2,1,0:T(8,128)S(1)} %collective-permute-done.18.refs_1_, f32[8,2,64,128]{3,2,1,0:T(8,128)S(1)} %collective-permute-done.19.refs_2_, ...), custom_call_target="tpu_custom_call", output_to_operand_aliasing={{}: (7, {})} | custom-call | flops 1048576 | bytes 8388608 | tf_op jit(solution)/shard_map/last_update/pallas_call | solution.py:274
  (51 shorter events, 0.4 us)
Async XLA Ops:
  4.2 13.9 %collective-permute-start.11 = (f32[8,2,64,128]{3,2,1,0:T(8,128)}, f32[8,2,64,128]{3,2,1,0:T(8,128)S(1)}, u32[]{:S(2)}, u32[]{:S(2)}) collective-permute-start(f32[8,2,64,128]{3,2,1,0:T(8,128)} %get-tuple-element.66), channel_id=1, source_target_pairs={{0,24},{8,16},{16,8},{24,0},{1,25},{9,17},{17,9},{25,1},{2,26},{10... | collective-permute-start | bytes 1572872 | tf_op jit(solution)/shard_map/ppermute | solution.py:293
  6.4 25.0 %collective-permute-start.10 = (f32[8,2,64,128]{3,2,1,0:T(8,128)}, f32[8,2,64,128]{3,2,1,0:T(8,128)S(1)}, u32[]{:S(2)}, u32[]{:S(2)}) collective-permute-start(f32[8,2,64,128]{3,2,1,0:T(8,128)} %get-tuple-element.67), channel_id=1, source_target_pairs={{0,16},{8,24},{16,0},{24,8},{1,17},{9,25},{17,1},{25,9},{2,18},{10... | collective-permute-start | bytes 1572872 | tf_op jit(solution)/shard_map/ppermute | solution.py:293
  6.6 27.4 %collective-permute-start.9 = (f32[8,2,64,128]{3,2,1,0:T(8,128)}, f32[8,2,64,128]{3,2,1,0:T(8,128)S(1)}, u32[]{:S(2)}, u32[]{:S(2)}) collective-permute-start(f32[8,2,64,128]{3,2,1,0:T(8,128)} %get-tuple-element.68), channel_id=1, source_target_pairs={{0,8},{8,0},{16,24},{24,16},{1,9},{9,1},{17,25},{25,17},{2,10},{10... | collective-permute-start | bytes 1572872 | tf_op jit(solution)/shard_map/ppermute | solution.py:293
  6.9 37.5 %collective-permute-start.2 = (f32[8,2,64,128]{3,2,1,0:T(8,128)}, f32[8,2,64,128]{3,2,1,0:T(8,128)S(1)}, u32[]{:S(2)}, u32[]{:S(2)}) collective-permute-start(f32[8,2,64,128]{3,2,1,0:T(8,128)} %get-tuple-element.69), channel_id=1, source_target_pairs={{0,24},{8,16},{16,8},{24,0},{1,25},{9,17},{17,9},{25,1},{2,26},{10... | collective-permute-start | bytes 1572872 | tf_op jit(solution)/shard_map/ppermute | solution.py:293
  9.1 43.8 %collective-permute-start.1 = (f32[8,2,64,128]{3,2,1,0:T(8,128)}, f32[8,2,64,128]{3,2,1,0:T(8,128)S(1)}, u32[]{:S(2)}, u32[]{:S(2)}) collective-permute-start(f32[8,2,64,128]{3,2,1,0:T(8,128)} %get-tuple-element.70), channel_id=1, source_target_pairs={{0,16},{8,24},{16,0},{24,8},{1,17},{9,25},{17,1},{25,9},{2,18},{10... | collective-permute-start | bytes 1572872 | tf_op jit(solution)/shard_map/ppermute | solution.py:293
  18.2 37.8 %collective-permute-start = (f32[8,2,64,128]{3,2,1,0:T(8,128)}, f32[8,2,64,128]{3,2,1,0:T(8,128)S(1)}, u32[]{:S(2)}, u32[]{:S(2)}) collective-permute-start(f32[8,2,64,128]{3,2,1,0:T(8,128)} %get-tuple-element.71), channel_id=1, source_target_pairs={{0,8},{8,0},{16,24},{24,16},{1,9},{9,1},{17,25},{25,17},{2,10},{10... | collective-permute-start | bytes 1572872 | tf_op jit(solution)/shard_map/ppermute | solution.py:293
  31.4 27.7 %collective-permute-start.7 = (f32[8,1,64,128]{3,2,1,0:T(8,128)S(1)}, f32[8,1,64,128]{3,2,1,0:T(8,128)S(1)}, u32[]{:S(2)}, u32[]{:S(2)}) collective-permute-start(f32[8,1,64,128]{3,2,1,0:T(8,128)S(1)} %get-tuple-element.72), channel_id=1, source_target_pairs={{1,0},{2,1},{3,2},{4,3},{5,4},{6,5},{7,6},{9,8},{10,9},{11,10},{12... | collective-permute-start | bytes 786440 | tf_op jit(solution)/shard_map/ppermute | solution.py:301
  34.1 0.8 copy-start.10
  34.9 33.1 %collective-permute-start.6 = (f32[8,1,64,128]{3,2,1,0:T(8,128)S(1)}, f32[8,1,64,128]{3,2,1,0:T(8,128)}, u32[]{:S(2)}, u32[]{:S(2)}) collective-permute-start(f32[8,1,64,128]{3,2,1,0:T(8,128)S(1)} %get-tuple-element.73), channel_id=1, source_target_pairs={{0,1},{1,2},{2,3},{3,4},{4,5},{5,6},{6,7},{8,9},{9,10},{10,11},{11... | collective-permute-start | bytes 786440 | tf_op jit(solution)/shard_map/ppermute | solution.py:301
  38.0 2.2 %copy-start = (f32[8,16,64,128]{3,2,1,0:T(8,128)S(1)}, f32[8,16,64,128]{3,2,1,0:T(8,128)}, u32[]{:S(2)}) copy-start(f32[8,16,64,128]{3,2,1,0:T(8,128)} %refs_6_.3) | copy-start | bytes 12582916
  40.2 1.0 copy-start.11
  44.4 16.7 %copy-start.15 = (f32[8]{0:T(128)S(1)}, f32[8]{0:T(128)}, u32[]{:S(2)}) copy-start(f32[8]{0:T(128)} %disp_ref.1) | copy-start | bytes 100
  44.4 16.7 %copy-start.16 = (f32[8]{0:T(128)S(1)}, f32[8]{0:T(128)}, u32[]{:S(2)}) copy-start(f32[8]{0:T(128)} %perm_ref.1) | copy-start | bytes 100
  44.4 32.4 %collective-permute-start.12 = (f32[8,2,64,128]{3,2,1,0:T(8,128)}, f32[8,2,64,128]{3,2,1,0:T(8,128)S(1)}, u32[]{:S(2)}, u32[]{:S(2)}) collective-permute-start(f32[8,2,64,128]{3,2,1,0:T(8,128)} %get-tuple-element.43), channel_id=1, source_target_pairs={{0,8},{8,0},{16,24},{24,16},{1,9},{9,1},{17,25},{25,17},{2,10},{10... | collective-permute-start | bytes 1572872 | tf_op jit(solution)/shard_map/ppermute | solution.py:293
  52.9 42.7 %collective-permute-start.13 = (f32[8,2,64,128]{3,2,1,0:T(8,128)}, f32[8,2,64,128]{3,2,1,0:T(8,128)}, u32[]{:S(2)}, u32[]{:S(2)}) collective-permute-start(f32[8,2,64,128]{3,2,1,0:T(8,128)} %get-tuple-element.44), channel_id=1, source_target_pairs={{0,16},{8,24},{16,0},{24,8},{1,17},{9,25},{17,1},{25,9},{2,18},{10... | collective-permute-start | bytes 1572872 | tf_op jit(solution)/shard_map/ppermute | solution.py:293
  56.0 39.7 %collective-permute-start.14 = (f32[8,2,64,128]{3,2,1,0:T(8,128)}, f32[8,2,64,128]{3,2,1,0:T(8,128)}, u32[]{:S(2)}, u32[]{:S(2)}) collective-permute-start(f32[8,2,64,128]{3,2,1,0:T(8,128)} %get-tuple-element.45), channel_id=1, source_target_pairs={{0,24},{8,16},{16,8},{24,0},{1,25},{9,17},{17,9},{25,1},{2,26},{10... | collective-permute-start | bytes 1572872 | tf_op jit(solution)/shard_map/ppermute | solution.py:293
  59.1 0.7 copy-start.13
  59.9 43.2 %collective-permute-start.3 = (f32[8,2,64,128]{3,2,1,0:T(8,128)}, f32[8,2,64,128]{3,2,1,0:T(8,128)}, u32[]{:S(2)}, u32[]{:S(2)}) collective-permute-start(f32[8,2,64,128]{3,2,1,0:T(8,128)} %get-tuple-element.34), channel_id=1, source_target_pairs={{0,8},{8,0},{16,24},{24,16},{1,9},{9,1},{17,25},{25,17},{2,10},{10... | collective-permute-start | bytes 1572872 | tf_op jit(solution)/shard_map/ppermute | solution.py:293
  61.2 4.6 %copy-start.2 = (s32[8,3,16,64,128]{4,3,2,1,0:T(8,128)S(1)}, s32[8,3,16,64,128]{4,3,2,1,0:T(8,128)}, u32[]{:S(2)}) copy-start(s32[8,3,16,64,128]{4,3,2,1,0:T(8,128)} %flags_ref.5) | copy-start | bytes 37748740
  65.7 1.0 copy-start.12
  66.8 10.3 %copy-start.1 = (f32[8,16,64,128]{3,2,1,0:T(8,128)S(1)}, f32[8,16,64,128]{3,2,1,0:T(8,128)}, u32[]{:S(2)}) copy-start(f32[8,16,64,128]{3,2,1,0:T(8,128)} %refs_6_.3) | copy-start | bytes 12582916
  66.8 10.3 %copy-start.5 = (f32[8,16,64,128]{3,2,1,0:T(8,128)S(1)}, f32[8,16,64,128]{3,2,1,0:T(8,128)}, u32[]{:S(2)}) copy-start(f32[8,16,64,128]{3,2,1,0:T(8,128)} %src_ref.3) | copy-start | bytes 12582916
  66.8 10.3 %copy-start.14 = (f32[8,1,64,128]{3,2,1,0:T(8,128)S(1)}, f32[8,1,64,128]{3,2,1,0:T(8,128)}, u32[]{:S(2)}) copy-start(f32[8,1,64,128]{3,2,1,0:T(8,128)} %copy-done.13) | copy-start | bytes 786436
  68.0 7.2 %collective-permute-start.8 = (f32[9,64,128]{2,1,0:T(8,128)S(1)}, f32[9,64,128]{2,1,0:T(8,128)S(1)}, u32[]{:S(2)}, u32[]{:S(2)}) collective-permute-start(f32[9,64,128]{2,1,0:T(8,128)S(1)} %get-tuple-element.39), channel_id=1, source_target_pairs={{0,1},{1,2},{2,3},{3,4},{4,5},{5,6},{6,7},{8,9},{9,10},{10,11},{11... | collective-permute-start | bytes 884744 | tf_op jit(solution)/shard_map/ppermute | solution.py:326
  75.2 28.2 %collective-permute-start.4 = (f32[8,2,64,128]{3,2,1,0:T(8,128)}, f32[8,2,64,128]{3,2,1,0:T(8,128)S(1)}, u32[]{:S(2)}, u32[]{:S(2)}) collective-permute-start(f32[8,2,64,128]{3,2,1,0:T(8,128)} %get-tuple-element.35), channel_id=1, source_target_pairs={{0,16},{8,24},{16,0},{24,8},{1,17},{9,25},{17,1},{25,9},{2,18},{10... | collective-permute-start | bytes 1572872 | tf_op jit(solution)/shard_map/ppermute | solution.py:293
  76.8 18.8 %copy-start.6 = (f32[8,2,64,128]{3,2,1,0:T(8,128)}, f32[8,2,64,128]{3,2,1,0:T(8,128)S(1)}, u32[]{:S(2)}) copy-start(f32[8,2,64,128]{3,2,1,0:T(8,128)S(1)} %collective-permute-done.12.refs_1_) | copy-start | bytes 1572868
  76.8 26.5 %collective-permute-start.5 = (f32[8,2,64,128]{3,2,1,0:T(8,128)}, f32[8,2,64,128]{3,2,1,0:T(8,128)S(1)}, u32[]{:S(2)}, u32[]{:S(2)}) collective-permute-start(f32[8,2,64,128]{3,2,1,0:T(8,128)} %get-tuple-element.36), channel_id=1, source_target_pairs={{0,24},{8,16},{16,8},{24,0},{1,25},{9,17},{17,9},{25,1},{2,26},{10... | collective-permute-start | bytes 1572872 | tf_op jit(solution)/shard_map/ppermute | solution.py:293
  77.1 4.6 %copy-start.3 = (s32[8,3,16,64,128]{4,3,2,1,0:T(8,128)S(1)}, s32[8,3,16,64,128]{4,3,2,1,0:T(8,128)}, u32[]{:S(2)}) copy-start(s32[8,3,16,64,128]{4,3,2,1,0:T(8,128)} %flags_ref.5) | copy-start | bytes 37748740
  95.7 1.0 copy-start.7
  100.7 11.6 %collective-permute-start.23 = (f32[8,2,64,128]{3,2,1,0:T(8,128)S(1)}, f32[8,2,64,128]{3,2,1,0:T(8,128)S(1)}, u32[]{:S(2)}, u32[]{:S(2)}) collective-permute-start(f32[8,2,64,128]{3,2,1,0:T(8,128)S(1)} %get-tuple-element.57), channel_id=1, source_target_pairs={{0,8},{8,0},{16,24},{24,16},{1,9},{9,1},{17,25},{25,17},{2,10},{10... | collective-permute-start | bytes 1572872 | tf_op jit(solution)/shard_map/ppermute | solution.py:293
  101.7 12.7 %collective-permute-start.24 = (f32[8,2,64,128]{3,2,1,0:T(8,128)S(1)}, f32[8,2,64,128]{3,2,1,0:T(8,128)S(1)}, u32[]{:S(2)}, u32[]{:S(2)}) collective-permute-start(f32[8,2,64,128]{3,2,1,0:T(8,128)S(1)} %get-tuple-element.58), channel_id=1, source_target_pairs={{0,16},{8,24},{16,0},{24,8},{1,17},{9,25},{17,1},{25,9},{2,18},{10... | collective-permute-start | bytes 1572872 | tf_op jit(solution)/shard_map/ppermute | solution.py:293
  103.1 21.1 %collective-permute-start.25 = (f32[8,2,64,128]{3,2,1,0:T(8,128)S(1)}, f32[8,2,64,128]{3,2,1,0:T(8,128)S(1)}, u32[]{:S(2)}, u32[]{:S(2)}) collective-permute-start(f32[8,2,64,128]{3,2,1,0:T(8,128)S(1)} %get-tuple-element.59), channel_id=1, source_target_pairs={{0,24},{8,16},{16,8},{24,0},{1,25},{9,17},{17,9},{25,1},{2,26},{10... | collective-permute-start | bytes 1572872 | tf_op jit(solution)/shard_map/ppermute | solution.py:293
  103.3 0.8 copy-start.8
  104.1 1.0 copy-start.9
  109.0 26.5 %collective-permute-start.15 = (f32[8,2,64,128]{3,2,1,0:T(8,128)S(1)}, f32[8,2,64,128]{3,2,1,0:T(8,128)S(1)}, u32[]{:S(2)}, u32[]{:S(2)}) collective-permute-start(f32[8,2,64,128]{3,2,1,0:T(8,128)S(1)} %get-tuple-element.50), channel_id=1, source_target_pairs={{0,8},{8,0},{16,24},{24,16},{1,9},{9,1},{17,25},{25,17},{2,10},{10... | collective-permute-start | bytes 1572872 | tf_op jit(solution)/shard_map/ppermute | solution.py:293
  110.0 33.0 %collective-permute-start.16 = (f32[8,2,64,128]{3,2,1,0:T(8,128)S(1)}, f32[8,2,64,128]{3,2,1,0:T(8,128)S(1)}, u32[]{:S(2)}, u32[]{:S(2)}) collective-permute-start(f32[8,2,64,128]{3,2,1,0:T(8,128)S(1)} %get-tuple-element.51), channel_id=1, source_target_pairs={{0,16},{8,24},{16,0},{24,8},{1,17},{9,25},{17,1},{25,9},{2,18},{10... | collective-permute-start | bytes 1572872 | tf_op jit(solution)/shard_map/ppermute | solution.py:293
  112.2 34.5 %collective-permute-start.17 = (f32[8,2,64,128]{3,2,1,0:T(8,128)S(1)}, f32[8,2,64,128]{3,2,1,0:T(8,128)S(1)}, u32[]{:S(2)}, u32[]{:S(2)}) collective-permute-start(f32[8,2,64,128]{3,2,1,0:T(8,128)S(1)} %get-tuple-element.52), channel_id=1, source_target_pairs={{0,24},{8,16},{16,8},{24,0},{1,25},{9,17},{17,9},{25,1},{2,26},{10... | collective-permute-start | bytes 1572872 | tf_op jit(solution)/shard_map/ppermute | solution.py:293
  126.6 30.7 %collective-permute-start.26 = (f32[8,2,64,128]{3,2,1,0:T(8,128)S(1)}, f32[8,2,64,128]{3,2,1,0:T(8,128)S(1)}, u32[]{:S(2)}, u32[]{:S(2)}) collective-permute-start(f32[8,2,64,128]{3,2,1,0:T(8,128)S(1)} %get-tuple-element.61), channel_id=1, source_target_pairs={{0,8},{8,0},{16,24},{24,16},{1,9},{9,1},{17,25},{25,17},{2,10},{10... | collective-permute-start | bytes 1572872 | tf_op jit(solution)/shard_map/ppermute | solution.py:293
  128.1 22.5 %collective-permute-start.22 = (f32[8,1,64,128]{3,2,1,0:T(8,128)S(1)}, f32[8,1,64,128]{3,2,1,0:T(8,128)S(1)}, u32[]{:S(2)}, u32[]{:S(2)}) collective-permute-start(f32[8,1,64,128]{3,2,1,0:T(8,128)S(1)} %get-tuple-element.64), channel_id=1, source_target_pairs={{1,0},{2,1},{3,2},{4,3},{5,4},{6,5},{7,6},{9,8},{10,9},{11,10},{12... | collective-permute-start | bytes 786440 | tf_op jit(solution)/shard_map/ppermute | solution.py:301
  135.5 15.3 %collective-permute-start.21 = (f32[8,1,64,128]{3,2,1,0:T(8,128)S(1)}, f32[8,1,64,128]{3,2,1,0:T(8,128)S(1)}, u32[]{:S(2)}, u32[]{:S(2)}) collective-permute-start(f32[8,1,64,128]{3,2,1,0:T(8,128)S(1)} %get-tuple-element.65), channel_id=1, source_target_pairs={{0,1},{1,2},{2,3},{3,4},{4,5},{5,6},{6,7},{8,9},{9,10},{10,11},{11... | collective-permute-start | bytes 786440 | tf_op jit(solution)/shard_map/ppermute | solution.py:301
  143.0 32.9 %collective-permute-start.27 = (f32[8,2,64,128]{3,2,1,0:T(8,128)S(1)}, f32[8,2,64,128]{3,2,1,0:T(8,128)S(1)}, u32[]{:S(2)}, u32[]{:S(2)}) collective-permute-start(f32[8,2,64,128]{3,2,1,0:T(8,128)S(1)} %get-tuple-element.62), channel_id=1, source_target_pairs={{0,16},{8,24},{16,0},{24,8},{1,17},{9,25},{17,1},{25,9},{2,18},{10... | collective-permute-start | bytes 1572872 | tf_op jit(solution)/shard_map/ppermute | solution.py:293
  146.7 29.2 %collective-permute-start.28 = (f32[8,2,64,128]{3,2,1,0:T(8,128)S(1)}, f32[8,2,64,128]{3,2,1,0:T(8,128)S(1)}, u32[]{:S(2)}, u32[]{:S(2)}) collective-permute-start(f32[8,2,64,128]{3,2,1,0:T(8,128)S(1)} %get-tuple-element.63), channel_id=1, source_target_pairs={{0,24},{8,16},{16,8},{24,0},{1,25},{9,17},{17,9},{25,1},{2,26},{10... | collective-permute-start | bytes 1572872 | tf_op jit(solution)/shard_map/ppermute | solution.py:293
  150.6 29.2 %collective-permute-start.18 = (f32[8,2,64,128]{3,2,1,0:T(8,128)S(1)}, f32[8,2,64,128]{3,2,1,0:T(8,128)S(1)}, u32[]{:S(2)}, u32[]{:S(2)}) collective-permute-start(f32[8,2,64,128]{3,2,1,0:T(8,128)S(1)} %get-tuple-element.54), channel_id=1, source_target_pairs={{0,8},{8,0},{16,24},{24,16},{1,9},{9,1},{17,25},{25,17},{2,10},{10... | collective-permute-start | bytes 1572872 | tf_op jit(solution)/shard_map/ppermute | solution.py:293
  150.8 28.9 %collective-permute-start.19 = (f32[8,2,64,128]{3,2,1,0:T(8,128)S(1)}, f32[8,2,64,128]{3,2,1,0:T(8,128)S(1)}, u32[]{:S(2)}, u32[]{:S(2)}) collective-permute-start(f32[8,2,64,128]{3,2,1,0:T(8,128)S(1)} %get-tuple-element.55), channel_id=1, source_target_pairs={{0,16},{8,24},{16,0},{24,8},{1,17},{9,25},{17,1},{25,9},{2,18},{10... | collective-permute-start | bytes 1572872 | tf_op jit(solution)/shard_map/ppermute | solution.py:293
  157.3 34.5 %collective-permute-start.20 = (f32[8,2,64,128]{3,2,1,0:T(8,128)S(1)}, f32[8,2,64,128]{3,2,1,0:T(8,128)S(1)}, u32[]{:S(2)}, u32[]{:S(2)}) collective-permute-start(f32[8,2,64,128]{3,2,1,0:T(8,128)S(1)} %get-tuple-element.56), channel_id=1, source_target_pairs={{0,24},{8,16},{16,8},{24,0},{1,25},{9,17},{17,9},{25,1},{2,26},{10... | collective-permute-start | bytes 1572872 | tf_op jit(solution)/shard_map/ppermute | solution.py:293
  159.4 4.6 %copy-start.4 = (s32[8,3,16,64,128]{4,3,2,1,0:T(8,128)S(1)}, s32[8,3,16,64,128]{4,3,2,1,0:T(8,128)}, u32[]{:S(2)}) copy-start(s32[8,3,16,64,128]{4,3,2,1,0:T(8,128)} %flags_ref.5) | copy-start | bytes 37748740

commit v2 on v1

v2 whole, which is shorter than its diff:
```python
import functools

import jax
import jax.numpy as jnp
from jax import lax
from jax.experimental import pallas as pl
from jax.experimental.pallas import tpu as pltpu
from jax.sharding import PartitionSpec as P

NT = 32


omega_scale = 0.25
decay_rate = 0.3
relax_weight = 0.8

CHUNKS = 2
PARTS = 2
SUB = 8
VMEM = 20 << 20
COST = pl.CostEstimate(flops=1 << 10, bytes_accessed=1 << 10, transcendentals=0)


def spectral_blocks(me, n, count):
    spots = jnp.arange(NT)
    moments = (me ^ (spots // count)) * count + spots % count
    diff = moments[:, None] - moments[None, :]
    angle = jnp.pi * diff.astype(jnp.float32) / NT
    parity = 1.0 - 2.0 * (diff % 2).astype(jnp.float32)
    safe = jnp.where(diff == 0, 1.0, jnp.sin(angle))
    dmat = omega_scale * jnp.where(diff == 0, 0.0, 0.5 * parity * jnp.cos(angle) / safe)
    rows = jnp.repeat(jnp.repeat(dmat, SUB, 0), SUB, 1)
    lane = jnp.arange(NT * SUB) % SUB
    return jnp.where(lane[:, None] == lane[None, :], rows, 0.0)


def in_hbm(*arrays):
    return [pltpu.with_memory_space_constraint(array, pltpu.HBM) for array in arrays]


def cut_kernel(me_ref, *refs):
    half = len(refs) // 2
    for source, out in zip(refs[:half], refs[half:]):
        out[...] = source[...]


def cut(me, field, n, chunk, part):
    count, depth, width, length = field.shape

    def block(m):
        return pl.BlockSpec(
            (count, 1, width, length), lambda i, me: (0, (chunk * n + (me[0] ^ m)) * part + i, 0, 0)
        )

    piece = pl.BlockSpec((count, 1, width, length), lambda i, me: (0, i, 0, 0))
    return pl.pallas_call(
        cut_kernel,
        grid_spec=pltpu.PrefetchScalarGridSpec(
            num_scalar_prefetch=1,
            grid=(part,),
            in_specs=[block(m) for m in range(1, n)],
            out_specs=[piece] * (n - 1),
        ),
        out_shape=[jax.ShapeDtypeStruct((count, part, width, length), jnp.float32)] * (n - 1),
        compiler_params=pltpu.CompilerParams(vmem_limit_bytes=VMEM),
        cost_estimate=COST,
        name="cut",
    )(me, *in_hbm(*[field] * (n - 1)))


def prep_kernel(
    disp_ref, perm_ref, tide_ref, material_ref, flags_ref, bottom_ref, last_ref, kappa_ref, speed_ref, up_ref, down_ref
):
    depth = material_ref.shape[0]
    count = flags_ref.shape[0]

    def layer(z, carry):
        material = material_ref[z]
        kappa = jnp.zeros(material.shape, jnp.float32)
        speed = jnp.zeros(material.shape, jnp.float32)
        for klass in range(disp_ref.shape[0]):
            here = material == klass
            kappa = jnp.where(here, disp_ref[klass], kappa)
            speed = jnp.where(here, perm_ref[klass], speed)
        kappa_ref[z] = kappa
        speed_ref[z] = speed
        return carry

    lax.fori_loop(0, depth, layer, 0)
    up_ref[2 * count] = kappa_ref[depth - 1]
    for t in range(count):
        flow = speed_ref[depth - 1] * tide_ref[t]
        up_ref[t] = last_ref[t, 0]
        up_ref[count + t] = jnp.where(flags_ref[t, 0, 0] != 0, -flow, flow)
        down_ref[t] = bottom_ref[t, 0]


def prep(disp_table, perm_table, tide, material, face_flags, field):
    count, _, depth, width, length = face_flags.shape
    smem = pl.BlockSpec(memory_space=pltpu.SMEM)
    cells = pl.BlockSpec((depth, width, length), lambda i: (0, 0, 0))
    up = (2 * count + 1, width, length)
    down = (count, width, length)
    return pl.pallas_call(
        prep_kernel,
        grid=(1,),
        in_specs=[
            smem,
            smem,
            smem,
            cells,
            pl.BlockSpec((count, 1, 1, width, length), lambda i: (0, 0, depth - 1, 0, 0)),
            pl.BlockSpec((count, 1, width, length), lambda i: (0, 0, 0, 0)),
            pl.BlockSpec((count, 1, width, length), lambda i: (0, depth - 1, 0, 0)),
        ],
        out_specs=[
            cells,
            cells,
            pl.BlockSpec(up, lambda i: (0, 0, 0)),
            pl.BlockSpec(down, lambda i: (0, 0, 0)),
        ],
        out_shape=[
            jax.ShapeDtypeStruct(material.shape, jnp.float32),
            jax.ShapeDtypeStruct(material.shape, jnp.float32),
            jax.ShapeDtypeStruct(up, jnp.float32),
            jax.ShapeDtypeStruct(down, jnp.float32),
        ],
        compiler_params=pltpu.CompilerParams(vmem_limit_bytes=VMEM),
        cost_estimate=COST,
        name="prep",
    )(disp_table, perm_table, tide, *in_hbm(material, face_flags, field, field))


def stencil_kernel(
    second, first, aliased, tide_ref, u_ref, low_ref, high_ref, flags_ref, src_ref, kappa_ref, speed_ref, below_k_ref, below_f_ref, *rest
):
    if second:
        winv_ref, out_ref = rest[0], rest[-1]
    else:
        out_ref, winv_ref = rest[aliased:]
    depth, width, length = u_ref.shape[1:]
    tide = tide_ref[first + pl.program_id(0)]
    row = lax.broadcasted_iota(jnp.int32, (width, length), 0)
    col = lax.broadcasted_iota(jnp.int32, (width, length), 1)
    last_row, last_col = row == width - 1, col == length - 1

    below_k, below_f = below_k_ref[0], below_f_ref[0]
    au_low = (below_k + jnp.maximum(below_f, 0.0)) * low_ref[0]
    b_low = below_k - jnp.minimum(below_f, 0.0)

    def layer(z, carry, u_up):
        au_low, b_low = carry
        u = u_ref[0, z]
        kappa = kappa_ref[z]
        full = kappa + speed_ref[z] * tide

        def coefs(dim):
            back = flags_ref[0, dim, z] != 0
            return jnp.where(back, kappa, full), jnp.where(back, full, kappa)

        a, b = coefs(0)
        total = b * u_up + au_low
        diag = (decay_rate + a) + b_low
        next_carry = (a * u, b)
        for dim, last in ((1, last_row), (2, last_col)):
            a, b = coefs(dim)
            size = u.shape[dim - 1]
            b = jnp.where(last, 0.0, b)
            au = jnp.where(last, 0.0, a * u)
            total = total + b * pltpu.roll(u, size - 1, dim - 1) + pltpu.roll(au, 1, dim - 1)
            if not second:
                diag = diag + (a + pltpu.roll(b, 1, dim - 1))
        if second:
            out_ref[0, z] = (1.0 - relax_weight) * u + winv_ref[0, z] * (total + src_ref[0, z])
        else:
            out_ref[0, z] = diag * u - total - src_ref[0, z]
            winv_ref[0, z] = relax_weight / diag
        return next_carry

    carry = lax.fori_loop(0, depth - 1, lambda z, c: layer(z, c, u_ref[0, z + 1]), (au_low, b_low))
    layer(depth - 1, carry, high_ref[0])


def stencil(second, part, tide, u, low, high, flags, src, kappa, speed, below, winv=None, before=()):
    count, depth, width, length = u.shape
    first, stop = count * part // PARTS, count * (part + 1) // PARTS
    field = pl.BlockSpec((1, depth, width, length), lambda t: (first + t, 0, 0, 0))
    plane = pl.BlockSpec((1, width, length), lambda t: (first + t, 0, 0))
    cells = pl.BlockSpec((depth, width, length), lambda t: (0, 0, 0))
    in_specs = [
        pl.BlockSpec(memory_space=pltpu.SMEM),
        field,
        plane,
        plane,
        pl.BlockSpec((1, 3, depth, width, length), lambda t: (first + t, 0, 0, 0, 0)),
        field,
        cells,
        cells,
        pl.BlockSpec((1, width, length), lambda t: (2 * count, 0, 0)),
        pl.BlockSpec((1, width, length), lambda t: (count + first + t, 0, 0)),
    ]
    args = [tide, *in_hbm(u), low, high, *in_hbm(flags, src), kappa, speed, below, below]
    if second:
        in_specs.append(field)
        args.extend(in_hbm(winv))
    aliases = {len(args) + i: i for i in range(len(before))}
    in_specs += [pl.BlockSpec(memory_space=pl.ANY)] * len(before)
    args.extend(in_hbm(*before))
    shape = pltpu.HBM(u.shape, jnp.float32)
    outs = 1 if second else 2
    return pl.pallas_call(
        functools.partial(stencil_kernel, second, first, len(before)),
        grid=(stop - first,),
        in_specs=in_specs,
        out_specs=[field] * outs,
        out_shape=[shape] * outs,
        input_output_aliases=aliases,
        compiler_params=pltpu.CompilerParams(vmem_limit_bytes=VMEM),
        cost_estimate=COST,
        name="stencil_two" if second else "stencil_one",
    )(*args)


def apply_kernel(n, me_ref, own_ref, *refs):
    received, mat_ref, outs = refs[: n - 1], refs[n - 1], refs[n:]
    parts = [own_ref, *received]
    count, _, width, length = own_ref.shape
    groups = width // SUB
    blocks = jnp.concatenate([part[:, 0] for part in parts], 0)
    wide = jnp.concatenate(
        [blocks[:, g * SUB : (g + 1) * SUB].reshape(NT * SUB, length) for g in range(groups)], 1
    )
    product = lax.dot_general(
        mat_ref[...],
        wide,
        (((1,), (0,)), ((), ())),
        precision=lax.Precision.HIGHEST,
        preferred_element_type=jnp.float32,
    )
    for g in range(groups):
        piece = product[:, g * length : (g + 1) * length].reshape(NT, SUB, length)
        for m, out in enumerate(outs):
            out[:, 0, g * SUB : (g + 1) * SUB] = piece[m * count : (m + 1) * count]


def apply_time(me, field, received, mat, chunk):
    n = len(received) + 1
    count, depth, width, length = field.shape
    part = received[0].shape[1]
    piece = pl.BlockSpec((count, 1, width, length), lambda i, me: (0, i, 0, 0))
    shape = jax.ShapeDtypeStruct(received[0].shape, jnp.float32)
    size = n * received[0].size
    return pl.pallas_call(
        functools.partial(apply_kernel, n),
        grid_spec=pltpu.PrefetchScalarGridSpec(
            num_scalar_prefetch=1,
            grid=(part,),
            in_specs=[
                pl.BlockSpec((count, 1, width, length), lambda i, me: (0, (chunk * n + me[0]) * part + i, 0, 0)),
                *([piece] * (n - 1)),
                pl.BlockSpec(mat.shape, lambda i, me: (0, 0)),
            ],
            out_specs=[piece] * n,
        ),
        out_shape=[shape] * n,
        compiler_params=pltpu.CompilerParams(vmem_limit_bytes=VMEM),
        cost_estimate=COST,
        name="apply_time",
    )(me, *in_hbm(field), *received, mat)


ROWS = 16


def first_kernel(n, aliased, me_ref, *refs):
    pieces, (s_ref, winv_ref, u_ref) = refs[:n], refs[n : n + 3]
    res_ref, mid_ref, first_ref, last_ref, *sends = refs[n + 3 + aliased :]
    part = pieces[0].shape[1]
    for m, piece in enumerate(pieces):
        for i in range(part):
            z = (me_ref[0] ^ m) * part + i
            res = s_ref[:, z] + piece[:, i]
            mid = u_ref[:, z] - winv_ref[:, z] * res
            res_ref[:, z] = res
            mid_ref[:, z] = mid
            if m:
                sends[m - 1][:, i] = mid
    first_ref[...] = mid_ref[:, 0]
    last_ref[...] = mid_ref[:, n * part - 1]


def first_update(me, pieces, s, winv, u, chunk, before):
    n = len(pieces)
    count, depth, width, length = u.shape
    part = pieces[0].shape[1]
    piece = pl.BlockSpec((count, part, ROWS, length), lambda i, me: (0, 0, i, 0))
    layers = pl.BlockSpec((count, n * part, ROWS, length), lambda i, me: (0, chunk, i, 0))
    whole = pltpu.HBM(u.shape, jnp.float32)
    aliased = len(before)
    size = n * pieces[0].size
    return pl.pallas_call(
        functools.partial(first_kernel, n, aliased),
        grid_spec=pltpu.PrefetchScalarGridSpec(
            num_scalar_prefetch=1,
            grid=(width // ROWS,),
            in_specs=[piece] * n + [layers] * 3 + [pl.BlockSpec(memory_space=pl.ANY)] * aliased,
            out_specs=[layers] * 2 + [pl.BlockSpec((count, ROWS, length), lambda i, me: (0, i, 0))] * 2 + [piece] * (n - 1),
        ),
        out_shape=[whole] * 2
        + [jax.ShapeDtypeStruct((count, width, length), jnp.float32)] * 2
        + [jax.ShapeDtypeStruct(pieces[0].shape, jnp.float32)] * (n - 1),
        input_output_aliases={n + 4 + i: i for i in range(aliased)},
        compiler_params=pltpu.CompilerParams(vmem_limit_bytes=VMEM),
        cost_estimate=COST,
        name="first_update",
    )(me, *pieces, *in_hbm(s, winv, u, *before))


def last_kernel(piece_ref, base_ref, winv_ref, *refs):
    refs[-1][...] = base_ref[...] - winv_ref[...] * piece_ref[...]


def last_update(spot, piece, base, winv, before):
    count, part, width, length = piece.shape
    layers = pl.BlockSpec((count, 1, width, length), lambda i, spot: (0, spot[0] * part + i, 0, 0))
    aliased = len(before)
    return pl.pallas_call(
        lambda spot_ref, *refs: last_kernel(*refs),
        grid_spec=pltpu.PrefetchScalarGridSpec(
            num_scalar_prefetch=1,
            grid=(part,),
            in_specs=[pl.BlockSpec((count, 1, width, length), lambda i, spot: (0, i, 0, 0)), layers, layers]
            + [pl.BlockSpec(memory_space=pl.ANY)] * aliased,
            out_specs=layers,
        ),
        out_shape=pltpu.HBM(base.shape, jnp.float32),
        input_output_aliases={4: 0} if aliased else {},
        compiler_params=pltpu.CompilerParams(vmem_limit_bytes=VMEM),
        cost_estimate=COST,
        name="last_update",
    )(spot, piece, *in_hbm(base, winv, *before))


def exchange(pieces):
    n = len(pieces) + 1
    return [
        lax.ppermute(piece, "inst", [(i, i ^ m) for i in range(n)]) for m, piece in enumerate(pieces, 1)
    ]


def after(arrays, *first):
    return lax.optimization_barrier((arrays, first))[0]


def upward(plane):
    return lax.ppermute(plane, "space", [(i, i + 1) for i in range(lax.axis_size("space") - 1)])


def downward(plane):
    return lax.ppermute(plane, "space", [(i + 1, i) for i in range(lax.axis_size("space") - 1)])


def body(field_start, source, material, face_flags, disp_table, perm_table):
    count, depth, width, length = field_start.shape
    n = lax.axis_size("inst")
    chunks = min(CHUNKS, depth // n)
    part = depth // (chunks * n)
    me = lax.axis_index("inst")
    me_array = me.reshape(1).astype(jnp.int32)

    going = cut(me_array, field_start, n, 0, part)
    there = [exchange(going)]
    start, flags, material = after((field_start, face_flags, material), *going)

    moments = (me * count + jnp.arange(count)).astype(jnp.float32)
    tide = 1.0 + 0.5 * jnp.cos(2.0 * jnp.pi * moments / NT)
    mat = spectral_blocks(me, n, count)
    kappa, speed, up, down = prep(disp_table, perm_table, tide, material, flags, start)
    below, high = upward(up), downward(down)
    start = after(start, below, high)
    for chunk in range(1, chunks):
        going = cut(me_array, start, n, chunk, part)
        there.append(exchange(going))
        start = after(start, *going)
    shared = (below, high, flags, source, kappa, speed, below)
    first = stencil(False, 0, tide, start, *shared)

    back = []
    there[0] = after(there[0], first)
    for chunk in range(chunks):
        own, *rest = apply_time(me_array, field_start, there[chunk], mat, chunk)
        back.append([own] + exchange(rest))
    for half in range(1, PARTS):
        first = stencil(False, half, tide, after(field_start, back[0][1]), *shared, before=first)
    plain, winv = first

    whole = []
    there = []
    low = high = None
    for chunk in range(chunks):
        if chunk:
            back[chunk] = after(back[chunk], high)
        done = first_update(me_array, back[chunk], plain, winv, field_start, chunk, whole)
        whole, (bottom, last), sends = done[:2], done[2:4], done[4:]
        if chunk == 0:
            high = downward(bottom)
        if chunk == chunks - 1:
            low = upward(last)
        there.append(exchange(sends))
    residual, middle = whole
    there[0] = after(there[0], low)

    back = []
    second = ()
    for chunk in range(chunks):
        own, *rest = apply_time(me_array, middle, there[chunk], mat, chunk)
        back.append([own] + exchange(rest))
        if chunk < PARTS:
            ready = there[1][0] if chunk == 0 else back[0][1]
            now = after(middle, ready)
            second = stencil(True, chunk, tide, now, low, high, face_flags, source, kappa, speed, below, winv, second)
            if chunk == 0:
                there[1] = after(there[1], *second)
    base = second[0]

    field = []
    for chunk in range(chunks):
        for m, piece in enumerate(back[chunk]):
            spot = (chunk * n + (me ^ m)).reshape(1).astype(jnp.int32)
            field = [last_update(spot, piece, base, winv, field)]
    return (residual, field[0])


def solution(mesh):
    return jax.shard_map(
        body,
        mesh=mesh,
        in_specs=(
            P("inst", "space", None, None),
            P("inst", "space", None, None),
            P("space", None, None),
            P("inst", None, "space", None, None),
            P(),
            P(),
        ),
        out_specs=(P("inst", "space", None, None), P("inst", "space", None, None)),
        check_vma=False,
    )
```

time: 197 us -> 191 us (0.970)
  Pallas kernels: 50.9 us -> 87.6 us
  local copies, waits for them, and re-layouts: 27.3 us -> 5.76 us
  waiting for transfers between devices: 62.2 us -> 50.2 us
  starting transfers between devices: 52.5 us -> 42.4 us
    pallas_call x4 -> x14, Pallas kernels: 30.8 us -> 59.1 us  [the longest x4 37.9 us: stencil(): pl.pallas_call(functools.partial(stencil_kernel, second, first, len(befor...]
    unnamed x34 -> x12, local copies, waits for them, and re-layouts: 22.4 us -> 1.63 us
    ppermute x24, waiting for transfers between devices: 58.6 us -> 40.6 us  [exchange(): lax.ppermute(piece, 'inst', [(i, i ^ m) for i in range(n)])]
    ppermute x5 -> x4, starting transfers between devices: 24.1 us -> 17.4 us  [the longest x2 10.4 us: upward(): lax.ppermute(plane, 'space', [(i, i + 1) for i in range(lax.axis_size('sp...]
    ppermute x5 -> x4, waiting for transfers between devices: 3.66 us -> 9.67 us  [the longest x2 9.66 us: downward(): lax.ppermute(plane, 'space', [(i + 1, i) for i in range(lax.axis_size('sp...]
    reshape x4, local copies, waits for them, and re-layouts: 0.23 us -> 4.13 us  [spectral_blocks(): rows = jnp.repeat(jnp.repeat(dmat, SUB, 0), SUB, 1)]
    dynamic_slice x1 -> x0, local copies, waits for them, and re-layouts: 3.57 us -> none  [body(): lax.dynamic_slice_in_dim(field_start, (chunk * n + (me ^ m)) * part, part...]
    pallas_call x4, Pallas kernels: 11.1 us -> 14.6 us  [apply_time(): pl.pallas_call(functools.partial(apply_kernel, n), grid_spec=pltpu.Prefet...]
  transfers between devices with their start and end apart: 29 -> 28, of which waited for: 10 -> 11; matrix products, arithmetic and copies ran while one was open for 1% -> 3% of each run, Pallas kernels for 25% -> 44%
where the time goes in v2:
time: 191 us; the launch traced here: 188 us
  Pallas kernels  87.6 us (46%)
  waiting for transfers between devices  50.2 us (26%)
  starting transfers between devices  42.4 us (22%)
  local copies, waits for them, and re-layouts  5.76 us (3%)
    ppermute x24, waiting for transfers between devices, exchange(): lax.ppermute(piece, 'inst', [(i, i ^ m) for i in range(n)])  40.6 us
    pallas_call x4, Pallas kernels, stencil(): pl.pallas_call(functools.partial(stencil_kernel, second, first, len(befor...  37.9 us
    ppermute x24, starting transfers between devices, exchange(): lax.ppermute(piece, 'inst', [(i, i ^ m) for i in range(n)])  25 us
    pallas_call x8, Pallas kernels, last_update(): pl.pallas_call(lambda spot_ref, *refs: last_kernel(*refs), grid_spec=pltp...  16.5 us
    pallas_call x4, Pallas kernels, apply_time(): pl.pallas_call(functools.partial(apply_kernel, n), grid_spec=pltpu.Prefet...  14.6 us
    pallas_call x2, Pallas kernels, first_update(): pl.pallas_call(functools.partial(first_kernel, n, aliased), grid_spec=plt...  11 us
    ppermute x2, starting transfers between devices, upward(): lax.ppermute(plane, 'space', [(i, i + 1) for i in range(lax.axis_size('sp...  10.4 us
    ppermute x2, waiting for transfers between devices, downward(): lax.ppermute(plane, 'space', [(i + 1, i) for i in range(lax.axis_size('sp...  9.66 us
  transfers between devices with their start and end apart: 28, of which 11 were waited for; matrix products, arithmetic and copies ran while one was open for 3% of the time, Pallas kernels for 44%

profile of v2, /device:TPU:9, one launch (start us, length us, event | category | flops | bytes accessed | tf_op | source)
XLA Modules:
  0.0 188.0 jit_solution(10450193547407319131)
XLA Ops:
  0.7 2.4 %cut.2 = (f32[8,2,64,128]{3,2,1,0:T(8,128)}, f32[8,2,64,128]{3,2,1,0:T(8,128)}, f32[8,2,64,128]{3,2,1,0:T(8,128)}) custom-call(s32[1]{0:T(128)} %bitcast.me_ref.spot_ref, f32[8,16,64,128]{3,2,1,0:T(8,128)} %refs_6_.3, f32[8,16,64,128]{3,2,1,0:T(8,128)} %refs_6_.3, f32[8,16,64,128]{3,2,1,0:T(8,128)} %refs_6_.3), custom_call_target="tpu_custom_call" | custom-call | flops 1024 | bytes 1024 | tf_op jit(solution)/shard_map/cut/pallas_call | solution.py:56
  3.1 2.2 %collective-permute-start.10 = (f32[8,2,64,128]{3,2,1,0:T(8,128)}, f32[8,2,64,128]{3,2,1,0:T(8,128)S(1)}, u32[]{:S(2)}, u32[]{:S(2)}) collective-permute-start(f32[8,2,64,128]{3,2,1,0:T(8,128)} %get-tuple-element.67), channel_id=1, source_target_pairs={{0,24},{8,16},{16,8},{24,0},{1,25},{9,17},{17,9},{25,1},{2,26},{10... | collective-permute-start | bytes 1572872 | tf_op jit(solution)/shard_map/ppermute | solution.py:347
  5.2 0.3 collective-permute-start.8
  5.5 0.2 collective-permute-start.9
  5.8 2.8 %prep.1 = (f32[16,64,128]{2,1,0:T(8,128)S(1)}, f32[16,64,128]{2,1,0:T(8,128)S(1)}, f32[17,64,128]{2,1,0:T(8,128)}, f32[8,64,128]{2,1,0:T(8,128)}) custom-call(f32[8]{0:T(128)S(1)} %copy-done.4, f32[8]{0:T(128)S(1)} %copy-done.5, f32[8]{0:T(128)S(1)} %multiply_add_fusion.tide_ref, s32[16,64,128]{2,1,0:T(8,128)} %material_ref, ...), custom_call_target="tpu_custom_call" | custom-call | flops 1024 | bytes 1024 | tf_op jit(solution)/shard_map/prep/pallas_call | solution.py:104
  8.6 4.6 %collective-permute-start = (f32[17,64,128]{2,1,0:T(8,128)}, f32[17,64,128]{2,1,0:T(8,128)S(1)}, u32[]{:S(2)}, u32[]{:S(2)}) collective-permute-start(f32[17,64,128]{2,1,0:T(8,128)} %get-tuple-element.71), channel_id=1, source_target_pairs={{0,1},{1,2},{2,3},{3,4},{4,5},{5,6},{6,7},{8,9},{9,10},{10,11},{11... | collective-permute-start | bytes 1671176 | tf_op jit(solution)/shard_map/ppermute | solution.py:356
  13.2 1.9 %collective-permute-start.1 = (f32[8,64,128]{2,1,0:T(8,128)}, f32[8,64,128]{2,1,0:T(8,128)S(1)}, u32[]{:S(2)}, u32[]{:S(2)}) collective-permute-start(f32[8,64,128]{2,1,0:T(8,128)} %get-tuple-element.72), channel_id=1, source_target_pairs={{1,0},{2,1},{3,2},{4,3},{5,4},{6,5},{7,6},{9,8},{10,9},{11,10},{12... | collective-permute-start | bytes 786440 | tf_op jit(solution)/shard_map/ppermute | solution.py:360
  15.3 0.7 broadcast_bitcast_fusion.1
  16.0 1.0 copy.21
  17.0 4.5 %collective-permute-done.1.high_ref = f32[8,64,128]{2,1,0:T(8,128)S(1)} collective-permute-done((f32[8,64,128]{2,1,0:T(8,128)}, f32[8,64,128]{2,1,0:T(8,128)S(1)}, u32[]{:S(2)}, u32[]{:S(2)}) %collective-permute-start.1) | collective-permute-done | bytes 262176 | tf_op jit(solution)/shard_map/ppermute | solution.py:360
  21.4 2.3 %cut.3 = (f32[8,2,64,128]{3,2,1,0:T(8,128)}, f32[8,2,64,128]{3,2,1,0:T(8,128)}, f32[8,2,64,128]{3,2,1,0:T(8,128)}) custom-call(s32[1]{0:T(128)} %bitcast.me_ref.spot_ref, f32[8,16,64,128]{3,2,1,0:T(8,128)} %refs_6_.3, f32[8,16,64,128]{3,2,1,0:T(8,128)} %refs_6_.3, f32[8,16,64,128]{3,2,1,0:T(8,128)} %refs_6_.3), custom_call_target="tpu_custom_call" | custom-call | flops 1024 | bytes 1024 | tf_op jit(solution)/shard_map/cut/pallas_call | solution.py:56
  23.8 1.2 collective-permute-start.2
  25.0 0.7 broadcast_bitcast_fusion
  25.7 1.2 collective-permute-start.3
  27.1 1.8 copy.22
  28.9 1.0 compare_select_fusion.refs_3_
  30.0 9.7 %stencil_one.2 = (f32[8,16,64,128]{3,2,1,0:T(8,128)}, f32[8,16,64,128]{3,2,1,0:T(8,128)}) custom-call(f32[8]{0:T(128)S(1)} %multiply_add_fusion.tide_ref, f32[8,16,64,128]{3,2,1,0:T(8,128)} %refs_6_.3, f32[17,64,128]{2,1,0:T(8,128)S(1)} %collective-permute-done.low_ref.below_k_ref.below_f_ref, f32[8,64,128]{2,1,0:T(8,128)S(1)} %collective-permute-done.1.high_ref, ...), custom_call_target="tpu_custom_call" | custom-call | flops 1024 | bytes 1024 | tf_op jit(solution)/shard_map/stencil_one/pallas_call | solution.py:211
  39.7 3.2 %apply_time.5 = (f32[8,2,64,128]{3,2,1,0:T(8,128)S(1)}, f32[8,2,64,128]{3,2,1,0:T(8,128)S(1)}, f32[8,2,64,128]{3,2,1,0:T(8,128)S(1)}, f32[8,2,64,128]{3,2,1,0:T(8,128)S(1)}) custom-call(s32[1]{0:T(128)} %bitcast.me_ref.spot_ref, f32[8,16,64,128]{3,2,1,0:T(8,128)} %refs_6_.3, f32[8,2,64,128]{3,2,1,0:T(8,128)S(1)} %collective-permute-done.8.refs_0_, ...), custom_call_target="tpu_custom_call" | custom-call | flops 1024 | bytes 1024 | tf_op jit(solution)/shard_map/apply_time/pallas_call | solution.py:253
  42.9 1.3 collective-permute-start.11
  44.2 1.2 collective-permute-start.12
  45.7 5.2 %collective-permute-done.4.refs_2_ = f32[8,2,64,128]{3,2,1,0:T(8,128)} collective-permute-done((f32[8,2,64,128]{3,2,1,0:T(8,128)}, f32[8,2,64,128]{3,2,1,0:T(8,128)}, u32[]{:S(2)}, u32[]{:S(2)}) %collective-permute-start.4) | collective-permute-done | bytes 524320 | tf_op jit(solution)/shard_map/ppermute | solution.py:347
  50.9 3.4 %apply_time.4 = (f32[8,2,64,128]{3,2,1,0:T(8,128)S(1)}, f32[8,2,64,128]{3,2,1,0:T(8,128)S(1)}, f32[8,2,64,128]{3,2,1,0:T(8,128)S(1)}, f32[8,2,64,128]{3,2,1,0:T(8,128)S(1)}) custom-call(s32[1]{0:T(128)} %bitcast.me_ref.spot_ref, f32[8,16,64,128]{3,2,1,0:T(8,128)} %refs_6_.3, f32[8,2,64,128]{3,2,1,0:T(8,128)} %collective-permute-done.2.refs_0_, ...), custom_call_target="tpu_custom_call" | custom-call | flops 1024 | bytes 1024 | tf_op jit(solution)/shard_map/apply_time/pallas_call | solution.py:253
  54.3 1.3 collective-permute-start.5
  55.6 6.5 %collective-permute-done.11.refs_1_ = f32[8,2,64,128]{3,2,1,0:T(8,128)S(1)} collective-permute-done((f32[8,2,64,128]{3,2,1,0:T(8,128)S(1)}, f32[8,2,64,128]{3,2,1,0:T(8,128)S(1)}, u32[]{:S(2)}, u32[]{:S(2)}) %collective-permute-start.11) | collective-permute-done | bytes 524320 | tf_op jit(solution)/shard_map/ppermute | solution.py:347
  62.1 0.2 collective-permute-start.6
  62.3 2.2 %collective-permute-start.7 = (f32[8,2,64,128]{3,2,1,0:T(8,128)S(1)}, f32[8,2,64,128]{3,2,1,0:T(8,128)S(1)}, u32[]{:S(2)}, u32[]{:S(2)}) collective-permute-start(f32[8,2,64,128]{3,2,1,0:T(8,128)S(1)} %get-tuple-element.80), channel_id=1, source_target_pairs={{0,24},{8,16},{16,8},{24,0},{1,25},{9,17},{17,9},{25,1},{2,26},{10... | collective-permute-start | bytes 1572872 | tf_op jit(solution)/shard_map/ppermute | solution.py:347
  64.5 9.9 %stencil_one.3 = (f32[8,16,64,128]{3,2,1,0:T(8,128)}, f32[8,16,64,128]{3,2,1,0:T(8,128)}) custom-call(f32[8]{0:T(128)S(1)} %multiply_add_fusion.tide_ref, f32[8,16,64,128]{3,2,1,0:T(8,128)} %refs_6_.3, f32[17,64,128]{2,1,0:T(8,128)S(1)} %collective-permute-done.low_ref.below_k_ref.below_f_ref, ...), custom_call_target="tpu_custom_call", output_to_operand_aliasing={{0}: (10, {}), {1}: (11, {})} | custom-call | flops 1024 | bytes 1024 | tf_op jit(solution)/shard_map/stencil_one/pallas_call | solution.py:211
  74.3 5.5 %first_update.2 = (f32[8,16,64,128]{3,2,1,0:T(8,128)}, f32[8,16,64,128]{3,2,1,0:T(8,128)}, f32[8,64,128]{2,1,0:T(8,128)S(1)}, f32[8,64,128]{2,1,0:T(8,128)}, f32...) custom-call(s32[1]{0:T(128)} %bitcast.me_ref.spot_ref, ...), custom_call_target="tpu_custom_call" | custom-call | flops 1024 | bytes 1024 | tf_op jit(solution)/shard_map/first_update/pallas_call | solution.py:301
  79.8 5.1 %collective-permute-start.14 = (f32[8,64,128]{2,1,0:T(8,128)S(1)}, f32[8,64,128]{2,1,0:T(8,128)S(1)}, u32[]{:S(2)}, u32[]{:S(2)}) collective-permute-start(f32[8,64,128]{2,1,0:T(8,128)S(1)} %get-tuple-element.96), channel_id=1, source_target_pairs={{1,0},{2,1},{3,2},{4,3},{5,4},{6,5},{7,6},{9,8},{10,9},{11,10},{12... | collective-permute-start | bytes 786440 | tf_op jit(solution)/shard_map/ppermute | solution.py:360
  85.0 0.3 collective-permute-start.20
  85.3 5.2 %collective-permute-done.14.high_ref = f32[8,64,128]{2,1,0:T(8,128)S(1)} collective-permute-done((f32[8,64,128]{2,1,0:T(8,128)S(1)}, f32[8,64,128]{2,1,0:T(8,128)S(1)}, u32[]{:S(2)}, u32[]{:S(2)}) %collective-permute-start.14) | collective-permute-done | bytes 262176 | tf_op jit(solution)/shard_map/ppermute | solution.py:360
  90.7 1.2 collective-permute-start.22
  91.9 3.8 %collective-permute-done.7.refs_3_ = f32[8,2,64,128]{3,2,1,0:T(8,128)S(1)} collective-permute-done((f32[8,2,64,128]{3,2,1,0:T(8,128)S(1)}, f32[8,2,64,128]{3,2,1,0:T(8,128)S(1)}, u32[]{:S(2)}, u32[]{:S(2)}) %collective-permute-start.7) | collective-permute-done | bytes 524320 | tf_op jit(solution)/shard_map/ppermute | solution.py:347
  95.8 5.5 %first_update.3 = (f32[8,16,64,128]{3,2,1,0:T(8,128)}, f32[8,16,64,128]{3,2,1,0:T(8,128)}, f32[8,64,128]{2,1,0:T(8,128)}, f32[8,64,128]{2,1,0:T(8,128)S(1)}, f32...) custom-call(s32[1]{0:T(128)} %bitcast.me_ref.spot_ref, ...), custom_call_target="tpu_custom_call", output_to_operand_aliasing={{0}: (8, {}), {1}: (9, {})} | custom-call | flops 1024 | bytes 1024 | tf_op jit(solution)/shard_map/first_update/pallas_call | solution.py:301
  101.3 5.8 %collective-permute-start.18 = (f32[8,64,128]{2,1,0:T(8,128)S(1)}, f32[8,64,128]{2,1,0:T(8,128)S(1)}, u32[]{:S(2)}, u32[]{:S(2)}) collective-permute-start(f32[8,64,128]{2,1,0:T(8,128)S(1)} %get-tuple-element.109), channel_id=1, source_target_pairs={{0,1},{1,2},{2,3},{3,4},{4,5},{5,6},{6,7},{8,9},{9,10},{10,11},{11... | collective-permute-start | bytes 786440 | tf_op jit(solution)/shard_map/ppermute | solution.py:356
  107.1 1.3 collective-permute-start.15
  108.4 1.2 collective-permute-start.16
  109.6 1.8 collective-permute-start.17
  111.4 6.9 %collective-permute-done.22.refs_2_ = f32[8,2,64,128]{3,2,1,0:T(8,128)S(1)} collective-permute-done((f32[8,2,64,128]{3,2,1,0:T(8,128)S(1)}, f32[8,2,64,128]{3,2,1,0:T(8,128)S(1)}, u32[]{:S(2)}, u32[]{:S(2)}) %collective-permute-start.22) | collective-permute-done | bytes 524320 | tf_op jit(solution)/shard_map/ppermute | solution.py:347
  118.3 3.9 %apply_time.7 = (f32[8,2,64,128]{3,2,1,0:T(8,128)S(1)}, f32[8,2,64,128]{3,2,1,0:T(8,128)S(1)}, f32[8,2,64,128]{3,2,1,0:T(8,128)}, f32[8,2,64,128]{3,2,1,0:T(8,128)}) custom-call(s32[1]{0:T(128)} %bitcast.me_ref.spot_ref, f32[8,16,64,128]{3,2,1,0:T(8,128)} %get-tuple-element.121.u_ref.own_ref, f32[8,2,64,128]{3,2,1,0:T(8,128)S(1)} %collective-permute-done.20.refs_0_, ...), custom_call_target="tpu_custom_call" | custom-call | flops 1024 | bytes 1024 | tf_op jit(solution)/shard_map/apply_time/pallas_call | solution.py:253
  122.2 1.2 collective-permute-start.23
  123.4 1.2 collective-permute-start.27
  124.7 4.9 %collective-permute-done.15.refs_0_ = f32[8,2,64,128]{3,2,1,0:T(8,128)S(1)} collective-permute-done((f32[8,2,64,128]{3,2,1,0:T(8,128)S(1)}, f32[8,2,64,128]{3,2,1,0:T(8,128)S(1)}, u32[]{:S(2)}, u32[]{:S(2)}) %collective-permute-start.15) | collective-permute-done | bytes 524320 | tf_op jit(solution)/shard_map/ppermute | solution.py:347
  129.6 1.2 collective-permute-start.26
  130.8 9.2 %stencil_two.2.rest_1_ = f32[8,16,64,128]{3,2,1,0:T(8,128)} custom-call(f32[8]{0:T(128)S(1)} %multiply_add_fusion.tide_ref, f32[8,16,64,128]{3,2,1,0:T(8,128)} %get-tuple-element.121.u_ref.own_ref, f32[8,64,128]{2,1,0:T(8,128)S(1)} %collective-permute-done.18.low_ref, f32[8,64,128]{2,1,0:T(8,128)S(1)} %collective-permute-done.14.high_ref, ...), custom_call_target="tpu_custom_call" | custom-call | flops 1024 | bytes 1024 | tf_op jit(solution)/shard_map/stencil_two/pallas_call | solution.py:211
  139.9 0.9 collective-permute-done.17.refs_2_
  140.8 4.0 %apply_time.6 = (f32[8,2,64,128]{3,2,1,0:T(8,128)S(1)}, f32[8,2,64,128]{3,2,1,0:T(8,128)}, f32[8,2,64,128]{3,2,1,0:T(8,128)}, f32[8,2,64,128]{3,2,1,0:T(8,128)}) custom-call(s32[1]{0:T(128)} %bitcast.me_ref.spot_ref, f32[8,16,64,128]{3,2,1,0:T(8,128)} %get-tuple-element.121.u_ref.own_ref, f32[8,2,64,128]{3,2,1,0:T(8,128)S(1)} %collective-permute-done.15.refs_0_, ...), custom_call_target="tpu_custom_call" | custom-call | flops 1024 | bytes 1024 | tf_op jit(solution)/shard_map/apply_time/pallas_call | solution.py:253
  144.8 0.8 copy-done.2
  145.6 1.2 collective-permute-start.25
  146.8 1.2 collective-permute-start.24
  148.1 4.0 %collective-permute-done.23.refs_0_ = f32[8,2,64,128]{3,2,1,0:T(8,128)S(1)} collective-permute-done((f32[8,2,64,128]{3,2,1,0:T(8,128)S(1)}, f32[8,2,64,128]{3,2,1,0:T(8,128)S(1)}, u32[]{:S(2)}, u32[]{:S(2)}) %collective-permute-start.23) | collective-permute-done | bytes 524320 | tf_op jit(solution)/shard_map/ppermute | solution.py:347
  152.1 0.8 copy-done
  152.9 1.2 collective-permute-start.19
  154.1 9.1 %stencil_two.3.refs_1_ = f32[8,16,64,128]{3,2,1,0:T(8,128)} custom-call(f32[8]{0:T(128)S(1)} %multiply_add_fusion.tide_ref, f32[8,16,64,128]{3,2,1,0:T(8,128)} %get-tuple-element.121.u_ref.own_ref, f32[8,64,128]{2,1,0:T(8,128)S(1)} %collective-permute-done.18.low_ref, ...), custom_call_target="tpu_custom_call", output_to_operand_aliasing={{}: (11, {})} | custom-call | flops 1024 | bytes 1024 | tf_op jit(solution)/shard_map/stencil_two/pallas_call | solution.py:211
  163.2 2.0 %last_update.8.refs_3_ = f32[8,16,64,128]{3,2,1,0:T(8,128)} custom-call(s32[1]{0:T(128)} %bitcast.me_ref.spot_ref, f32[8,2,64,128]{3,2,1,0:T(8,128)S(1)} %get-tuple-element.127.refs_0_, f32[8,16,64,128]{3,2,1,0:T(8,128)} %stencil_two.3.refs_1_, f32[8,16,64,128]{3,2,1,0:T(8,128)} %get-tuple-element.95.refs_5_.rest_0_.refs_2_), custom_call_target="tpu_custom_call" | custom-call | flops 1024 | bytes 1024 | tf_op jit(solution)/shard_map/last_update/pallas_call | solution.py:327
  165.3 2.0 %last_update.9.refs_3_ = f32[8,16,64,128]{3,2,1,0:T(8,128)} custom-call(s32[1]{0:T(128)} %bitcast.9.spot_ref, f32[8,2,64,128]{3,2,1,0:T(8,128)S(1)} %copy-done.1, f32[8,16,64,128]{3,2,1,0:T(8,128)} %stencil_two.3.refs_1_, f32[8,16,64,128]{3,2,1,0:T(8,128)} %get-tuple-element.95.refs_5_.rest_0_.refs_2_, ...), custom_call_target="tpu_custom_call", output_to_operand_aliasing={{}: (4, {})} | custom-call | flops 1024 | bytes 1024 | tf_op jit(solution)/shard_map/last_update/pallas_call | solution.py:327
  167.2 2.0 %last_update.10.refs_3_ = f32[8,16,64,128]{3,2,1,0:T(8,128)} custom-call(s32[1]{0:T(128)} %bitcast.8.spot_ref, f32[8,2,64,128]{3,2,1,0:T(8,128)S(1)} %collective-permute-done.27.refs_0_, f32[8,16,64,128]{3,2,1,0:T(8,128)} %stencil_two.3.refs_1_, f32[8,16,64,128]{3,2,1,0:T(8,128)} %get-tuple-element.95.refs_5_.rest_0_.refs_2_, ...), custom_call_target="tpu_custom_call", output_to_operand_aliasing={{}: (4, {})} | custom-call | flops 1024 | bytes 1024 | tf_op jit(solution)/shard_map/last_update/pallas_call | solution.py:327
  169.2 2.2 %last_update.11.refs_3_ = f32[8,16,64,128]{3,2,1,0:T(8,128)} custom-call(s32[1]{0:T(128)} %bitcast.7.spot_ref, f32[8,2,64,128]{3,2,1,0:T(8,128)} %collective-permute-done.26.refs_0_, f32[8,16,64,128]{3,2,1,0:T(8,128)} %stencil_two.3.refs_1_, f32[8,16,64,128]{3,2,1,0:T(8,128)} %get-tuple-element.95.refs_5_.rest_0_.refs_2_, ...), custom_call_target="tpu_custom_call", output_to_operand_aliasing={{}: (4, {})} | custom-call | flops 1024 | bytes 1024 | tf_op jit(solution)/shard_map/last_update/pallas_call | solution.py:327
  171.4 2.0 %last_update.12.refs_3_ = f32[8,16,64,128]{3,2,1,0:T(8,128)} custom-call(s32[1]{0:T(128)} %bitcast.6.spot_ref, f32[8,2,64,128]{3,2,1,0:T(8,128)S(1)} %copy-done.3, f32[8,16,64,128]{3,2,1,0:T(8,128)} %stencil_two.3.refs_1_, f32[8,16,64,128]{3,2,1,0:T(8,128)} %get-tuple-element.95.refs_5_.rest_0_.refs_2_, ...), custom_call_target="tpu_custom_call", output_to_operand_aliasing={{}: (4, {})} | custom-call | flops 1024 | bytes 1024 | tf_op jit(solution)/shard_map/last_update/pallas_call | solution.py:327
  173.4 1.3 collective-permute-done.25.refs_0_
  174.7 2.1 %last_update.13.refs_3_ = f32[8,16,64,128]{3,2,1,0:T(8,128)} custom-call(s32[1]{0:T(128)} %bitcast.5.spot_ref, f32[8,2,64,128]{3,2,1,0:T(8,128)} %collective-permute-done.25.refs_0_, f32[8,16,64,128]{3,2,1,0:T(8,128)} %stencil_two.3.refs_1_, f32[8,16,64,128]{3,2,1,0:T(8,128)} %get-tuple-element.95.refs_5_.rest_0_.refs_2_, ...), custom_call_target="tpu_custom_call", output_to_operand_aliasing={{}: (4, {})} | custom-call | flops 1024 | bytes 1024 | tf_op jit(solution)/shard_map/last_update/pallas_call | solution.py:327
  176.8 2.1 %last_update.14.refs_3_ = f32[8,16,64,128]{3,2,1,0:T(8,128)} custom-call(s32[1]{0:T(128)} %bitcast.4.spot_ref, f32[8,2,64,128]{3,2,1,0:T(8,128)} %collective-permute-done.24.refs_0_, f32[8,16,64,128]{3,2,1,0:T(8,128)} %stencil_two.3.refs_1_, f32[8,16,64,128]{3,2,1,0:T(8,128)} %get-tuple-element.95.refs_5_.rest_0_.refs_2_, ...), custom_call_target="tpu_custom_call", output_to_operand_aliasing={{}: (4, {})} | custom-call | flops 1024 | bytes 1024 | tf_op jit(solution)/shard_map/last_update/pallas_call | solution.py:327
  179.0 7.0 %collective-permute-done.19.refs_0_ = f32[8,2,64,128]{3,2,1,0:T(8,128)} collective-permute-done((f32[8,2,64,128]{3,2,1,0:T(8,128)}, f32[8,2,64,128]{3,2,1,0:T(8,128)}, u32[]{:S(2)}, u32[]{:S(2)}) %collective-permute-start.19) | collective-permute-done | bytes 524320 | tf_op jit(solution)/shard_map/ppermute | solution.py:347
  185.9 2.1 %last_update.15 = f32[8,16,64,128]{3,2,1,0:T(8,128)} custom-call(s32[1]{0:T(128)} %bitcast.3.spot_ref, f32[8,2,64,128]{3,2,1,0:T(8,128)} %collective-permute-done.19.refs_0_, f32[8,16,64,128]{3,2,1,0:T(8,128)} %stencil_two.3.refs_1_, f32[8,16,64,128]{3,2,1,0:T(8,128)} %get-tuple-element.95.refs_5_.rest_0_.refs_2_, ...), custom_call_target="tpu_custom_call", output_to_operand_aliasing={{}: (4, {})} | custom-call | flops 1024 | bytes 1024 | tf_op jit(solution)/shard_map/last_update/pallas_call | solution.py:327
  (34 shorter events, 0.9 us)
Async XLA Ops:
  0.6 5.1 %copy-start.4 = (f32[8]{0:T(128)S(1)}, f32[8]{0:T(128)}, u32[]{:S(2)}) copy-start(f32[8]{0:T(128)} %disp_ref.1) | copy-start | bytes 100
  0.6 5.1 %copy-start.5 = (f32[8]{0:T(128)S(1)}, f32[8]{0:T(128)}, u32[]{:S(2)}) copy-start(f32[8]{0:T(128)} %perm_ref.1) | copy-start | bytes 100
  3.1 23.9 %collective-permute-start.10 = (f32[8,2,64,128]{3,2,1,0:T(8,128)}, f32[8,2,64,128]{3,2,1,0:T(8,128)S(1)}, u32[]{:S(2)}, u32[]{:S(2)}) collective-permute-start(f32[8,2,64,128]{3,2,1,0:T(8,128)} %get-tuple-element.67), channel_id=1, source_target_pairs={{0,24},{8,16},{16,8},{24,0},{1,25},{9,17},{17,9},{25,1},{2,26},{10... | collective-permute-start | bytes 1572872 | tf_op jit(solution)/shard_map/ppermute | solution.py:347
  5.2 34.5 %collective-permute-start.8 = (f32[8,2,64,128]{3,2,1,0:T(8,128)}, f32[8,2,64,128]{3,2,1,0:T(8,128)S(1)}, u32[]{:S(2)}, u32[]{:S(2)}) collective-permute-start(f32[8,2,64,128]{3,2,1,0:T(8,128)} %get-tuple-element.65), channel_id=1, source_target_pairs={{0,8},{8,0},{16,24},{24,16},{1,9},{9,1},{17,25},{25,17},{2,10},{10... | collective-permute-start | bytes 1572872 | tf_op jit(solution)/shard_map/ppermute | solution.py:347
  5.5 34.2 %collective-permute-start.9 = (f32[8,2,64,128]{3,2,1,0:T(8,128)}, f32[8,2,64,128]{3,2,1,0:T(8,128)S(1)}, u32[]{:S(2)}, u32[]{:S(2)}) collective-permute-start(f32[8,2,64,128]{3,2,1,0:T(8,128)} %get-tuple-element.66), channel_id=1, source_target_pairs={{0,16},{8,24},{16,0},{24,8},{1,17},{9,25},{17,1},{25,9},{2,18},{10... | collective-permute-start | bytes 1572872 | tf_op jit(solution)/shard_map/ppermute | solution.py:347
  8.6 12.8 %collective-permute-start = (f32[17,64,128]{2,1,0:T(8,128)}, f32[17,64,128]{2,1,0:T(8,128)S(1)}, u32[]{:S(2)}, u32[]{:S(2)}) collective-permute-start(f32[17,64,128]{2,1,0:T(8,128)} %get-tuple-element.71), channel_id=1, source_target_pairs={{0,1},{1,2},{2,3},{3,4},{4,5},{5,6},{6,7},{8,9},{9,10},{10,11},{11... | collective-permute-start | bytes 1671176 | tf_op jit(solution)/shard_map/ppermute | solution.py:356
  13.2 8.2 %collective-permute-start.1 = (f32[8,64,128]{2,1,0:T(8,128)}, f32[8,64,128]{2,1,0:T(8,128)S(1)}, u32[]{:S(2)}, u32[]{:S(2)}) collective-permute-start(f32[8,64,128]{2,1,0:T(8,128)} %get-tuple-element.72), channel_id=1, source_target_pairs={{1,0},{2,1},{3,2},{4,3},{5,4},{6,5},{7,6},{9,8},{10,9},{11,10},{12... | collective-permute-start | bytes 786440 | tf_op jit(solution)/shard_map/ppermute | solution.py:360
  23.8 21.7 %collective-permute-start.2 = (f32[8,2,64,128]{3,2,1,0:T(8,128)}, f32[8,2,64,128]{3,2,1,0:T(8,128)}, u32[]{:S(2)}, u32[]{:S(2)}) collective-permute-start(f32[8,2,64,128]{3,2,1,0:T(8,128)} %get-tuple-element.74), channel_id=1, source_target_pairs={{0,8},{8,0},{16,24},{24,16},{1,9},{9,1},{17,25},{25,17},{2,10},{10... | collective-permute-start | bytes 1572872 | tf_op jit(solution)/shard_map/ppermute | solution.py:347
  25.7 20.0 %collective-permute-start.3 = (f32[8,2,64,128]{3,2,1,0:T(8,128)}, f32[8,2,64,128]{3,2,1,0:T(8,128)}, u32[]{:S(2)}, u32[]{:S(2)}) collective-permute-start(f32[8,2,64,128]{3,2,1,0:T(8,128)} %get-tuple-element.75), channel_id=1, source_target_pairs={{0,16},{8,24},{16,0},{24,8},{1,17},{9,25},{17,1},{25,9},{2,18},{10... | collective-permute-start | bytes 1572872 | tf_op jit(solution)/shard_map/ppermute | solution.py:347
  26.9 23.9 %collective-permute-start.4 = (f32[8,2,64,128]{3,2,1,0:T(8,128)}, f32[8,2,64,128]{3,2,1,0:T(8,128)}, u32[]{:S(2)}, u32[]{:S(2)}) collective-permute-start(f32[8,2,64,128]{3,2,1,0:T(8,128)} %get-tuple-element.76), channel_id=1, source_target_pairs={{0,24},{8,16},{16,8},{24,0},{1,25},{9,17},{17,9},{25,1},{2,26},{10... | collective-permute-start | bytes 1572872 | tf_op jit(solution)/shard_map/ppermute | solution.py:347
  42.9 19.1 %collective-permute-start.11 = (f32[8,2,64,128]{3,2,1,0:T(8,128)S(1)}, f32[8,2,64,128]{3,2,1,0:T(8,128)S(1)}, u32[]{:S(2)}, u32[]{:S(2)}) collective-permute-start(f32[8,2,64,128]{3,2,1,0:T(8,128)S(1)} %get-tuple-element.90), channel_id=1, source_target_pairs={{0,8},{8,0},{16,24},{24,16},{1,9},{9,1},{17,25},{25,17},{2,10},{10... | collective-permute-start | bytes 1572872 | tf_op jit(solution)/shard_map/ppermute | solution.py:347
  44.2 30.1 %collective-permute-start.12 = (f32[8,2,64,128]{3,2,1,0:T(8,128)S(1)}, f32[8,2,64,128]{3,2,1,0:T(8,128)S(1)}, u32[]{:S(2)}, u32[]{:S(2)}) collective-permute-start(f32[8,2,64,128]{3,2,1,0:T(8,128)S(1)} %get-tuple-element.91), channel_id=1, source_target_pairs={{0,16},{8,24},{16,0},{24,8},{1,17},{9,25},{17,1},{25,9},{2,18},{10... | collective-permute-start | bytes 1572872 | tf_op jit(solution)/shard_map/ppermute | solution.py:347
  45.5 28.8 %collective-permute-start.13 = (f32[8,2,64,128]{3,2,1,0:T(8,128)S(1)}, f32[8,2,64,128]{3,2,1,0:T(8,128)S(1)}, u32[]{:S(2)}, u32[]{:S(2)}) collective-permute-start(f32[8,2,64,128]{3,2,1,0:T(8,128)S(1)} %get-tuple-element.92), channel_id=1, source_target_pairs={{0,24},{8,16},{16,8},{24,0},{1,25},{9,17},{17,9},{25,1},{2,26},{10... | collective-permute-start | bytes 1572872 | tf_op jit(solution)/shard_map/ppermute | solution.py:347
  54.3 36.4 %collective-permute-start.5 = (f32[8,2,64,128]{3,2,1,0:T(8,128)S(1)}, f32[8,2,64,128]{3,2,1,0:T(8,128)S(1)}, u32[]{:S(2)}, u32[]{:S(2)}) collective-permute-start(f32[8,2,64,128]{3,2,1,0:T(8,128)S(1)} %get-tuple-element.78), channel_id=1, source_target_pairs={{0,8},{8,0},{16,24},{24,16},{1,9},{9,1},{17,25},{25,17},{2,10},{10... | collective-permute-start | bytes 1572872 | tf_op jit(solution)/shard_map/ppermute | solution.py:347
  62.1 29.9 %collective-permute-start.6 = (f32[8,2,64,128]{3,2,1,0:T(8,128)S(1)}, f32[8,2,64,128]{3,2,1,0:T(8,128)S(1)}, u32[]{:S(2)}, u32[]{:S(2)}) collective-permute-start(f32[8,2,64,128]{3,2,1,0:T(8,128)S(1)} %get-tuple-element.79), channel_id=1, source_target_pairs={{0,16},{8,24},{16,0},{24,8},{1,17},{9,25},{17,1},{25,9},{2,18},{10... | collective-permute-start | bytes 1572872 | tf_op jit(solution)/shard_map/ppermute | solution.py:347
  62.3 33.5 %collective-permute-start.7 = (f32[8,2,64,128]{3,2,1,0:T(8,128)S(1)}, f32[8,2,64,128]{3,2,1,0:T(8,128)S(1)}, u32[]{:S(2)}, u32[]{:S(2)}) collective-permute-start(f32[8,2,64,128]{3,2,1,0:T(8,128)S(1)} %get-tuple-element.80), channel_id=1, source_target_pairs={{0,24},{8,16},{16,8},{24,0},{1,25},{9,17},{17,9},{25,1},{2,26},{10... | collective-permute-start | bytes 1572872 | tf_op jit(solution)/shard_map/ppermute | solution.py:347
  79.8 10.7 %collective-permute-start.14 = (f32[8,64,128]{2,1,0:T(8,128)S(1)}, f32[8,64,128]{2,1,0:T(8,128)S(1)}, u32[]{:S(2)}, u32[]{:S(2)}) collective-permute-start(f32[8,64,128]{2,1,0:T(8,128)S(1)} %get-tuple-element.96), channel_id=1, source_target_pairs={{1,0},{2,1},{3,2},{4,3},{5,4},{6,5},{7,6},{9,8},{10,9},{11,10},{12... | collective-permute-start | bytes 786440 | tf_op jit(solution)/shard_map/ppermute | solution.py:360
  85.0 23.4 %collective-permute-start.20 = (f32[8,2,64,128]{3,2,1,0:T(8,128)S(1)}, f32[8,2,64,128]{3,2,1,0:T(8,128)S(1)}, u32[]{:S(2)}, u32[]{:S(2)}) collective-permute-start(f32[8,2,64,128]{3,2,1,0:T(8,128)S(1)} %get-tuple-element.114), channel_id=1, source_target_pairs={{0,8},{8,0},{16,24},{24,16},{1,9},{9,1},{17,25},{25,17},{2,10},{10... | collective-permute-start | bytes 1572872 | tf_op jit(solution)/shard_map/ppermute | solution.py:347
  90.5 19.1 %collective-permute-start.21 = (f32[8,2,64,128]{3,2,1,0:T(8,128)S(1)}, f32[8,2,64,128]{3,2,1,0:T(8,128)S(1)}, u32[]{:S(2)}, u32[]{:S(2)}) collective-permute-start(f32[8,2,64,128]{3,2,1,0:T(8,128)S(1)} %get-tuple-element.115), channel_id=1, source_target_pairs={{0,16},{8,24},{16,0},{24,8},{1,17},{9,25},{17,1},{25,9},{2,18},{10... | collective-permute-start | bytes 1572872 | tf_op jit(solution)/shard_map/ppermute | solution.py:347
  90.7 27.6 %collective-permute-start.22 = (f32[8,2,64,128]{3,2,1,0:T(8,128)S(1)}, f32[8,2,64,128]{3,2,1,0:T(8,128)S(1)}, u32[]{:S(2)}, u32[]{:S(2)}) collective-permute-start(f32[8,2,64,128]{3,2,1,0:T(8,128)S(1)} %get-tuple-element.116), channel_id=1, source_target_pairs={{0,24},{8,16},{16,8},{24,0},{1,25},{9,17},{17,9},{25,1},{2,26},{10... | collective-permute-start | bytes 1572872 | tf_op jit(solution)/shard_map/ppermute | solution.py:347
  101.3 17.0 %collective-permute-start.18 = (f32[8,64,128]{2,1,0:T(8,128)S(1)}, f32[8,64,128]{2,1,0:T(8,128)S(1)}, u32[]{:S(2)}, u32[]{:S(2)}) collective-permute-start(f32[8,64,128]{2,1,0:T(8,128)S(1)} %get-tuple-element.109), channel_id=1, source_target_pairs={{0,1},{1,2},{2,3},{3,4},{4,5},{5,6},{6,7},{8,9},{9,10},{10,11},{11... | collective-permute-start | bytes 786440 | tf_op jit(solution)/shard_map/ppermute | solution.py:356
  107.1 22.5 %collective-permute-start.15 = (f32[8,2,64,128]{3,2,1,0:T(8,128)S(1)}, f32[8,2,64,128]{3,2,1,0:T(8,128)S(1)}, u32[]{:S(2)}, u32[]{:S(2)}) collective-permute-start(f32[8,2,64,128]{3,2,1,0:T(8,128)S(1)} %get-tuple-element.105), channel_id=1, source_target_pairs={{0,8},{8,0},{16,24},{24,16},{1,9},{9,1},{17,25},{25,17},{2,10},{10... | collective-permute-start | bytes 1572872 | tf_op jit(solution)/shard_map/ppermute | solution.py:347
  108.4 31.6 %collective-permute-start.16 = (f32[8,2,64,128]{3,2,1,0:T(8,128)S(1)}, f32[8,2,64,128]{3,2,1,0:T(8,128)S(1)}, u32[]{:S(2)}, u32[]{:S(2)}) collective-permute-start(f32[8,2,64,128]{3,2,1,0:T(8,128)S(1)} %get-tuple-element.106), channel_id=1, source_target_pairs={{0,16},{8,24},{16,0},{24,8},{1,17},{9,25},{17,1},{25,9},{2,18},{10... | collective-permute-start | bytes 1572872 | tf_op jit(solution)/shard_map/ppermute | solution.py:347
  109.6 31.2 %collective-permute-start.17 = (f32[8,2,64,128]{3,2,1,0:T(8,128)S(1)}, f32[8,2,64,128]{3,2,1,0:T(8,128)S(1)}, u32[]{:S(2)}, u32[]{:S(2)}) collective-permute-start(f32[8,2,64,128]{3,2,1,0:T(8,128)S(1)} %get-tuple-element.107), channel_id=1, source_target_pairs={{0,24},{8,16},{16,8},{24,0},{1,25},{9,17},{17,9},{25,1},{2,26},{10... | collective-permute-start | bytes 1572872 | tf_op jit(solution)/shard_map/ppermute | solution.py:347
  122.2 29.9 %collective-permute-start.23 = (f32[8,2,64,128]{3,2,1,0:T(8,128)S(1)}, f32[8,2,64,128]{3,2,1,0:T(8,128)S(1)}, u32[]{:S(2)}, u32[]{:S(2)}) collective-permute-start(f32[8,2,64,128]{3,2,1,0:T(8,128)S(1)} %get-tuple-element.120), channel_id=1, source_target_pairs={{0,8},{8,0},{16,24},{24,16},{1,9},{9,1},{17,25},{25,17},{2,10},{10... | collective-permute-start | bytes 1572872 | tf_op jit(solution)/shard_map/ppermute | solution.py:347
  123.4 43.8 %collective-permute-start.27 = (f32[8,2,64,128]{3,2,1,0:T(8,128)}, f32[8,2,64,128]{3,2,1,0:T(8,128)S(1)}, u32[]{:S(2)}, u32[]{:S(2)}) collective-permute-start(f32[8,2,64,128]{3,2,1,0:T(8,128)} %get-tuple-element.126), channel_id=1, source_target_pairs={{0,16},{8,24},{16,0},{24,8},{1,17},{9,25},{17,1},{25,9},{2,18},{10... | collective-permute-start | bytes 1572872 | tf_op jit(solution)/shard_map/ppermute | solution.py:347
  129.6 39.6 %collective-permute-start.26 = (f32[8,2,64,128]{3,2,1,0:T(8,128)}, f32[8,2,64,128]{3,2,1,0:T(8,128)}, u32[]{:S(2)}, u32[]{:S(2)}) collective-permute-start(f32[8,2,64,128]{3,2,1,0:T(8,128)} %get-tuple-element.125), channel_id=1, source_target_pairs={{0,24},{8,16},{16,8},{24,0},{1,25},{9,17},{17,9},{25,1},{2,26},{10... | collective-permute-start | bytes 1572872 | tf_op jit(solution)/shard_map/ppermute | solution.py:347
  144.8 0.8 copy-start.2
  145.6 29.1 %collective-permute-start.25 = (f32[8,2,64,128]{3,2,1,0:T(8,128)}, f32[8,2,64,128]{3,2,1,0:T(8,128)}, u32[]{:S(2)}, u32[]{:S(2)}) collective-permute-start(f32[8,2,64,128]{3,2,1,0:T(8,128)} %get-tuple-element.123), channel_id=1, source_target_pairs={{0,8},{8,0},{16,24},{24,16},{1,9},{9,1},{17,25},{25,17},{2,10},{10... | collective-permute-start | bytes 1572872 | tf_op jit(solution)/shard_map/ppermute | solution.py:347
  146.8 30.0 %collective-permute-start.24 = (f32[8,2,64,128]{3,2,1,0:T(8,128)}, f32[8,2,64,128]{3,2,1,0:T(8,128)}, u32[]{:S(2)}, u32[]{:S(2)}) collective-permute-start(f32[8,2,64,128]{3,2,1,0:T(8,128)} %get-tuple-element.122), channel_id=1, source_target_pairs={{0,16},{8,24},{16,0},{24,8},{1,17},{9,25},{17,1},{25,9},{2,18},{10... | collective-permute-start | bytes 1572872 | tf_op jit(solution)/shard_map/ppermute | solution.py:347
  152.1 0.8 copy-start
  152.9 33.0 %collective-permute-start.19 = (f32[8,2,64,128]{3,2,1,0:T(8,128)}, f32[8,2,64,128]{3,2,1,0:T(8,128)}, u32[]{:S(2)}, u32[]{:S(2)}) collective-permute-start(f32[8,2,64,128]{3,2,1,0:T(8,128)} %get-tuple-element.113), channel_id=1, source_target_pairs={{0,24},{8,16},{16,8},{24,0},{1,25},{9,17},{17,9},{25,1},{2,26},{10... | collective-permute-start | bytes 1572872 | tf_op jit(solution)/shard_map/ppermute | solution.py:347
  163.2 2.0 %copy-start.1 = (f32[8,2,64,128]{3,2,1,0:T(8,128)S(1)}, f32[8,2,64,128]{3,2,1,0:T(8,128)}, u32[]{:S(2)}) copy-start(f32[8,2,64,128]{3,2,1,0:T(8,128)} %copy-done) | copy-start | bytes 1572868
  169.2 2.2 %copy-start.3 = (f32[8,2,64,128]{3,2,1,0:T(8,128)S(1)}, f32[8,2,64,128]{3,2,1,0:T(8,128)}, u32[]{:S(2)}) copy-start(f32[8,2,64,128]{3,2,1,0:T(8,128)} %copy-done.2) | copy-start | bytes 1572868

commit v3 on v2

--- a/solution.py
+++ b/solution.py
@@ -44,8 +44,9 @@
         out[...] = source[...]
 
 
-def cut(me, field, n, chunk, part):
+def cut(me, field, n, chunk, part, partners=None):
     count, depth, width, length = field.shape
+    partners = range(1, n) if partners is None else partners
 
     def block(m):
         return pl.BlockSpec(
@@ -58,14 +59,14 @@
         grid_spec=pltpu.PrefetchScalarGridSpec(
             num_scalar_prefetch=1,
             grid=(part,),
-            in_specs=[block(m) for m in range(1, n)],
-            out_specs=[piece] * (n - 1),
-        ),
-        out_shape=[jax.ShapeDtypeStruct((count, part, width, length), jnp.float32)] * (n - 1),
+            in_specs=[block(m) for m in partners],
+            out_specs=[piece] * len(partners),
+        ),
+        out_shape=[jax.ShapeDtypeStruct((count, part, width, length), jnp.float32)] * len(partners),
         compiler_params=pltpu.CompilerParams(vmem_limit_bytes=VMEM),
         cost_estimate=COST,
         name="cut",
-    )(me, *in_hbm(*[field] * (n - 1)))
+    )(me, *in_hbm(*[field] * len(partners)))
 
 
 def prep_kernel(
@@ -320,25 +321,56 @@
     refs[-1][...] = base_ref[...] - winv_ref[...] * piece_ref[...]
 
 
-def last_update(spot, piece, base, winv, before):
+def last_update(me, piece, base, winv, n, chunk, m, before, held=None):
     count, part, width, length = piece.shape
-    layers = pl.BlockSpec((count, 1, width, length), lambda i, spot: (0, spot[0] * part + i, 0, 0))
-    aliased = len(before)
-    return pl.pallas_call(
-        lambda spot_ref, *refs: last_kernel(*refs),
+    layers = pl.BlockSpec((count, part, width, length), lambda i, me: (0, chunk * n + (me[0] ^ m), 0, 0))
+    block = pl.BlockSpec((count, part, width, length), lambda i, me: (0, 0, 0, 0))
+    return pl.pallas_call(
+        lambda me_ref, *refs: last_kernel(*refs),
         grid_spec=pltpu.PrefetchScalarGridSpec(
             num_scalar_prefetch=1,
-            grid=(part,),
-            in_specs=[pl.BlockSpec((count, 1, width, length), lambda i, spot: (0, i, 0, 0)), layers, layers]
-            + [pl.BlockSpec(memory_space=pl.ANY)] * aliased,
+            grid=(1,),
+            in_specs=[block] + [block if held else layers] * 2 + [pl.BlockSpec(memory_space=pl.ANY)],
             out_specs=layers,
         ),
         out_shape=pltpu.HBM(base.shape, jnp.float32),
-        input_output_aliases={4: 0} if aliased else {},
+        input_output_aliases={4: 0},
         compiler_params=pltpu.CompilerParams(vmem_limit_bytes=VMEM),
         cost_estimate=COST,
         name="last_update",
-    )(spot, piece, *in_hbm(base, winv, *before))
+    )(me, piece, *(held or in_hbm(base, winv)), *in_hbm(before))
+
+
+def chunk_kernel(n, me_ref, *refs):
+    pieces, (base_ref, winv_ref) = refs[:n], refs[n : n + 2]
+    out_ref = refs[-1]
+    part = pieces[0].shape[1]
+    for m, piece in enumerate(pieces):
+        for i in range(part):
+            z = (me_ref[0] ^ m) * part + i
+            out_ref[:, z] = base_ref[:, z] - winv_ref[:, z] * piece[:, i]
+
+
+def chunk_update(me, pieces, base, winv, chunk, before):
+    n = len(pieces)
+    count, depth, width, length = base.shape
+    part = pieces[0].shape[1]
+    piece = pl.BlockSpec((count, part, ROWS, length), lambda i, me: (0, 0, i, 0))
+    layers = pl.BlockSpec((count, n * part, ROWS, length), lambda i, me: (0, chunk, i, 0))
+    return pl.pallas_call(
+        functools.partial(chunk_kernel, n),
+        grid_spec=pltpu.PrefetchScalarGridSpec(
+            num_scalar_prefetch=1,
+            grid=(width // ROWS,),
+            in_specs=[piece] * n + [layers] * 2 + [pl.BlockSpec(memory_space=pl.ANY)] * len(before),
+            out_specs=layers,
+        ),
+        out_shape=pltpu.HBM(base.shape, jnp.float32),
+        input_output_aliases={n + 3: 0} if before else {},
+        compiler_params=pltpu.CompilerParams(vmem_limit_bytes=VMEM),
+        cost_estimate=COST,
+        name="chunk_update",
+    )(me, *pieces, *in_hbm(base, winv, *before))
 
 
 def exchange(pieces):
@@ -368,7 +400,9 @@
     me = lax.axis_index("inst")
     me_array = me.reshape(1).astype(jnp.int32)
 
-    going = cut(me_array, field_start, n, 0, part)
+    far = cut(me_array, field_start, n, 0, part, [n - 1])
+    near = cut(me_array, after(field_start, *far), n, 0, part, range(1, n - 1))
+    going = near + far
     there = [exchange(going)]
     start, flags, material = after((field_start, face_flags, material), *going)
 
@@ -424,10 +458,15 @@
     base = second[0]
 
     field = []
-    for chunk in range(chunks):
-        for m, piece in enumerate(back[chunk]):
-            spot = (chunk * n + (me ^ m)).reshape(1).astype(jnp.int32)
-            field = [last_update(spot, piece, base, winv, field)]
+    for chunk in range(chunks - 1):
+        field = [chunk_update(me_array, back[chunk], base, winv, chunk, field)]
+    chunk = chunks - 1
+    held = [cut(me_array, array, n, chunk, part) for array in (base, winv)]
+    for m, piece in enumerate(back[chunk]):
+        there = [pieces[m - 1] for pieces in held] if m else None
+        field = [last_update(me_array, piece, base, winv, n, chunk, m, field[0], there)]
+        if m == 0:
+            held, field = after((held, field), held)
     return (residual, field[0])
 
 

time: 191 us -> 189 us (0.990); the launches traced: 188 us -> 188 us
  waiting for transfers between devices: 50.2 us -> 63.4 us
  starting transfers between devices: 42.4 us -> 36 us
  Pallas kernels: 87.6 us -> 82.7 us
    ppermute x24, waiting for transfers between devices: 40.6 us -> 53.6 us  [exchange(): lax.ppermute(piece, 'inst', [(i, i ^ m) for i in range(n)])]
    pallas_call x8 -> x5, Pallas kernels: 16.5 us -> 9.2 us  [the longest x4 4.73 us: last_update(): pl.pallas_call(lambda me_ref, *refs: last_kernel(*refs), grid_spec=pltpu....]
    pallas_call x2 -> x5, Pallas kernels: 4.75 us -> 8.57 us  [cut(): pl.pallas_call(cut_kernel, grid_spec=pltpu.PrefetchScalarGridSpec(num_sca...]
    ppermute x24, starting transfers between devices: 25 us -> 22.5 us  [exchange(): lax.ppermute(piece, 'inst', [(i, i ^ m) for i in range(n)])]
    ppermute x2, starting transfers between devices: 7.07 us -> 4.95 us  [downward(): lax.ppermute(plane, 'space', [(i + 1, i) for i in range(lax.axis_size('sp...]
  transfers between devices with their start and end apart: 28 -> 28, of which waited for: 11 -> 13; matrix products, arithmetic and copies ran while one was open for 3% -> 3% of each run, Pallas kernels for 44% -> 43%
where the time goes in v3:
time: 189 us; the launch traced here: 188 us
  Pallas kernels  82.7 us (44%)
  waiting for transfers between devices  63.4 us (34%)
  starting transfers between devices  36 us (19%)
  local copies, waits for them, and re-layouts  4.14 us (2%)
    ppermute x24, waiting for transfers between devices, exchange(): lax.ppermute(piece, 'inst', [(i, i ^ m) for i in range(n)])  53.6 us
    pallas_call x4, Pallas kernels, stencil(): pl.pallas_call(functools.partial(stencil_kernel, second, first, len(befor...  37.9 us
    ppermute x24, starting transfers between devices, exchange(): lax.ppermute(piece, 'inst', [(i, i ^ m) for i in range(n)])  22.5 us
    pallas_call x4, Pallas kernels, apply_time(): pl.pallas_call(functools.partial(apply_kernel, n), grid_spec=pltpu.Prefet...  13.2 us
    pallas_call x2, Pallas kernels, first_update(): pl.pallas_call(functools.partial(first_kernel, n, aliased), grid_spec=plt...  11 us
    ppermute x2, waiting for transfers between devices, downward(): lax.ppermute(plane, 'space', [(i + 1, i) for i in range(lax.axis_size('sp...  9.76 us
    ppermute x2, starting transfers between devices, upward(): lax.ppermute(plane, 'space', [(i, i + 1) for i in range(lax.axis_size('sp...  8.62 us
    pallas_call x5, Pallas kernels, cut(): pl.pallas_call(cut_kernel, grid_spec=pltpu.PrefetchScalarGridSpec(num_sca...  8.57 us
  transfers between devices with their start and end apart: 28, of which 13 were waited for; matrix products, arithmetic and copies ran while one was open for 3% of the time, Pallas kernels for 43%

profile of v3, /device:TPU:9, one launch (start us, length us, event | category | flops | bytes accessed | tf_op | source)
XLA Modules:
  0.0 188.3 jit_solution(8205011961564120909)
XLA Ops:
  0.6 1.1 cut.5
  1.8 2.2 %collective-permute-start.10 = (f32[8,2,64,128]{3,2,1,0:T(8,128)S(1)}, f32[8,2,64,128]{3,2,1,0:T(8,128)S(1)}, u32[]{:S(2)}, u32[]{:S(2)}) collective-permute-start(f32[8,2,64,128]{3,2,1,0:T(8,128)S(1)} %cut.5), channel_id=1, source_target_pairs={{0,24},{8,16},{16,8},{24,0},{1,25},{9,17},{17,9},{25,1},{2,26},{10... | collective-permute-start | bytes 1572872 | tf_op jit(solution)/shard_map/ppermute | solution.py:379
  4.0 2.1 %cut.6 = (f32[8,2,64,128]{3,2,1,0:T(8,128)}, f32[8,2,64,128]{3,2,1,0:T(8,128)}) custom-call(s32[1]{0:T(128)} %bitcast.me_ref, f32[8,16,64,128]{3,2,1,0:T(8,128)} %refs_6_.3, f32[8,16,64,128]{3,2,1,0:T(8,128)} %refs_6_.3), custom_call_target="tpu_custom_call" | custom-call | flops 1024 | bytes 1024 | tf_op jit(solution)/shard_map/cut/pallas_call | solution.py:57
  6.1 0.3 collective-permute-start.8
  6.6 2.8 %prep.1 = (f32[16,64,128]{2,1,0:T(8,128)S(1)}, f32[16,64,128]{2,1,0:T(8,128)S(1)}, f32[17,64,128]{2,1,0:T(8,128)}, f32[8,64,128]{2,1,0:T(8,128)}) custom-call(f32[8]{0:T(128)S(1)} %copy-done, f32[8]{0:T(128)S(1)} %copy-done.1, f32[8]{0:T(128)S(1)} %multiply_add_fusion.tide_ref, s32[16,64,128]{2,1,0:T(8,128)} %material_ref, s32[8,3,16,64,128]{4,3,2,1,0:T(8,128)} %flags_ref.6, ...), custom_call_target="tpu_custom_call" | custom-call | flops 1024 | bytes 1024 | tf_op jit(solution)/shard_map/prep/pallas_call | solution.py:105
  9.4 4.6 %collective-permute-start = (f32[17,64,128]{2,1,0:T(8,128)}, f32[17,64,128]{2,1,0:T(8,128)S(1)}, u32[]{:S(2)}, u32[]{:S(2)}) collective-permute-start(f32[17,64,128]{2,1,0:T(8,128)} %get-tuple-element.84), channel_id=1, source_target_pairs={{0,1},{1,2},{2,3},{3,4},{4,5},{5,6},{6,7},{8,9},{9,10},{10,11},{11... | collective-permute-start | bytes 1671176 | tf_op jit(solution)/shard_map/ppermute | solution.py:388
  14.0 1.9 %collective-permute-start.1 = (f32[8,64,128]{2,1,0:T(8,128)}, f32[8,64,128]{2,1,0:T(8,128)S(1)}, u32[]{:S(2)}, u32[]{:S(2)}) collective-permute-start(f32[8,64,128]{2,1,0:T(8,128)} %get-tuple-element.85), channel_id=1, source_target_pairs={{1,0},{2,1},{3,2},{4,3},{5,4},{6,5},{7,6},{9,8},{10,9},{11,10},{12... | collective-permute-start | bytes 786440 | tf_op jit(solution)/shard_map/ppermute | solution.py:392
  16.1 0.7 broadcast_bitcast_fusion.1
  16.8 1.0 copy.18
  17.8 4.6 %collective-permute-done.1.high_ref = f32[8,64,128]{2,1,0:T(8,128)S(1)} collective-permute-done((f32[8,64,128]{2,1,0:T(8,128)}, f32[8,64,128]{2,1,0:T(8,128)S(1)}, u32[]{:S(2)}, u32[]{:S(2)}) %collective-permute-start.1) | collective-permute-done | bytes 262176 | tf_op jit(solution)/shard_map/ppermute | solution.py:392
  22.3 2.3 %cut.7 = (f32[8,2,64,128]{3,2,1,0:T(8,128)}, f32[8,2,64,128]{3,2,1,0:T(8,128)}, f32[8,2,64,128]{3,2,1,0:T(8,128)}) custom-call(s32[1]{0:T(128)} %bitcast.me_ref, f32[8,16,64,128]{3,2,1,0:T(8,128)} %refs_6_.3, f32[8,16,64,128]{3,2,1,0:T(8,128)} %refs_6_.3, f32[8,16,64,128]{3,2,1,0:T(8,128)} %refs_6_.3), custom_call_target="tpu_custom_call" | custom-call | flops 1024 | bytes 1024 | tf_op jit(solution)/shard_map/cut/pallas_call | solution.py:57
  24.7 1.2 collective-permute-start.2
  25.9 0.7 broadcast_bitcast_fusion
  26.6 1.2 collective-permute-start.3
  27.9 0.3 collective-permute-start.4
  28.1 1.8 copy.19
  29.9 1.0 compare_select_fusion.refs_3_
  31.0 9.7 %stencil_one.2 = (f32[8,16,64,128]{3,2,1,0:T(8,128)}, f32[8,16,64,128]{3,2,1,0:T(8,128)}) custom-call(f32[8]{0:T(128)S(1)} %multiply_add_fusion.tide_ref, f32[8,16,64,128]{3,2,1,0:T(8,128)} %refs_6_.3, f32[17,64,128]{2,1,0:T(8,128)S(1)} %collective-permute-done.low_ref.below_k_ref.below_f_ref, f32[8,64,128]{2,1,0:T(8,128)S(1)} %collective-permute-done.1.high_ref, ...), custom_call_target="tpu_custom_call" | custom-call | flops 1024 | bytes 1024 | tf_op jit(solution)/shard_map/stencil_one/pallas_call | solution.py:212
  40.7 3.3 %apply_time.5 = (f32[8,2,64,128]{3,2,1,0:T(8,128)S(1)}, f32[8,2,64,128]{3,2,1,0:T(8,128)S(1)}, f32[8,2,64,128]{3,2,1,0:T(8,128)S(1)}, f32[8,2,64,128]{3,2,1,0:T(8,128)S(1)}) custom-call(s32[1]{0:T(128)} %bitcast.me_ref, f32[8,16,64,128]{3,2,1,0:T(8,128)} %refs_6_.3, f32[8,2,64,128]{3,2,1,0:T(8,128)S(1)} %collective-permute-done.8.refs_0_, ...), custom_call_target="tpu_custom_call" | custom-call | flops 1024 | bytes 1024 | tf_op jit(solution)/shard_map/apply_time/pallas_call | solution.py:254
  44.0 1.2 collective-permute-start.11
  45.2 1.2 collective-permute-start.12
  46.5 0.3 collective-permute-start.13
  46.8 5.1 %collective-permute-done.3.refs_1_ = f32[8,2,64,128]{3,2,1,0:T(8,128)} collective-permute-done((f32[8,2,64,128]{3,2,1,0:T(8,128)}, f32[8,2,64,128]{3,2,1,0:T(8,128)}, u32[]{:S(2)}, u32[]{:S(2)}) %collective-permute-start.3) | collective-permute-done | bytes 524320 | tf_op jit(solution)/shard_map/ppermute | solution.py:379
  51.8 3.5 %apply_time.4 = (f32[8,2,64,128]{3,2,1,0:T(8,128)S(1)}, f32[8,2,64,128]{3,2,1,0:T(8,128)S(1)}, f32[8,2,64,128]{3,2,1,0:T(8,128)S(1)}, f32[8,2,64,128]{3,2,1,0:T(8,128)S(1)}) custom-call(s32[1]{0:T(128)} %bitcast.me_ref, f32[8,16,64,128]{3,2,1,0:T(8,128)} %refs_6_.3, f32[8,2,64,128]{3,2,1,0:T(8,128)} %collective-permute-done.2.refs_0_, ...), custom_call_target="tpu_custom_call" | custom-call | flops 1024 | bytes 1024 | tf_op jit(solution)/shard_map/apply_time/pallas_call | solution.py:254
  55.3 0.5 collective-permute-start.5
  55.8 5.6 %collective-permute-done.11.refs_1_ = f32[8,2,64,128]{3,2,1,0:T(8,128)S(1)} collective-permute-done((f32[8,2,64,128]{3,2,1,0:T(8,128)S(1)}, f32[8,2,64,128]{3,2,1,0:T(8,128)S(1)}, u32[]{:S(2)}, u32[]{:S(2)}) %collective-permute-start.11) | collective-permute-done | bytes 524320 | tf_op jit(solution)/shard_map/ppermute | solution.py:379
  61.4 1.1 collective-permute-start.6
  62.5 1.3 collective-permute-start.7
  63.8 9.8 %stencil_one.3 = (f32[8,16,64,128]{3,2,1,0:T(8,128)}, f32[8,16,64,128]{3,2,1,0:T(8,128)}) custom-call(f32[8]{0:T(128)S(1)} %multiply_add_fusion.tide_ref, f32[8,16,64,128]{3,2,1,0:T(8,128)} %refs_6_.3, f32[17,64,128]{2,1,0:T(8,128)S(1)} %collective-permute-done.low_ref.below_k_ref.below_f_ref, ...), custom_call_target="tpu_custom_call", output_to_operand_aliasing={{0}: (10, {}), {1}: (11, {})} | custom-call | flops 1024 | bytes 1024 | tf_op jit(solution)/shard_map/stencil_one/pallas_call | solution.py:212
  73.7 0.5 collective-permute-done.12.refs_2_
  74.2 5.6 %first_update.2 = (f32[8,16,64,128]{3,2,1,0:T(8,128)}, f32[8,16,64,128]{3,2,1,0:T(8,128)}, f32[8,64,128]{2,1,0:T(8,128)S(1)}, f32[8,64,128]{2,1,0:T(8,128)}, f32...) custom-call(s32[1]{0:T(128)} %bitcast.me_ref, ...), custom_call_target="tpu_custom_call" | custom-call | flops 1024 | bytes 1024 | tf_op jit(solution)/shard_map/first_update/pallas_call | solution.py:302
  79.8 3.0 %collective-permute-start.14 = (f32[8,64,128]{2,1,0:T(8,128)S(1)}, f32[8,64,128]{2,1,0:T(8,128)S(1)}, u32[]{:S(2)}, u32[]{:S(2)}) collective-permute-start(f32[8,64,128]{2,1,0:T(8,128)S(1)} %get-tuple-element.109), channel_id=1, source_target_pairs={{1,0},{2,1},{3,2},{4,3},{5,4},{6,5},{7,6},{9,8},{10,9},{11,10},{12... | collective-permute-start | bytes 786440 | tf_op jit(solution)/shard_map/ppermute | solution.py:392
  82.8 0.3 collective-permute-start.20
  83.1 5.2 %collective-permute-done.14.high_ref = f32[8,64,128]{2,1,0:T(8,128)S(1)} collective-permute-done((f32[8,64,128]{2,1,0:T(8,128)S(1)}, f32[8,64,128]{2,1,0:T(8,128)S(1)}, u32[]{:S(2)}, u32[]{:S(2)}) %collective-permute-start.14) | collective-permute-done | bytes 262176 | tf_op jit(solution)/shard_map/ppermute | solution.py:392
  88.3 1.1 collective-permute-start.21
  89.4 0.4 collective-permute-start.22
  89.8 6.9 %collective-permute-done.6.refs_2_ = f32[8,2,64,128]{3,2,1,0:T(8,128)S(1)} collective-permute-done((f32[8,2,64,128]{3,2,1,0:T(8,128)S(1)}, f32[8,2,64,128]{3,2,1,0:T(8,128)S(1)}, u32[]{:S(2)}, u32[]{:S(2)}) %collective-permute-start.6) | collective-permute-done | bytes 524320 | tf_op jit(solution)/shard_map/ppermute | solution.py:379
  96.7 5.5 %first_update.3 = (f32[8,16,64,128]{3,2,1,0:T(8,128)}, f32[8,16,64,128]{3,2,1,0:T(8,128)}, f32[8,64,128]{2,1,0:T(8,128)}, f32[8,64,128]{2,1,0:T(8,128)S(1)}, f32...) custom-call(s32[1]{0:T(128)} %bitcast.me_ref, ...), custom_call_target="tpu_custom_call", output_to_operand_aliasing={{0}: (8, {}), {1}: (9, {})} | custom-call | flops 1024 | bytes 1024 | tf_op jit(solution)/shard_map/first_update/pallas_call | solution.py:302
  102.1 4.0 %collective-permute-start.18 = (f32[8,64,128]{2,1,0:T(8,128)S(1)}, f32[8,64,128]{2,1,0:T(8,128)S(1)}, u32[]{:S(2)}, u32[]{:S(2)}) collective-permute-start(f32[8,64,128]{2,1,0:T(8,128)S(1)} %get-tuple-element.122), channel_id=1, source_target_pairs={{0,1},{1,2},{2,3},{3,4},{4,5},{5,6},{6,7},{8,9},{9,10},{10,11},{11... | collective-permute-start | bytes 786440 | tf_op jit(solution)/shard_map/ppermute | solution.py:388
  106.2 0.2 collective-permute-start.15
  106.5 1.3 collective-permute-start.16
  107.7 11.4 %collective-permute-done.21.refs_1_ = f32[8,2,64,128]{3,2,1,0:T(8,128)S(1)} collective-permute-done((f32[8,2,64,128]{3,2,1,0:T(8,128)S(1)}, f32[8,2,64,128]{3,2,1,0:T(8,128)S(1)}, u32[]{:S(2)}, u32[]{:S(2)}) %collective-permute-start.21) | collective-permute-done | bytes 524320 | tf_op jit(solution)/shard_map/ppermute | solution.py:379
  119.1 1.0 collective-permute-start.17
  120.2 3.2 %apply_time.7 = (f32[8,2,64,128]{3,2,1,0:T(8,128)S(1)}, f32[8,2,64,128]{3,2,1,0:T(8,128)S(1)}, f32[8,2,64,128]{3,2,1,0:T(8,128)S(1)}, f32[8,2,64,128]{3,2,1,0:T(8,128)S(1)}) custom-call(s32[1]{0:T(128)} %bitcast.me_ref, f32[8,16,64,128]{3,2,1,0:T(8,128)} %get-tuple-element.134.u_ref.own_ref, f32[8,2,64,128]{3,2,1,0:T(8,128)S(1)} %collective-permute-done.20.refs_0_, ...), custom_call_target="tpu_custom_call" | custom-call | flops 1024 | bytes 1024 | tf_op jit(solution)/shard_map/apply_time/pallas_call | solution.py:254
  123.4 1.5 collective-permute-start.23
  125.1 3.9 %collective-permute-done.15.refs_0_ = f32[8,2,64,128]{3,2,1,0:T(8,128)S(1)} collective-permute-done((f32[8,2,64,128]{3,2,1,0:T(8,128)S(1)}, f32[8,2,64,128]{3,2,1,0:T(8,128)S(1)}, u32[]{:S(2)}, u32[]{:S(2)}) %collective-permute-start.15) | collective-permute-done | bytes 524320 | tf_op jit(solution)/shard_map/ppermute | solution.py:379
  129.0 2.0 %collective-permute-start.25 = (f32[8,2,64,128]{3,2,1,0:T(8,128)S(1)}, f32[8,2,64,128]{3,2,1,0:T(8,128)S(1)}, u32[]{:S(2)}, u32[]{:S(2)}) collective-permute-start(f32[8,2,64,128]{3,2,1,0:T(8,128)S(1)} %get-tuple-element.144), channel_id=1, source_target_pairs={{0,24},{8,16},{16,8},{24,0},{1,25},{9,17},{17,9},{25,1},{2,26},{10... | collective-permute-start | bytes 1572872 | tf_op jit(solution)/shard_map/ppermute | solution.py:379
  131.0 9.2 %stencil_two.2.rest_1_ = f32[8,16,64,128]{3,2,1,0:T(8,128)} custom-call(f32[8]{0:T(128)S(1)} %multiply_add_fusion.tide_ref, f32[8,16,64,128]{3,2,1,0:T(8,128)} %get-tuple-element.134.u_ref.own_ref, f32[8,64,128]{2,1,0:T(8,128)S(1)} %collective-permute-done.18.low_ref, f32[8,64,128]{2,1,0:T(8,128)S(1)} %collective-permute-done.14.high_ref, ...), custom_call_target="tpu_custom_call" | custom-call | flops 1024 | bytes 1024 | tf_op jit(solution)/shard_map/stencil_two/pallas_call | solution.py:212
  140.1 1.5 collective-permute-done.16.refs_1_
  141.6 3.2 %apply_time.6 = (f32[8,2,64,128]{3,2,1,0:T(8,128)S(1)}, f32[8,2,64,128]{3,2,1,0:T(8,128)S(1)}, f32[8,2,64,128]{3,2,1,0:T(8,128)S(1)}, f32[8,2,64,128]{3,2,1,0:T(8,128)S(1)}) custom-call(s32[1]{0:T(128)} %bitcast.me_ref, f32[8,16,64,128]{3,2,1,0:T(8,128)} %get-tuple-element.134.u_ref.own_ref, f32[8,2,64,128]{3,2,1,0:T(8,128)S(1)} %collective-permute-done.15.refs_0_, ...), custom_call_target="tpu_custom_call" | custom-call | flops 1024 | bytes 1024 | tf_op jit(solution)/shard_map/apply_time/pallas_call | solution.py:254
  144.8 0.7 collective-permute-start.27
  145.5 0.7 collective-permute-start.26
  146.2 5.3 %collective-permute-done.23.refs_1_ = f32[8,2,64,128]{3,2,1,0:T(8,128)S(1)} collective-permute-done((f32[8,2,64,128]{3,2,1,0:T(8,128)S(1)}, f32[8,2,64,128]{3,2,1,0:T(8,128)S(1)}, u32[]{:S(2)}, u32[]{:S(2)}) %collective-permute-start.23) | collective-permute-done | bytes 524320 | tf_op jit(solution)/shard_map/ppermute | solution.py:379
  151.5 2.0 %collective-permute-start.19 = (f32[8,2,64,128]{3,2,1,0:T(8,128)S(1)}, f32[8,2,64,128]{3,2,1,0:T(8,128)S(1)}, u32[]{:S(2)}, u32[]{:S(2)}) collective-permute-start(f32[8,2,64,128]{3,2,1,0:T(8,128)S(1)} %get-tuple-element.126), channel_id=1, source_target_pairs={{0,24},{8,16},{16,8},{24,0},{1,25},{9,17},{17,9},{25,1},{2,26},{10... | collective-permute-start | bytes 1572872 | tf_op jit(solution)/shard_map/ppermute | solution.py:379
  153.5 9.2 %stencil_two.3.refs_0_.refs_1_.refs_2_.refs_4_ = f32[8,16,64,128]{3,2,1,0:T(8,128)} custom-call(f32[8]{0:T(128)S(1)} %multiply_add_fusion.tide_ref, f32[8,16,64,128]{3,2,1,0:T(8,128)} %get-tuple-element.134.u_ref.own_ref, f32[8,64,128]{2,1,0:T(8,128)S(1)} %collective-permute-done.18.low_ref, ...), custom_call_target="tpu_custom_call", output_to_operand_aliasing={{}: (11, {})} | custom-call | flops 1024 | bytes 1024 | tf_op jit(solution)/shard_map/stencil_two/pallas_call | solution.py:212
  162.6 1.5 cut.9
  164.2 1.6 cut.8
  165.7 4.5 %chunk_update.1.refs_3_ = f32[8,16,64,128]{3,2,1,0:T(8,128)} custom-call(s32[1]{0:T(128)} %bitcast.me_ref, f32[8,2,64,128]{3,2,1,0:T(8,128)S(1)} %get-tuple-element.142.refs_0_, f32[8,2,64,128]{3,2,1,0:T(8,128)S(1)} %collective-permute-done.23.refs_1_, f32[8,2,64,128]{3,2,1,0:T(8,128)S(1)} %collective-permute-done.24.refs_2_, ...), custom_call_target="tpu_custom_call" | custom-call | flops 1024 | bytes 1024 | tf_op jit(solution)/shard_map/chunk_update/pallas_call | solution.py:360
  170.2 2.1 %last_update.4.refs_3_ = f32[8,16,64,128]{3,2,1,0:T(8,128)} custom-call(s32[1]{0:T(128)} %bitcast.me_ref, f32[8,2,64,128]{3,2,1,0:T(8,128)S(1)} %get-tuple-element.141.refs_0_, f32[8,16,64,128]{3,2,1,0:T(8,128)} %stencil_two.3.refs_0_.refs_1_.refs_2_.refs_4_, ...), custom_call_target="tpu_custom_call", output_to_operand_aliasing={{}: (4, {})} | custom-call | flops 1024 | bytes 1024 | tf_op jit(solution)/shard_map/last_update/pallas_call | solution.py:328
  172.3 1.7 collective-permute-done.27.refs_0_
  174.0 0.9 last_update.5.refs_3_
  174.9 11.7 %collective-permute-done.26.refs_0_ = f32[8,2,64,128]{3,2,1,0:T(8,128)S(1)} collective-permute-done((f32[8,2,64,128]{3,2,1,0:T(8,128)S(1)}, f32[8,2,64,128]{3,2,1,0:T(8,128)S(1)}, u32[]{:S(2)}, u32[]{:S(2)}) %collective-permute-start.26) | collective-permute-done | bytes 524320 | tf_op jit(solution)/shard_map/ppermute | solution.py:379
  186.6 0.9 last_update.6.refs_3_
  187.4 0.9 last_update.7
  (26 shorter events, 0.8 us)
Async XLA Ops:
  1.8 4.8 %copy-start = (f32[8]{0:T(128)S(1)}, f32[8]{0:T(128)}, u32[]{:S(2)}) copy-start(f32[8]{0:T(128)} %disp_ref.1) | copy-start | bytes 100
  1.8 4.8 %copy-start.1 = (f32[8]{0:T(128)S(1)}, f32[8]{0:T(128)}, u32[]{:S(2)}) copy-start(f32[8]{0:T(128)} %perm_ref.1) | copy-start | bytes 100
  1.8 38.9 %collective-permute-start.10 = (f32[8,2,64,128]{3,2,1,0:T(8,128)S(1)}, f32[8,2,64,128]{3,2,1,0:T(8,128)S(1)}, u32[]{:S(2)}, u32[]{:S(2)}) collective-permute-start(f32[8,2,64,128]{3,2,1,0:T(8,128)S(1)} %cut.5), channel_id=1, source_target_pairs={{0,24},{8,16},{16,8},{24,0},{1,25},{9,17},{17,9},{25,1},{2,26},{10... | collective-permute-start | bytes 1572872 | tf_op jit(solution)/shard_map/ppermute | solution.py:379
  6.1 21.8 %collective-permute-start.8 = (f32[8,2,64,128]{3,2,1,0:T(8,128)}, f32[8,2,64,128]{3,2,1,0:T(8,128)S(1)}, u32[]{:S(2)}, u32[]{:S(2)}) collective-permute-start(f32[8,2,64,128]{3,2,1,0:T(8,128)} %get-tuple-element.79), channel_id=1, source_target_pairs={{0,8},{8,0},{16,24},{24,16},{1,9},{9,1},{17,25},{25,17},{2,10},{10... | collective-permute-start | bytes 1572872 | tf_op jit(solution)/shard_map/ppermute | solution.py:379
  6.3 34.4 %collective-permute-start.9 = (f32[8,2,64,128]{3,2,1,0:T(8,128)}, f32[8,2,64,128]{3,2,1,0:T(8,128)}, u32[]{:S(2)}, u32[]{:S(2)}) collective-permute-start(f32[8,2,64,128]{3,2,1,0:T(8,128)} %get-tuple-element.80), channel_id=1, source_target_pairs={{0,16},{8,24},{16,0},{24,8},{1,17},{9,25},{17,1},{25,9},{2,18},{10... | collective-permute-start | bytes 1572872 | tf_op jit(solution)/shard_map/ppermute | solution.py:379
  9.4 12.9 %collective-permute-start = (f32[17,64,128]{2,1,0:T(8,128)}, f32[17,64,128]{2,1,0:T(8,128)S(1)}, u32[]{:S(2)}, u32[]{:S(2)}) collective-permute-start(f32[17,64,128]{2,1,0:T(8,128)} %get-tuple-element.84), channel_id=1, source_target_pairs={{0,1},{1,2},{2,3},{3,4},{4,5},{5,6},{6,7},{8,9},{9,10},{10,11},{11... | collective-permute-start | bytes 1671176 | tf_op jit(solution)/shard_map/ppermute | solution.py:388
  14.0 8.3 %collective-permute-start.1 = (f32[8,64,128]{2,1,0:T(8,128)}, f32[8,64,128]{2,1,0:T(8,128)S(1)}, u32[]{:S(2)}, u32[]{:S(2)}) collective-permute-start(f32[8,64,128]{2,1,0:T(8,128)} %get-tuple-element.85), channel_id=1, source_target_pairs={{1,0},{2,1},{3,2},{4,3},{5,4},{6,5},{7,6},{9,8},{10,9},{11,10},{12... | collective-permute-start | bytes 786440 | tf_op jit(solution)/shard_map/ppermute | solution.py:392
  24.7 21.8 %collective-permute-start.2 = (f32[8,2,64,128]{3,2,1,0:T(8,128)}, f32[8,2,64,128]{3,2,1,0:T(8,128)}, u32[]{:S(2)}, u32[]{:S(2)}) collective-permute-start(f32[8,2,64,128]{3,2,1,0:T(8,128)} %get-tuple-element.87), channel_id=1, source_target_pairs={{0,8},{8,0},{16,24},{24,16},{1,9},{9,1},{17,25},{25,17},{2,10},{10... | collective-permute-start | bytes 1572872 | tf_op jit(solution)/shard_map/ppermute | solution.py:379
  26.6 25.2 %collective-permute-start.3 = (f32[8,2,64,128]{3,2,1,0:T(8,128)}, f32[8,2,64,128]{3,2,1,0:T(8,128)}, u32[]{:S(2)}, u32[]{:S(2)}) collective-permute-start(f32[8,2,64,128]{3,2,1,0:T(8,128)} %get-tuple-element.88), channel_id=1, source_target_pairs={{0,16},{8,24},{16,0},{24,8},{1,17},{9,25},{17,1},{25,9},{2,18},{10... | collective-permute-start | bytes 1572872 | tf_op jit(solution)/shard_map/ppermute | solution.py:379
  27.9 24.0 %collective-permute-start.4 = (f32[8,2,64,128]{3,2,1,0:T(8,128)}, f32[8,2,64,128]{3,2,1,0:T(8,128)}, u32[]{:S(2)}, u32[]{:S(2)}) collective-permute-start(f32[8,2,64,128]{3,2,1,0:T(8,128)} %get-tuple-element.89), channel_id=1, source_target_pairs={{0,24},{8,16},{16,8},{24,0},{1,25},{9,17},{17,9},{25,1},{2,26},{10... | collective-permute-start | bytes 1572872 | tf_op jit(solution)/shard_map/ppermute | solution.py:379
  44.0 17.4 %collective-permute-start.11 = (f32[8,2,64,128]{3,2,1,0:T(8,128)S(1)}, f32[8,2,64,128]{3,2,1,0:T(8,128)S(1)}, u32[]{:S(2)}, u32[]{:S(2)}) collective-permute-start(f32[8,2,64,128]{3,2,1,0:T(8,128)S(1)} %get-tuple-element.103), channel_id=1, source_target_pairs={{0,8},{8,0},{16,24},{24,16},{1,9},{9,1},{17,25},{25,17},{2,10},{10... | collective-permute-start | bytes 1572872 | tf_op jit(solution)/shard_map/ppermute | solution.py:379
  45.2 29.0 %collective-permute-start.12 = (f32[8,2,64,128]{3,2,1,0:T(8,128)S(1)}, f32[8,2,64,128]{3,2,1,0:T(8,128)S(1)}, u32[]{:S(2)}, u32[]{:S(2)}) collective-permute-start(f32[8,2,64,128]{3,2,1,0:T(8,128)S(1)} %get-tuple-element.104), channel_id=1, source_target_pairs={{0,16},{8,24},{16,0},{24,8},{1,17},{9,25},{17,1},{25,9},{2,18},{10... | collective-permute-start | bytes 1572872 | tf_op jit(solution)/shard_map/ppermute | solution.py:379
  46.5 27.7 %collective-permute-start.13 = (f32[8,2,64,128]{3,2,1,0:T(8,128)S(1)}, f32[8,2,64,128]{3,2,1,0:T(8,128)S(1)}, u32[]{:S(2)}, u32[]{:S(2)}) collective-permute-start(f32[8,2,64,128]{3,2,1,0:T(8,128)S(1)} %get-tuple-element.105), channel_id=1, source_target_pairs={{0,24},{8,16},{16,8},{24,0},{1,25},{9,17},{17,9},{25,1},{2,26},{10... | collective-permute-start | bytes 1572872 | tf_op jit(solution)/shard_map/ppermute | solution.py:379
  55.3 34.1 %collective-permute-start.5 = (f32[8,2,64,128]{3,2,1,0:T(8,128)S(1)}, f32[8,2,64,128]{3,2,1,0:T(8,128)S(1)}, u32[]{:S(2)}, u32[]{:S(2)}) collective-permute-start(f32[8,2,64,128]{3,2,1,0:T(8,128)S(1)} %get-tuple-element.91), channel_id=1, source_target_pairs={{0,8},{8,0},{16,24},{24,16},{1,9},{9,1},{17,25},{25,17},{2,10},{10... | collective-permute-start | bytes 1572872 | tf_op jit(solution)/shard_map/ppermute | solution.py:379
  61.4 35.2 %collective-permute-start.6 = (f32[8,2,64,128]{3,2,1,0:T(8,128)S(1)}, f32[8,2,64,128]{3,2,1,0:T(8,128)S(1)}, u32[]{:S(2)}, u32[]{:S(2)}) collective-permute-start(f32[8,2,64,128]{3,2,1,0:T(8,128)S(1)} %get-tuple-element.92), channel_id=1, source_target_pairs={{0,16},{8,24},{16,0},{24,8},{1,17},{9,25},{17,1},{25,9},{2,18},{10... | collective-permute-start | bytes 1572872 | tf_op jit(solution)/shard_map/ppermute | solution.py:379
  62.5 34.2 %collective-permute-start.7 = (f32[8,2,64,128]{3,2,1,0:T(8,128)S(1)}, f32[8,2,64,128]{3,2,1,0:T(8,128)S(1)}, u32[]{:S(2)}, u32[]{:S(2)}) collective-permute-start(f32[8,2,64,128]{3,2,1,0:T(8,128)S(1)} %get-tuple-element.93), channel_id=1, source_target_pairs={{0,24},{8,16},{16,8},{24,0},{1,25},{9,17},{17,9},{25,1},{2,26},{10... | collective-permute-start | bytes 1572872 | tf_op jit(solution)/shard_map/ppermute | solution.py:379
  79.8 8.6 %collective-permute-start.14 = (f32[8,64,128]{2,1,0:T(8,128)S(1)}, f32[8,64,128]{2,1,0:T(8,128)S(1)}, u32[]{:S(2)}, u32[]{:S(2)}) collective-permute-start(f32[8,64,128]{2,1,0:T(8,128)S(1)} %get-tuple-element.109), channel_id=1, source_target_pairs={{1,0},{2,1},{3,2},{4,3},{5,4},{6,5},{7,6},{9,8},{10,9},{11,10},{12... | collective-permute-start | bytes 786440 | tf_op jit(solution)/shard_map/ppermute | solution.py:392
  82.8 23.7 %collective-permute-start.20 = (f32[8,2,64,128]{3,2,1,0:T(8,128)S(1)}, f32[8,2,64,128]{3,2,1,0:T(8,128)S(1)}, u32[]{:S(2)}, u32[]{:S(2)}) collective-permute-start(f32[8,2,64,128]{3,2,1,0:T(8,128)S(1)} %get-tuple-element.127), channel_id=1, source_target_pairs={{0,8},{8,0},{16,24},{24,16},{1,9},{9,1},{17,25},{25,17},{2,10},{10... | collective-permute-start | bytes 1572872 | tf_op jit(solution)/shard_map/ppermute | solution.py:379
  88.3 30.8 %collective-permute-start.21 = (f32[8,2,64,128]{3,2,1,0:T(8,128)S(1)}, f32[8,2,64,128]{3,2,1,0:T(8,128)S(1)}, u32[]{:S(2)}, u32[]{:S(2)}) collective-permute-start(f32[8,2,64,128]{3,2,1,0:T(8,128)S(1)} %get-tuple-element.128), channel_id=1, source_target_pairs={{0,16},{8,24},{16,0},{24,8},{1,17},{9,25},{17,1},{25,9},{2,18},{10... | collective-permute-start | bytes 1572872 | tf_op jit(solution)/shard_map/ppermute | solution.py:379
  89.4 30.8 %collective-permute-start.22 = (f32[8,2,64,128]{3,2,1,0:T(8,128)S(1)}, f32[8,2,64,128]{3,2,1,0:T(8,128)S(1)}, u32[]{:S(2)}, u32[]{:S(2)}) collective-permute-start(f32[8,2,64,128]{3,2,1,0:T(8,128)S(1)} %get-tuple-element.129), channel_id=1, source_target_pairs={{0,24},{8,16},{16,8},{24,0},{1,25},{9,17},{17,9},{25,1},{2,26},{10... | collective-permute-start | bytes 1572872 | tf_op jit(solution)/shard_map/ppermute | solution.py:379
  102.1 18.0 %collective-permute-start.18 = (f32[8,64,128]{2,1,0:T(8,128)S(1)}, f32[8,64,128]{2,1,0:T(8,128)S(1)}, u32[]{:S(2)}, u32[]{:S(2)}) collective-permute-start(f32[8,64,128]{2,1,0:T(8,128)S(1)} %get-tuple-element.122), channel_id=1, source_target_pairs={{0,1},{1,2},{2,3},{3,4},{4,5},{5,6},{6,7},{8,9},{9,10},{10,11},{11... | collective-permute-start | bytes 786440 | tf_op jit(solution)/shard_map/ppermute | solution.py:388
  106.2 22.8 %collective-permute-start.15 = (f32[8,2,64,128]{3,2,1,0:T(8,128)S(1)}, f32[8,2,64,128]{3,2,1,0:T(8,128)S(1)}, u32[]{:S(2)}, u32[]{:S(2)}) collective-permute-start(f32[8,2,64,128]{3,2,1,0:T(8,128)S(1)} %get-tuple-element.118), channel_id=1, source_target_pairs={{0,8},{8,0},{16,24},{24,16},{1,9},{9,1},{17,25},{25,17},{2,10},{10... | collective-permute-start | bytes 1572872 | tf_op jit(solution)/shard_map/ppermute | solution.py:379
  106.5 35.2 %collective-permute-start.16 = (f32[8,2,64,128]{3,2,1,0:T(8,128)S(1)}, f32[8,2,64,128]{3,2,1,0:T(8,128)S(1)}, u32[]{:S(2)}, u32[]{:S(2)}) collective-permute-start(f32[8,2,64,128]{3,2,1,0:T(8,128)S(1)} %get-tuple-element.119), channel_id=1, source_target_pairs={{0,16},{8,24},{16,0},{24,8},{1,17},{9,25},{17,1},{25,9},{2,18},{10... | collective-permute-start | bytes 1572872 | tf_op jit(solution)/shard_map/ppermute | solution.py:379
  119.1 22.5 %collective-permute-start.17 = (f32[8,2,64,128]{3,2,1,0:T(8,128)S(1)}, f32[8,2,64,128]{3,2,1,0:T(8,128)S(1)}, u32[]{:S(2)}, u32[]{:S(2)}) collective-permute-start(f32[8,2,64,128]{3,2,1,0:T(8,128)S(1)} %get-tuple-element.120), channel_id=1, source_target_pairs={{0,24},{8,16},{16,8},{24,0},{1,25},{9,17},{17,9},{25,1},{2,26},{10... | collective-permute-start | bytes 1572872 | tf_op jit(solution)/shard_map/ppermute | solution.py:379
  123.4 28.1 %collective-permute-start.23 = (f32[8,2,64,128]{3,2,1,0:T(8,128)S(1)}, f32[8,2,64,128]{3,2,1,0:T(8,128)S(1)}, u32[]{:S(2)}, u32[]{:S(2)}) collective-permute-start(f32[8,2,64,128]{3,2,1,0:T(8,128)S(1)} %get-tuple-element.133), channel_id=1, source_target_pairs={{0,8},{8,0},{16,24},{24,16},{1,9},{9,1},{17,25},{25,17},{2,10},{10... | collective-permute-start | bytes 1572872 | tf_op jit(solution)/shard_map/ppermute | solution.py:379
  124.8 40.9 %collective-permute-start.24 = (f32[8,2,64,128]{3,2,1,0:T(8,128)S(1)}, f32[8,2,64,128]{3,2,1,0:T(8,128)S(1)}, u32[]{:S(2)}, u32[]{:S(2)}) collective-permute-start(f32[8,2,64,128]{3,2,1,0:T(8,128)S(1)} %get-tuple-element.143), channel_id=1, source_target_pairs={{0,16},{8,24},{16,0},{24,8},{1,17},{9,25},{17,1},{25,9},{2,18},{10... | collective-permute-start | bytes 1572872 | tf_op jit(solution)/shard_map/ppermute | solution.py:379
  129.0 36.8 %collective-permute-start.25 = (f32[8,2,64,128]{3,2,1,0:T(8,128)S(1)}, f32[8,2,64,128]{3,2,1,0:T(8,128)S(1)}, u32[]{:S(2)}, u32[]{:S(2)}) collective-permute-start(f32[8,2,64,128]{3,2,1,0:T(8,128)S(1)} %get-tuple-element.144), channel_id=1, source_target_pairs={{0,24},{8,16},{16,8},{24,0},{1,25},{9,17},{17,9},{25,1},{2,26},{10... | collective-permute-start | bytes 1572872 | tf_op jit(solution)/shard_map/ppermute | solution.py:379
  144.8 29.2 %collective-permute-start.27 = (f32[8,2,64,128]{3,2,1,0:T(8,128)S(1)}, f32[8,2,64,128]{3,2,1,0:T(8,128)S(1)}, u32[]{:S(2)}, u32[]{:S(2)}) collective-permute-start(f32[8,2,64,128]{3,2,1,0:T(8,128)S(1)} %get-tuple-element.150), channel_id=1, source_target_pairs={{0,8},{8,0},{16,24},{24,16},{1,9},{9,1},{17,25},{25,17},{2,10},{10... | collective-permute-start | bytes 1572872 | tf_op jit(solution)/shard_map/ppermute | solution.py:379
  145.5 41.0 %collective-permute-start.26 = (f32[8,2,64,128]{3,2,1,0:T(8,128)S(1)}, f32[8,2,64,128]{3,2,1,0:T(8,128)S(1)}, u32[]{:S(2)}, u32[]{:S(2)}) collective-permute-start(f32[8,2,64,128]{3,2,1,0:T(8,128)S(1)} %get-tuple-element.147), channel_id=1, source_target_pairs={{0,16},{8,24},{16,0},{24,8},{1,17},{9,25},{17,1},{25,9},{2,18},{10... | collective-permute-start | bytes 1572872 | tf_op jit(solution)/shard_map/ppermute | solution.py:379
  151.5 35.9 %collective-permute-start.19 = (f32[8,2,64,128]{3,2,1,0:T(8,128)S(1)}, f32[8,2,64,128]{3,2,1,0:T(8,128)S(1)}, u32[]{:S(2)}, u32[]{:S(2)}) collective-permute-start(f32[8,2,64,128]{3,2,1,0:T(8,128)S(1)} %get-tuple-element.126), channel_id=1, source_target_pairs={{0,24},{8,16},{16,8},{24,0},{1,25},{9,17},{17,9},{25,1},{2,26},{10... | collective-permute-start | bytes 1572872 | tf_op jit(solution)/shard_map/ppermute | solution.py:379

commit v4 on v3

--- a/solution.py
+++ b/solution.py
@@ -21,9 +21,13 @@
 COST = pl.CostEstimate(flops=1 << 10, bytes_accessed=1 << 10, transcendentals=0)
 
 
+def code(m, n):
+    return (n - m) % n
+
+
 def spectral_blocks(me, n, count):
     spots = jnp.arange(NT)
-    moments = (me ^ (spots // count)) * count + spots % count
+    moments = (me ^ code(spots // count, n)) * count + spots % count
     diff = moments[:, None] - moments[None, :]
     angle = jnp.pi * diff.astype(jnp.float32) / NT
     parity = 1.0 - 2.0 * (diff % 2).astype(jnp.float32)
@@ -50,15 +54,15 @@
 
     def block(m):
         return pl.BlockSpec(
-            (count, 1, width, length), lambda i, me: (0, (chunk * n + (me[0] ^ m)) * part + i, 0, 0)
+            (count, part, width, length), lambda i, me: (0, chunk * n + (me[0] ^ code(m, n)), 0, 0)
         )
 
-    piece = pl.BlockSpec((count, 1, width, length), lambda i, me: (0, i, 0, 0))
+    piece = pl.BlockSpec((count, part, width, length), lambda i, me: (0, 0, 0, 0))
     return pl.pallas_call(
         cut_kernel,
         grid_spec=pltpu.PrefetchScalarGridSpec(
             num_scalar_prefetch=1,
-            grid=(part,),
+            grid=(1,),
             in_specs=[block(m) for m in partners],
             out_specs=[piece] * len(partners),
         ),
@@ -279,7 +283,7 @@
     part = pieces[0].shape[1]
     for m, piece in enumerate(pieces):
         for i in range(part):
-            z = (me_ref[0] ^ m) * part + i
+            z = (me_ref[0] ^ code(m, n)) * part + i
             res = s_ref[:, z] + piece[:, i]
             mid = u_ref[:, z] - winv_ref[:, z] * res
             res_ref[:, z] = res
@@ -323,7 +327,7 @@
 
 def last_update(me, piece, base, winv, n, chunk, m, before, held=None):
     count, part, width, length = piece.shape
-    layers = pl.BlockSpec((count, part, width, length), lambda i, me: (0, chunk * n + (me[0] ^ m), 0, 0))
+    layers = pl.BlockSpec((count, part, width, length), lambda i, me: (0, chunk * n + (me[0] ^ code(m, n)), 0, 0))
     block = pl.BlockSpec((count, part, width, length), lambda i, me: (0, 0, 0, 0))
     return pl.pallas_call(
         lambda me_ref, *refs: last_kernel(*refs),
@@ -341,13 +345,52 @@
     )(me, piece, *(held or in_hbm(base, winv)), *in_hbm(before))
 
 
+def final_kernel(n, spots, me_ref, *refs):
+    count = len(spots)
+    pieces, bases, winvs = refs[:count], refs[count : 2 * count], refs[2 * count : 3 * count]
+    out_ref, sums, sems = refs[3 * count + 1 :]
+    part = pieces[0].shape[1]
+    copies = []
+    for p, (first, m) in enumerate(spots):
+        for i in range(part):
+            sums[p, :, i] = bases[p][:, i] - winvs[p][:, i] * pieces[p][:, i]
+            place = (first + (me_ref[0] ^ code(m, n))) * part + i
+            copy = pltpu.make_async_copy(
+                sums.at[p, :, pl.ds(i, 1)], out_ref.at[:, pl.ds(place, 1)], sems.at[p, i]
+            )
+            copy.start()
+            copies.append(copy)
+    for copy in copies:
+        copy.wait()
+
+
+def final_update(me, pieces, bases, winvs, n, spots, before):
+    vmem = pl.BlockSpec(memory_space=pltpu.VMEM)
+    anywhere = pl.BlockSpec(memory_space=pl.ANY)
+    count = len(pieces)
+    return pl.pallas_call(
+        functools.partial(final_kernel, n, spots),
+        in_specs=[pl.BlockSpec(memory_space=pltpu.SMEM)] + [vmem] * (3 * count) + [anywhere],
+        out_specs=anywhere,
+        out_shape=pltpu.HBM(before.shape, jnp.float32),
+        scratch_shapes=[
+            pltpu.VMEM((count, *pieces[0].shape), jnp.float32),
+            pltpu.SemaphoreType.DMA((count, pieces[0].shape[1])),
+        ],
+        input_output_aliases={3 * count + 1: 0},
+        compiler_params=pltpu.CompilerParams(vmem_limit_bytes=VMEM),
+        cost_estimate=COST,
+        name="final_update",
+    )(me, *pieces, *bases, *winvs, *in_hbm(before))
+
+
 def chunk_kernel(n, me_ref, *refs):
     pieces, (base_ref, winv_ref) = refs[:n], refs[n : n + 2]
     out_ref = refs[-1]
     part = pieces[0].shape[1]
     for m, piece in enumerate(pieces):
         for i in range(part):
-            z = (me_ref[0] ^ m) * part + i
+            z = (me_ref[0] ^ code(m, n)) * part + i
             out_ref[:, z] = base_ref[:, z] - winv_ref[:, z] * piece[:, i]
 
 
@@ -376,7 +419,7 @@
 def exchange(pieces):
     n = len(pieces) + 1
     return [
-        lax.ppermute(piece, "inst", [(i, i ^ m) for i in range(n)]) for m, piece in enumerate(pieces, 1)
+        lax.ppermute(piece, "inst", [(i, i ^ code(m, n)) for i in range(n)]) for m, piece in enumerate(pieces, 1)
     ]
 
 
@@ -400,9 +443,9 @@
     me = lax.axis_index("inst")
     me_array = me.reshape(1).astype(jnp.int32)
 
-    far = cut(me_array, field_start, n, 0, part, [n - 1])
-    near = cut(me_array, after(field_start, *far), n, 0, part, range(1, n - 1))
-    going = near + far
+    far = cut(me_array, field_start, n, 0, part, [1])
+    near = cut(me_array, after(field_start, *far), n, 0, part, range(2, n))
+    going = far + near
     there = [exchange(going)]
     start, flags, material = after((field_start, face_flags, material), *going)
 
@@ -462,12 +505,15 @@
         field = [chunk_update(me_array, back[chunk], base, winv, chunk, field)]
     chunk = chunks - 1
     held = [cut(me_array, array, n, chunk, part) for array in (base, winv)]
-    for m, piece in enumerate(back[chunk]):
+    late = max(1, n - 2)
+    for m, piece in enumerate(back[chunk][:late]):
         there = [pieces[m - 1] for pieces in held] if m else None
         field = [last_update(me_array, piece, base, winv, n, chunk, m, field[0], there)]
         if m == 0:
             held, field = after((held, field), held)
-    return (residual, field[0])
+    bases, winvs = (pieces[late - 1 :] for pieces in held)
+    spots = [(chunk * n, m) for m in range(late, n)]
+    return (residual, final_update(me_array, back[chunk][late:], bases, winvs, n, spots, field[0]))
 
 
 def solution(mesh):

time: 189 us -> 188 us (level)
  waiting for transfers between devices: 63.4 us -> 60.9 us
  starting transfers between devices: 36 us -> 38.1 us
    ppermute x24, waiting for transfers between devices: 53.6 us -> 51.2 us  [exchange(): lax.ppermute(piece, 'inst', [(i, i ^ code(m, n)) for i in range(n)])]
    ppermute x24, starting transfers between devices: 22.5 us -> 24.8 us  [exchange(): lax.ppermute(piece, 'inst', [(i, i ^ code(m, n)) for i in range(n)])]
    pallas_call x4 -> x2, Pallas kernels: 4.73 us -> 2.94 us  [last_update(): pl.pallas_call(lambda me_ref, *refs: last_kernel(*refs), grid_spec=pltpu....]
  transfers between devices with their start and end apart: 28 -> 28, of which waited for: 13 -> 15; matrix products, arithmetic and copies ran while one was open for 3% -> 3% of each run, Pallas kernels for 43% -> 43%
where the time goes in v4:
time: 188 us; the launch traced here: 187 us
  Pallas kernels  82.2 us (44%)
  waiting for transfers between devices  60.9 us (32%)
  starting transfers between devices  38.1 us (20%)
  local copies, waits for them, and re-layouts  4.14 us (2%)
    ppermute x24, waiting for transfers between devices, exchange(): lax.ppermute(piece, 'inst', [(i, i ^ code(m, n)) for i in range(n)])  51.2 us
    pallas_call x4, Pallas kernels, stencil(): pl.pallas_call(functools.partial(stencil_kernel, second, first, len(befor...  38 us
    ppermute x24, starting transfers between devices, exchange(): lax.ppermute(piece, 'inst', [(i, i ^ code(m, n)) for i in range(n)])  24.8 us
    pallas_call x4, Pallas kernels, apply_time(): pl.pallas_call(functools.partial(apply_kernel, n), grid_spec=pltpu.Prefet...  13.2 us
    pallas_call x2, Pallas kernels, first_update(): pl.pallas_call(functools.partial(first_kernel, n, aliased), grid_spec=plt...  11 us
    ppermute x2, waiting for transfers between devices, downward(): lax.ppermute(plane, 'space', [(i + 1, i) for i in range(lax.axis_size('sp...  9.6 us
    pallas_call x5, Pallas kernels, cut(): pl.pallas_call(cut_kernel, grid_spec=pltpu.PrefetchScalarGridSpec(num_sca...  8.75 us
    ppermute x2, starting transfers between devices, upward(): lax.ppermute(plane, 'space', [(i, i + 1) for i in range(lax.axis_size('sp...  8.3 us
  transfers between devices with their start and end apart: 28, of which 15 were waited for; matrix products, arithmetic and copies ran while one was open for 3% of the time, Pallas kernels for 43%

profile of v4, /device:TPU:9, one launch (start us, length us, event | category | flops | bytes accessed | tf_op | source)
XLA Modules:
  0.0 187.4 jit_solution(12416581000027316150)
XLA Ops:
  0.6 1.1 cut.5
  1.7 2.2 %collective-permute-start.8 = (f32[8,2,64,128]{3,2,1,0:T(8,128)S(1)}, f32[8,2,64,128]{3,2,1,0:T(8,128)S(1)}, u32[]{:S(2)}, u32[]{:S(2)}) collective-permute-start(f32[8,2,64,128]{3,2,1,0:T(8,128)S(1)} %cut.5), channel_id=1, source_target_pairs={{0,24},{8,16},{16,8},{24,0},{1,25},{9,17},{17,9},{25,1},{2,26},{10... | collective-permute-start | bytes 1572872 | tf_op jit(solution)/shard_map/ppermute | solution.py:422
  4.0 2.2 %cut.6 = (f32[8,2,64,128]{3,2,1,0:T(8,128)}, f32[8,2,64,128]{3,2,1,0:T(8,128)}) custom-call(s32[1]{0:T(128)} %bitcast.me_ref, f32[8,16,64,128]{3,2,1,0:T(8,128)} %refs_6_.3, f32[8,16,64,128]{3,2,1,0:T(8,128)} %refs_6_.3), custom_call_target="tpu_custom_call" | custom-call | flops 1024 | bytes 1024 | tf_op jit(solution)/shard_map/cut/pallas_call | solution.py:61
  6.2 0.3 collective-permute-start.10
  6.4 0.2 collective-permute-start.9
  6.7 2.8 %prep.1 = (f32[16,64,128]{2,1,0:T(8,128)S(1)}, f32[16,64,128]{2,1,0:T(8,128)S(1)}, f32[17,64,128]{2,1,0:T(8,128)}, f32[8,64,128]{2,1,0:T(8,128)}) custom-call(f32[8]{0:T(128)S(1)} %copy-done, f32[8]{0:T(128)S(1)} %copy-done.1, f32[8]{0:T(128)S(1)} %multiply_add_fusion.tide_ref, s32[16,64,128]{2,1,0:T(8,128)} %material_ref, s32[8,3,16,64,128]{4,3,2,1,0:T(8,128)} %flags_ref.6, ...), custom_call_target="tpu_custom_call" | custom-call | flops 1024 | bytes 1024 | tf_op jit(solution)/shard_map/prep/pallas_call | solution.py:109
  9.5 4.6 %collective-permute-start = (f32[17,64,128]{2,1,0:T(8,128)}, f32[17,64,128]{2,1,0:T(8,128)S(1)}, u32[]{:S(2)}, u32[]{:S(2)}) collective-permute-start(f32[17,64,128]{2,1,0:T(8,128)} %get-tuple-element.84), channel_id=1, source_target_pairs={{0,1},{1,2},{2,3},{3,4},{4,5},{5,6},{6,7},{8,9},{9,10},{10,11},{11... | collective-permute-start | bytes 1671176 | tf_op jit(solution)/shard_map/ppermute | solution.py:431
  14.1 1.9 %collective-permute-start.1 = (f32[8,64,128]{2,1,0:T(8,128)}, f32[8,64,128]{2,1,0:T(8,128)S(1)}, u32[]{:S(2)}, u32[]{:S(2)}) collective-permute-start(f32[8,64,128]{2,1,0:T(8,128)} %get-tuple-element.85), channel_id=1, source_target_pairs={{1,0},{2,1},{3,2},{4,3},{5,4},{6,5},{7,6},{9,8},{10,9},{11,10},{12... | collective-permute-start | bytes 786440 | tf_op jit(solution)/shard_map/ppermute | solution.py:435
  16.2 0.7 broadcast_bitcast_fusion.1
  16.9 1.0 copy.17
  17.9 4.6 %collective-permute-done.1.high_ref = f32[8,64,128]{2,1,0:T(8,128)S(1)} collective-permute-done((f32[8,64,128]{2,1,0:T(8,128)}, f32[8,64,128]{2,1,0:T(8,128)S(1)}, u32[]{:S(2)}, u32[]{:S(2)}) %collective-permute-start.1) | collective-permute-done | bytes 262176 | tf_op jit(solution)/shard_map/ppermute | solution.py:435
  22.4 2.6 %cut.7 = (f32[8,2,64,128]{3,2,1,0:T(8,128)}, f32[8,2,64,128]{3,2,1,0:T(8,128)}, f32[8,2,64,128]{3,2,1,0:T(8,128)}) custom-call(s32[1]{0:T(128)} %bitcast.me_ref, f32[8,16,64,128]{3,2,1,0:T(8,128)} %refs_6_.3, f32[8,16,64,128]{3,2,1,0:T(8,128)} %refs_6_.3, f32[8,16,64,128]{3,2,1,0:T(8,128)} %refs_6_.3), custom_call_target="tpu_custom_call" | custom-call | flops 1024 | bytes 1024 | tf_op jit(solution)/shard_map/cut/pallas_call | solution.py:61
  25.0 2.2 %collective-permute-start.2 = (f32[8,2,64,128]{3,2,1,0:T(8,128)}, f32[8,2,64,128]{3,2,1,0:T(8,128)}, u32[]{:S(2)}, u32[]{:S(2)}) collective-permute-start(f32[8,2,64,128]{3,2,1,0:T(8,128)} %get-tuple-element.87), channel_id=1, source_target_pairs={{0,24},{8,16},{16,8},{24,0},{1,25},{9,17},{17,9},{25,1},{2,26},{10... | collective-permute-start | bytes 1572872 | tf_op jit(solution)/shard_map/ppermute | solution.py:422
  27.2 0.7 broadcast_bitcast_fusion
  27.9 0.2 collective-permute-start.3
  28.1 0.3 collective-permute-start.4
  28.4 1.8 copy.18
  30.1 1.0 compare_select_fusion.refs_3_
  31.2 9.8 %stencil_one.2 = (f32[8,16,64,128]{3,2,1,0:T(8,128)}, f32[8,16,64,128]{3,2,1,0:T(8,128)}) custom-call(f32[8]{0:T(128)S(1)} %multiply_add_fusion.tide_ref, f32[8,16,64,128]{3,2,1,0:T(8,128)} %refs_6_.3, f32[17,64,128]{2,1,0:T(8,128)S(1)} %collective-permute-done.low_ref.below_k_ref.below_f_ref, f32[8,64,128]{2,1,0:T(8,128)S(1)} %collective-permute-done.1.high_ref, ...), custom_call_target="tpu_custom_call" | custom-call | flops 1024 | bytes 1024 | tf_op jit(solution)/shard_map/stencil_one/pallas_call | solution.py:216
  41.0 3.3 %apply_time.5 = (f32[8,2,64,128]{3,2,1,0:T(8,128)S(1)}, f32[8,2,64,128]{3,2,1,0:T(8,128)S(1)}, f32[8,2,64,128]{3,2,1,0:T(8,128)S(1)}, f32[8,2,64,128]{3,2,1,0:T(8,128)S(1)}) custom-call(s32[1]{0:T(128)} %bitcast.me_ref, f32[8,16,64,128]{3,2,1,0:T(8,128)} %refs_6_.3, f32[8,2,64,128]{3,2,1,0:T(8,128)S(1)} %collective-permute-done.8.refs_0_, ...), custom_call_target="tpu_custom_call" | custom-call | flops 1024 | bytes 1024 | tf_op jit(solution)/shard_map/apply_time/pallas_call | solution.py:258
  44.4 2.2 %collective-permute-start.11 = (f32[8,2,64,128]{3,2,1,0:T(8,128)S(1)}, f32[8,2,64,128]{3,2,1,0:T(8,128)S(1)}, u32[]{:S(2)}, u32[]{:S(2)}) collective-permute-start(f32[8,2,64,128]{3,2,1,0:T(8,128)S(1)} %get-tuple-element.103), channel_id=1, source_target_pairs={{0,24},{8,16},{16,8},{24,0},{1,25},{9,17},{17,9},{25,1},{2,26},{10... | collective-permute-start | bytes 1572872 | tf_op jit(solution)/shard_map/ppermute | solution.py:422
  46.8 0.3 collective-permute-start.13
  47.1 4.3 %collective-permute-done.3.refs_1_ = f32[8,2,64,128]{3,2,1,0:T(8,128)} collective-permute-done((f32[8,2,64,128]{3,2,1,0:T(8,128)}, f32[8,2,64,128]{3,2,1,0:T(8,128)}, u32[]{:S(2)}, u32[]{:S(2)}) %collective-permute-start.3) | collective-permute-done | bytes 524320 | tf_op jit(solution)/shard_map/ppermute | solution.py:422
  51.4 3.5 %apply_time.4 = (f32[8,2,64,128]{3,2,1,0:T(8,128)S(1)}, f32[8,2,64,128]{3,2,1,0:T(8,128)S(1)}, f32[8,2,64,128]{3,2,1,0:T(8,128)S(1)}, f32[8,2,64,128]{3,2,1,0:T(8,128)S(1)}) custom-call(s32[1]{0:T(128)} %bitcast.me_ref, f32[8,16,64,128]{3,2,1,0:T(8,128)} %refs_6_.3, f32[8,2,64,128]{3,2,1,0:T(8,128)} %collective-permute-done.2.refs_0_, ...), custom_call_target="tpu_custom_call" | custom-call | flops 1024 | bytes 1024 | tf_op jit(solution)/shard_map/apply_time/pallas_call | solution.py:258
  54.8 2.2 %collective-permute-start.5 = (f32[8,2,64,128]{3,2,1,0:T(8,128)S(1)}, f32[8,2,64,128]{3,2,1,0:T(8,128)S(1)}, u32[]{:S(2)}, u32[]{:S(2)}) collective-permute-start(f32[8,2,64,128]{3,2,1,0:T(8,128)S(1)} %get-tuple-element.91), channel_id=1, source_target_pairs={{0,24},{8,16},{16,8},{24,0},{1,25},{9,17},{17,9},{25,1},{2,26},{10... | collective-permute-start | bytes 1572872 | tf_op jit(solution)/shard_map/ppermute | solution.py:422
  57.1 5.4 %collective-permute-done.11.refs_1_ = f32[8,2,64,128]{3,2,1,0:T(8,128)S(1)} collective-permute-done((f32[8,2,64,128]{3,2,1,0:T(8,128)S(1)}, f32[8,2,64,128]{3,2,1,0:T(8,128)S(1)}, u32[]{:S(2)}, u32[]{:S(2)}) %collective-permute-start.11) | collective-permute-done | bytes 524320 | tf_op jit(solution)/shard_map/ppermute | solution.py:422
  62.5 1.2 collective-permute-start.6
  63.7 1.2 collective-permute-start.7
  64.9 9.8 %stencil_one.3 = (f32[8,16,64,128]{3,2,1,0:T(8,128)}, f32[8,16,64,128]{3,2,1,0:T(8,128)}) custom-call(f32[8]{0:T(128)S(1)} %multiply_add_fusion.tide_ref, f32[8,16,64,128]{3,2,1,0:T(8,128)} %refs_6_.3, f32[17,64,128]{2,1,0:T(8,128)S(1)} %collective-permute-done.low_ref.below_k_ref.below_f_ref, ...), custom_call_target="tpu_custom_call", output_to_operand_aliasing={{0}: (10, {}), {1}: (11, {})} | custom-call | flops 1024 | bytes 1024 | tf_op jit(solution)/shard_map/stencil_one/pallas_call | solution.py:216
  74.8 5.6 %first_update.2 = (f32[8,16,64,128]{3,2,1,0:T(8,128)}, f32[8,16,64,128]{3,2,1,0:T(8,128)}, f32[8,64,128]{2,1,0:T(8,128)S(1)}, f32[8,64,128]{2,1,0:T(8,128)}, f32...) custom-call(s32[1]{0:T(128)} %bitcast.me_ref, ...), custom_call_target="tpu_custom_call" | custom-call | flops 1024 | bytes 1024 | tf_op jit(solution)/shard_map/first_update/pallas_call | solution.py:306
  80.4 3.1 %collective-permute-start.14 = (f32[8,64,128]{2,1,0:T(8,128)S(1)}, f32[8,64,128]{2,1,0:T(8,128)S(1)}, u32[]{:S(2)}, u32[]{:S(2)}) collective-permute-start(f32[8,64,128]{2,1,0:T(8,128)S(1)} %get-tuple-element.109), channel_id=1, source_target_pairs={{1,0},{2,1},{3,2},{4,3},{5,4},{6,5},{7,6},{9,8},{10,9},{11,10},{12... | collective-permute-start | bytes 786440 | tf_op jit(solution)/shard_map/ppermute | solution.py:435
  83.5 0.5 collective-permute-start.21
  83.9 5.0 %collective-permute-done.14.high_ref = f32[8,64,128]{2,1,0:T(8,128)S(1)} collective-permute-done((f32[8,64,128]{2,1,0:T(8,128)S(1)}, f32[8,64,128]{2,1,0:T(8,128)S(1)}, u32[]{:S(2)}, u32[]{:S(2)}) %collective-permute-start.14) | collective-permute-done | bytes 262176 | tf_op jit(solution)/shard_map/ppermute | solution.py:435
  89.0 0.2 collective-permute-start.22
  89.2 0.5 collective-permute-start.23
  89.7 6.5 %collective-permute-done.6.refs_2_ = f32[8,2,64,128]{3,2,1,0:T(8,128)S(1)} collective-permute-done((f32[8,2,64,128]{3,2,1,0:T(8,128)S(1)}, f32[8,2,64,128]{3,2,1,0:T(8,128)S(1)}, u32[]{:S(2)}, u32[]{:S(2)}) %collective-permute-start.6) | collective-permute-done | bytes 524320 | tf_op jit(solution)/shard_map/ppermute | solution.py:422
  96.3 5.4 %first_update.3 = (f32[8,16,64,128]{3,2,1,0:T(8,128)}, f32[8,16,64,128]{3,2,1,0:T(8,128)}, f32[8,64,128]{2,1,0:T(8,128)}, f32[8,64,128]{2,1,0:T(8,128)S(1)}, f32...) custom-call(s32[1]{0:T(128)} %bitcast.me_ref, ...), custom_call_target="tpu_custom_call", output_to_operand_aliasing={{0}: (8, {}), {1}: (9, {})} | custom-call | flops 1024 | bytes 1024 | tf_op jit(solution)/shard_map/first_update/pallas_call | solution.py:306
  101.7 3.7 %collective-permute-start.18 = (f32[8,64,128]{2,1,0:T(8,128)S(1)}, f32[8,64,128]{2,1,0:T(8,128)S(1)}, u32[]{:S(2)}, u32[]{:S(2)}) collective-permute-start(f32[8,64,128]{2,1,0:T(8,128)S(1)} %get-tuple-element.122), channel_id=1, source_target_pairs={{0,1},{1,2},{2,3},{3,4},{4,5},{5,6},{6,7},{8,9},{9,10},{10,11},{11... | collective-permute-start | bytes 786440 | tf_op jit(solution)/shard_map/ppermute | solution.py:431
  105.5 2.0 %collective-permute-start.15 = (f32[8,2,64,128]{3,2,1,0:T(8,128)S(1)}, f32[8,2,64,128]{3,2,1,0:T(8,128)S(1)}, u32[]{:S(2)}, u32[]{:S(2)}) collective-permute-start(f32[8,2,64,128]{3,2,1,0:T(8,128)S(1)} %get-tuple-element.118), channel_id=1, source_target_pairs={{0,24},{8,16},{16,8},{24,0},{1,25},{9,17},{17,9},{25,1},{2,26},{10... | collective-permute-start | bytes 1572872 | tf_op jit(solution)/shard_map/ppermute | solution.py:422
  107.5 1.2 collective-permute-start.16
  108.8 9.9 %collective-permute-done.22.refs_1_ = f32[8,2,64,128]{3,2,1,0:T(8,128)S(1)} collective-permute-done((f32[8,2,64,128]{3,2,1,0:T(8,128)S(1)}, f32[8,2,64,128]{3,2,1,0:T(8,128)S(1)}, u32[]{:S(2)}, u32[]{:S(2)}) %collective-permute-start.22) | collective-permute-done | bytes 524320 | tf_op jit(solution)/shard_map/ppermute | solution.py:422
  118.7 1.2 collective-permute-start.17
  119.9 3.2 %apply_time.7 = (f32[8,2,64,128]{3,2,1,0:T(8,128)S(1)}, f32[8,2,64,128]{3,2,1,0:T(8,128)S(1)}, f32[8,2,64,128]{3,2,1,0:T(8,128)S(1)}, f32[8,2,64,128]{3,2,1,0:T(8,128)S(1)}) custom-call(s32[1]{0:T(128)} %bitcast.me_ref, f32[8,16,64,128]{3,2,1,0:T(8,128)} %get-tuple-element.135.u_ref.own_ref, f32[8,2,64,128]{3,2,1,0:T(8,128)S(1)} %collective-permute-done.21.refs_0_, ...), custom_call_target="tpu_custom_call" | custom-call | flops 1024 | bytes 1024 | tf_op jit(solution)/shard_map/apply_time/pallas_call | solution.py:258
  123.1 1.3 collective-permute-start.24
  124.4 0.2 collective-permute-start.25
  124.6 5.4 %collective-permute-done.15.refs_0_ = f32[8,2,64,128]{3,2,1,0:T(8,128)S(1)} collective-permute-done((f32[8,2,64,128]{3,2,1,0:T(8,128)S(1)}, f32[8,2,64,128]{3,2,1,0:T(8,128)S(1)}, u32[]{:S(2)}, u32[]{:S(2)}) %collective-permute-start.15) | collective-permute-done | bytes 524320 | tf_op jit(solution)/shard_map/ppermute | solution.py:422
  130.0 1.2 collective-permute-start.26
  131.2 9.2 %stencil_two.2.rest_1_ = f32[8,16,64,128]{3,2,1,0:T(8,128)} custom-call(f32[8]{0:T(128)S(1)} %multiply_add_fusion.tide_ref, f32[8,16,64,128]{3,2,1,0:T(8,128)} %get-tuple-element.135.u_ref.own_ref, f32[8,64,128]{2,1,0:T(8,128)S(1)} %collective-permute-done.18.low_ref, f32[8,64,128]{2,1,0:T(8,128)S(1)} %collective-permute-done.14.high_ref, ...), custom_call_target="tpu_custom_call" | custom-call | flops 1024 | bytes 1024 | tf_op jit(solution)/shard_map/stencil_two/pallas_call | solution.py:216
  140.4 0.7 collective-permute-done.16.refs_1_
  141.3 3.2 %apply_time.6 = (f32[8,2,64,128]{3,2,1,0:T(8,128)S(1)}, f32[8,2,64,128]{3,2,1,0:T(8,128)S(1)}, f32[8,2,64,128]{3,2,1,0:T(8,128)S(1)}, f32[8,2,64,128]{3,2,1,0:T(8,128)S(1)}) custom-call(s32[1]{0:T(128)} %bitcast.me_ref, f32[8,16,64,128]{3,2,1,0:T(8,128)} %get-tuple-element.135.u_ref.own_ref, f32[8,2,64,128]{3,2,1,0:T(8,128)S(1)} %collective-permute-done.15.refs_0_, ...), custom_call_target="tpu_custom_call" | custom-call | flops 1024 | bytes 1024 | tf_op jit(solution)/shard_map/apply_time/pallas_call | solution.py:258
  144.5 2.0 %collective-permute-start.27 = (f32[8,2,64,128]{3,2,1,0:T(8,128)S(1)}, f32[8,2,64,128]{3,2,1,0:T(8,128)S(1)}, u32[]{:S(2)}, u32[]{:S(2)}) collective-permute-start(f32[8,2,64,128]{3,2,1,0:T(8,128)S(1)} %get-tuple-element.150), channel_id=1, source_target_pairs={{0,24},{8,16},{16,8},{24,0},{1,25},{9,17},{17,9},{25,1},{2,26},{10... | collective-permute-start | bytes 1572872 | tf_op jit(solution)/shard_map/ppermute | solution.py:422
  146.6 0.4 collective-permute-start.19
  147.0 5.6 %collective-permute-done.24.refs_1_ = f32[8,2,64,128]{3,2,1,0:T(8,128)S(1)} collective-permute-done((f32[8,2,64,128]{3,2,1,0:T(8,128)S(1)}, f32[8,2,64,128]{3,2,1,0:T(8,128)S(1)}, u32[]{:S(2)}, u32[]{:S(2)}) %collective-permute-start.24) | collective-permute-done | bytes 524320 | tf_op jit(solution)/shard_map/ppermute | solution.py:422
  152.5 1.2 collective-permute-start.20
  153.8 9.2 %stencil_two.3.refs_0_.refs_1_.refs_2_.refs_4_ = f32[8,16,64,128]{3,2,1,0:T(8,128)} custom-call(f32[8]{0:T(128)S(1)} %multiply_add_fusion.tide_ref, f32[8,16,64,128]{3,2,1,0:T(8,128)} %get-tuple-element.135.u_ref.own_ref, f32[8,64,128]{2,1,0:T(8,128)S(1)} %collective-permute-done.18.low_ref, ...), custom_call_target="tpu_custom_call", output_to_operand_aliasing={{}: (11, {})} | custom-call | flops 1024 | bytes 1024 | tf_op jit(solution)/shard_map/stencil_two/pallas_call | solution.py:216
  162.9 1.5 cut.9
  164.4 1.5 cut.8
  165.9 4.5 %chunk_update.1.refs_3_ = f32[8,16,64,128]{3,2,1,0:T(8,128)} custom-call(s32[1]{0:T(128)} %bitcast.me_ref, f32[8,2,64,128]{3,2,1,0:T(8,128)S(1)} %get-tuple-element.143.refs_0_, f32[8,2,64,128]{3,2,1,0:T(8,128)S(1)} %collective-permute-done.24.refs_1_, f32[8,2,64,128]{3,2,1,0:T(8,128)S(1)} %collective-permute-done.25.refs_2_, ...), custom_call_target="tpu_custom_call" | custom-call | flops 1024 | bytes 1024 | tf_op jit(solution)/shard_map/chunk_update/pallas_call | solution.py:403
  170.4 2.1 %last_update.2.refs_3_ = f32[8,16,64,128]{3,2,1,0:T(8,128)} custom-call(s32[1]{0:T(128)} %bitcast.me_ref, f32[8,2,64,128]{3,2,1,0:T(8,128)S(1)} %get-tuple-element.142.refs_0_, f32[8,16,64,128]{3,2,1,0:T(8,128)} %stencil_two.3.refs_0_.refs_1_.refs_2_.refs_4_, ...), custom_call_target="tpu_custom_call", output_to_operand_aliasing={{}: (4, {})} | custom-call | flops 1024 | bytes 1024 | tf_op jit(solution)/shard_map/last_update/pallas_call | solution.py:332
  172.4 2.6 %collective-permute-done.27.refs_0_ = f32[8,2,64,128]{3,2,1,0:T(8,128)S(1)} collective-permute-done((f32[8,2,64,128]{3,2,1,0:T(8,128)S(1)}, f32[8,2,64,128]{3,2,1,0:T(8,128)S(1)}, u32[]{:S(2)}, u32[]{:S(2)}) %collective-permute-start.27) | collective-permute-done | bytes 524320 | tf_op jit(solution)/shard_map/ppermute | solution.py:422
  175.1 0.9 last_update.3.refs_6_
  175.9 10.1 %collective-permute-done.19.refs_0_ = f32[8,2,64,128]{3,2,1,0:T(8,128)S(1)} collective-permute-done((f32[8,2,64,128]{3,2,1,0:T(8,128)S(1)}, f32[8,2,64,128]{3,2,1,0:T(8,128)S(1)}, u32[]{:S(2)}, u32[]{:S(2)}) %collective-permute-start.19) | collective-permute-done | bytes 524320 | tf_op jit(solution)/shard_map/ppermute | solution.py:422
  186.1 0.3 collective-permute-done.20.refs_1_
  186.4 1.0 final_update.1
  (25 shorter events, 0.9 us)
Async XLA Ops:
  1.7 5.0 %copy-start = (f32[8]{0:T(128)S(1)}, f32[8]{0:T(128)}, u32[]{:S(2)}) copy-start(f32[8]{0:T(128)} %disp_ref.1) | copy-start | bytes 100
  1.7 5.0 %copy-start.1 = (f32[8]{0:T(128)S(1)}, f32[8]{0:T(128)}, u32[]{:S(2)}) copy-start(f32[8]{0:T(128)} %perm_ref.1) | copy-start | bytes 100
  1.7 39.3 %collective-permute-start.8 = (f32[8,2,64,128]{3,2,1,0:T(8,128)S(1)}, f32[8,2,64,128]{3,2,1,0:T(8,128)S(1)}, u32[]{:S(2)}, u32[]{:S(2)}) collective-permute-start(f32[8,2,64,128]{3,2,1,0:T(8,128)S(1)} %cut.5), channel_id=1, source_target_pairs={{0,24},{8,16},{16,8},{24,0},{1,25},{9,17},{17,9},{25,1},{2,26},{10... | collective-permute-start | bytes 1572872 | tf_op jit(solution)/shard_map/ppermute | solution.py:422
  6.2 22.0 %collective-permute-start.10 = (f32[8,2,64,128]{3,2,1,0:T(8,128)}, f32[8,2,64,128]{3,2,1,0:T(8,128)S(1)}, u32[]{:S(2)}, u32[]{:S(2)}) collective-permute-start(f32[8,2,64,128]{3,2,1,0:T(8,128)} %get-tuple-element.80), channel_id=1, source_target_pairs={{0,8},{8,0},{16,24},{24,16},{1,9},{9,1},{17,25},{25,17},{2,10},{10... | collective-permute-start | bytes 1572872 | tf_op jit(solution)/shard_map/ppermute | solution.py:422
  6.4 34.6 %collective-permute-start.9 = (f32[8,2,64,128]{3,2,1,0:T(8,128)}, f32[8,2,64,128]{3,2,1,0:T(8,128)}, u32[]{:S(2)}, u32[]{:S(2)}) collective-permute-start(f32[8,2,64,128]{3,2,1,0:T(8,128)} %get-tuple-element.79), channel_id=1, source_target_pairs={{0,16},{8,24},{16,0},{24,8},{1,17},{9,25},{17,1},{25,9},{2,18},{10... | collective-permute-start | bytes 1572872 | tf_op jit(solution)/shard_map/ppermute | solution.py:422
  9.5 12.9 %collective-permute-start = (f32[17,64,128]{2,1,0:T(8,128)}, f32[17,64,128]{2,1,0:T(8,128)S(1)}, u32[]{:S(2)}, u32[]{:S(2)}) collective-permute-start(f32[17,64,128]{2,1,0:T(8,128)} %get-tuple-element.84), channel_id=1, source_target_pairs={{0,1},{1,2},{2,3},{3,4},{4,5},{5,6},{6,7},{8,9},{9,10},{10,11},{11... | collective-permute-start | bytes 1671176 | tf_op jit(solution)/shard_map/ppermute | solution.py:431
  14.1 8.3 %collective-permute-start.1 = (f32[8,64,128]{2,1,0:T(8,128)}, f32[8,64,128]{2,1,0:T(8,128)S(1)}, u32[]{:S(2)}, u32[]{:S(2)}) collective-permute-start(f32[8,64,128]{2,1,0:T(8,128)} %get-tuple-element.85), channel_id=1, source_target_pairs={{1,0},{2,1},{3,2},{4,3},{5,4},{6,5},{7,6},{9,8},{10,9},{11,10},{12... | collective-permute-start | bytes 786440 | tf_op jit(solution)/shard_map/ppermute | solution.py:435
  25.0 21.8 %collective-permute-start.2 = (f32[8,2,64,128]{3,2,1,0:T(8,128)}, f32[8,2,64,128]{3,2,1,0:T(8,128)}, u32[]{:S(2)}, u32[]{:S(2)}) collective-permute-start(f32[8,2,64,128]{3,2,1,0:T(8,128)} %get-tuple-element.87), channel_id=1, source_target_pairs={{0,24},{8,16},{16,8},{24,0},{1,25},{9,17},{17,9},{25,1},{2,26},{10... | collective-permute-start | bytes 1572872 | tf_op jit(solution)/shard_map/ppermute | solution.py:422
  27.9 23.5 %collective-permute-start.3 = (f32[8,2,64,128]{3,2,1,0:T(8,128)}, f32[8,2,64,128]{3,2,1,0:T(8,128)}, u32[]{:S(2)}, u32[]{:S(2)}) collective-permute-start(f32[8,2,64,128]{3,2,1,0:T(8,128)} %get-tuple-element.88), channel_id=1, source_target_pairs={{0,16},{8,24},{16,0},{24,8},{1,17},{9,25},{17,1},{25,9},{2,18},{10... | collective-permute-start | bytes 1572872 | tf_op jit(solution)/shard_map/ppermute | solution.py:422
  28.1 23.3 %collective-permute-start.4 = (f32[8,2,64,128]{3,2,1,0:T(8,128)}, f32[8,2,64,128]{3,2,1,0:T(8,128)}, u32[]{:S(2)}, u32[]{:S(2)}) collective-permute-start(f32[8,2,64,128]{3,2,1,0:T(8,128)} %get-tuple-element.89), channel_id=1, source_target_pairs={{0,8},{8,0},{16,24},{24,16},{1,9},{9,1},{17,25},{25,17},{2,10},{10... | collective-permute-start | bytes 1572872 | tf_op jit(solution)/shard_map/ppermute | solution.py:422
  44.4 18.1 %collective-permute-start.11 = (f32[8,2,64,128]{3,2,1,0:T(8,128)S(1)}, f32[8,2,64,128]{3,2,1,0:T(8,128)S(1)}, u32[]{:S(2)}, u32[]{:S(2)}) collective-permute-start(f32[8,2,64,128]{3,2,1,0:T(8,128)S(1)} %get-tuple-element.103), channel_id=1, source_target_pairs={{0,24},{8,16},{16,8},{24,0},{1,25},{9,17},{17,9},{25,1},{2,26},{10... | collective-permute-start | bytes 1572872 | tf_op jit(solution)/shard_map/ppermute | solution.py:422
  46.6 28.2 %collective-permute-start.12 = (f32[8,2,64,128]{3,2,1,0:T(8,128)S(1)}, f32[8,2,64,128]{3,2,1,0:T(8,128)S(1)}, u32[]{:S(2)}, u32[]{:S(2)}) collective-permute-start(f32[8,2,64,128]{3,2,1,0:T(8,128)S(1)} %get-tuple-element.104), channel_id=1, source_target_pairs={{0,16},{8,24},{16,0},{24,8},{1,17},{9,25},{17,1},{25,9},{2,18},{10... | collective-permute-start | bytes 1572872 | tf_op jit(solution)/shard_map/ppermute | solution.py:422
  46.8 28.0 %collective-permute-start.13 = (f32[8,2,64,128]{3,2,1,0:T(8,128)S(1)}, f32[8,2,64,128]{3,2,1,0:T(8,128)S(1)}, u32[]{:S(2)}, u32[]{:S(2)}) collective-permute-start(f32[8,2,64,128]{3,2,1,0:T(8,128)S(1)} %get-tuple-element.105), channel_id=1, source_target_pairs={{0,8},{8,0},{16,24},{24,16},{1,9},{9,1},{17,25},{25,17},{2,10},{10... | collective-permute-start | bytes 1572872 | tf_op jit(solution)/shard_map/ppermute | solution.py:422
  54.8 34.4 %collective-permute-start.5 = (f32[8,2,64,128]{3,2,1,0:T(8,128)S(1)}, f32[8,2,64,128]{3,2,1,0:T(8,128)S(1)}, u32[]{:S(2)}, u32[]{:S(2)}) collective-permute-start(f32[8,2,64,128]{3,2,1,0:T(8,128)S(1)} %get-tuple-element.91), channel_id=1, source_target_pairs={{0,24},{8,16},{16,8},{24,0},{1,25},{9,17},{17,9},{25,1},{2,26},{10... | collective-permute-start | bytes 1572872 | tf_op jit(solution)/shard_map/ppermute | solution.py:422
  62.5 33.7 %collective-permute-start.6 = (f32[8,2,64,128]{3,2,1,0:T(8,128)S(1)}, f32[8,2,64,128]{3,2,1,0:T(8,128)S(1)}, u32[]{:S(2)}, u32[]{:S(2)}) collective-permute-start(f32[8,2,64,128]{3,2,1,0:T(8,128)S(1)} %get-tuple-element.92), channel_id=1, source_target_pairs={{0,16},{8,24},{16,0},{24,8},{1,17},{9,25},{17,1},{25,9},{2,18},{10... | collective-permute-start | bytes 1572872 | tf_op jit(solution)/shard_map/ppermute | solution.py:422
  63.7 32.6 %collective-permute-start.7 = (f32[8,2,64,128]{3,2,1,0:T(8,128)S(1)}, f32[8,2,64,128]{3,2,1,0:T(8,128)S(1)}, u32[]{:S(2)}, u32[]{:S(2)}) collective-permute-start(f32[8,2,64,128]{3,2,1,0:T(8,128)S(1)} %get-tuple-element.93), channel_id=1, source_target_pairs={{0,8},{8,0},{16,24},{24,16},{1,9},{9,1},{17,25},{25,17},{2,10},{10... | collective-permute-start | bytes 1572872 | tf_op jit(solution)/shard_map/ppermute | solution.py:422
  80.4 8.6 %collective-permute-start.14 = (f32[8,64,128]{2,1,0:T(8,128)S(1)}, f32[8,64,128]{2,1,0:T(8,128)S(1)}, u32[]{:S(2)}, u32[]{:S(2)}) collective-permute-start(f32[8,64,128]{2,1,0:T(8,128)S(1)} %get-tuple-element.109), channel_id=1, source_target_pairs={{1,0},{2,1},{3,2},{4,3},{5,4},{6,5},{7,6},{9,8},{10,9},{11,10},{12... | collective-permute-start | bytes 786440 | tf_op jit(solution)/shard_map/ppermute | solution.py:435
  83.5 24.0 %collective-permute-start.21 = (f32[8,2,64,128]{3,2,1,0:T(8,128)S(1)}, f32[8,2,64,128]{3,2,1,0:T(8,128)S(1)}, u32[]{:S(2)}, u32[]{:S(2)}) collective-permute-start(f32[8,2,64,128]{3,2,1,0:T(8,128)S(1)} %get-tuple-element.128), channel_id=1, source_target_pairs={{0,24},{8,16},{16,8},{24,0},{1,25},{9,17},{17,9},{25,1},{2,26},{10... | collective-permute-start | bytes 1572872 | tf_op jit(solution)/shard_map/ppermute | solution.py:422
  89.0 29.7 %collective-permute-start.22 = (f32[8,2,64,128]{3,2,1,0:T(8,128)S(1)}, f32[8,2,64,128]{3,2,1,0:T(8,128)S(1)}, u32[]{:S(2)}, u32[]{:S(2)}) collective-permute-start(f32[8,2,64,128]{3,2,1,0:T(8,128)S(1)} %get-tuple-element.129), channel_id=1, source_target_pairs={{0,16},{8,24},{16,0},{24,8},{1,17},{9,25},{17,1},{25,9},{2,18},{10... | collective-permute-start | bytes 1572872 | tf_op jit(solution)/shard_map/ppermute | solution.py:422
  89.2 30.7 %collective-permute-start.23 = (f32[8,2,64,128]{3,2,1,0:T(8,128)S(1)}, f32[8,2,64,128]{3,2,1,0:T(8,128)S(1)}, u32[]{:S(2)}, u32[]{:S(2)}) collective-permute-start(f32[8,2,64,128]{3,2,1,0:T(8,128)S(1)} %get-tuple-element.130), channel_id=1, source_target_pairs={{0,8},{8,0},{16,24},{24,16},{1,9},{9,1},{17,25},{25,17},{2,10},{10... | collective-permute-start | bytes 1572872 | tf_op jit(solution)/shard_map/ppermute | solution.py:422
  101.7 18.1 %collective-permute-start.18 = (f32[8,64,128]{2,1,0:T(8,128)S(1)}, f32[8,64,128]{2,1,0:T(8,128)S(1)}, u32[]{:S(2)}, u32[]{:S(2)}) collective-permute-start(f32[8,64,128]{2,1,0:T(8,128)S(1)} %get-tuple-element.122), channel_id=1, source_target_pairs={{0,1},{1,2},{2,3},{3,4},{4,5},{5,6},{6,7},{8,9},{9,10},{10,11},{11... | collective-permute-start | bytes 786440 | tf_op jit(solution)/shard_map/ppermute | solution.py:431
  105.5 24.6 %collective-permute-start.15 = (f32[8,2,64,128]{3,2,1,0:T(8,128)S(1)}, f32[8,2,64,128]{3,2,1,0:T(8,128)S(1)}, u32[]{:S(2)}, u32[]{:S(2)}) collective-permute-start(f32[8,2,64,128]{3,2,1,0:T(8,128)S(1)} %get-tuple-element.118), channel_id=1, source_target_pairs={{0,24},{8,16},{16,8},{24,0},{1,25},{9,17},{17,9},{25,1},{2,26},{10... | collective-permute-start | bytes 1572872 | tf_op jit(solution)/shard_map/ppermute | solution.py:422
  107.5 33.6 %collective-permute-start.16 = (f32[8,2,64,128]{3,2,1,0:T(8,128)S(1)}, f32[8,2,64,128]{3,2,1,0:T(8,128)S(1)}, u32[]{:S(2)}, u32[]{:S(2)}) collective-permute-start(f32[8,2,64,128]{3,2,1,0:T(8,128)S(1)} %get-tuple-element.119), channel_id=1, source_target_pairs={{0,16},{8,24},{16,0},{24,8},{1,17},{9,25},{17,1},{25,9},{2,18},{10... | collective-permute-start | bytes 1572872 | tf_op jit(solution)/shard_map/ppermute | solution.py:422
  118.7 22.7 %collective-permute-start.17 = (f32[8,2,64,128]{3,2,1,0:T(8,128)S(1)}, f32[8,2,64,128]{3,2,1,0:T(8,128)S(1)}, u32[]{:S(2)}, u32[]{:S(2)}) collective-permute-start(f32[8,2,64,128]{3,2,1,0:T(8,128)S(1)} %get-tuple-element.120), channel_id=1, source_target_pairs={{0,8},{8,0},{16,24},{24,16},{1,9},{9,1},{17,25},{25,17},{2,10},{10... | collective-permute-start | bytes 1572872 | tf_op jit(solution)/shard_map/ppermute | solution.py:422
  123.1 29.5 %collective-permute-start.24 = (f32[8,2,64,128]{3,2,1,0:T(8,128)S(1)}, f32[8,2,64,128]{3,2,1,0:T(8,128)S(1)}, u32[]{:S(2)}, u32[]{:S(2)}) collective-permute-start(f32[8,2,64,128]{3,2,1,0:T(8,128)S(1)} %get-tuple-element.134), channel_id=1, source_target_pairs={{0,24},{8,16},{16,8},{24,0},{1,25},{9,17},{17,9},{25,1},{2,26},{10... | collective-permute-start | bytes 1572872 | tf_op jit(solution)/shard_map/ppermute | solution.py:422
  124.4 41.5 %collective-permute-start.25 = (f32[8,2,64,128]{3,2,1,0:T(8,128)S(1)}, f32[8,2,64,128]{3,2,1,0:T(8,128)S(1)}, u32[]{:S(2)}, u32[]{:S(2)}) collective-permute-start(f32[8,2,64,128]{3,2,1,0:T(8,128)S(1)} %get-tuple-element.144), channel_id=1, source_target_pairs={{0,16},{8,24},{16,0},{24,8},{1,17},{9,25},{17,1},{25,9},{2,18},{10... | collective-permute-start | bytes 1572872 | tf_op jit(solution)/shard_map/ppermute | solution.py:422
  130.0 35.9 %collective-permute-start.26 = (f32[8,2,64,128]{3,2,1,0:T(8,128)S(1)}, f32[8,2,64,128]{3,2,1,0:T(8,128)S(1)}, u32[]{:S(2)}, u32[]{:S(2)}) collective-permute-start(f32[8,2,64,128]{3,2,1,0:T(8,128)S(1)} %get-tuple-element.145), channel_id=1, source_target_pairs={{0,8},{8,0},{16,24},{24,16},{1,9},{9,1},{17,25},{25,17},{2,10},{10... | collective-permute-start | bytes 1572872 | tf_op jit(solution)/shard_map/ppermute | solution.py:422
  144.5 30.5 %collective-permute-start.27 = (f32[8,2,64,128]{3,2,1,0:T(8,128)S(1)}, f32[8,2,64,128]{3,2,1,0:T(8,128)S(1)}, u32[]{:S(2)}, u32[]{:S(2)}) collective-permute-start(f32[8,2,64,128]{3,2,1,0:T(8,128)S(1)} %get-tuple-element.150), channel_id=1, source_target_pairs={{0,24},{8,16},{16,8},{24,0},{1,25},{9,17},{17,9},{25,1},{2,26},{10... | collective-permute-start | bytes 1572872 | tf_op jit(solution)/shard_map/ppermute | solution.py:422
  146.6 39.5 %collective-permute-start.19 = (f32[8,2,64,128]{3,2,1,0:T(8,128)S(1)}, f32[8,2,64,128]{3,2,1,0:T(8,128)S(1)}, u32[]{:S(2)}, u32[]{:S(2)}) collective-permute-start(f32[8,2,64,128]{3,2,1,0:T(8,128)S(1)} %get-tuple-element.126), channel_id=1, source_target_pairs={{0,16},{8,24},{16,0},{24,8},{1,17},{9,25},{17,1},{25,9},{2,18},{10... | collective-permute-start | bytes 1572872 | tf_op jit(solution)/shard_map/ppermute | solution.py:422
  152.5 33.8 %collective-permute-start.20 = (f32[8,2,64,128]{3,2,1,0:T(8,128)S(1)}, f32[8,2,64,128]{3,2,1,0:T(8,128)S(1)}, u32[]{:S(2)}, u32[]{:S(2)}) collective-permute-start(f32[8,2,64,128]{3,2,1,0:T(8,128)S(1)} %get-tuple-element.127), channel_id=1, source_target_pairs={{0,8},{8,0},{16,24},{24,16},{1,9},{9,1},{17,25},{25,17},{2,10},{10... | collective-permute-start | bytes 1572872 | tf_op jit(solution)/shard_map/ppermute | solution.py:422

commit v5 on v4

--- a/solution.py
+++ b/solution.py
@@ -454,7 +454,7 @@
     mat = spectral_blocks(me, n, count)
     kappa, speed, up, down = prep(disp_table, perm_table, tide, material, flags, start)
     below, high = upward(up), downward(down)
-    start = after(start, below, high)
+    start = after(start, up, down)
     for chunk in range(1, chunks):
         going = cut(me_array, start, n, chunk, part)
         there.append(exchange(going))

time: 188 us -> 189 us (level); the launches traced: 187 us -> 186 us
  waiting for transfers between devices: 60.9 us -> 44.2 us
  starting transfers between devices: 38.1 us -> 51.9 us
  local copies, waits for them, and re-layouts: 4.14 us -> 6.55 us
    ppermute x2, starting transfers between devices: 5.01 us -> 14.9 us  [downward(): lax.ppermute(plane, 'space', [(i + 1, i) for i in range(lax.axis_size('sp...]
    ppermute x2, waiting for transfers between devices: 9.6 us -> 0.01 us  [downward(): lax.ppermute(plane, 'space', [(i + 1, i) for i in range(lax.axis_size('sp...]
    ppermute x24, waiting for transfers between devices: 51.2 us -> 44.2 us  [exchange(): lax.ppermute(piece, 'inst', [(i, i ^ code(m, n)) for i in range(n)])]
    ppermute x24, starting transfers between devices: 24.8 us -> 27.9 us  [exchange(): lax.ppermute(piece, 'inst', [(i, i ^ code(m, n)) for i in range(n)])]
    unnamed x4 -> x10, local copies, waits for them, and re-layouts: 0.01 us -> 2.39 us
  transfers between devices with their start and end apart: 28 -> 28, of which waited for: 15 -> 11; matrix products, arithmetic and copies ran while one was open for 3% -> 3% of each run, Pallas kernels for 43% -> 43%
where the time goes in v5:
time: 189 us; the launch traced here: 186 us
  Pallas kernels  81.2 us (43%)
  starting transfers between devices  51.9 us (27%)
  waiting for transfers between devices  44.2 us (23%)
  local copies, waits for them, and re-layouts  6.55 us (3%)
    ppermute x24, waiting for transfers between devices, exchange(): lax.ppermute(piece, 'inst', [(i, i ^ code(m, n)) for i in range(n)])  44.2 us
    pallas_call x4, Pallas kernels, stencil(): pl.pallas_call(functools.partial(stencil_kernel, second, first, len(befor...  38 us
    ppermute x24, starting transfers between devices, exchange(): lax.ppermute(piece, 'inst', [(i, i ^ code(m, n)) for i in range(n)])  27.9 us
    ppermute x2, starting transfers between devices, downward(): lax.ppermute(plane, 'space', [(i + 1, i) for i in range(lax.axis_size('sp...  14.9 us
    pallas_call x4, Pallas kernels, apply_time(): pl.pallas_call(functools.partial(apply_kernel, n), grid_spec=pltpu.Prefet...  13.2 us
    pallas_call x2, Pallas kernels, first_update(): pl.pallas_call(functools.partial(first_kernel, n, aliased), grid_spec=plt...  11 us
    ppermute x2, starting transfers between devices, upward(): lax.ppermute(plane, 'space', [(i, i + 1) for i in range(lax.axis_size('sp...  9.1 us
    pallas_call x5, Pallas kernels, cut(): pl.pallas_call(cut_kernel, grid_spec=pltpu.PrefetchScalarGridSpec(num_sca...  7.66 us
  transfers between devices with their start and end apart: 28, of which 11 were waited for; matrix products, arithmetic and copies ran while one was open for 3% of the time, Pallas kernels for 43%

profile of v5, /device:TPU:9, one launch (start us, length us, event | category | flops | bytes accessed | tf_op | source)
XLA Modules:
  0.0 186.0 jit_solution(11758507549226021846)
XLA Ops:
  0.6 1.1 cut.5
  1.7 2.2 %collective-permute-start.6 = (f32[8,2,64,128]{3,2,1,0:T(8,128)S(1)}, f32[8,2,64,128]{3,2,1,0:T(8,128)S(1)}, u32[]{:S(2)}, u32[]{:S(2)}) collective-permute-start(f32[8,2,64,128]{3,2,1,0:T(8,128)S(1)} %cut.5), channel_id=1, source_target_pairs={{0,24},{8,16},{16,8},{24,0},{1,25},{9,17},{17,9},{25,1},{2,26},{10... | collective-permute-start | bytes 1572872 | tf_op jit(solution)/shard_map/ppermute | solution.py:422
  4.0 2.2 %cut.6 = (f32[8,2,64,128]{3,2,1,0:T(8,128)}, f32[8,2,64,128]{3,2,1,0:T(8,128)}) custom-call(s32[1]{0:T(128)} %bitcast.me_ref, f32[8,16,64,128]{3,2,1,0:T(8,128)} %refs_6_.3, f32[8,16,64,128]{3,2,1,0:T(8,128)} %refs_6_.3), custom_call_target="tpu_custom_call" | custom-call | flops 1024 | bytes 1024 | tf_op jit(solution)/shard_map/cut/pallas_call | solution.py:61
  6.2 0.2 collective-permute-start.7
  6.4 0.3 collective-permute-start.8
  6.7 2.8 %prep.1 = (f32[16,64,128]{2,1,0:T(8,128)S(1)}, f32[16,64,128]{2,1,0:T(8,128)S(1)}, f32[17,64,128]{2,1,0:T(8,128)}, f32[8,64,128]{2,1,0:T(8,128)}) custom-call(f32[8]{0:T(128)S(1)} %copy-done, f32[8]{0:T(128)S(1)} %copy-done.1, f32[8]{0:T(128)S(1)} %multiply_add_fusion.tide_ref, s32[16,64,128]{2,1,0:T(8,128)} %material_ref, s32[8,3,16,64,128]{4,3,2,1,0:T(8,128)} %flags_ref.6, ...), custom_call_target="tpu_custom_call" | custom-call | flops 1024 | bytes 1024 | tf_op jit(solution)/shard_map/prep/pallas_call | solution.py:109
  9.5 4.6 %collective-permute-start.9 = (f32[17,64,128]{2,1,0:T(8,128)}, f32[17,64,128]{2,1,0:T(8,128)S(1)}, u32[]{:S(2)}, u32[]{:S(2)}) collective-permute-start(f32[17,64,128]{2,1,0:T(8,128)} %get-tuple-element.84), channel_id=1, source_target_pairs={{0,1},{1,2},{2,3},{3,4},{4,5},{5,6},{6,7},{8,9},{9,10},{10,11},{11... | collective-permute-start | bytes 1671176 | tf_op jit(solution)/shard_map/ppermute | solution.py:431
  14.1 1.9 %collective-permute-start.10 = (f32[8,64,128]{2,1,0:T(8,128)}, f32[8,64,128]{2,1,0:T(8,128)S(1)}, u32[]{:S(2)}, u32[]{:S(2)}) collective-permute-start(f32[8,64,128]{2,1,0:T(8,128)} %get-tuple-element.85), channel_id=1, source_target_pairs={{1,0},{2,1},{3,2},{4,3},{5,4},{6,5},{7,6},{9,8},{10,9},{11,10},{12... | collective-permute-start | bytes 786440 | tf_op jit(solution)/shard_map/ppermute | solution.py:435
  16.2 0.7 broadcast_bitcast_fusion.1
  16.9 1.5 cut.7
  18.4 0.8 copy-done.2
  19.2 0.8 copy-done.3
  20.0 0.8 copy-done.4
  20.8 1.0 copy.17
  21.7 0.7 broadcast_bitcast_fusion
  22.5 2.2 %collective-permute-start = (f32[8,2,64,128]{3,2,1,0:T(8,128)}, f32[8,2,64,128]{3,2,1,0:T(8,128)}, u32[]{:S(2)}, u32[]{:S(2)}) collective-permute-start(f32[8,2,64,128]{3,2,1,0:T(8,128)} %copy-done.4), channel_id=1, source_target_pairs={{0,24},{8,16},{16,8},{24,0},{1,25},{9,17},{17,9},{25,1},{2,26},{10... | collective-permute-start | bytes 1572872 | tf_op jit(solution)/shard_map/ppermute | solution.py:422
  24.6 4.3 %collective-permute-done.7.refs_1_ = f32[8,2,64,128]{3,2,1,0:T(8,128)S(1)} collective-permute-done((f32[8,2,64,128]{3,2,1,0:T(8,128)}, f32[8,2,64,128]{3,2,1,0:T(8,128)S(1)}, u32[]{:S(2)}, u32[]{:S(2)}) %collective-permute-start.7) | collective-permute-done | bytes 524320 | tf_op jit(solution)/shard_map/ppermute | solution.py:422
  28.9 1.1 collective-permute-start.1
  30.0 1.2 collective-permute-start.2
  31.3 1.8 copy.18
  33.0 1.0 compare_select_fusion.refs_3_
  34.1 9.8 %stencil_one.2 = (f32[8,16,64,128]{3,2,1,0:T(8,128)}, f32[8,16,64,128]{3,2,1,0:T(8,128)}) custom-call(f32[8]{0:T(128)S(1)} %multiply_add_fusion.tide_ref, f32[8,16,64,128]{3,2,1,0:T(8,128)} %refs_6_.3, f32[17,64,128]{2,1,0:T(8,128)S(1)} %collective-permute-done.9.low_ref.below_k_ref.below_f_ref, f32[8,64,128]{2,1,0:T(8,128)S(1)} %collective-permute-done.10.high_ref, ...), custom_call_target="tpu_custom_call" | custom-call | flops 1024 | bytes 1024 | tf_op jit(solution)/shard_map/stencil_one/pallas_call | solution.py:216
  43.9 3.3 %apply_time.5 = (f32[8,2,64,128]{3,2,1,0:T(8,128)S(1)}, f32[8,2,64,128]{3,2,1,0:T(8,128)S(1)}, f32[8,2,64,128]{3,2,1,0:T(8,128)S(1)}, f32[8,2,64,128]{3,2,1,0:T(8,128)S(1)}) custom-call(s32[1]{0:T(128)} %bitcast.me_ref, f32[8,16,64,128]{3,2,1,0:T(8,128)} %refs_6_.3, f32[8,2,64,128]{3,2,1,0:T(8,128)S(1)} %collective-permute-done.6.refs_0_, ...), custom_call_target="tpu_custom_call" | custom-call | flops 1024 | bytes 1024 | tf_op jit(solution)/shard_map/apply_time/pallas_call | solution.py:258
  47.3 0.4 collective-permute-start.11
  47.6 1.1 collective-permute-start.12
  48.8 1.2 collective-permute-start.13
  50.0 0.4 collective-permute-done.1.refs_1_
  50.4 3.4 %apply_time.4 = (f32[8,2,64,128]{3,2,1,0:T(8,128)S(1)}, f32[8,2,64,128]{3,2,1,0:T(8,128)S(1)}, f32[8,2,64,128]{3,2,1,0:T(8,128)S(1)}, f32[8,2,64,128]{3,2,1,0:T(8,128)S(1)}) custom-call(s32[1]{0:T(128)} %bitcast.me_ref, f32[8,16,64,128]{3,2,1,0:T(8,128)} %refs_6_.3, f32[8,2,64,128]{3,2,1,0:T(8,128)} %collective-permute-done.refs_0_, ...), custom_call_target="tpu_custom_call" | custom-call | flops 1024 | bytes 1024 | tf_op jit(solution)/shard_map/apply_time/pallas_call | solution.py:258
  53.9 3.2 %collective-permute-start.3 = (f32[8,2,64,128]{3,2,1,0:T(8,128)S(1)}, f32[8,2,64,128]{3,2,1,0:T(8,128)S(1)}, u32[]{:S(2)}, u32[]{:S(2)}) collective-permute-start(f32[8,2,64,128]{3,2,1,0:T(8,128)S(1)} %get-tuple-element.91), channel_id=1, source_target_pairs={{0,24},{8,16},{16,8},{24,0},{1,25},{9,17},{17,9},{25,1},{2,26},{10... | collective-permute-start | bytes 1572872 | tf_op jit(solution)/shard_map/ppermute | solution.py:422
  57.1 3.5 %collective-permute-done.11.refs_1_ = f32[8,2,64,128]{3,2,1,0:T(8,128)S(1)} collective-permute-done((f32[8,2,64,128]{3,2,1,0:T(8,128)S(1)}, f32[8,2,64,128]{3,2,1,0:T(8,128)S(1)}, u32[]{:S(2)}, u32[]{:S(2)}) %collective-permute-start.11) | collective-permute-done | bytes 524320 | tf_op jit(solution)/shard_map/ppermute | solution.py:422
  60.6 1.2 collective-permute-start.5
  61.7 9.8 %stencil_one.3 = (f32[8,16,64,128]{3,2,1,0:T(8,128)}, f32[8,16,64,128]{3,2,1,0:T(8,128)}) custom-call(f32[8]{0:T(128)S(1)} %multiply_add_fusion.tide_ref, f32[8,16,64,128]{3,2,1,0:T(8,128)} %refs_6_.3, f32[17,64,128]{2,1,0:T(8,128)S(1)} %collective-permute-done.9.low_ref.below_k_ref.below_f_ref, ...), custom_call_target="tpu_custom_call", output_to_operand_aliasing={{0}: (10, {}), {1}: (11, {})} | custom-call | flops 1024 | bytes 1024 | tf_op jit(solution)/shard_map/stencil_one/pallas_call | solution.py:216
  71.6 1.0 collective-permute-done.12.refs_2_
  72.6 5.5 %first_update.2 = (f32[8,16,64,128]{3,2,1,0:T(8,128)}, f32[8,16,64,128]{3,2,1,0:T(8,128)}, f32[8,64,128]{2,1,0:T(8,128)S(1)}, f32[8,64,128]{2,1,0:T(8,128)}, f32...) custom-call(s32[1]{0:T(128)} %bitcast.me_ref, ...), custom_call_target="tpu_custom_call" | custom-call | flops 1024 | bytes 1024 | tf_op jit(solution)/shard_map/first_update/pallas_call | solution.py:306
  78.1 13.0 %collective-permute-start.14 = (f32[8,64,128]{2,1,0:T(8,128)S(1)}, f32[8,64,128]{2,1,0:T(8,128)S(1)}, u32[]{:S(2)}, u32[]{:S(2)}) collective-permute-start(f32[8,64,128]{2,1,0:T(8,128)S(1)} %get-tuple-element.109), channel_id=1, source_target_pairs={{1,0},{2,1},{3,2},{4,3},{5,4},{6,5},{7,6},{9,8},{10,9},{11,10},{12... | collective-permute-start | bytes 786440 | tf_op jit(solution)/shard_map/ppermute | solution.py:435
  91.0 2.2 %collective-permute-start.21 = (f32[8,2,64,128]{3,2,1,0:T(8,128)S(1)}, f32[8,2,64,128]{3,2,1,0:T(8,128)S(1)}, u32[]{:S(2)}, u32[]{:S(2)}) collective-permute-start(f32[8,2,64,128]{3,2,1,0:T(8,128)S(1)} %get-tuple-element.128), channel_id=1, source_target_pairs={{0,24},{8,16},{16,8},{24,0},{1,25},{9,17},{17,9},{25,1},{2,26},{10... | collective-permute-start | bytes 1572872 | tf_op jit(solution)/shard_map/ppermute | solution.py:422
  93.3 0.2 collective-permute-start.22
  93.5 1.2 collective-permute-done.4.refs_2_
  94.7 2.1 %collective-permute-start.23 = (f32[8,2,64,128]{3,2,1,0:T(8,128)S(1)}, f32[8,2,64,128]{3,2,1,0:T(8,128)S(1)}, u32[]{:S(2)}, u32[]{:S(2)}) collective-permute-start(f32[8,2,64,128]{3,2,1,0:T(8,128)S(1)} %get-tuple-element.130), channel_id=1, source_target_pairs={{0,8},{8,0},{16,24},{24,16},{1,9},{9,1},{17,25},{25,17},{2,10},{10... | collective-permute-start | bytes 1572872 | tf_op jit(solution)/shard_map/ppermute | solution.py:422
  96.8 5.5 %first_update.3 = (f32[8,16,64,128]{3,2,1,0:T(8,128)}, f32[8,16,64,128]{3,2,1,0:T(8,128)}, f32[8,64,128]{2,1,0:T(8,128)}, f32[8,64,128]{2,1,0:T(8,128)S(1)}, f32...) custom-call(s32[1]{0:T(128)} %bitcast.me_ref, ...), custom_call_target="tpu_custom_call", output_to_operand_aliasing={{0}: (8, {}), {1}: (9, {})} | custom-call | flops 1024 | bytes 1024 | tf_op jit(solution)/shard_map/first_update/pallas_call | solution.py:306
  102.3 4.5 %collective-permute-start.18 = (f32[8,64,128]{2,1,0:T(8,128)S(1)}, f32[8,64,128]{2,1,0:T(8,128)S(1)}, u32[]{:S(2)}, u32[]{:S(2)}) collective-permute-start(f32[8,64,128]{2,1,0:T(8,128)S(1)} %get-tuple-element.122), channel_id=1, source_target_pairs={{0,1},{1,2},{2,3},{3,4},{4,5},{5,6},{6,7},{8,9},{9,10},{10,11},{11... | collective-permute-start | bytes 786440 | tf_op jit(solution)/shard_map/ppermute | solution.py:431
  106.8 1.2 collective-permute-start.15
  108.1 9.6 %collective-permute-done.22.refs_1_ = f32[8,2,64,128]{3,2,1,0:T(8,128)S(1)} collective-permute-done((f32[8,2,64,128]{3,2,1,0:T(8,128)S(1)}, f32[8,2,64,128]{3,2,1,0:T(8,128)S(1)}, u32[]{:S(2)}, u32[]{:S(2)}) %collective-permute-start.22) | collective-permute-done | bytes 524320 | tf_op jit(solution)/shard_map/ppermute | solution.py:422
  117.7 1.4 collective-permute-start.17
  119.2 3.2 %apply_time.7 = (f32[8,2,64,128]{3,2,1,0:T(8,128)S(1)}, f32[8,2,64,128]{3,2,1,0:T(8,128)S(1)}, f32[8,2,64,128]{3,2,1,0:T(8,128)S(1)}, f32[8,2,64,128]{3,2,1,0:T(8,128)S(1)}) custom-call(s32[1]{0:T(128)} %bitcast.me_ref, f32[8,16,64,128]{3,2,1,0:T(8,128)} %get-tuple-element.135.u_ref.own_ref, f32[8,2,64,128]{3,2,1,0:T(8,128)S(1)} %collective-permute-done.21.refs_0_, ...), custom_call_target="tpu_custom_call" | custom-call | flops 1024 | bytes 1024 | tf_op jit(solution)/shard_map/apply_time/pallas_call | solution.py:258
  122.4 1.2 collective-permute-start.24
  123.7 4.9 %collective-permute-done.15.refs_0_ = f32[8,2,64,128]{3,2,1,0:T(8,128)S(1)} collective-permute-done((f32[8,2,64,128]{3,2,1,0:T(8,128)S(1)}, f32[8,2,64,128]{3,2,1,0:T(8,128)S(1)}, u32[]{:S(2)}, u32[]{:S(2)}) %collective-permute-start.15) | collective-permute-done | bytes 524320 | tf_op jit(solution)/shard_map/ppermute | solution.py:422
  128.6 1.2 collective-permute-start.26
  129.7 9.2 %stencil_two.2.rest_1_ = f32[8,16,64,128]{3,2,1,0:T(8,128)} custom-call(f32[8]{0:T(128)S(1)} %multiply_add_fusion.tide_ref, f32[8,16,64,128]{3,2,1,0:T(8,128)} %get-tuple-element.135.u_ref.own_ref, f32[8,64,128]{2,1,0:T(8,128)S(1)} %collective-permute-done.18.low_ref, f32[8,64,128]{2,1,0:T(8,128)S(1)} %collective-permute-done.14.high_ref, ...), custom_call_target="tpu_custom_call" | custom-call | flops 1024 | bytes 1024 | tf_op jit(solution)/shard_map/stencil_two/pallas_call | solution.py:216
  138.9 1.3 collective-permute-done.16.refs_1_
  140.2 3.2 %apply_time.6 = (f32[8,2,64,128]{3,2,1,0:T(8,128)S(1)}, f32[8,2,64,128]{3,2,1,0:T(8,128)S(1)}, f32[8,2,64,128]{3,2,1,0:T(8,128)S(1)}, f32[8,2,64,128]{3,2,1,0:T(8,128)S(1)}) custom-call(s32[1]{0:T(128)} %bitcast.me_ref, f32[8,16,64,128]{3,2,1,0:T(8,128)} %get-tuple-element.135.u_ref.own_ref, f32[8,2,64,128]{3,2,1,0:T(8,128)S(1)} %collective-permute-done.15.refs_0_, ...), custom_call_target="tpu_custom_call" | custom-call | flops 1024 | bytes 1024 | tf_op jit(solution)/shard_map/apply_time/pallas_call | solution.py:258
  143.4 2.4 %collective-permute-start.27 = (f32[8,2,64,128]{3,2,1,0:T(8,128)S(1)}, f32[8,2,64,128]{3,2,1,0:T(8,128)S(1)}, u32[]{:S(2)}, u32[]{:S(2)}) collective-permute-start(f32[8,2,64,128]{3,2,1,0:T(8,128)S(1)} %get-tuple-element.150), channel_id=1, source_target_pairs={{0,24},{8,16},{16,8},{24,0},{1,25},{9,17},{17,9},{25,1},{2,26},{10... | collective-permute-start | bytes 1572872 | tf_op jit(solution)/shard_map/ppermute | solution.py:422
  145.8 0.3 collective-permute-start.19
  146.1 5.0 %collective-permute-done.24.refs_1_ = f32[8,2,64,128]{3,2,1,0:T(8,128)S(1)} collective-permute-done((f32[8,2,64,128]{3,2,1,0:T(8,128)S(1)}, f32[8,2,64,128]{3,2,1,0:T(8,128)S(1)}, u32[]{:S(2)}, u32[]{:S(2)}) %collective-permute-start.24) | collective-permute-done | bytes 524320 | tf_op jit(solution)/shard_map/ppermute | solution.py:422
  151.1 1.2 collective-permute-start.20
  152.2 9.2 %stencil_two.3.refs_0_.refs_1_.refs_2_.refs_4_ = f32[8,16,64,128]{3,2,1,0:T(8,128)} custom-call(f32[8]{0:T(128)S(1)} %multiply_add_fusion.tide_ref, f32[8,16,64,128]{3,2,1,0:T(8,128)} %get-tuple-element.135.u_ref.own_ref, f32[8,64,128]{2,1,0:T(8,128)S(1)} %collective-permute-done.18.low_ref, ...), custom_call_target="tpu_custom_call", output_to_operand_aliasing={{}: (11, {})} | custom-call | flops 1024 | bytes 1024 | tf_op jit(solution)/shard_map/stencil_two/pallas_call | solution.py:216
  161.4 1.5 cut.9
  162.9 1.5 cut.8
  164.4 4.5 %chunk_update.1.refs_3_ = f32[8,16,64,128]{3,2,1,0:T(8,128)} custom-call(s32[1]{0:T(128)} %bitcast.me_ref, f32[8,2,64,128]{3,2,1,0:T(8,128)S(1)} %get-tuple-element.143.refs_0_, f32[8,2,64,128]{3,2,1,0:T(8,128)S(1)} %collective-permute-done.24.refs_1_, f32[8,2,64,128]{3,2,1,0:T(8,128)S(1)} %collective-permute-done.25.refs_2_, ...), custom_call_target="tpu_custom_call" | custom-call | flops 1024 | bytes 1024 | tf_op jit(solution)/shard_map/chunk_update/pallas_call | solution.py:403
  168.9 2.1 %last_update.2.refs_3_ = f32[8,16,64,128]{3,2,1,0:T(8,128)} custom-call(s32[1]{0:T(128)} %bitcast.me_ref, f32[8,2,64,128]{3,2,1,0:T(8,128)S(1)} %get-tuple-element.142.refs_0_, f32[8,16,64,128]{3,2,1,0:T(8,128)} %stencil_two.3.refs_0_.refs_1_.refs_2_.refs_4_, ...), custom_call_target="tpu_custom_call", output_to_operand_aliasing={{}: (4, {})} | custom-call | flops 1024 | bytes 1024 | tf_op jit(solution)/shard_map/last_update/pallas_call | solution.py:332
  170.9 2.7 %collective-permute-done.27.refs_0_ = f32[8,2,64,128]{3,2,1,0:T(8,128)S(1)} collective-permute-done((f32[8,2,64,128]{3,2,1,0:T(8,128)S(1)}, f32[8,2,64,128]{3,2,1,0:T(8,128)S(1)}, u32[]{:S(2)}, u32[]{:S(2)}) %collective-permute-start.27) | collective-permute-done | bytes 524320 | tf_op jit(solution)/shard_map/ppermute | solution.py:422
  173.6 0.9 last_update.3.refs_6_
  174.5 10.5 %collective-permute-done.19.refs_0_ = f32[8,2,64,128]{3,2,1,0:T(8,128)S(1)} collective-permute-done((f32[8,2,64,128]{3,2,1,0:T(8,128)S(1)}, f32[8,2,64,128]{3,2,1,0:T(8,128)S(1)}, u32[]{:S(2)}, u32[]{:S(2)}) %collective-permute-start.19) | collective-permute-done | bytes 524320 | tf_op jit(solution)/shard_map/ppermute | solution.py:422
  184.9 1.0 final_update.1
  (31 shorter events, 0.5 us)
Async XLA Ops:
  1.7 5.0 %copy-start = (f32[8]{0:T(128)S(1)}, f32[8]{0:T(128)}, u32[]{:S(2)}) copy-start(f32[8]{0:T(128)} %disp_ref.1) | copy-start | bytes 100
  1.7 5.0 %copy-start.1 = (f32[8]{0:T(128)S(1)}, f32[8]{0:T(128)}, u32[]{:S(2)}) copy-start(f32[8]{0:T(128)} %perm_ref.1) | copy-start | bytes 100
  1.7 42.2 %collective-permute-start.6 = (f32[8,2,64,128]{3,2,1,0:T(8,128)S(1)}, f32[8,2,64,128]{3,2,1,0:T(8,128)S(1)}, u32[]{:S(2)}, u32[]{:S(2)}) collective-permute-start(f32[8,2,64,128]{3,2,1,0:T(8,128)S(1)} %cut.5), channel_id=1, source_target_pairs={{0,24},{8,16},{16,8},{24,0},{1,25},{9,17},{17,9},{25,1},{2,26},{10... | collective-permute-start | bytes 1572872 | tf_op jit(solution)/shard_map/ppermute | solution.py:422
  6.2 22.7 %collective-permute-start.7 = (f32[8,2,64,128]{3,2,1,0:T(8,128)}, f32[8,2,64,128]{3,2,1,0:T(8,128)S(1)}, u32[]{:S(2)}, u32[]{:S(2)}) collective-permute-start(f32[8,2,64,128]{3,2,1,0:T(8,128)} %get-tuple-element.79), channel_id=1, source_target_pairs={{0,16},{8,24},{16,0},{24,8},{1,17},{9,25},{17,1},{25,9},{2,18},{10... | collective-permute-start | bytes 1572872 | tf_op jit(solution)/shard_map/ppermute | solution.py:422
  6.4 37.5 %collective-permute-start.8 = (f32[8,2,64,128]{3,2,1,0:T(8,128)}, f32[8,2,64,128]{3,2,1,0:T(8,128)}, u32[]{:S(2)}, u32[]{:S(2)}) collective-permute-start(f32[8,2,64,128]{3,2,1,0:T(8,128)} %get-tuple-element.80), channel_id=1, source_target_pairs={{0,8},{8,0},{16,24},{24,16},{1,9},{9,1},{17,25},{25,17},{2,10},{10... | collective-permute-start | bytes 1572872 | tf_op jit(solution)/shard_map/ppermute | solution.py:422
  9.5 20.5 %collective-permute-start.9 = (f32[17,64,128]{2,1,0:T(8,128)}, f32[17,64,128]{2,1,0:T(8,128)S(1)}, u32[]{:S(2)}, u32[]{:S(2)}) collective-permute-start(f32[17,64,128]{2,1,0:T(8,128)} %get-tuple-element.84), channel_id=1, source_target_pairs={{0,1},{1,2},{2,3},{3,4},{4,5},{5,6},{6,7},{8,9},{9,10},{10,11},{11... | collective-permute-start | bytes 1671176 | tf_op jit(solution)/shard_map/ppermute | solution.py:431
  14.1 8.3 %collective-permute-start.10 = (f32[8,64,128]{2,1,0:T(8,128)}, f32[8,64,128]{2,1,0:T(8,128)S(1)}, u32[]{:S(2)}, u32[]{:S(2)}) collective-permute-start(f32[8,64,128]{2,1,0:T(8,128)} %get-tuple-element.85), channel_id=1, source_target_pairs={{1,0},{2,1},{3,2},{4,3},{5,4},{6,5},{7,6},{9,8},{10,9},{11,10},{12... | collective-permute-start | bytes 786440 | tf_op jit(solution)/shard_map/ppermute | solution.py:435
  18.4 0.8 copy-start.2
  19.2 0.8 copy-start.3
  20.0 0.8 copy-start.4
  22.5 26.3 %collective-permute-start = (f32[8,2,64,128]{3,2,1,0:T(8,128)}, f32[8,2,64,128]{3,2,1,0:T(8,128)}, u32[]{:S(2)}, u32[]{:S(2)}) collective-permute-start(f32[8,2,64,128]{3,2,1,0:T(8,128)} %copy-done.4), channel_id=1, source_target_pairs={{0,24},{8,16},{16,8},{24,0},{1,25},{9,17},{17,9},{25,1},{2,26},{10... | collective-permute-start | bytes 1572872 | tf_op jit(solution)/shard_map/ppermute | solution.py:422
  28.9 21.5 %collective-permute-start.1 = (f32[8,2,64,128]{3,2,1,0:T(8,128)}, f32[8,2,64,128]{3,2,1,0:T(8,128)}, u32[]{:S(2)}, u32[]{:S(2)}) collective-permute-start(f32[8,2,64,128]{3,2,1,0:T(8,128)} %copy-done.3), channel_id=1, source_target_pairs={{0,16},{8,24},{16,0},{24,8},{1,17},{9,25},{17,1},{25,9},{2,18},{10... | collective-permute-start | bytes 1572872 | tf_op jit(solution)/shard_map/ppermute | solution.py:422
  30.0 20.4 %collective-permute-start.2 = (f32[8,2,64,128]{3,2,1,0:T(8,128)}, f32[8,2,64,128]{3,2,1,0:T(8,128)}, u32[]{:S(2)}, u32[]{:S(2)}) collective-permute-start(f32[8,2,64,128]{3,2,1,0:T(8,128)} %copy-done.2), channel_id=1, source_target_pairs={{0,8},{8,0},{16,24},{24,16},{1,9},{9,1},{17,25},{25,17},{2,10},{10... | collective-permute-start | bytes 1572872 | tf_op jit(solution)/shard_map/ppermute | solution.py:422
  47.3 13.3 %collective-permute-start.11 = (f32[8,2,64,128]{3,2,1,0:T(8,128)S(1)}, f32[8,2,64,128]{3,2,1,0:T(8,128)S(1)}, u32[]{:S(2)}, u32[]{:S(2)}) collective-permute-start(f32[8,2,64,128]{3,2,1,0:T(8,128)S(1)} %get-tuple-element.103), channel_id=1, source_target_pairs={{0,24},{8,16},{16,8},{24,0},{1,25},{9,17},{17,9},{25,1},{2,26},{10... | collective-permute-start | bytes 1572872 | tf_op jit(solution)/shard_map/ppermute | solution.py:422
  47.6 24.9 %collective-permute-start.12 = (f32[8,2,64,128]{3,2,1,0:T(8,128)S(1)}, f32[8,2,64,128]{3,2,1,0:T(8,128)S(1)}, u32[]{:S(2)}, u32[]{:S(2)}) collective-permute-start(f32[8,2,64,128]{3,2,1,0:T(8,128)S(1)} %get-tuple-element.104), channel_id=1, source_target_pairs={{0,16},{8,24},{16,0},{24,8},{1,17},{9,25},{17,1},{25,9},{2,18},{10... | collective-permute-start | bytes 1572872 | tf_op jit(solution)/shard_map/ppermute | solution.py:422
  48.8 23.8 %collective-permute-start.13 = (f32[8,2,64,128]{3,2,1,0:T(8,128)S(1)}, f32[8,2,64,128]{3,2,1,0:T(8,128)S(1)}, u32[]{:S(2)}, u32[]{:S(2)}) collective-permute-start(f32[8,2,64,128]{3,2,1,0:T(8,128)S(1)} %get-tuple-element.105), channel_id=1, source_target_pairs={{0,8},{8,0},{16,24},{24,16},{1,9},{9,1},{17,25},{25,17},{2,10},{10... | collective-permute-start | bytes 1572872 | tf_op jit(solution)/shard_map/ppermute | solution.py:422
  53.9 39.4 %collective-permute-start.3 = (f32[8,2,64,128]{3,2,1,0:T(8,128)S(1)}, f32[8,2,64,128]{3,2,1,0:T(8,128)S(1)}, u32[]{:S(2)}, u32[]{:S(2)}) collective-permute-start(f32[8,2,64,128]{3,2,1,0:T(8,128)S(1)} %get-tuple-element.91), channel_id=1, source_target_pairs={{0,24},{8,16},{16,8},{24,0},{1,25},{9,17},{17,9},{25,1},{2,26},{10... | collective-permute-start | bytes 1572872 | tf_op jit(solution)/shard_map/ppermute | solution.py:422
  57.1 37.5 %collective-permute-start.4 = (f32[8,2,64,128]{3,2,1,0:T(8,128)S(1)}, f32[8,2,64,128]{3,2,1,0:T(8,128)S(1)}, u32[]{:S(2)}, u32[]{:S(2)}) collective-permute-start(f32[8,2,64,128]{3,2,1,0:T(8,128)S(1)} %get-tuple-element.92), channel_id=1, source_target_pairs={{0,16},{8,24},{16,0},{24,8},{1,17},{9,25},{17,1},{25,9},{2,18},{10... | collective-permute-start | bytes 1572872 | tf_op jit(solution)/shard_map/ppermute | solution.py:422
  60.6 36.2 %collective-permute-start.5 = (f32[8,2,64,128]{3,2,1,0:T(8,128)S(1)}, f32[8,2,64,128]{3,2,1,0:T(8,128)S(1)}, u32[]{:S(2)}, u32[]{:S(2)}) collective-permute-start(f32[8,2,64,128]{3,2,1,0:T(8,128)S(1)} %get-tuple-element.93), channel_id=1, source_target_pairs={{0,8},{8,0},{16,24},{24,16},{1,9},{9,1},{17,25},{25,17},{2,10},{10... | collective-permute-start | bytes 1572872 | tf_op jit(solution)/shard_map/ppermute | solution.py:422
  78.1 18.7 %collective-permute-start.14 = (f32[8,64,128]{2,1,0:T(8,128)S(1)}, f32[8,64,128]{2,1,0:T(8,128)S(1)}, u32[]{:S(2)}, u32[]{:S(2)}) collective-permute-start(f32[8,64,128]{2,1,0:T(8,128)S(1)} %get-tuple-element.109), channel_id=1, source_target_pairs={{1,0},{2,1},{3,2},{4,3},{5,4},{6,5},{7,6},{9,8},{10,9},{11,10},{12... | collective-permute-start | bytes 786440 | tf_op jit(solution)/shard_map/ppermute | solution.py:435
  91.0 17.0 %collective-permute-start.21 = (f32[8,2,64,128]{3,2,1,0:T(8,128)S(1)}, f32[8,2,64,128]{3,2,1,0:T(8,128)S(1)}, u32[]{:S(2)}, u32[]{:S(2)}) collective-permute-start(f32[8,2,64,128]{3,2,1,0:T(8,128)S(1)} %get-tuple-element.128), channel_id=1, source_target_pairs={{0,24},{8,16},{16,8},{24,0},{1,25},{9,17},{17,9},{25,1},{2,26},{10... | collective-permute-start | bytes 1572872 | tf_op jit(solution)/shard_map/ppermute | solution.py:422
  93.3 24.5 %collective-permute-start.22 = (f32[8,2,64,128]{3,2,1,0:T(8,128)S(1)}, f32[8,2,64,128]{3,2,1,0:T(8,128)S(1)}, u32[]{:S(2)}, u32[]{:S(2)}) collective-permute-start(f32[8,2,64,128]{3,2,1,0:T(8,128)S(1)} %get-tuple-element.129), channel_id=1, source_target_pairs={{0,16},{8,24},{16,0},{24,8},{1,17},{9,25},{17,1},{25,9},{2,18},{10... | collective-permute-start | bytes 1572872 | tf_op jit(solution)/shard_map/ppermute | solution.py:422
  94.7 24.5 %collective-permute-start.23 = (f32[8,2,64,128]{3,2,1,0:T(8,128)S(1)}, f32[8,2,64,128]{3,2,1,0:T(8,128)S(1)}, u32[]{:S(2)}, u32[]{:S(2)}) collective-permute-start(f32[8,2,64,128]{3,2,1,0:T(8,128)S(1)} %get-tuple-element.130), channel_id=1, source_target_pairs={{0,8},{8,0},{16,24},{24,16},{1,9},{9,1},{17,25},{25,17},{2,10},{10... | collective-permute-start | bytes 1572872 | tf_op jit(solution)/shard_map/ppermute | solution.py:422
  102.3 16.9 %collective-permute-start.18 = (f32[8,64,128]{2,1,0:T(8,128)S(1)}, f32[8,64,128]{2,1,0:T(8,128)S(1)}, u32[]{:S(2)}, u32[]{:S(2)}) collective-permute-start(f32[8,64,128]{2,1,0:T(8,128)S(1)} %get-tuple-element.122), channel_id=1, source_target_pairs={{0,1},{1,2},{2,3},{3,4},{4,5},{5,6},{6,7},{8,9},{9,10},{10,11},{11... | collective-permute-start | bytes 786440 | tf_op jit(solution)/shard_map/ppermute | solution.py:431
  106.8 21.8 %collective-permute-start.15 = (f32[8,2,64,128]{3,2,1,0:T(8,128)S(1)}, f32[8,2,64,128]{3,2,1,0:T(8,128)S(1)}, u32[]{:S(2)}, u32[]{:S(2)}) collective-permute-start(f32[8,2,64,128]{3,2,1,0:T(8,128)S(1)} %get-tuple-element.118), channel_id=1, source_target_pairs={{0,24},{8,16},{16,8},{24,0},{1,25},{9,17},{17,9},{25,1},{2,26},{10... | collective-permute-start | bytes 1572872 | tf_op jit(solution)/shard_map/ppermute | solution.py:422
  108.0 32.1 %collective-permute-start.16 = (f32[8,2,64,128]{3,2,1,0:T(8,128)S(1)}, f32[8,2,64,128]{3,2,1,0:T(8,128)S(1)}, u32[]{:S(2)}, u32[]{:S(2)}) collective-permute-start(f32[8,2,64,128]{3,2,1,0:T(8,128)S(1)} %get-tuple-element.119), channel_id=1, source_target_pairs={{0,16},{8,24},{16,0},{24,8},{1,17},{9,25},{17,1},{25,9},{2,18},{10... | collective-permute-start | bytes 1572872 | tf_op jit(solution)/shard_map/ppermute | solution.py:422
  117.7 22.4 %collective-permute-start.17 = (f32[8,2,64,128]{3,2,1,0:T(8,128)S(1)}, f32[8,2,64,128]{3,2,1,0:T(8,128)S(1)}, u32[]{:S(2)}, u32[]{:S(2)}) collective-permute-start(f32[8,2,64,128]{3,2,1,0:T(8,128)S(1)} %get-tuple-element.120), channel_id=1, source_target_pairs={{0,8},{8,0},{16,24},{24,16},{1,9},{9,1},{17,25},{25,17},{2,10},{10... | collective-permute-start | bytes 1572872 | tf_op jit(solution)/shard_map/ppermute | solution.py:422
  122.4 28.7 %collective-permute-start.24 = (f32[8,2,64,128]{3,2,1,0:T(8,128)S(1)}, f32[8,2,64,128]{3,2,1,0:T(8,128)S(1)}, u32[]{:S(2)}, u32[]{:S(2)}) collective-permute-start(f32[8,2,64,128]{3,2,1,0:T(8,128)S(1)} %get-tuple-element.134), channel_id=1, source_target_pairs={{0,24},{8,16},{16,8},{24,0},{1,25},{9,17},{17,9},{25,1},{2,26},{10... | collective-permute-start | bytes 1572872 | tf_op jit(solution)/shard_map/ppermute | solution.py:422
  123.6 40.8 %collective-permute-start.25 = (f32[8,2,64,128]{3,2,1,0:T(8,128)S(1)}, f32[8,2,64,128]{3,2,1,0:T(8,128)S(1)}, u32[]{:S(2)}, u32[]{:S(2)}) collective-permute-start(f32[8,2,64,128]{3,2,1,0:T(8,128)S(1)} %get-tuple-element.144), channel_id=1, source_target_pairs={{0,16},{8,24},{16,0},{24,8},{1,17},{9,25},{17,1},{25,9},{2,18},{10... | collective-permute-start | bytes 1572872 | tf_op jit(solution)/shard_map/ppermute | solution.py:422
  128.6 35.8 %collective-permute-start.26 = (f32[8,2,64,128]{3,2,1,0:T(8,128)S(1)}, f32[8,2,64,128]{3,2,1,0:T(8,128)S(1)}, u32[]{:S(2)}, u32[]{:S(2)}) collective-permute-start(f32[8,2,64,128]{3,2,1,0:T(8,128)S(1)} %get-tuple-element.145), channel_id=1, source_target_pairs={{0,8},{8,0},{16,24},{24,16},{1,9},{9,1},{17,25},{25,17},{2,10},{10... | collective-permute-start | bytes 1572872 | tf_op jit(solution)/shard_map/ppermute | solution.py:422
  143.4 30.2 %collective-permute-start.27 = (f32[8,2,64,128]{3,2,1,0:T(8,128)S(1)}, f32[8,2,64,128]{3,2,1,0:T(8,128)S(1)}, u32[]{:S(2)}, u32[]{:S(2)}) collective-permute-start(f32[8,2,64,128]{3,2,1,0:T(8,128)S(1)} %get-tuple-element.150), channel_id=1, source_target_pairs={{0,24},{8,16},{16,8},{24,0},{1,25},{9,17},{17,9},{25,1},{2,26},{10... | collective-permute-start | bytes 1572872 | tf_op jit(solution)/shard_map/ppermute | solution.py:422
  145.8 39.2 %collective-permute-start.19 = (f32[8,2,64,128]{3,2,1,0:T(8,128)S(1)}, f32[8,2,64,128]{3,2,1,0:T(8,128)S(1)}, u32[]{:S(2)}, u32[]{:S(2)}) collective-permute-start(f32[8,2,64,128]{3,2,1,0:T(8,128)S(1)} %get-tuple-element.126), channel_id=1, source_target_pairs={{0,16},{8,24},{16,0},{24,8},{1,17},{9,25},{17,1},{25,9},{2,18},{10... | collective-permute-start | bytes 1572872 | tf_op jit(solution)/shard_map/ppermute | solution.py:422
  151.1 33.8 %collective-permute-start.20 = (f32[8,2,64,128]{3,2,1,0:T(8,128)S(1)}, f32[8,2,64,128]{3,2,1,0:T(8,128)S(1)}, u32[]{:S(2)}, u32[]{:S(2)}) collective-permute-start(f32[8,2,64,128]{3,2,1,0:T(8,128)S(1)} %get-tuple-element.127), channel_id=1, source_target_pairs={{0,8},{8,0},{16,24},{24,16},{1,9},{9,1},{17,25},{25,17},{2,10},{10... | collective-permute-start | bytes 1572872 | tf_op jit(solution)/shard_map/ppermute | solution.py:422

commit v6 on v5

--- a/solution.py
+++ b/solution.py
@@ -188,7 +188,8 @@
 
 def stencil(second, part, tide, u, low, high, flags, src, kappa, speed, below, winv=None, before=()):
     count, depth, width, length = u.shape
-    first, stop = count * part // PARTS, count * (part + 1) // PARTS
+    ends = (0, count // 2, count) if second else (0, count // 4, count)
+    first, stop = ends[part : part + 2]
     field = pl.BlockSpec((1, depth, width, length), lambda t: (first + t, 0, 0, 0))
     plane = pl.BlockSpec((1, width, length), lambda t: (first + t, 0, 0))
     cells = pl.BlockSpec((depth, width, length), lambda t: (0, 0, 0))

time: 189 us -> 189 us (level)
  waiting for transfers between devices: 44.2 us -> 55.4 us
  starting transfers between devices: 51.9 us -> 40.9 us
    ppermute x24, waiting for transfers between devices: 44.2 us -> 55.4 us  [exchange(): lax.ppermute(piece, 'inst', [(i, i ^ code(m, n)) for i in range(n)])]
    ppermute x2, starting transfers between devices: 14.9 us -> 6.79 us  [downward(): lax.ppermute(plane, 'space', [(i + 1, i) for i in range(lax.axis_size('sp...]
    ppermute x24, starting transfers between devices: 27.9 us -> 25.4 us  [exchange(): lax.ppermute(piece, 'inst', [(i, i ^ code(m, n)) for i in range(n)])]
  transfers between devices with their start and end apart: 28 -> 28, of which waited for: 11 -> 10; matrix products, arithmetic and copies ran while one was open for 3% -> 3% of each run, Pallas kernels for 43% -> 42%
where the time goes in v6:
time: 189 us; the launch traced here: 186 us
  Pallas kernels  81.2 us (43%)
  waiting for transfers between devices  55.4 us (29%)
  starting transfers between devices  40.9 us (22%)
  local copies, waits for them, and re-layouts  6.55 us (3%)
    ppermute x24, waiting for transfers between devices, exchange(): lax.ppermute(piece, 'inst', [(i, i ^ code(m, n)) for i in range(n)])  55.4 us
    pallas_call x4, Pallas kernels, stencil(): pl.pallas_call(functools.partial(stencil_kernel, second, first, len(befor...  38 us
    ppermute x24, starting transfers between devices, exchange(): lax.ppermute(piece, 'inst', [(i, i ^ code(m, n)) for i in range(n)])  25.4 us
    pallas_call x4, Pallas kernels, apply_time(): pl.pallas_call(functools.partial(apply_kernel, n), grid_spec=pltpu.Prefet...  13.2 us
    pallas_call x2, Pallas kernels, first_update(): pl.pallas_call(functools.partial(first_kernel, n, aliased), grid_spec=plt...  11.1 us
    ppermute x2, starting transfers between devices, upward(): lax.ppermute(plane, 'space', [(i, i + 1) for i in range(lax.axis_size('sp...  8.71 us
    pallas_call x5, Pallas kernels, cut(): pl.pallas_call(cut_kernel, grid_spec=pltpu.PrefetchScalarGridSpec(num_sca...  7.66 us
    ppermute x2, starting transfers between devices, downward(): lax.ppermute(plane, 'space', [(i + 1, i) for i in range(lax.axis_size('sp...  6.79 us
  transfers between devices with their start and end apart: 28, of which 10 were waited for; matrix products, arithmetic and copies ran while one was open for 3% of the time, Pallas kernels for 42%

profile of v6, /device:TPU:9, one launch (start us, length us, event | category | flops | bytes accessed | tf_op | source)
XLA Modules:
  0.0 186.2 jit_solution(2126001640272543629)
XLA Ops:
  0.6 1.1 cut.5
  1.7 2.2 %collective-permute-start.6 = (f32[8,2,64,128]{3,2,1,0:T(8,128)S(1)}, f32[8,2,64,128]{3,2,1,0:T(8,128)S(1)}, u32[]{:S(2)}, u32[]{:S(2)}) collective-permute-start(f32[8,2,64,128]{3,2,1,0:T(8,128)S(1)} %cut.5), channel_id=1, source_target_pairs={{0,24},{8,16},{16,8},{24,0},{1,25},{9,17},{17,9},{25,1},{2,26},{10... | collective-permute-start | bytes 1572872 | tf_op jit(solution)/shard_map/ppermute | solution.py:423
  4.0 2.2 %cut.6 = (f32[8,2,64,128]{3,2,1,0:T(8,128)}, f32[8,2,64,128]{3,2,1,0:T(8,128)}) custom-call(s32[1]{0:T(128)} %bitcast.me_ref, f32[8,16,64,128]{3,2,1,0:T(8,128)} %refs_6_.3, f32[8,16,64,128]{3,2,1,0:T(8,128)} %refs_6_.3), custom_call_target="tpu_custom_call" | custom-call | flops 1024 | bytes 1024 | tf_op jit(solution)/shard_map/cut/pallas_call | solution.py:61
  6.4 0.3 collective-permute-start.8
  6.7 2.8 %prep.1 = (f32[16,64,128]{2,1,0:T(8,128)S(1)}, f32[16,64,128]{2,1,0:T(8,128)S(1)}, f32[17,64,128]{2,1,0:T(8,128)}, f32[8,64,128]{2,1,0:T(8,128)}) custom-call(f32[8]{0:T(128)S(1)} %copy-done, f32[8]{0:T(128)S(1)} %copy-done.1, f32[8]{0:T(128)S(1)} %multiply_add_fusion.tide_ref, s32[16,64,128]{2,1,0:T(8,128)} %material_ref, s32[8,3,16,64,128]{4,3,2,1,0:T(8,128)} %flags_ref.6, ...), custom_call_target="tpu_custom_call" | custom-call | flops 1024 | bytes 1024 | tf_op jit(solution)/shard_map/prep/pallas_call | solution.py:109
  9.5 4.6 %collective-permute-start.9 = (f32[17,64,128]{2,1,0:T(8,128)}, f32[17,64,128]{2,1,0:T(8,128)S(1)}, u32[]{:S(2)}, u32[]{:S(2)}) collective-permute-start(f32[17,64,128]{2,1,0:T(8,128)} %get-tuple-element.84), channel_id=1, source_target_pairs={{0,1},{1,2},{2,3},{3,4},{4,5},{5,6},{6,7},{8,9},{9,10},{10,11},{11... | collective-permute-start | bytes 1671176 | tf_op jit(solution)/shard_map/ppermute | solution.py:432
  14.1 1.9 %collective-permute-start.10 = (f32[8,64,128]{2,1,0:T(8,128)}, f32[8,64,128]{2,1,0:T(8,128)S(1)}, u32[]{:S(2)}, u32[]{:S(2)}) collective-permute-start(f32[8,64,128]{2,1,0:T(8,128)} %get-tuple-element.85), channel_id=1, source_target_pairs={{1,0},{2,1},{3,2},{4,3},{5,4},{6,5},{7,6},{9,8},{10,9},{11,10},{12... | collective-permute-start | bytes 786440 | tf_op jit(solution)/shard_map/ppermute | solution.py:436
  16.2 0.7 broadcast_bitcast_fusion.1
  16.9 1.5 cut.7
  18.4 0.8 copy-done.2
  19.2 0.8 copy-done.3
  20.0 0.8 copy-done.4
  20.8 1.0 copy.17
  21.7 0.7 broadcast_bitcast_fusion
  22.5 2.2 %collective-permute-start = (f32[8,2,64,128]{3,2,1,0:T(8,128)}, f32[8,2,64,128]{3,2,1,0:T(8,128)}, u32[]{:S(2)}, u32[]{:S(2)}) collective-permute-start(f32[8,2,64,128]{3,2,1,0:T(8,128)} %copy-done.4), channel_id=1, source_target_pairs={{0,24},{8,16},{16,8},{24,0},{1,25},{9,17},{17,9},{25,1},{2,26},{10... | collective-permute-start | bytes 1572872 | tf_op jit(solution)/shard_map/ppermute | solution.py:423
  24.6 4.3 %collective-permute-done.7.refs_1_ = f32[8,2,64,128]{3,2,1,0:T(8,128)S(1)} collective-permute-done((f32[8,2,64,128]{3,2,1,0:T(8,128)}, f32[8,2,64,128]{3,2,1,0:T(8,128)S(1)}, u32[]{:S(2)}, u32[]{:S(2)}) %collective-permute-start.7) | collective-permute-done | bytes 524320 | tf_op jit(solution)/shard_map/ppermute | solution.py:423
  28.9 1.1 collective-permute-start.1
  30.0 1.2 collective-permute-start.2
  31.3 1.8 copy.18
  33.0 1.0 compare_select_fusion.refs_3_
  34.1 6.0 %stencil_one.2 = (f32[8,16,64,128]{3,2,1,0:T(8,128)}, f32[8,16,64,128]{3,2,1,0:T(8,128)}) custom-call(f32[8]{0:T(128)S(1)} %multiply_add_fusion.tide_ref, f32[8,16,64,128]{3,2,1,0:T(8,128)} %refs_6_.3, f32[17,64,128]{2,1,0:T(8,128)S(1)} %collective-permute-done.9.low_ref.below_k_ref.below_f_ref, f32[8,64,128]{2,1,0:T(8,128)S(1)} %collective-permute-done.10.high_ref, ...), custom_call_target="tpu_custom_call" | custom-call | flops 1024 | bytes 1024 | tf_op jit(solution)/shard_map/stencil_one/pallas_call | solution.py:217
  40.1 3.3 %apply_time.5 = (f32[8,2,64,128]{3,2,1,0:T(8,128)S(1)}, f32[8,2,64,128]{3,2,1,0:T(8,128)S(1)}, f32[8,2,64,128]{3,2,1,0:T(8,128)S(1)}, f32[8,2,64,128]{3,2,1,0:T(8,128)S(1)}) custom-call(s32[1]{0:T(128)} %bitcast.me_ref, f32[8,16,64,128]{3,2,1,0:T(8,128)} %refs_6_.3, f32[8,2,64,128]{3,2,1,0:T(8,128)S(1)} %collective-permute-done.6.refs_0_, ...), custom_call_target="tpu_custom_call" | custom-call | flops 1024 | bytes 1024 | tf_op jit(solution)/shard_map/apply_time/pallas_call | solution.py:259
  43.4 0.4 collective-permute-start.11
  43.8 1.1 collective-permute-start.12
  44.9 1.2 collective-permute-start.13
  46.2 5.3 %collective-permute-done.1.refs_1_ = f32[8,2,64,128]{3,2,1,0:T(8,128)} collective-permute-done((f32[8,2,64,128]{3,2,1,0:T(8,128)}, f32[8,2,64,128]{3,2,1,0:T(8,128)}, u32[]{:S(2)}, u32[]{:S(2)}) %collective-permute-start.1) | collective-permute-done | bytes 524320 | tf_op jit(solution)/shard_map/ppermute | solution.py:423
  51.4 3.4 %apply_time.4 = (f32[8,2,64,128]{3,2,1,0:T(8,128)S(1)}, f32[8,2,64,128]{3,2,1,0:T(8,128)S(1)}, f32[8,2,64,128]{3,2,1,0:T(8,128)S(1)}, f32[8,2,64,128]{3,2,1,0:T(8,128)S(1)}) custom-call(s32[1]{0:T(128)} %bitcast.me_ref, f32[8,16,64,128]{3,2,1,0:T(8,128)} %refs_6_.3, f32[8,2,64,128]{3,2,1,0:T(8,128)} %collective-permute-done.refs_0_, ...), custom_call_target="tpu_custom_call" | custom-call | flops 1024 | bytes 1024 | tf_op jit(solution)/shard_map/apply_time/pallas_call | solution.py:259
  54.9 2.2 %collective-permute-start.3 = (f32[8,2,64,128]{3,2,1,0:T(8,128)S(1)}, f32[8,2,64,128]{3,2,1,0:T(8,128)S(1)}, u32[]{:S(2)}, u32[]{:S(2)}) collective-permute-start(f32[8,2,64,128]{3,2,1,0:T(8,128)S(1)} %get-tuple-element.91), channel_id=1, source_target_pairs={{0,24},{8,16},{16,8},{24,0},{1,25},{9,17},{17,9},{25,1},{2,26},{10... | collective-permute-start | bytes 1572872 | tf_op jit(solution)/shard_map/ppermute | solution.py:423
  57.1 0.2 collective-permute-start.4
  57.3 3.2 %collective-permute-done.11.refs_1_ = f32[8,2,64,128]{3,2,1,0:T(8,128)S(1)} collective-permute-done((f32[8,2,64,128]{3,2,1,0:T(8,128)S(1)}, f32[8,2,64,128]{3,2,1,0:T(8,128)S(1)}, u32[]{:S(2)}, u32[]{:S(2)}) %collective-permute-start.11) | collective-permute-done | bytes 524320 | tf_op jit(solution)/shard_map/ppermute | solution.py:423
  60.6 1.2 collective-permute-start.5
  61.8 13.6 %stencil_one.3 = (f32[8,16,64,128]{3,2,1,0:T(8,128)}, f32[8,16,64,128]{3,2,1,0:T(8,128)}) custom-call(f32[8]{0:T(128)S(1)} %multiply_add_fusion.tide_ref, f32[8,16,64,128]{3,2,1,0:T(8,128)} %refs_6_.3, f32[17,64,128]{2,1,0:T(8,128)S(1)} %collective-permute-done.9.low_ref.below_k_ref.below_f_ref, ...), custom_call_target="tpu_custom_call", output_to_operand_aliasing={{0}: (10, {}), {1}: (11, {})} | custom-call | flops 1024 | bytes 1024 | tf_op jit(solution)/shard_map/stencil_one/pallas_call | solution.py:217
  75.4 5.5 %first_update.2 = (f32[8,16,64,128]{3,2,1,0:T(8,128)}, f32[8,16,64,128]{3,2,1,0:T(8,128)}, f32[8,64,128]{2,1,0:T(8,128)S(1)}, f32[8,64,128]{2,1,0:T(8,128)}, f32...) custom-call(s32[1]{0:T(128)} %bitcast.me_ref, ...), custom_call_target="tpu_custom_call" | custom-call | flops 1024 | bytes 1024 | tf_op jit(solution)/shard_map/first_update/pallas_call | solution.py:307
  81.0 4.9 %collective-permute-start.14 = (f32[8,64,128]{2,1,0:T(8,128)S(1)}, f32[8,64,128]{2,1,0:T(8,128)S(1)}, u32[]{:S(2)}, u32[]{:S(2)}) collective-permute-start(f32[8,64,128]{2,1,0:T(8,128)S(1)} %get-tuple-element.109), channel_id=1, source_target_pairs={{1,0},{2,1},{3,2},{4,3},{5,4},{6,5},{7,6},{9,8},{10,9},{11,10},{12... | collective-permute-start | bytes 786440 | tf_op jit(solution)/shard_map/ppermute | solution.py:436
  85.8 1.3 collective-permute-start.21
  87.1 0.2 collective-permute-start.22
  87.3 8.8 %collective-permute-done.4.refs_2_ = f32[8,2,64,128]{3,2,1,0:T(8,128)S(1)} collective-permute-done((f32[8,2,64,128]{3,2,1,0:T(8,128)S(1)}, f32[8,2,64,128]{3,2,1,0:T(8,128)S(1)}, u32[]{:S(2)}, u32[]{:S(2)}) %collective-permute-start.4) | collective-permute-done | bytes 524320 | tf_op jit(solution)/shard_map/ppermute | solution.py:423
  96.2 1.2 collective-permute-start.23
  97.4 5.5 %first_update.3 = (f32[8,16,64,128]{3,2,1,0:T(8,128)}, f32[8,16,64,128]{3,2,1,0:T(8,128)}, f32[8,64,128]{2,1,0:T(8,128)}, f32[8,64,128]{2,1,0:T(8,128)S(1)}, f32...) custom-call(s32[1]{0:T(128)} %bitcast.me_ref, ...), custom_call_target="tpu_custom_call", output_to_operand_aliasing={{0}: (8, {}), {1}: (9, {})} | custom-call | flops 1024 | bytes 1024 | tf_op jit(solution)/shard_map/first_update/pallas_call | solution.py:307
  102.9 4.1 %collective-permute-start.18 = (f32[8,64,128]{2,1,0:T(8,128)S(1)}, f32[8,64,128]{2,1,0:T(8,128)S(1)}, u32[]{:S(2)}, u32[]{:S(2)}) collective-permute-start(f32[8,64,128]{2,1,0:T(8,128)S(1)} %get-tuple-element.122), channel_id=1, source_target_pairs={{0,1},{1,2},{2,3},{3,4},{4,5},{5,6},{6,7},{8,9},{9,10},{10,11},{11... | collective-permute-start | bytes 786440 | tf_op jit(solution)/shard_map/ppermute | solution.py:432
  107.0 1.3 collective-permute-start.15
  108.6 10.0 %collective-permute-done.22.refs_1_ = f32[8,2,64,128]{3,2,1,0:T(8,128)S(1)} collective-permute-done((f32[8,2,64,128]{3,2,1,0:T(8,128)S(1)}, f32[8,2,64,128]{3,2,1,0:T(8,128)S(1)}, u32[]{:S(2)}, u32[]{:S(2)}) %collective-permute-start.22) | collective-permute-done | bytes 524320 | tf_op jit(solution)/shard_map/ppermute | solution.py:423
  118.6 1.2 collective-permute-start.17
  119.8 3.2 %apply_time.7 = (f32[8,2,64,128]{3,2,1,0:T(8,128)S(1)}, f32[8,2,64,128]{3,2,1,0:T(8,128)S(1)}, f32[8,2,64,128]{3,2,1,0:T(8,128)S(1)}, f32[8,2,64,128]{3,2,1,0:T(8,128)S(1)}) custom-call(s32[1]{0:T(128)} %bitcast.me_ref, f32[8,16,64,128]{3,2,1,0:T(8,128)} %get-tuple-element.135.u_ref.own_ref, f32[8,2,64,128]{3,2,1,0:T(8,128)S(1)} %collective-permute-done.21.refs_0_, ...), custom_call_target="tpu_custom_call" | custom-call | flops 1024 | bytes 1024 | tf_op jit(solution)/shard_map/apply_time/pallas_call | solution.py:259
  123.0 1.3 collective-permute-start.24
  124.3 0.2 collective-permute-start.25
  124.5 3.6 %collective-permute-done.15.refs_0_ = f32[8,2,64,128]{3,2,1,0:T(8,128)S(1)} collective-permute-done((f32[8,2,64,128]{3,2,1,0:T(8,128)S(1)}, f32[8,2,64,128]{3,2,1,0:T(8,128)S(1)}, u32[]{:S(2)}, u32[]{:S(2)}) %collective-permute-start.15) | collective-permute-done | bytes 524320 | tf_op jit(solution)/shard_map/ppermute | solution.py:423
  128.1 1.2 collective-permute-start.26
  129.3 9.2 %stencil_two.2.rest_1_ = f32[8,16,64,128]{3,2,1,0:T(8,128)} custom-call(f32[8]{0:T(128)S(1)} %multiply_add_fusion.tide_ref, f32[8,16,64,128]{3,2,1,0:T(8,128)} %get-tuple-element.135.u_ref.own_ref, f32[8,64,128]{2,1,0:T(8,128)S(1)} %collective-permute-done.18.low_ref, f32[8,64,128]{2,1,0:T(8,128)S(1)} %collective-permute-done.14.high_ref, ...), custom_call_target="tpu_custom_call" | custom-call | flops 1024 | bytes 1024 | tf_op jit(solution)/shard_map/stencil_two/pallas_call | solution.py:217
  138.5 2.5 %collective-permute-done.16.refs_1_ = f32[8,2,64,128]{3,2,1,0:T(8,128)S(1)} collective-permute-done((f32[8,2,64,128]{3,2,1,0:T(8,128)S(1)}, f32[8,2,64,128]{3,2,1,0:T(8,128)S(1)}, u32[]{:S(2)}, u32[]{:S(2)}) %collective-permute-start.16) | collective-permute-done | bytes 524320 | tf_op jit(solution)/shard_map/ppermute | solution.py:423
  141.0 3.2 %apply_time.6 = (f32[8,2,64,128]{3,2,1,0:T(8,128)S(1)}, f32[8,2,64,128]{3,2,1,0:T(8,128)S(1)}, f32[8,2,64,128]{3,2,1,0:T(8,128)S(1)}, f32[8,2,64,128]{3,2,1,0:T(8,128)S(1)}) custom-call(s32[1]{0:T(128)} %bitcast.me_ref, f32[8,16,64,128]{3,2,1,0:T(8,128)} %get-tuple-element.135.u_ref.own_ref, f32[8,2,64,128]{3,2,1,0:T(8,128)S(1)} %collective-permute-done.15.refs_0_, ...), custom_call_target="tpu_custom_call" | custom-call | flops 1024 | bytes 1024 | tf_op jit(solution)/shard_map/apply_time/pallas_call | solution.py:259
  144.2 2.2 %collective-permute-start.27 = (f32[8,2,64,128]{3,2,1,0:T(8,128)S(1)}, f32[8,2,64,128]{3,2,1,0:T(8,128)S(1)}, u32[]{:S(2)}, u32[]{:S(2)}) collective-permute-start(f32[8,2,64,128]{3,2,1,0:T(8,128)S(1)} %get-tuple-element.150), channel_id=1, source_target_pairs={{0,24},{8,16},{16,8},{24,0},{1,25},{9,17},{17,9},{25,1},{2,26},{10... | collective-permute-start | bytes 1572872 | tf_op jit(solution)/shard_map/ppermute | solution.py:423
  146.5 0.2 collective-permute-start.19
  146.7 3.9 %collective-permute-done.24.refs_1_ = f32[8,2,64,128]{3,2,1,0:T(8,128)S(1)} collective-permute-done((f32[8,2,64,128]{3,2,1,0:T(8,128)S(1)}, f32[8,2,64,128]{3,2,1,0:T(8,128)S(1)}, u32[]{:S(2)}, u32[]{:S(2)}) %collective-permute-start.24) | collective-permute-done | bytes 524320 | tf_op jit(solution)/shard_map/ppermute | solution.py:423
  150.6 1.2 collective-permute-start.20
  151.8 9.2 %stencil_two.3.refs_0_.refs_1_.refs_2_.refs_4_ = f32[8,16,64,128]{3,2,1,0:T(8,128)} custom-call(f32[8]{0:T(128)S(1)} %multiply_add_fusion.tide_ref, f32[8,16,64,128]{3,2,1,0:T(8,128)} %get-tuple-element.135.u_ref.own_ref, f32[8,64,128]{2,1,0:T(8,128)S(1)} %collective-permute-done.18.low_ref, ...), custom_call_target="tpu_custom_call", output_to_operand_aliasing={{}: (11, {})} | custom-call | flops 1024 | bytes 1024 | tf_op jit(solution)/shard_map/stencil_two/pallas_call | solution.py:217
  161.0 1.5 cut.9
  162.5 1.5 cut.8
  164.0 4.5 %chunk_update.1.refs_3_ = f32[8,16,64,128]{3,2,1,0:T(8,128)} custom-call(s32[1]{0:T(128)} %bitcast.me_ref, f32[8,2,64,128]{3,2,1,0:T(8,128)S(1)} %get-tuple-element.143.refs_0_, f32[8,2,64,128]{3,2,1,0:T(8,128)S(1)} %collective-permute-done.24.refs_1_, f32[8,2,64,128]{3,2,1,0:T(8,128)S(1)} %collective-permute-done.25.refs_2_, ...), custom_call_target="tpu_custom_call" | custom-call | flops 1024 | bytes 1024 | tf_op jit(solution)/shard_map/chunk_update/pallas_call | solution.py:404
  168.5 2.1 %last_update.2.refs_3_ = f32[8,16,64,128]{3,2,1,0:T(8,128)} custom-call(s32[1]{0:T(128)} %bitcast.me_ref, f32[8,2,64,128]{3,2,1,0:T(8,128)S(1)} %get-tuple-element.142.refs_0_, f32[8,16,64,128]{3,2,1,0:T(8,128)} %stencil_two.3.refs_0_.refs_1_.refs_2_.refs_4_, ...), custom_call_target="tpu_custom_call", output_to_operand_aliasing={{}: (4, {})} | custom-call | flops 1024 | bytes 1024 | tf_op jit(solution)/shard_map/last_update/pallas_call | solution.py:333
  170.5 2.6 %collective-permute-done.27.refs_0_ = f32[8,2,64,128]{3,2,1,0:T(8,128)S(1)} collective-permute-done((f32[8,2,64,128]{3,2,1,0:T(8,128)S(1)}, f32[8,2,64,128]{3,2,1,0:T(8,128)S(1)}, u32[]{:S(2)}, u32[]{:S(2)}) %collective-permute-start.27) | collective-permute-done | bytes 524320 | tf_op jit(solution)/shard_map/ppermute | solution.py:423
  173.1 0.9 last_update.3.refs_6_
  174.0 11.1 %collective-permute-done.19.refs_0_ = f32[8,2,64,128]{3,2,1,0:T(8,128)S(1)} collective-permute-done((f32[8,2,64,128]{3,2,1,0:T(8,128)S(1)}, f32[8,2,64,128]{3,2,1,0:T(8,128)S(1)}, u32[]{:S(2)}, u32[]{:S(2)}) %collective-permute-start.19) | collective-permute-done | bytes 524320 | tf_op jit(solution)/shard_map/ppermute | solution.py:423
  185.1 1.0 final_update.1
  (31 shorter events, 0.7 us)
Async XLA Ops:
  1.7 5.0 %copy-start = (f32[8]{0:T(128)S(1)}, f32[8]{0:T(128)}, u32[]{:S(2)}) copy-start(f32[8]{0:T(128)} %disp_ref.1) | copy-start | bytes 100
  1.7 5.0 %copy-start.1 = (f32[8]{0:T(128)S(1)}, f32[8]{0:T(128)}, u32[]{:S(2)}) copy-start(f32[8]{0:T(128)} %perm_ref.1) | copy-start | bytes 100
  1.7 38.4 %collective-permute-start.6 = (f32[8,2,64,128]{3,2,1,0:T(8,128)S(1)}, f32[8,2,64,128]{3,2,1,0:T(8,128)S(1)}, u32[]{:S(2)}, u32[]{:S(2)}) collective-permute-start(f32[8,2,64,128]{3,2,1,0:T(8,128)S(1)} %cut.5), channel_id=1, source_target_pairs={{0,24},{8,16},{16,8},{24,0},{1,25},{9,17},{17,9},{25,1},{2,26},{10... | collective-permute-start | bytes 1572872 | tf_op jit(solution)/shard_map/ppermute | solution.py:423
  6.2 22.7 %collective-permute-start.7 = (f32[8,2,64,128]{3,2,1,0:T(8,128)}, f32[8,2,64,128]{3,2,1,0:T(8,128)S(1)}, u32[]{:S(2)}, u32[]{:S(2)}) collective-permute-start(f32[8,2,64,128]{3,2,1,0:T(8,128)} %get-tuple-element.79), channel_id=1, source_target_pairs={{0,16},{8,24},{16,0},{24,8},{1,17},{9,25},{17,1},{25,9},{2,18},{10... | collective-permute-start | bytes 1572872 | tf_op jit(solution)/shard_map/ppermute | solution.py:423
  6.4 33.7 %collective-permute-start.8 = (f32[8,2,64,128]{3,2,1,0:T(8,128)}, f32[8,2,64,128]{3,2,1,0:T(8,128)}, u32[]{:S(2)}, u32[]{:S(2)}) collective-permute-start(f32[8,2,64,128]{3,2,1,0:T(8,128)} %get-tuple-element.80), channel_id=1, source_target_pairs={{0,8},{8,0},{16,24},{24,16},{1,9},{9,1},{17,25},{25,17},{2,10},{10... | collective-permute-start | bytes 1572872 | tf_op jit(solution)/shard_map/ppermute | solution.py:423
  9.5 20.5 %collective-permute-start.9 = (f32[17,64,128]{2,1,0:T(8,128)}, f32[17,64,128]{2,1,0:T(8,128)S(1)}, u32[]{:S(2)}, u32[]{:S(2)}) collective-permute-start(f32[17,64,128]{2,1,0:T(8,128)} %get-tuple-element.84), channel_id=1, source_target_pairs={{0,1},{1,2},{2,3},{3,4},{4,5},{5,6},{6,7},{8,9},{9,10},{10,11},{11... | collective-permute-start | bytes 1671176 | tf_op jit(solution)/shard_map/ppermute | solution.py:432
  14.1 8.3 %collective-permute-start.10 = (f32[8,64,128]{2,1,0:T(8,128)}, f32[8,64,128]{2,1,0:T(8,128)S(1)}, u32[]{:S(2)}, u32[]{:S(2)}) collective-permute-start(f32[8,64,128]{2,1,0:T(8,128)} %get-tuple-element.85), channel_id=1, source_target_pairs={{1,0},{2,1},{3,2},{4,3},{5,4},{6,5},{7,6},{9,8},{10,9},{11,10},{12... | collective-permute-start | bytes 786440 | tf_op jit(solution)/shard_map/ppermute | solution.py:436
  18.4 0.8 copy-start.2
  19.2 0.8 copy-start.3
  20.0 0.8 copy-start.4
  22.5 22.5 %collective-permute-start = (f32[8,2,64,128]{3,2,1,0:T(8,128)}, f32[8,2,64,128]{3,2,1,0:T(8,128)}, u32[]{:S(2)}, u32[]{:S(2)}) collective-permute-start(f32[8,2,64,128]{3,2,1,0:T(8,128)} %copy-done.4), channel_id=1, source_target_pairs={{0,24},{8,16},{16,8},{24,0},{1,25},{9,17},{17,9},{25,1},{2,26},{10... | collective-permute-start | bytes 1572872 | tf_op jit(solution)/shard_map/ppermute | solution.py:423
  28.9 22.5 %collective-permute-start.1 = (f32[8,2,64,128]{3,2,1,0:T(8,128)}, f32[8,2,64,128]{3,2,1,0:T(8,128)}, u32[]{:S(2)}, u32[]{:S(2)}) collective-permute-start(f32[8,2,64,128]{3,2,1,0:T(8,128)} %copy-done.3), channel_id=1, source_target_pairs={{0,16},{8,24},{16,0},{24,8},{1,17},{9,25},{17,1},{25,9},{2,18},{10... | collective-permute-start | bytes 1572872 | tf_op jit(solution)/shard_map/ppermute | solution.py:423
  30.0 21.4 %collective-permute-start.2 = (f32[8,2,64,128]{3,2,1,0:T(8,128)}, f32[8,2,64,128]{3,2,1,0:T(8,128)}, u32[]{:S(2)}, u32[]{:S(2)}) collective-permute-start(f32[8,2,64,128]{3,2,1,0:T(8,128)} %copy-done.2), channel_id=1, source_target_pairs={{0,8},{8,0},{16,24},{24,16},{1,9},{9,1},{17,25},{25,17},{2,10},{10... | collective-permute-start | bytes 1572872 | tf_op jit(solution)/shard_map/ppermute | solution.py:423
  43.4 17.1 %collective-permute-start.11 = (f32[8,2,64,128]{3,2,1,0:T(8,128)S(1)}, f32[8,2,64,128]{3,2,1,0:T(8,128)S(1)}, u32[]{:S(2)}, u32[]{:S(2)}) collective-permute-start(f32[8,2,64,128]{3,2,1,0:T(8,128)S(1)} %get-tuple-element.103), channel_id=1, source_target_pairs={{0,24},{8,16},{16,8},{24,0},{1,25},{9,17},{17,9},{25,1},{2,26},{10... | collective-permute-start | bytes 1572872 | tf_op jit(solution)/shard_map/ppermute | solution.py:423
  43.8 31.6 %collective-permute-start.12 = (f32[8,2,64,128]{3,2,1,0:T(8,128)S(1)}, f32[8,2,64,128]{3,2,1,0:T(8,128)S(1)}, u32[]{:S(2)}, u32[]{:S(2)}) collective-permute-start(f32[8,2,64,128]{3,2,1,0:T(8,128)S(1)} %get-tuple-element.104), channel_id=1, source_target_pairs={{0,16},{8,24},{16,0},{24,8},{1,17},{9,25},{17,1},{25,9},{2,18},{10... | collective-permute-start | bytes 1572872 | tf_op jit(solution)/shard_map/ppermute | solution.py:423
  44.9 30.5 %collective-permute-start.13 = (f32[8,2,64,128]{3,2,1,0:T(8,128)S(1)}, f32[8,2,64,128]{3,2,1,0:T(8,128)S(1)}, u32[]{:S(2)}, u32[]{:S(2)}) collective-permute-start(f32[8,2,64,128]{3,2,1,0:T(8,128)S(1)} %get-tuple-element.105), channel_id=1, source_target_pairs={{0,8},{8,0},{16,24},{24,16},{1,9},{9,1},{17,25},{25,17},{2,10},{10... | collective-permute-start | bytes 1572872 | tf_op jit(solution)/shard_map/ppermute | solution.py:423
  54.9 32.2 %collective-permute-start.3 = (f32[8,2,64,128]{3,2,1,0:T(8,128)S(1)}, f32[8,2,64,128]{3,2,1,0:T(8,128)S(1)}, u32[]{:S(2)}, u32[]{:S(2)}) collective-permute-start(f32[8,2,64,128]{3,2,1,0:T(8,128)S(1)} %get-tuple-element.91), channel_id=1, source_target_pairs={{0,24},{8,16},{16,8},{24,0},{1,25},{9,17},{17,9},{25,1},{2,26},{10... | collective-permute-start | bytes 1572872 | tf_op jit(solution)/shard_map/ppermute | solution.py:423
  57.1 39.1 %collective-permute-start.4 = (f32[8,2,64,128]{3,2,1,0:T(8,128)S(1)}, f32[8,2,64,128]{3,2,1,0:T(8,128)S(1)}, u32[]{:S(2)}, u32[]{:S(2)}) collective-permute-start(f32[8,2,64,128]{3,2,1,0:T(8,128)S(1)} %get-tuple-element.92), channel_id=1, source_target_pairs={{0,16},{8,24},{16,0},{24,8},{1,17},{9,25},{17,1},{25,9},{2,18},{10... | collective-permute-start | bytes 1572872 | tf_op jit(solution)/shard_map/ppermute | solution.py:423
  60.6 36.8 %collective-permute-start.5 = (f32[8,2,64,128]{3,2,1,0:T(8,128)S(1)}, f32[8,2,64,128]{3,2,1,0:T(8,128)S(1)}, u32[]{:S(2)}, u32[]{:S(2)}) collective-permute-start(f32[8,2,64,128]{3,2,1,0:T(8,128)S(1)} %get-tuple-element.93), channel_id=1, source_target_pairs={{0,8},{8,0},{16,24},{24,16},{1,9},{9,1},{17,25},{25,17},{2,10},{10... | collective-permute-start | bytes 1572872 | tf_op jit(solution)/shard_map/ppermute | solution.py:423
  81.0 16.4 %collective-permute-start.14 = (f32[8,64,128]{2,1,0:T(8,128)S(1)}, f32[8,64,128]{2,1,0:T(8,128)S(1)}, u32[]{:S(2)}, u32[]{:S(2)}) collective-permute-start(f32[8,64,128]{2,1,0:T(8,128)S(1)} %get-tuple-element.109), channel_id=1, source_target_pairs={{1,0},{2,1},{3,2},{4,3},{5,4},{6,5},{7,6},{9,8},{10,9},{11,10},{12... | collective-permute-start | bytes 786440 | tf_op jit(solution)/shard_map/ppermute | solution.py:436
  85.8 22.5 %collective-permute-start.21 = (f32[8,2,64,128]{3,2,1,0:T(8,128)S(1)}, f32[8,2,64,128]{3,2,1,0:T(8,128)S(1)}, u32[]{:S(2)}, u32[]{:S(2)}) collective-permute-start(f32[8,2,64,128]{3,2,1,0:T(8,128)S(1)} %get-tuple-element.128), channel_id=1, source_target_pairs={{0,24},{8,16},{16,8},{24,0},{1,25},{9,17},{17,9},{25,1},{2,26},{10... | collective-permute-start | bytes 1572872 | tf_op jit(solution)/shard_map/ppermute | solution.py:423
  87.1 31.5 %collective-permute-start.22 = (f32[8,2,64,128]{3,2,1,0:T(8,128)S(1)}, f32[8,2,64,128]{3,2,1,0:T(8,128)S(1)}, u32[]{:S(2)}, u32[]{:S(2)}) collective-permute-start(f32[8,2,64,128]{3,2,1,0:T(8,128)S(1)} %get-tuple-element.129), channel_id=1, source_target_pairs={{0,16},{8,24},{16,0},{24,8},{1,17},{9,25},{17,1},{25,9},{2,18},{10... | collective-permute-start | bytes 1572872 | tf_op jit(solution)/shard_map/ppermute | solution.py:423
  96.2 23.6 %collective-permute-start.23 = (f32[8,2,64,128]{3,2,1,0:T(8,128)S(1)}, f32[8,2,64,128]{3,2,1,0:T(8,128)S(1)}, u32[]{:S(2)}, u32[]{:S(2)}) collective-permute-start(f32[8,2,64,128]{3,2,1,0:T(8,128)S(1)} %get-tuple-element.130), channel_id=1, source_target_pairs={{0,8},{8,0},{16,24},{24,16},{1,9},{9,1},{17,25},{25,17},{2,10},{10... | collective-permute-start | bytes 1572872 | tf_op jit(solution)/shard_map/ppermute | solution.py:423
  102.9 16.9 %collective-permute-start.18 = (f32[8,64,128]{2,1,0:T(8,128)S(1)}, f32[8,64,128]{2,1,0:T(8,128)S(1)}, u32[]{:S(2)}, u32[]{:S(2)}) collective-permute-start(f32[8,64,128]{2,1,0:T(8,128)S(1)} %get-tuple-element.122), channel_id=1, source_target_pairs={{0,1},{1,2},{2,3},{3,4},{4,5},{5,6},{6,7},{8,9},{9,10},{10,11},{11... | collective-permute-start | bytes 786440 | tf_op jit(solution)/shard_map/ppermute | solution.py:432
  107.0 21.1 %collective-permute-start.15 = (f32[8,2,64,128]{3,2,1,0:T(8,128)S(1)}, f32[8,2,64,128]{3,2,1,0:T(8,128)S(1)}, u32[]{:S(2)}, u32[]{:S(2)}) collective-permute-start(f32[8,2,64,128]{3,2,1,0:T(8,128)S(1)} %get-tuple-element.118), channel_id=1, source_target_pairs={{0,24},{8,16},{16,8},{24,0},{1,25},{9,17},{17,9},{25,1},{2,26},{10... | collective-permute-start | bytes 1572872 | tf_op jit(solution)/shard_map/ppermute | solution.py:423
  108.3 32.7 %collective-permute-start.16 = (f32[8,2,64,128]{3,2,1,0:T(8,128)S(1)}, f32[8,2,64,128]{3,2,1,0:T(8,128)S(1)}, u32[]{:S(2)}, u32[]{:S(2)}) collective-permute-start(f32[8,2,64,128]{3,2,1,0:T(8,128)S(1)} %get-tuple-element.119), channel_id=1, source_target_pairs={{0,16},{8,24},{16,0},{24,8},{1,17},{9,25},{17,1},{25,9},{2,18},{10... | collective-permute-start | bytes 1572872 | tf_op jit(solution)/shard_map/ppermute | solution.py:423
  118.6 22.4 %collective-permute-start.17 = (f32[8,2,64,128]{3,2,1,0:T(8,128)S(1)}, f32[8,2,64,128]{3,2,1,0:T(8,128)S(1)}, u32[]{:S(2)}, u32[]{:S(2)}) collective-permute-start(f32[8,2,64,128]{3,2,1,0:T(8,128)S(1)} %get-tuple-element.120), channel_id=1, source_target_pairs={{0,8},{8,0},{16,24},{24,16},{1,9},{9,1},{17,25},{25,17},{2,10},{10... | collective-permute-start | bytes 1572872 | tf_op jit(solution)/shard_map/ppermute | solution.py:423
  123.0 27.6 %collective-permute-start.24 = (f32[8,2,64,128]{3,2,1,0:T(8,128)S(1)}, f32[8,2,64,128]{3,2,1,0:T(8,128)S(1)}, u32[]{:S(2)}, u32[]{:S(2)}) collective-permute-start(f32[8,2,64,128]{3,2,1,0:T(8,128)S(1)} %get-tuple-element.134), channel_id=1, source_target_pairs={{0,24},{8,16},{16,8},{24,0},{1,25},{9,17},{17,9},{25,1},{2,26},{10... | collective-permute-start | bytes 1572872 | tf_op jit(solution)/shard_map/ppermute | solution.py:423
  124.3 39.7 %collective-permute-start.25 = (f32[8,2,64,128]{3,2,1,0:T(8,128)S(1)}, f32[8,2,64,128]{3,2,1,0:T(8,128)S(1)}, u32[]{:S(2)}, u32[]{:S(2)}) collective-permute-start(f32[8,2,64,128]{3,2,1,0:T(8,128)S(1)} %get-tuple-element.144), channel_id=1, source_target_pairs={{0,16},{8,24},{16,0},{24,8},{1,17},{9,25},{17,1},{25,9},{2,18},{10... | collective-permute-start | bytes 1572872 | tf_op jit(solution)/shard_map/ppermute | solution.py:423
  128.1 35.9 %collective-permute-start.26 = (f32[8,2,64,128]{3,2,1,0:T(8,128)S(1)}, f32[8,2,64,128]{3,2,1,0:T(8,128)S(1)}, u32[]{:S(2)}, u32[]{:S(2)}) collective-permute-start(f32[8,2,64,128]{3,2,1,0:T(8,128)S(1)} %get-tuple-element.145), channel_id=1, source_target_pairs={{0,8},{8,0},{16,24},{24,16},{1,9},{9,1},{17,25},{25,17},{2,10},{10... | collective-permute-start | bytes 1572872 | tf_op jit(solution)/shard_map/ppermute | solution.py:423
  144.2 28.9 %collective-permute-start.27 = (f32[8,2,64,128]{3,2,1,0:T(8,128)S(1)}, f32[8,2,64,128]{3,2,1,0:T(8,128)S(1)}, u32[]{:S(2)}, u32[]{:S(2)}) collective-permute-start(f32[8,2,64,128]{3,2,1,0:T(8,128)S(1)} %get-tuple-element.150), channel_id=1, source_target_pairs={{0,24},{8,16},{16,8},{24,0},{1,25},{9,17},{17,9},{25,1},{2,26},{10... | collective-permute-start | bytes 1572872 | tf_op jit(solution)/shard_map/ppermute | solution.py:423
  146.5 38.7 %collective-permute-start.19 = (f32[8,2,64,128]{3,2,1,0:T(8,128)S(1)}, f32[8,2,64,128]{3,2,1,0:T(8,128)S(1)}, u32[]{:S(2)}, u32[]{:S(2)}) collective-permute-start(f32[8,2,64,128]{3,2,1,0:T(8,128)S(1)} %get-tuple-element.126), channel_id=1, source_target_pairs={{0,16},{8,24},{16,0},{24,8},{1,17},{9,25},{17,1},{25,9},{2,18},{10... | collective-permute-start | bytes 1572872 | tf_op jit(solution)/shard_map/ppermute | solution.py:423
  150.6 34.5 %collective-permute-start.20 = (f32[8,2,64,128]{3,2,1,0:T(8,128)S(1)}, f32[8,2,64,128]{3,2,1,0:T(8,128)S(1)}, u32[]{:S(2)}, u32[]{:S(2)}) collective-permute-start(f32[8,2,64,128]{3,2,1,0:T(8,128)S(1)} %get-tuple-element.127), channel_id=1, source_target_pairs={{0,8},{8,0},{16,24},{24,16},{1,9},{9,1},{17,25},{25,17},{2,10},{10... | collective-permute-start | bytes 1572872 | tf_op jit(solution)/shard_map/ppermute | solution.py:423

commit v7 on v6

--- a/solution.py
+++ b/solution.py
@@ -455,7 +455,7 @@
     mat = spectral_blocks(me, n, count)
     kappa, speed, up, down = prep(disp_table, perm_table, tide, material, flags, start)
     below, high = upward(up), downward(down)
-    start = after(start, up, down)
+    start = after(start, below, high)
     for chunk in range(1, chunks):
         going = cut(me_array, start, n, chunk, part)
         there.append(exchange(going))

time: 189 us -> 188 us (level); the launches traced: 186 us -> 187 us
  waiting for transfers between devices: 55.4 us -> 61.4 us
  starting transfers between devices: 40.9 us -> 37.6 us
  local copies, waits for them, and re-layouts: 6.55 us -> 4.14 us
    ppermute x2, waiting for transfers between devices: 0.01 us -> 9.81 us  [downward(): lax.ppermute(plane, 'space', [(i + 1, i) for i in range(lax.axis_size('sp...]
    ppermute x24, waiting for transfers between devices: 55.4 us -> 51.6 us  [exchange(): lax.ppermute(piece, 'inst', [(i, i ^ code(m, n)) for i in range(n)])]
    unnamed x10 -> x4, local copies, waits for them, and re-layouts: 2.39 us -> 0.01 us
  transfers between devices with their start and end apart: 28 -> 28, of which waited for: 10 -> 15; matrix products, arithmetic and copies ran while one was open for 3% -> 3% of each run, Pallas kernels for 42% -> 43%
where the time goes in v7:
time: 188 us; the launch traced here: 187 us
  Pallas kernels  82.2 us (44%)
  waiting for transfers between devices  61.4 us (33%)
  starting transfers between devices  37.6 us (20%)
  local copies, waits for them, and re-layouts  4.14 us (2%)
    ppermute x24, waiting for transfers between devices, exchange(): lax.ppermute(piece, 'inst', [(i, i ^ code(m, n)) for i in range(n)])  51.6 us
    pallas_call x4, Pallas kernels, stencil(): pl.pallas_call(functools.partial(stencil_kernel, second, first, len(befor...  38 us
    ppermute x24, starting transfers between devices, exchange(): lax.ppermute(piece, 'inst', [(i, i ^ code(m, n)) for i in range(n)])  24.3 us
    pallas_call x4, Pallas kernels, apply_time(): pl.pallas_call(functools.partial(apply_kernel, n), grid_spec=pltpu.Prefet...  13.2 us
    pallas_call x2, Pallas kernels, first_update(): pl.pallas_call(functools.partial(first_kernel, n, aliased), grid_spec=plt...  11 us
    ppermute x2, waiting for transfers between devices, downward(): lax.ppermute(plane, 'space', [(i + 1, i) for i in range(lax.axis_size('sp...  9.81 us
    pallas_call x5, Pallas kernels, cut(): pl.pallas_call(cut_kernel, grid_spec=pltpu.PrefetchScalarGridSpec(num_sca...  8.75 us
    ppermute x2, starting transfers between devices, upward(): lax.ppermute(plane, 'space', [(i, i + 1) for i in range(lax.axis_size('sp...  8.3 us
  transfers between devices with their start and end apart: 28, of which 15 were waited for; matrix products, arithmetic and copies ran while one was open for 3% of the time, Pallas kernels for 43%

profile of v7, /device:TPU:9, one launch (start us, length us, event | category | flops | bytes accessed | tf_op | source)
XLA Modules:
  0.0 187.4 jit_solution(1444869090012397654)
XLA Ops:
  0.6 1.1 cut.5
  1.7 2.2 %collective-permute-start.8 = (f32[8,2,64,128]{3,2,1,0:T(8,128)S(1)}, f32[8,2,64,128]{3,2,1,0:T(8,128)S(1)}, u32[]{:S(2)}, u32[]{:S(2)}) collective-permute-start(f32[8,2,64,128]{3,2,1,0:T(8,128)S(1)} %cut.5), channel_id=1, source_target_pairs={{0,24},{8,16},{16,8},{24,0},{1,25},{9,17},{17,9},{25,1},{2,26},{10... | collective-permute-start | bytes 1572872 | tf_op jit(solution)/shard_map/ppermute | solution.py:423
  4.0 2.2 %cut.6 = (f32[8,2,64,128]{3,2,1,0:T(8,128)}, f32[8,2,64,128]{3,2,1,0:T(8,128)}) custom-call(s32[1]{0:T(128)} %bitcast.me_ref, f32[8,16,64,128]{3,2,1,0:T(8,128)} %refs_6_.3, f32[8,16,64,128]{3,2,1,0:T(8,128)} %refs_6_.3), custom_call_target="tpu_custom_call" | custom-call | flops 1024 | bytes 1024 | tf_op jit(solution)/shard_map/cut/pallas_call | solution.py:61
  6.2 0.3 collective-permute-start.10
  6.4 0.2 collective-permute-start.9
  6.7 2.8 %prep.1 = (f32[16,64,128]{2,1,0:T(8,128)S(1)}, f32[16,64,128]{2,1,0:T(8,128)S(1)}, f32[17,64,128]{2,1,0:T(8,128)}, f32[8,64,128]{2,1,0:T(8,128)}) custom-call(f32[8]{0:T(128)S(1)} %copy-done, f32[8]{0:T(128)S(1)} %copy-done.1, f32[8]{0:T(128)S(1)} %multiply_add_fusion.tide_ref, s32[16,64,128]{2,1,0:T(8,128)} %material_ref, s32[8,3,16,64,128]{4,3,2,1,0:T(8,128)} %flags_ref.6, ...), custom_call_target="tpu_custom_call" | custom-call | flops 1024 | bytes 1024 | tf_op jit(solution)/shard_map/prep/pallas_call | solution.py:109
  9.5 4.6 %collective-permute-start = (f32[17,64,128]{2,1,0:T(8,128)}, f32[17,64,128]{2,1,0:T(8,128)S(1)}, u32[]{:S(2)}, u32[]{:S(2)}) collective-permute-start(f32[17,64,128]{2,1,0:T(8,128)} %get-tuple-element.84), channel_id=1, source_target_pairs={{0,1},{1,2},{2,3},{3,4},{4,5},{5,6},{6,7},{8,9},{9,10},{10,11},{11... | collective-permute-start | bytes 1671176 | tf_op jit(solution)/shard_map/ppermute | solution.py:432
  14.1 1.9 %collective-permute-start.1 = (f32[8,64,128]{2,1,0:T(8,128)}, f32[8,64,128]{2,1,0:T(8,128)S(1)}, u32[]{:S(2)}, u32[]{:S(2)}) collective-permute-start(f32[8,64,128]{2,1,0:T(8,128)} %get-tuple-element.85), channel_id=1, source_target_pairs={{1,0},{2,1},{3,2},{4,3},{5,4},{6,5},{7,6},{9,8},{10,9},{11,10},{12... | collective-permute-start | bytes 786440 | tf_op jit(solution)/shard_map/ppermute | solution.py:436
  16.2 0.7 broadcast_bitcast_fusion.1
  16.9 1.0 copy.17
  17.9 4.6 %collective-permute-done.1.high_ref = f32[8,64,128]{2,1,0:T(8,128)S(1)} collective-permute-done((f32[8,64,128]{2,1,0:T(8,128)}, f32[8,64,128]{2,1,0:T(8,128)S(1)}, u32[]{:S(2)}, u32[]{:S(2)}) %collective-permute-start.1) | collective-permute-done | bytes 262176 | tf_op jit(solution)/shard_map/ppermute | solution.py:436
  22.4 2.6 %cut.7 = (f32[8,2,64,128]{3,2,1,0:T(8,128)}, f32[8,2,64,128]{3,2,1,0:T(8,128)}, f32[8,2,64,128]{3,2,1,0:T(8,128)}) custom-call(s32[1]{0:T(128)} %bitcast.me_ref, f32[8,16,64,128]{3,2,1,0:T(8,128)} %refs_6_.3, f32[8,16,64,128]{3,2,1,0:T(8,128)} %refs_6_.3, f32[8,16,64,128]{3,2,1,0:T(8,128)} %refs_6_.3), custom_call_target="tpu_custom_call" | custom-call | flops 1024 | bytes 1024 | tf_op jit(solution)/shard_map/cut/pallas_call | solution.py:61
  25.0 2.2 %collective-permute-start.2 = (f32[8,2,64,128]{3,2,1,0:T(8,128)}, f32[8,2,64,128]{3,2,1,0:T(8,128)}, u32[]{:S(2)}, u32[]{:S(2)}) collective-permute-start(f32[8,2,64,128]{3,2,1,0:T(8,128)} %get-tuple-element.87), channel_id=1, source_target_pairs={{0,24},{8,16},{16,8},{24,0},{1,25},{9,17},{17,9},{25,1},{2,26},{10... | collective-permute-start | bytes 1572872 | tf_op jit(solution)/shard_map/ppermute | solution.py:423
  27.2 0.7 broadcast_bitcast_fusion
  27.9 0.2 collective-permute-start.3
  28.1 0.3 collective-permute-start.4
  28.4 1.8 copy.18
  30.1 1.0 compare_select_fusion.refs_3_
  31.2 6.0 %stencil_one.2 = (f32[8,16,64,128]{3,2,1,0:T(8,128)}, f32[8,16,64,128]{3,2,1,0:T(8,128)}) custom-call(f32[8]{0:T(128)S(1)} %multiply_add_fusion.tide_ref, f32[8,16,64,128]{3,2,1,0:T(8,128)} %refs_6_.3, f32[17,64,128]{2,1,0:T(8,128)S(1)} %collective-permute-done.low_ref.below_k_ref.below_f_ref, f32[8,64,128]{2,1,0:T(8,128)S(1)} %collective-permute-done.1.high_ref, ...), custom_call_target="tpu_custom_call" | custom-call | flops 1024 | bytes 1024 | tf_op jit(solution)/shard_map/stencil_one/pallas_call | solution.py:217
  37.2 3.3 %apply_time.5 = (f32[8,2,64,128]{3,2,1,0:T(8,128)S(1)}, f32[8,2,64,128]{3,2,1,0:T(8,128)S(1)}, f32[8,2,64,128]{3,2,1,0:T(8,128)S(1)}, f32[8,2,64,128]{3,2,1,0:T(8,128)S(1)}) custom-call(s32[1]{0:T(128)} %bitcast.me_ref, f32[8,16,64,128]{3,2,1,0:T(8,128)} %refs_6_.3, f32[8,2,64,128]{3,2,1,0:T(8,128)S(1)} %collective-permute-done.8.refs_0_, ...), custom_call_target="tpu_custom_call" | custom-call | flops 1024 | bytes 1024 | tf_op jit(solution)/shard_map/apply_time/pallas_call | solution.py:259
  40.5 2.2 %collective-permute-start.11 = (f32[8,2,64,128]{3,2,1,0:T(8,128)S(1)}, f32[8,2,64,128]{3,2,1,0:T(8,128)S(1)}, u32[]{:S(2)}, u32[]{:S(2)}) collective-permute-start(f32[8,2,64,128]{3,2,1,0:T(8,128)S(1)} %get-tuple-element.103), channel_id=1, source_target_pairs={{0,24},{8,16},{16,8},{24,0},{1,25},{9,17},{17,9},{25,1},{2,26},{10... | collective-permute-start | bytes 1572872 | tf_op jit(solution)/shard_map/ppermute | solution.py:423
  42.8 0.2 collective-permute-start.12
  43.0 0.3 collective-permute-start.13
  43.3 8.1 %collective-permute-done.3.refs_1_ = f32[8,2,64,128]{3,2,1,0:T(8,128)} collective-permute-done((f32[8,2,64,128]{3,2,1,0:T(8,128)}, f32[8,2,64,128]{3,2,1,0:T(8,128)}, u32[]{:S(2)}, u32[]{:S(2)}) %collective-permute-start.3) | collective-permute-done | bytes 524320 | tf_op jit(solution)/shard_map/ppermute | solution.py:423
  51.4 3.5 %apply_time.4 = (f32[8,2,64,128]{3,2,1,0:T(8,128)S(1)}, f32[8,2,64,128]{3,2,1,0:T(8,128)S(1)}, f32[8,2,64,128]{3,2,1,0:T(8,128)S(1)}, f32[8,2,64,128]{3,2,1,0:T(8,128)S(1)}) custom-call(s32[1]{0:T(128)} %bitcast.me_ref, f32[8,16,64,128]{3,2,1,0:T(8,128)} %refs_6_.3, f32[8,2,64,128]{3,2,1,0:T(8,128)} %collective-permute-done.2.refs_0_, ...), custom_call_target="tpu_custom_call" | custom-call | flops 1024 | bytes 1024 | tf_op jit(solution)/shard_map/apply_time/pallas_call | solution.py:259
  54.8 2.2 %collective-permute-start.5 = (f32[8,2,64,128]{3,2,1,0:T(8,128)S(1)}, f32[8,2,64,128]{3,2,1,0:T(8,128)S(1)}, u32[]{:S(2)}, u32[]{:S(2)}) collective-permute-start(f32[8,2,64,128]{3,2,1,0:T(8,128)S(1)} %get-tuple-element.91), channel_id=1, source_target_pairs={{0,24},{8,16},{16,8},{24,0},{1,25},{9,17},{17,9},{25,1},{2,26},{10... | collective-permute-start | bytes 1572872 | tf_op jit(solution)/shard_map/ppermute | solution.py:423
  57.1 5.4 %collective-permute-done.11.refs_1_ = f32[8,2,64,128]{3,2,1,0:T(8,128)S(1)} collective-permute-done((f32[8,2,64,128]{3,2,1,0:T(8,128)S(1)}, f32[8,2,64,128]{3,2,1,0:T(8,128)S(1)}, u32[]{:S(2)}, u32[]{:S(2)}) %collective-permute-start.11) | collective-permute-done | bytes 524320 | tf_op jit(solution)/shard_map/ppermute | solution.py:423
  62.5 1.2 collective-permute-start.6
  63.7 1.2 collective-permute-start.7
  64.9 13.6 %stencil_one.3 = (f32[8,16,64,128]{3,2,1,0:T(8,128)}, f32[8,16,64,128]{3,2,1,0:T(8,128)}) custom-call(f32[8]{0:T(128)S(1)} %multiply_add_fusion.tide_ref, f32[8,16,64,128]{3,2,1,0:T(8,128)} %refs_6_.3, f32[17,64,128]{2,1,0:T(8,128)S(1)} %collective-permute-done.low_ref.below_k_ref.below_f_ref, ...), custom_call_target="tpu_custom_call", output_to_operand_aliasing={{0}: (10, {}), {1}: (11, {})} | custom-call | flops 1024 | bytes 1024 | tf_op jit(solution)/shard_map/stencil_one/pallas_call | solution.py:217
  78.6 5.6 %first_update.2 = (f32[8,16,64,128]{3,2,1,0:T(8,128)}, f32[8,16,64,128]{3,2,1,0:T(8,128)}, f32[8,64,128]{2,1,0:T(8,128)S(1)}, f32[8,64,128]{2,1,0:T(8,128)}, f32...) custom-call(s32[1]{0:T(128)} %bitcast.me_ref, ...), custom_call_target="tpu_custom_call" | custom-call | flops 1024 | bytes 1024 | tf_op jit(solution)/shard_map/first_update/pallas_call | solution.py:307
  84.1 3.1 %collective-permute-start.14 = (f32[8,64,128]{2,1,0:T(8,128)S(1)}, f32[8,64,128]{2,1,0:T(8,128)S(1)}, u32[]{:S(2)}, u32[]{:S(2)}) collective-permute-start(f32[8,64,128]{2,1,0:T(8,128)S(1)} %get-tuple-element.109), channel_id=1, source_target_pairs={{1,0},{2,1},{3,2},{4,3},{5,4},{6,5},{7,6},{9,8},{10,9},{11,10},{12... | collective-permute-start | bytes 786440 | tf_op jit(solution)/shard_map/ppermute | solution.py:436
  87.2 0.3 collective-permute-start.21
  87.5 5.3 %collective-permute-done.14.high_ref = f32[8,64,128]{2,1,0:T(8,128)S(1)} collective-permute-done((f32[8,64,128]{2,1,0:T(8,128)S(1)}, f32[8,64,128]{2,1,0:T(8,128)S(1)}, u32[]{:S(2)}, u32[]{:S(2)}) %collective-permute-start.14) | collective-permute-done | bytes 262176 | tf_op jit(solution)/shard_map/ppermute | solution.py:436
  93.0 0.3 collective-permute-start.23
  93.2 2.9 %collective-permute-done.6.refs_2_ = f32[8,2,64,128]{3,2,1,0:T(8,128)S(1)} collective-permute-done((f32[8,2,64,128]{3,2,1,0:T(8,128)S(1)}, f32[8,2,64,128]{3,2,1,0:T(8,128)S(1)}, u32[]{:S(2)}, u32[]{:S(2)}) %collective-permute-start.6) | collective-permute-done | bytes 524320 | tf_op jit(solution)/shard_map/ppermute | solution.py:423
  96.3 5.4 %first_update.3 = (f32[8,16,64,128]{3,2,1,0:T(8,128)}, f32[8,16,64,128]{3,2,1,0:T(8,128)}, f32[8,64,128]{2,1,0:T(8,128)}, f32[8,64,128]{2,1,0:T(8,128)S(1)}, f32...) custom-call(s32[1]{0:T(128)} %bitcast.me_ref, ...), custom_call_target="tpu_custom_call", output_to_operand_aliasing={{0}: (8, {}), {1}: (9, {})} | custom-call | flops 1024 | bytes 1024 | tf_op jit(solution)/shard_map/first_update/pallas_call | solution.py:307
  101.7 3.7 %collective-permute-start.18 = (f32[8,64,128]{2,1,0:T(8,128)S(1)}, f32[8,64,128]{2,1,0:T(8,128)S(1)}, u32[]{:S(2)}, u32[]{:S(2)}) collective-permute-start(f32[8,64,128]{2,1,0:T(8,128)S(1)} %get-tuple-element.122), channel_id=1, source_target_pairs={{0,1},{1,2},{2,3},{3,4},{4,5},{5,6},{6,7},{8,9},{9,10},{10,11},{11... | collective-permute-start | bytes 786440 | tf_op jit(solution)/shard_map/ppermute | solution.py:432
  105.5 1.9 %collective-permute-start.15 = (f32[8,2,64,128]{3,2,1,0:T(8,128)S(1)}, f32[8,2,64,128]{3,2,1,0:T(8,128)S(1)}, u32[]{:S(2)}, u32[]{:S(2)}) collective-permute-start(f32[8,2,64,128]{3,2,1,0:T(8,128)S(1)} %get-tuple-element.118), channel_id=1, source_target_pairs={{0,24},{8,16},{16,8},{24,0},{1,25},{9,17},{17,9},{25,1},{2,26},{10... | collective-permute-start | bytes 1572872 | tf_op jit(solution)/shard_map/ppermute | solution.py:423
  107.5 1.2 collective-permute-start.16
  108.8 9.9 %collective-permute-done.22.refs_1_ = f32[8,2,64,128]{3,2,1,0:T(8,128)S(1)} collective-permute-done((f32[8,2,64,128]{3,2,1,0:T(8,128)S(1)}, f32[8,2,64,128]{3,2,1,0:T(8,128)S(1)}, u32[]{:S(2)}, u32[]{:S(2)}) %collective-permute-start.22) | collective-permute-done | bytes 524320 | tf_op jit(solution)/shard_map/ppermute | solution.py:423
  118.7 1.2 collective-permute-start.17
  119.9 3.2 %apply_time.7 = (f32[8,2,64,128]{3,2,1,0:T(8,128)S(1)}, f32[8,2,64,128]{3,2,1,0:T(8,128)S(1)}, f32[8,2,64,128]{3,2,1,0:T(8,128)S(1)}, f32[8,2,64,128]{3,2,1,0:T(8,128)S(1)}) custom-call(s32[1]{0:T(128)} %bitcast.me_ref, f32[8,16,64,128]{3,2,1,0:T(8,128)} %get-tuple-element.135.u_ref.own_ref, f32[8,2,64,128]{3,2,1,0:T(8,128)S(1)} %collective-permute-done.21.refs_0_, ...), custom_call_target="tpu_custom_call" | custom-call | flops 1024 | bytes 1024 | tf_op jit(solution)/shard_map/apply_time/pallas_call | solution.py:259
  123.1 1.3 collective-permute-start.24
  124.4 0.2 collective-permute-start.25
  124.6 5.4 %collective-permute-done.15.refs_0_ = f32[8,2,64,128]{3,2,1,0:T(8,128)S(1)} collective-permute-done((f32[8,2,64,128]{3,2,1,0:T(8,128)S(1)}, f32[8,2,64,128]{3,2,1,0:T(8,128)S(1)}, u32[]{:S(2)}, u32[]{:S(2)}) %collective-permute-start.15) | collective-permute-done | bytes 524320 | tf_op jit(solution)/shard_map/ppermute | solution.py:423
  130.0 1.2 collective-permute-start.26
  131.2 9.2 %stencil_two.2.rest_1_ = f32[8,16,64,128]{3,2,1,0:T(8,128)} custom-call(f32[8]{0:T(128)S(1)} %multiply_add_fusion.tide_ref, f32[8,16,64,128]{3,2,1,0:T(8,128)} %get-tuple-element.135.u_ref.own_ref, f32[8,64,128]{2,1,0:T(8,128)S(1)} %collective-permute-done.18.low_ref, f32[8,64,128]{2,1,0:T(8,128)S(1)} %collective-permute-done.14.high_ref, ...), custom_call_target="tpu_custom_call" | custom-call | flops 1024 | bytes 1024 | tf_op jit(solution)/shard_map/stencil_two/pallas_call | solution.py:217
  140.4 0.7 collective-permute-done.16.refs_1_
  141.3 3.2 %apply_time.6 = (f32[8,2,64,128]{3,2,1,0:T(8,128)S(1)}, f32[8,2,64,128]{3,2,1,0:T(8,128)S(1)}, f32[8,2,64,128]{3,2,1,0:T(8,128)S(1)}, f32[8,2,64,128]{3,2,1,0:T(8,128)S(1)}) custom-call(s32[1]{0:T(128)} %bitcast.me_ref, f32[8,16,64,128]{3,2,1,0:T(8,128)} %get-tuple-element.135.u_ref.own_ref, f32[8,2,64,128]{3,2,1,0:T(8,128)S(1)} %collective-permute-done.15.refs_0_, ...), custom_call_target="tpu_custom_call" | custom-call | flops 1024 | bytes 1024 | tf_op jit(solution)/shard_map/apply_time/pallas_call | solution.py:259
  144.5 2.0 %collective-permute-start.27 = (f32[8,2,64,128]{3,2,1,0:T(8,128)S(1)}, f32[8,2,64,128]{3,2,1,0:T(8,128)S(1)}, u32[]{:S(2)}, u32[]{:S(2)}) collective-permute-start(f32[8,2,64,128]{3,2,1,0:T(8,128)S(1)} %get-tuple-element.150), channel_id=1, source_target_pairs={{0,24},{8,16},{16,8},{24,0},{1,25},{9,17},{17,9},{25,1},{2,26},{10... | collective-permute-start | bytes 1572872 | tf_op jit(solution)/shard_map/ppermute | solution.py:423
  146.6 0.4 collective-permute-start.19
  147.0 5.6 %collective-permute-done.24.refs_1_ = f32[8,2,64,128]{3,2,1,0:T(8,128)S(1)} collective-permute-done((f32[8,2,64,128]{3,2,1,0:T(8,128)S(1)}, f32[8,2,64,128]{3,2,1,0:T(8,128)S(1)}, u32[]{:S(2)}, u32[]{:S(2)}) %collective-permute-start.24) | collective-permute-done | bytes 524320 | tf_op jit(solution)/shard_map/ppermute | solution.py:423
  152.5 1.2 collective-permute-start.20
  153.8 9.2 %stencil_two.3.refs_0_.refs_1_.refs_2_.refs_4_ = f32[8,16,64,128]{3,2,1,0:T(8,128)} custom-call(f32[8]{0:T(128)S(1)} %multiply_add_fusion.tide_ref, f32[8,16,64,128]{3,2,1,0:T(8,128)} %get-tuple-element.135.u_ref.own_ref, f32[8,64,128]{2,1,0:T(8,128)S(1)} %collective-permute-done.18.low_ref, ...), custom_call_target="tpu_custom_call", output_to_operand_aliasing={{}: (11, {})} | custom-call | flops 1024 | bytes 1024 | tf_op jit(solution)/shard_map/stencil_two/pallas_call | solution.py:217
  162.9 1.5 cut.9
  164.4 1.5 cut.8
  165.9 4.5 %chunk_update.1.refs_3_ = f32[8,16,64,128]{3,2,1,0:T(8,128)} custom-call(s32[1]{0:T(128)} %bitcast.me_ref, f32[8,2,64,128]{3,2,1,0:T(8,128)S(1)} %get-tuple-element.143.refs_0_, f32[8,2,64,128]{3,2,1,0:T(8,128)S(1)} %collective-permute-done.24.refs_1_, f32[8,2,64,128]{3,2,1,0:T(8,128)S(1)} %collective-permute-done.25.refs_2_, ...), custom_call_target="tpu_custom_call" | custom-call | flops 1024 | bytes 1024 | tf_op jit(solution)/shard_map/chunk_update/pallas_call | solution.py:404
  170.4 2.1 %last_update.2.refs_3_ = f32[8,16,64,128]{3,2,1,0:T(8,128)} custom-call(s32[1]{0:T(128)} %bitcast.me_ref, f32[8,2,64,128]{3,2,1,0:T(8,128)S(1)} %get-tuple-element.142.refs_0_, f32[8,16,64,128]{3,2,1,0:T(8,128)} %stencil_two.3.refs_0_.refs_1_.refs_2_.refs_4_, ...), custom_call_target="tpu_custom_call", output_to_operand_aliasing={{}: (4, {})} | custom-call | flops 1024 | bytes 1024 | tf_op jit(solution)/shard_map/last_update/pallas_call | solution.py:333
  172.4 2.6 %collective-permute-done.27.refs_0_ = f32[8,2,64,128]{3,2,1,0:T(8,128)S(1)} collective-permute-done((f32[8,2,64,128]{3,2,1,0:T(8,128)S(1)}, f32[8,2,64,128]{3,2,1,0:T(8,128)S(1)}, u32[]{:S(2)}, u32[]{:S(2)}) %collective-permute-start.27) | collective-permute-done | bytes 524320 | tf_op jit(solution)/shard_map/ppermute | solution.py:423
  175.1 0.9 last_update.3.refs_6_
  175.9 10.1 %collective-permute-done.19.refs_0_ = f32[8,2,64,128]{3,2,1,0:T(8,128)S(1)} collective-permute-done((f32[8,2,64,128]{3,2,1,0:T(8,128)S(1)}, f32[8,2,64,128]{3,2,1,0:T(8,128)S(1)}, u32[]{:S(2)}, u32[]{:S(2)}) %collective-permute-start.19) | collective-permute-done | bytes 524320 | tf_op jit(solution)/shard_map/ppermute | solution.py:423
  186.1 0.3 collective-permute-done.20.refs_1_
  186.4 1.0 final_update.1
  (25 shorter events, 0.9 us)
Async XLA Ops:
  1.7 5.0 %copy-start = (f32[8]{0:T(128)S(1)}, f32[8]{0:T(128)}, u32[]{:S(2)}) copy-start(f32[8]{0:T(128)} %disp_ref.1) | copy-start | bytes 100
  1.7 5.0 %copy-start.1 = (f32[8]{0:T(128)S(1)}, f32[8]{0:T(128)}, u32[]{:S(2)}) copy-start(f32[8]{0:T(128)} %perm_ref.1) | copy-start | bytes 100
  1.7 35.5 %collective-permute-start.8 = (f32[8,2,64,128]{3,2,1,0:T(8,128)S(1)}, f32[8,2,64,128]{3,2,1,0:T(8,128)S(1)}, u32[]{:S(2)}, u32[]{:S(2)}) collective-permute-start(f32[8,2,64,128]{3,2,1,0:T(8,128)S(1)} %cut.5), channel_id=1, source_target_pairs={{0,24},{8,16},{16,8},{24,0},{1,25},{9,17},{17,9},{25,1},{2,26},{10... | collective-permute-start | bytes 1572872 | tf_op jit(solution)/shard_map/ppermute | solution.py:423
  6.2 22.0 %collective-permute-start.10 = (f32[8,2,64,128]{3,2,1,0:T(8,128)}, f32[8,2,64,128]{3,2,1,0:T(8,128)S(1)}, u32[]{:S(2)}, u32[]{:S(2)}) collective-permute-start(f32[8,2,64,128]{3,2,1,0:T(8,128)} %get-tuple-element.80), channel_id=1, source_target_pairs={{0,8},{8,0},{16,24},{24,16},{1,9},{9,1},{17,25},{25,17},{2,10},{10... | collective-permute-start | bytes 1572872 | tf_op jit(solution)/shard_map/ppermute | solution.py:423
  6.4 30.8 %collective-permute-start.9 = (f32[8,2,64,128]{3,2,1,0:T(8,128)}, f32[8,2,64,128]{3,2,1,0:T(8,128)}, u32[]{:S(2)}, u32[]{:S(2)}) collective-permute-start(f32[8,2,64,128]{3,2,1,0:T(8,128)} %get-tuple-element.79), channel_id=1, source_target_pairs={{0,16},{8,24},{16,0},{24,8},{1,17},{9,25},{17,1},{25,9},{2,18},{10... | collective-permute-start | bytes 1572872 | tf_op jit(solution)/shard_map/ppermute | solution.py:423
  9.5 12.9 %collective-permute-start = (f32[17,64,128]{2,1,0:T(8,128)}, f32[17,64,128]{2,1,0:T(8,128)S(1)}, u32[]{:S(2)}, u32[]{:S(2)}) collective-permute-start(f32[17,64,128]{2,1,0:T(8,128)} %get-tuple-element.84), channel_id=1, source_target_pairs={{0,1},{1,2},{2,3},{3,4},{4,5},{5,6},{6,7},{8,9},{9,10},{10,11},{11... | collective-permute-start | bytes 1671176 | tf_op jit(solution)/shard_map/ppermute | solution.py:432
  14.1 8.3 %collective-permute-start.1 = (f32[8,64,128]{2,1,0:T(8,128)}, f32[8,64,128]{2,1,0:T(8,128)S(1)}, u32[]{:S(2)}, u32[]{:S(2)}) collective-permute-start(f32[8,64,128]{2,1,0:T(8,128)} %get-tuple-element.85), channel_id=1, source_target_pairs={{1,0},{2,1},{3,2},{4,3},{5,4},{6,5},{7,6},{9,8},{10,9},{11,10},{12... | collective-permute-start | bytes 786440 | tf_op jit(solution)/shard_map/ppermute | solution.py:436
  25.0 18.0 %collective-permute-start.2 = (f32[8,2,64,128]{3,2,1,0:T(8,128)}, f32[8,2,64,128]{3,2,1,0:T(8,128)}, u32[]{:S(2)}, u32[]{:S(2)}) collective-permute-start(f32[8,2,64,128]{3,2,1,0:T(8,128)} %get-tuple-element.87), channel_id=1, source_target_pairs={{0,24},{8,16},{16,8},{24,0},{1,25},{9,17},{17,9},{25,1},{2,26},{10... | collective-permute-start | bytes 1572872 | tf_op jit(solution)/shard_map/ppermute | solution.py:423
  27.9 23.5 %collective-permute-start.3 = (f32[8,2,64,128]{3,2,1,0:T(8,128)}, f32[8,2,64,128]{3,2,1,0:T(8,128)}, u32[]{:S(2)}, u32[]{:S(2)}) collective-permute-start(f32[8,2,64,128]{3,2,1,0:T(8,128)} %get-tuple-element.88), channel_id=1, source_target_pairs={{0,16},{8,24},{16,0},{24,8},{1,17},{9,25},{17,1},{25,9},{2,18},{10... | collective-permute-start | bytes 1572872 | tf_op jit(solution)/shard_map/ppermute | solution.py:423
  28.1 23.3 %collective-permute-start.4 = (f32[8,2,64,128]{3,2,1,0:T(8,128)}, f32[8,2,64,128]{3,2,1,0:T(8,128)}, u32[]{:S(2)}, u32[]{:S(2)}) collective-permute-start(f32[8,2,64,128]{3,2,1,0:T(8,128)} %get-tuple-element.89), channel_id=1, source_target_pairs={{0,8},{8,0},{16,24},{24,16},{1,9},{9,1},{17,25},{25,17},{2,10},{10... | collective-permute-start | bytes 1572872 | tf_op jit(solution)/shard_map/ppermute | solution.py:423
  40.5 21.9 %collective-permute-start.11 = (f32[8,2,64,128]{3,2,1,0:T(8,128)S(1)}, f32[8,2,64,128]{3,2,1,0:T(8,128)S(1)}, u32[]{:S(2)}, u32[]{:S(2)}) collective-permute-start(f32[8,2,64,128]{3,2,1,0:T(8,128)S(1)} %get-tuple-element.103), channel_id=1, source_target_pairs={{0,24},{8,16},{16,8},{24,0},{1,25},{9,17},{17,9},{25,1},{2,26},{10... | collective-permute-start | bytes 1572872 | tf_op jit(solution)/shard_map/ppermute | solution.py:423
  42.8 35.8 %collective-permute-start.12 = (f32[8,2,64,128]{3,2,1,0:T(8,128)S(1)}, f32[8,2,64,128]{3,2,1,0:T(8,128)S(1)}, u32[]{:S(2)}, u32[]{:S(2)}) collective-permute-start(f32[8,2,64,128]{3,2,1,0:T(8,128)S(1)} %get-tuple-element.104), channel_id=1, source_target_pairs={{0,16},{8,24},{16,0},{24,8},{1,17},{9,25},{17,1},{25,9},{2,18},{10... | collective-permute-start | bytes 1572872 | tf_op jit(solution)/shard_map/ppermute | solution.py:423
  43.0 35.6 %collective-permute-start.13 = (f32[8,2,64,128]{3,2,1,0:T(8,128)S(1)}, f32[8,2,64,128]{3,2,1,0:T(8,128)S(1)}, u32[]{:S(2)}, u32[]{:S(2)}) collective-permute-start(f32[8,2,64,128]{3,2,1,0:T(8,128)S(1)} %get-tuple-element.105), channel_id=1, source_target_pairs={{0,8},{8,0},{16,24},{24,16},{1,9},{9,1},{17,25},{25,17},{2,10},{10... | collective-permute-start | bytes 1572872 | tf_op jit(solution)/shard_map/ppermute | solution.py:423
  54.8 38.1 %collective-permute-start.5 = (f32[8,2,64,128]{3,2,1,0:T(8,128)S(1)}, f32[8,2,64,128]{3,2,1,0:T(8,128)S(1)}, u32[]{:S(2)}, u32[]{:S(2)}) collective-permute-start(f32[8,2,64,128]{3,2,1,0:T(8,128)S(1)} %get-tuple-element.91), channel_id=1, source_target_pairs={{0,24},{8,16},{16,8},{24,0},{1,25},{9,17},{17,9},{25,1},{2,26},{10... | collective-permute-start | bytes 1572872 | tf_op jit(solution)/shard_map/ppermute | solution.py:423
  62.5 33.7 %collective-permute-start.6 = (f32[8,2,64,128]{3,2,1,0:T(8,128)S(1)}, f32[8,2,64,128]{3,2,1,0:T(8,128)S(1)}, u32[]{:S(2)}, u32[]{:S(2)}) collective-permute-start(f32[8,2,64,128]{3,2,1,0:T(8,128)S(1)} %get-tuple-element.92), channel_id=1, source_target_pairs={{0,16},{8,24},{16,0},{24,8},{1,17},{9,25},{17,1},{25,9},{2,18},{10... | collective-permute-start | bytes 1572872 | tf_op jit(solution)/shard_map/ppermute | solution.py:423
  63.7 32.6 %collective-permute-start.7 = (f32[8,2,64,128]{3,2,1,0:T(8,128)S(1)}, f32[8,2,64,128]{3,2,1,0:T(8,128)S(1)}, u32[]{:S(2)}, u32[]{:S(2)}) collective-permute-start(f32[8,2,64,128]{3,2,1,0:T(8,128)S(1)} %get-tuple-element.93), channel_id=1, source_target_pairs={{0,8},{8,0},{16,24},{24,16},{1,9},{9,1},{17,25},{25,17},{2,10},{10... | collective-permute-start | bytes 1572872 | tf_op jit(solution)/shard_map/ppermute | solution.py:423
  84.1 8.6 %collective-permute-start.14 = (f32[8,64,128]{2,1,0:T(8,128)S(1)}, f32[8,64,128]{2,1,0:T(8,128)S(1)}, u32[]{:S(2)}, u32[]{:S(2)}) collective-permute-start(f32[8,64,128]{2,1,0:T(8,128)S(1)} %get-tuple-element.109), channel_id=1, source_target_pairs={{1,0},{2,1},{3,2},{4,3},{5,4},{6,5},{7,6},{9,8},{10,9},{11,10},{12... | collective-permute-start | bytes 786440 | tf_op jit(solution)/shard_map/ppermute | solution.py:436
  87.2 20.3 %collective-permute-start.21 = (f32[8,2,64,128]{3,2,1,0:T(8,128)S(1)}, f32[8,2,64,128]{3,2,1,0:T(8,128)S(1)}, u32[]{:S(2)}, u32[]{:S(2)}) collective-permute-start(f32[8,2,64,128]{3,2,1,0:T(8,128)S(1)} %get-tuple-element.128), channel_id=1, source_target_pairs={{0,24},{8,16},{16,8},{24,0},{1,25},{9,17},{17,9},{25,1},{2,26},{10... | collective-permute-start | bytes 1572872 | tf_op jit(solution)/shard_map/ppermute | solution.py:423
  92.8 25.9 %collective-permute-start.22 = (f32[8,2,64,128]{3,2,1,0:T(8,128)S(1)}, f32[8,2,64,128]{3,2,1,0:T(8,128)S(1)}, u32[]{:S(2)}, u32[]{:S(2)}) collective-permute-start(f32[8,2,64,128]{3,2,1,0:T(8,128)S(1)} %get-tuple-element.129), channel_id=1, source_target_pairs={{0,16},{8,24},{16,0},{24,8},{1,17},{9,25},{17,1},{25,9},{2,18},{10... | collective-permute-start | bytes 1572872 | tf_op jit(solution)/shard_map/ppermute | solution.py:423
  93.0 26.9 %collective-permute-start.23 = (f32[8,2,64,128]{3,2,1,0:T(8,128)S(1)}, f32[8,2,64,128]{3,2,1,0:T(8,128)S(1)}, u32[]{:S(2)}, u32[]{:S(2)}) collective-permute-start(f32[8,2,64,128]{3,2,1,0:T(8,128)S(1)} %get-tuple-element.130), channel_id=1, source_target_pairs={{0,8},{8,0},{16,24},{24,16},{1,9},{9,1},{17,25},{25,17},{2,10},{10... | collective-permute-start | bytes 1572872 | tf_op jit(solution)/shard_map/ppermute | solution.py:423
  101.7 18.1 %collective-permute-start.18 = (f32[8,64,128]{2,1,0:T(8,128)S(1)}, f32[8,64,128]{2,1,0:T(8,128)S(1)}, u32[]{:S(2)}, u32[]{:S(2)}) collective-permute-start(f32[8,64,128]{2,1,0:T(8,128)S(1)} %get-tuple-element.122), channel_id=1, source_target_pairs={{0,1},{1,2},{2,3},{3,4},{4,5},{5,6},{6,7},{8,9},{9,10},{10,11},{11... | collective-permute-start | bytes 786440 | tf_op jit(solution)/shard_map/ppermute | solution.py:432
  105.5 24.6 %collective-permute-start.15 = (f32[8,2,64,128]{3,2,1,0:T(8,128)S(1)}, f32[8,2,64,128]{3,2,1,0:T(8,128)S(1)}, u32[]{:S(2)}, u32[]{:S(2)}) collective-permute-start(f32[8,2,64,128]{3,2,1,0:T(8,128)S(1)} %get-tuple-element.118), channel_id=1, source_target_pairs={{0,24},{8,16},{16,8},{24,0},{1,25},{9,17},{17,9},{25,1},{2,26},{10... | collective-permute-start | bytes 1572872 | tf_op jit(solution)/shard_map/ppermute | solution.py:423
  107.5 33.6 %collective-permute-start.16 = (f32[8,2,64,128]{3,2,1,0:T(8,128)S(1)}, f32[8,2,64,128]{3,2,1,0:T(8,128)S(1)}, u32[]{:S(2)}, u32[]{:S(2)}) collective-permute-start(f32[8,2,64,128]{3,2,1,0:T(8,128)S(1)} %get-tuple-element.119), channel_id=1, source_target_pairs={{0,16},{8,24},{16,0},{24,8},{1,17},{9,25},{17,1},{25,9},{2,18},{10... | collective-permute-start | bytes 1572872 | tf_op jit(solution)/shard_map/ppermute | solution.py:423
  118.7 22.7 %collective-permute-start.17 = (f32[8,2,64,128]{3,2,1,0:T(8,128)S(1)}, f32[8,2,64,128]{3,2,1,0:T(8,128)S(1)}, u32[]{:S(2)}, u32[]{:S(2)}) collective-permute-start(f32[8,2,64,128]{3,2,1,0:T(8,128)S(1)} %get-tuple-element.120), channel_id=1, source_target_pairs={{0,8},{8,0},{16,24},{24,16},{1,9},{9,1},{17,25},{25,17},{2,10},{10... | collective-permute-start | bytes 1572872 | tf_op jit(solution)/shard_map/ppermute | solution.py:423
  123.1 29.5 %collective-permute-start.24 = (f32[8,2,64,128]{3,2,1,0:T(8,128)S(1)}, f32[8,2,64,128]{3,2,1,0:T(8,128)S(1)}, u32[]{:S(2)}, u32[]{:S(2)}) collective-permute-start(f32[8,2,64,128]{3,2,1,0:T(8,128)S(1)} %get-tuple-element.134), channel_id=1, source_target_pairs={{0,24},{8,16},{16,8},{24,0},{1,25},{9,17},{17,9},{25,1},{2,26},{10... | collective-permute-start | bytes 1572872 | tf_op jit(solution)/shard_map/ppermute | solution.py:423
  124.4 41.5 %collective-permute-start.25 = (f32[8,2,64,128]{3,2,1,0:T(8,128)S(1)}, f32[8,2,64,128]{3,2,1,0:T(8,128)S(1)}, u32[]{:S(2)}, u32[]{:S(2)}) collective-permute-start(f32[8,2,64,128]{3,2,1,0:T(8,128)S(1)} %get-tuple-element.144), channel_id=1, source_target_pairs={{0,16},{8,24},{16,0},{24,8},{1,17},{9,25},{17,1},{25,9},{2,18},{10... | collective-permute-start | bytes 1572872 | tf_op jit(solution)/shard_map/ppermute | solution.py:423
  130.0 35.9 %collective-permute-start.26 = (f32[8,2,64,128]{3,2,1,0:T(8,128)S(1)}, f32[8,2,64,128]{3,2,1,0:T(8,128)S(1)}, u32[]{:S(2)}, u32[]{:S(2)}) collective-permute-start(f32[8,2,64,128]{3,2,1,0:T(8,128)S(1)} %get-tuple-element.145), channel_id=1, source_target_pairs={{0,8},{8,0},{16,24},{24,16},{1,9},{9,1},{17,25},{25,17},{2,10},{10... | collective-permute-start | bytes 1572872 | tf_op jit(solution)/shard_map/ppermute | solution.py:423
  144.5 30.5 %collective-permute-start.27 = (f32[8,2,64,128]{3,2,1,0:T(8,128)S(1)}, f32[8,2,64,128]{3,2,1,0:T(8,128)S(1)}, u32[]{:S(2)}, u32[]{:S(2)}) collective-permute-start(f32[8,2,64,128]{3,2,1,0:T(8,128)S(1)} %get-tuple-element.150), channel_id=1, source_target_pairs={{0,24},{8,16},{16,8},{24,0},{1,25},{9,17},{17,9},{25,1},{2,26},{10... | collective-permute-start | bytes 1572872 | tf_op jit(solution)/shard_map/ppermute | solution.py:423
  146.6 39.5 %collective-permute-start.19 = (f32[8,2,64,128]{3,2,1,0:T(8,128)S(1)}, f32[8,2,64,128]{3,2,1,0:T(8,128)S(1)}, u32[]{:S(2)}, u32[]{:S(2)}) collective-permute-start(f32[8,2,64,128]{3,2,1,0:T(8,128)S(1)} %get-tuple-element.126), channel_id=1, source_target_pairs={{0,16},{8,24},{16,0},{24,8},{1,17},{9,25},{17,1},{25,9},{2,18},{10... | collective-permute-start | bytes 1572872 | tf_op jit(solution)/shard_map/ppermute | solution.py:423
  152.5 33.8 %collective-permute-start.20 = (f32[8,2,64,128]{3,2,1,0:T(8,128)S(1)}, f32[8,2,64,128]{3,2,1,0:T(8,128)S(1)}, u32[]{:S(2)}, u32[]{:S(2)}) collective-permute-start(f32[8,2,64,128]{3,2,1,0:T(8,128)S(1)} %get-tuple-element.127), channel_id=1, source_target_pairs={{0,8},{8,0},{16,24},{24,16},{1,9},{9,1},{17,25},{25,17},{2,10},{10... | collective-permute-start | bytes 1572872 | tf_op jit(solution)/shard_map/ppermute | solution.py:423

commit v8 on v7

--- a/solution.py
+++ b/solution.py
@@ -476,8 +476,6 @@
     there = []
     low = high = None
     for chunk in range(chunks):
-        if chunk:
-            back[chunk] = after(back[chunk], high)
         done = first_update(me_array, back[chunk], plain, winv, field_start, chunk, whole)
         whole, (bottom, last), sends = done[:2], done[2:4], done[4:]
         if chunk == 0:
@@ -486,7 +484,7 @@
             low = upward(last)
         there.append(exchange(sends))
     residual, middle = whole
-    there[0] = after(there[0], low)
+    there[0] = after(there[0], low, high)
 
     back = []
     second = ()

time: 188 us -> 188 us (level)
    ppermute x24, waiting for transfers between devices: 51.6 us -> 58.1 us  [exchange(): lax.ppermute(piece, 'inst', [(i, i ^ code(m, n)) for i in range(n)])]
    ppermute x2, waiting for transfers between devices: 9.81 us -> 3.82 us  [downward(): lax.ppermute(plane, 'space', [(i + 1, i) for i in range(lax.axis_size('sp...]
  transfers between devices with their start and end apart: 28 -> 28, of which waited for: 15 -> 13; matrix products, arithmetic and copies ran while one was open for 3% -> 3% of each run, Pallas kernels for 43% -> 43%
where the time goes in v8:
time: 188 us; the launch traced here: 187 us
  Pallas kernels  82.2 us (44%)
  waiting for transfers between devices  61.9 us (33%)
  starting transfers between devices  37 us (20%)
  local copies, waits for them, and re-layouts  4.17 us (2%)
    ppermute x24, waiting for transfers between devices, exchange(): lax.ppermute(piece, 'inst', [(i, i ^ code(m, n)) for i in range(n)])  58.1 us
    pallas_call x4, Pallas kernels, stencil(): pl.pallas_call(functools.partial(stencil_kernel, second, first, len(befor...  38 us
    ppermute x24, starting transfers between devices, exchange(): lax.ppermute(piece, 'inst', [(i, i ^ code(m, n)) for i in range(n)])  24.9 us
    pallas_call x4, Pallas kernels, apply_time(): pl.pallas_call(functools.partial(apply_kernel, n), grid_spec=pltpu.Prefet...  13.2 us
    pallas_call x2, Pallas kernels, first_update(): pl.pallas_call(functools.partial(first_kernel, n, aliased), grid_spec=plt...  11 us
    pallas_call x5, Pallas kernels, cut(): pl.pallas_call(cut_kernel, grid_spec=pltpu.PrefetchScalarGridSpec(num_sca...  8.75 us
    ppermute x2, starting transfers between devices, upward(): lax.ppermute(plane, 'space', [(i, i + 1) for i in range(lax.axis_size('sp...  7.75 us
    pallas_call x1, Pallas kernels, chunk_update(): pl.pallas_call(functools.partial(chunk_kernel, n), grid_spec=pltpu.Prefet...  4.47 us
  transfers between devices with their start and end apart: 28, of which 13 were waited for; matrix products, arithmetic and copies ran while one was open for 3% of the time, Pallas kernels for 43%

profile of v8, /device:TPU:9, one launch (start us, length us, event | category | flops | bytes accessed | tf_op | source)
XLA Modules:
  0.0 187.4 jit_solution(1395784418880919355)
XLA Ops:
  0.6 1.1 cut.5
  1.7 2.2 %collective-permute-start.8 = (f32[8,2,64,128]{3,2,1,0:T(8,128)S(1)}, f32[8,2,64,128]{3,2,1,0:T(8,128)S(1)}, u32[]{:S(2)}, u32[]{:S(2)}) collective-permute-start(f32[8,2,64,128]{3,2,1,0:T(8,128)S(1)} %cut.5), channel_id=1, source_target_pairs={{0,24},{8,16},{16,8},{24,0},{1,25},{9,17},{17,9},{25,1},{2,26},{10... | collective-permute-start | bytes 1572872 | tf_op jit(solution)/shard_map/ppermute | solution.py:423
  4.0 2.2 %cut.6 = (f32[8,2,64,128]{3,2,1,0:T(8,128)}, f32[8,2,64,128]{3,2,1,0:T(8,128)}) custom-call(s32[1]{0:T(128)} %bitcast.me_ref, f32[8,16,64,128]{3,2,1,0:T(8,128)} %refs_6_.3, f32[8,16,64,128]{3,2,1,0:T(8,128)} %refs_6_.3), custom_call_target="tpu_custom_call" | custom-call | flops 1024 | bytes 1024 | tf_op jit(solution)/shard_map/cut/pallas_call | solution.py:61
  6.2 0.3 collective-permute-start.10
  6.4 0.2 collective-permute-start.9
  6.7 2.8 %prep.1 = (f32[16,64,128]{2,1,0:T(8,128)S(1)}, f32[16,64,128]{2,1,0:T(8,128)S(1)}, f32[17,64,128]{2,1,0:T(8,128)}, f32[8,64,128]{2,1,0:T(8,128)}) custom-call(f32[8]{0:T(128)S(1)} %copy-done, f32[8]{0:T(128)S(1)} %copy-done.1, f32[8]{0:T(128)S(1)} %multiply_add_fusion.tide_ref, s32[16,64,128]{2,1,0:T(8,128)} %material_ref, s32[8,3,16,64,128]{4,3,2,1,0:T(8,128)} %flags_ref.6, ...), custom_call_target="tpu_custom_call" | custom-call | flops 1024 | bytes 1024 | tf_op jit(solution)/shard_map/prep/pallas_call | solution.py:109
  9.5 4.6 %collective-permute-start = (f32[17,64,128]{2,1,0:T(8,128)}, f32[17,64,128]{2,1,0:T(8,128)S(1)}, u32[]{:S(2)}, u32[]{:S(2)}) collective-permute-start(f32[17,64,128]{2,1,0:T(8,128)} %get-tuple-element.80), channel_id=1, source_target_pairs={{0,1},{1,2},{2,3},{3,4},{4,5},{5,6},{6,7},{8,9},{9,10},{10,11},{11... | collective-permute-start | bytes 1671176 | tf_op jit(solution)/shard_map/ppermute | solution.py:432
  14.1 1.9 %collective-permute-start.1 = (f32[8,64,128]{2,1,0:T(8,128)}, f32[8,64,128]{2,1,0:T(8,128)S(1)}, u32[]{:S(2)}, u32[]{:S(2)}) collective-permute-start(f32[8,64,128]{2,1,0:T(8,128)} %get-tuple-element.81), channel_id=1, source_target_pairs={{1,0},{2,1},{3,2},{4,3},{5,4},{6,5},{7,6},{9,8},{10,9},{11,10},{12... | collective-permute-start | bytes 786440 | tf_op jit(solution)/shard_map/ppermute | solution.py:436
  16.2 0.7 broadcast_bitcast_fusion.1
  16.9 1.0 copy.17
  17.9 0.7 broadcast_bitcast_fusion
  18.6 3.8 %collective-permute-done.1.high_ref = f32[8,64,128]{2,1,0:T(8,128)S(1)} collective-permute-done((f32[8,64,128]{2,1,0:T(8,128)}, f32[8,64,128]{2,1,0:T(8,128)S(1)}, u32[]{:S(2)}, u32[]{:S(2)}) %collective-permute-start.1) | collective-permute-done | bytes 262176 | tf_op jit(solution)/shard_map/ppermute | solution.py:436
  22.4 2.6 %cut.7 = (f32[8,2,64,128]{3,2,1,0:T(8,128)}, f32[8,2,64,128]{3,2,1,0:T(8,128)}, f32[8,2,64,128]{3,2,1,0:T(8,128)}) custom-call(s32[1]{0:T(128)} %bitcast.me_ref, f32[8,16,64,128]{3,2,1,0:T(8,128)} %refs_6_.3, f32[8,16,64,128]{3,2,1,0:T(8,128)} %refs_6_.3, f32[8,16,64,128]{3,2,1,0:T(8,128)} %refs_6_.3), custom_call_target="tpu_custom_call" | custom-call | flops 1024 | bytes 1024 | tf_op jit(solution)/shard_map/cut/pallas_call | solution.py:61
  25.0 2.2 %collective-permute-start.2 = (f32[8,2,64,128]{3,2,1,0:T(8,128)}, f32[8,2,64,128]{3,2,1,0:T(8,128)}, u32[]{:S(2)}, u32[]{:S(2)}) collective-permute-start(f32[8,2,64,128]{3,2,1,0:T(8,128)} %get-tuple-element.83), channel_id=1, source_target_pairs={{0,24},{8,16},{16,8},{24,0},{1,25},{9,17},{17,9},{25,1},{2,26},{10... | collective-permute-start | bytes 1572872 | tf_op jit(solution)/shard_map/ppermute | solution.py:423
  27.2 0.2 collective-permute-start.3
  27.4 0.8 collective-permute-start.4
  28.2 1.8 copy.18
  29.9 1.0 compare_select_fusion.refs_3_
  31.0 6.0 %stencil_one.2 = (f32[8,16,64,128]{3,2,1,0:T(8,128)}, f32[8,16,64,128]{3,2,1,0:T(8,128)}) custom-call(f32[8]{0:T(128)S(1)} %multiply_add_fusion.tide_ref, f32[8,16,64,128]{3,2,1,0:T(8,128)} %refs_6_.3, f32[17,64,128]{2,1,0:T(8,128)S(1)} %collective-permute-done.low_ref.below_k_ref.below_f_ref, f32[8,64,128]{2,1,0:T(8,128)S(1)} %collective-permute-done.1.high_ref, ...), custom_call_target="tpu_custom_call" | custom-call | flops 1024 | bytes 1024 | tf_op jit(solution)/shard_map/stencil_one/pallas_call | solution.py:217
  37.0 3.3 %apply_time.5 = (f32[8,2,64,128]{3,2,1,0:T(8,128)S(1)}, f32[8,2,64,128]{3,2,1,0:T(8,128)S(1)}, f32[8,2,64,128]{3,2,1,0:T(8,128)S(1)}, f32[8,2,64,128]{3,2,1,0:T(8,128)S(1)}) custom-call(s32[1]{0:T(128)} %bitcast.me_ref, f32[8,16,64,128]{3,2,1,0:T(8,128)} %refs_6_.3, f32[8,2,64,128]{3,2,1,0:T(8,128)S(1)} %collective-permute-done.8.refs_0_, ...), custom_call_target="tpu_custom_call" | custom-call | flops 1024 | bytes 1024 | tf_op jit(solution)/shard_map/apply_time/pallas_call | solution.py:259
  40.3 1.7 collective-permute-start.11
  42.3 0.8 collective-permute-start.13
  43.1 8.3 %collective-permute-done.3.refs_1_ = f32[8,2,64,128]{3,2,1,0:T(8,128)} collective-permute-done((f32[8,2,64,128]{3,2,1,0:T(8,128)}, f32[8,2,64,128]{3,2,1,0:T(8,128)}, u32[]{:S(2)}, u32[]{:S(2)}) %collective-permute-start.3) | collective-permute-done | bytes 524320 | tf_op jit(solution)/shard_map/ppermute | solution.py:423
  51.4 3.5 %apply_time.4 = (f32[8,2,64,128]{3,2,1,0:T(8,128)S(1)}, f32[8,2,64,128]{3,2,1,0:T(8,128)S(1)}, f32[8,2,64,128]{3,2,1,0:T(8,128)S(1)}, f32[8,2,64,128]{3,2,1,0:T(8,128)S(1)}) custom-call(s32[1]{0:T(128)} %bitcast.me_ref, f32[8,16,64,128]{3,2,1,0:T(8,128)} %refs_6_.3, f32[8,2,64,128]{3,2,1,0:T(8,128)} %collective-permute-done.2.refs_0_, ...), custom_call_target="tpu_custom_call" | custom-call | flops 1024 | bytes 1024 | tf_op jit(solution)/shard_map/apply_time/pallas_call | solution.py:259
  54.8 1.2 collective-permute-start.5
  56.1 1.2 collective-permute-start.6
  57.3 5.2 %collective-permute-done.11.refs_1_ = f32[8,2,64,128]{3,2,1,0:T(8,128)S(1)} collective-permute-done((f32[8,2,64,128]{3,2,1,0:T(8,128)S(1)}, f32[8,2,64,128]{3,2,1,0:T(8,128)S(1)}, u32[]{:S(2)}, u32[]{:S(2)}) %collective-permute-start.11) | collective-permute-done | bytes 524320 | tf_op jit(solution)/shard_map/ppermute | solution.py:423
  62.5 1.2 collective-permute-start.7
  63.7 13.6 %stencil_one.3 = (f32[8,16,64,128]{3,2,1,0:T(8,128)}, f32[8,16,64,128]{3,2,1,0:T(8,128)}) custom-call(f32[8]{0:T(128)S(1)} %multiply_add_fusion.tide_ref, f32[8,16,64,128]{3,2,1,0:T(8,128)} %refs_6_.3, f32[17,64,128]{2,1,0:T(8,128)S(1)} %collective-permute-done.low_ref.below_k_ref.below_f_ref, ...), custom_call_target="tpu_custom_call", output_to_operand_aliasing={{0}: (10, {}), {1}: (11, {})} | custom-call | flops 1024 | bytes 1024 | tf_op jit(solution)/shard_map/stencil_one/pallas_call | solution.py:217
  77.3 5.6 %first_update.2 = (f32[8,16,64,128]{3,2,1,0:T(8,128)}, f32[8,16,64,128]{3,2,1,0:T(8,128)}, f32[8,64,128]{2,1,0:T(8,128)S(1)}, f32[8,64,128]{2,1,0:T(8,128)}, f32...) custom-call(s32[1]{0:T(128)} %bitcast.me_ref, ...), custom_call_target="tpu_custom_call" | custom-call | flops 1024 | bytes 1024 | tf_op jit(solution)/shard_map/first_update/pallas_call | solution.py:307
  82.9 1.2 collective-permute-start.21
  84.1 0.2 collective-permute-start.22
  84.3 0.7 collective-permute-done.5.refs_1_
  85.0 1.2 collective-permute-start.23
  86.2 10.0 %collective-permute-done.6.refs_2_ = f32[8,2,64,128]{3,2,1,0:T(8,128)S(1)} collective-permute-done((f32[8,2,64,128]{3,2,1,0:T(8,128)S(1)}, f32[8,2,64,128]{3,2,1,0:T(8,128)S(1)}, u32[]{:S(2)}, u32[]{:S(2)}) %collective-permute-start.6) | collective-permute-done | bytes 524320 | tf_op jit(solution)/shard_map/ppermute | solution.py:423
  96.2 2.4 %collective-permute-start.18 = (f32[8,64,128]{2,1,0:T(8,128)S(1)}, f32[8,64,128]{2,1,0:T(8,128)S(1)}, u32[]{:S(2)}, u32[]{:S(2)}) collective-permute-start(f32[8,64,128]{2,1,0:T(8,128)S(1)} %get-tuple-element.114), channel_id=1, source_target_pairs={{1,0},{2,1},{3,2},{4,3},{5,4},{6,5},{7,6},{9,8},{10,9},{11,10},{12... | collective-permute-start | bytes 786440 | tf_op jit(solution)/shard_map/ppermute | solution.py:436
  98.6 5.5 %first_update.3 = (f32[8,16,64,128]{3,2,1,0:T(8,128)}, f32[8,16,64,128]{3,2,1,0:T(8,128)}, f32[8,64,128]{2,1,0:T(8,128)}, f32[8,64,128]{2,1,0:T(8,128)S(1)}, f32...) custom-call(s32[1]{0:T(128)} %bitcast.me_ref, ...), custom_call_target="tpu_custom_call", output_to_operand_aliasing={{0}: (8, {}), {1}: (9, {})} | custom-call | flops 1024 | bytes 1024 | tf_op jit(solution)/shard_map/first_update/pallas_call | solution.py:307
  104.1 3.2 %collective-permute-start.17 = (f32[8,64,128]{2,1,0:T(8,128)S(1)}, f32[8,64,128]{2,1,0:T(8,128)S(1)}, u32[]{:S(2)}, u32[]{:S(2)}) collective-permute-start(f32[8,64,128]{2,1,0:T(8,128)S(1)} %get-tuple-element.113), channel_id=1, source_target_pairs={{0,1},{1,2},{2,3},{3,4},{4,5},{5,6},{6,7},{8,9},{9,10},{10,11},{11... | collective-permute-start | bytes 786440 | tf_op jit(solution)/shard_map/ppermute | solution.py:432
  107.2 1.7 collective-permute-start.14
  109.0 0.7 collective-permute-start.15
  109.7 9.0 %collective-permute-done.22.refs_1_ = f32[8,2,64,128]{3,2,1,0:T(8,128)S(1)} collective-permute-done((f32[8,2,64,128]{3,2,1,0:T(8,128)S(1)}, f32[8,2,64,128]{3,2,1,0:T(8,128)S(1)}, u32[]{:S(2)}, u32[]{:S(2)}) %collective-permute-start.22) | collective-permute-done | bytes 524320 | tf_op jit(solution)/shard_map/ppermute | solution.py:423
  118.7 1.2 collective-permute-start.16
  119.9 3.2 %apply_time.7 = (f32[8,2,64,128]{3,2,1,0:T(8,128)S(1)}, f32[8,2,64,128]{3,2,1,0:T(8,128)S(1)}, f32[8,2,64,128]{3,2,1,0:T(8,128)S(1)}, f32[8,2,64,128]{3,2,1,0:T(8,128)S(1)}) custom-call(s32[1]{0:T(128)} %bitcast.me_ref, f32[8,16,64,128]{3,2,1,0:T(8,128)} %get-tuple-element.127.u_ref.own_ref, f32[8,2,64,128]{3,2,1,0:T(8,128)S(1)} %collective-permute-done.21.refs_0_, ...), custom_call_target="tpu_custom_call" | custom-call | flops 1024 | bytes 1024 | tf_op jit(solution)/shard_map/apply_time/pallas_call | solution.py:259
  123.1 1.3 collective-permute-start.24
  124.4 0.2 collective-permute-start.25
  124.6 5.4 %collective-permute-done.14.refs_0_ = f32[8,2,64,128]{3,2,1,0:T(8,128)S(1)} collective-permute-done((f32[8,2,64,128]{3,2,1,0:T(8,128)S(1)}, f32[8,2,64,128]{3,2,1,0:T(8,128)S(1)}, u32[]{:S(2)}, u32[]{:S(2)}) %collective-permute-start.14) | collective-permute-done | bytes 524320 | tf_op jit(solution)/shard_map/ppermute | solution.py:423
  130.0 1.2 collective-permute-start.26
  131.2 9.2 %stencil_two.2.rest_1_ = f32[8,16,64,128]{3,2,1,0:T(8,128)} custom-call(f32[8]{0:T(128)S(1)} %multiply_add_fusion.tide_ref, f32[8,16,64,128]{3,2,1,0:T(8,128)} %get-tuple-element.127.u_ref.own_ref, f32[8,64,128]{2,1,0:T(8,128)S(1)} %collective-permute-done.17.low_ref, f32[8,64,128]{2,1,0:T(8,128)S(1)} %collective-permute-done.18.high_ref, ...), custom_call_target="tpu_custom_call" | custom-call | flops 1024 | bytes 1024 | tf_op jit(solution)/shard_map/stencil_two/pallas_call | solution.py:217
  140.4 0.7 collective-permute-done.15.refs_1_
  141.3 3.2 %apply_time.6 = (f32[8,2,64,128]{3,2,1,0:T(8,128)S(1)}, f32[8,2,64,128]{3,2,1,0:T(8,128)S(1)}, f32[8,2,64,128]{3,2,1,0:T(8,128)S(1)}, f32[8,2,64,128]{3,2,1,0:T(8,128)S(1)}) custom-call(s32[1]{0:T(128)} %bitcast.me_ref, f32[8,16,64,128]{3,2,1,0:T(8,128)} %get-tuple-element.127.u_ref.own_ref, f32[8,2,64,128]{3,2,1,0:T(8,128)S(1)} %collective-permute-done.14.refs_0_, ...), custom_call_target="tpu_custom_call" | custom-call | flops 1024 | bytes 1024 | tf_op jit(solution)/shard_map/apply_time/pallas_call | solution.py:259
  144.5 1.2 collective-permute-start.27
  145.8 1.2 collective-permute-start.19
  147.0 5.6 %collective-permute-done.24.refs_1_ = f32[8,2,64,128]{3,2,1,0:T(8,128)S(1)} collective-permute-done((f32[8,2,64,128]{3,2,1,0:T(8,128)S(1)}, f32[8,2,64,128]{3,2,1,0:T(8,128)S(1)}, u32[]{:S(2)}, u32[]{:S(2)}) %collective-permute-start.24) | collective-permute-done | bytes 524320 | tf_op jit(solution)/shard_map/ppermute | solution.py:423
  152.5 1.2 collective-permute-start.20
  153.8 9.2 %stencil_two.3.refs_0_.refs_1_.refs_2_.refs_4_ = f32[8,16,64,128]{3,2,1,0:T(8,128)} custom-call(f32[8]{0:T(128)S(1)} %multiply_add_fusion.tide_ref, f32[8,16,64,128]{3,2,1,0:T(8,128)} %get-tuple-element.127.u_ref.own_ref, f32[8,64,128]{2,1,0:T(8,128)S(1)} %collective-permute-done.17.low_ref, ...), custom_call_target="tpu_custom_call", output_to_operand_aliasing={{}: (11, {})} | custom-call | flops 1024 | bytes 1024 | tf_op jit(solution)/shard_map/stencil_two/pallas_call | solution.py:217
  162.9 1.5 cut.9
  164.4 1.5 cut.8
  165.9 4.5 %chunk_update.1.refs_3_ = f32[8,16,64,128]{3,2,1,0:T(8,128)} custom-call(s32[1]{0:T(128)} %bitcast.me_ref, f32[8,2,64,128]{3,2,1,0:T(8,128)S(1)} %get-tuple-element.135.refs_0_, f32[8,2,64,128]{3,2,1,0:T(8,128)S(1)} %collective-permute-done.24.refs_1_, f32[8,2,64,128]{3,2,1,0:T(8,128)S(1)} %collective-permute-done.25.refs_2_, ...), custom_call_target="tpu_custom_call" | custom-call | flops 1024 | bytes 1024 | tf_op jit(solution)/shard_map/chunk_update/pallas_call | solution.py:404
  170.4 2.1 %last_update.2.refs_3_ = f32[8,16,64,128]{3,2,1,0:T(8,128)} custom-call(s32[1]{0:T(128)} %bitcast.me_ref, f32[8,2,64,128]{3,2,1,0:T(8,128)S(1)} %get-tuple-element.134.refs_0_, f32[8,16,64,128]{3,2,1,0:T(8,128)} %stencil_two.3.refs_0_.refs_1_.refs_2_.refs_4_, ...), custom_call_target="tpu_custom_call", output_to_operand_aliasing={{}: (4, {})} | custom-call | flops 1024 | bytes 1024 | tf_op jit(solution)/shard_map/last_update/pallas_call | solution.py:333
  172.4 2.6 %collective-permute-done.27.refs_0_ = f32[8,2,64,128]{3,2,1,0:T(8,128)S(1)} collective-permute-done((f32[8,2,64,128]{3,2,1,0:T(8,128)S(1)}, f32[8,2,64,128]{3,2,1,0:T(8,128)S(1)}, u32[]{:S(2)}, u32[]{:S(2)}) %collective-permute-start.27) | collective-permute-done | bytes 524320 | tf_op jit(solution)/shard_map/ppermute | solution.py:423
  175.1 0.9 last_update.3.refs_6_
  175.9 10.1 %collective-permute-done.19.refs_0_ = f32[8,2,64,128]{3,2,1,0:T(8,128)S(1)} collective-permute-done((f32[8,2,64,128]{3,2,1,0:T(8,128)S(1)}, f32[8,2,64,128]{3,2,1,0:T(8,128)S(1)}, u32[]{:S(2)}, u32[]{:S(2)}) %collective-permute-start.19) | collective-permute-done | bytes 524320 | tf_op jit(solution)/shard_map/ppermute | solution.py:423
  186.1 0.3 collective-permute-done.20.refs_1_
  186.4 1.0 final_update.1
  (25 shorter events, 0.7 us)
Async XLA Ops:
  1.7 5.0 %copy-start = (f32[8]{0:T(128)S(1)}, f32[8]{0:T(128)}, u32[]{:S(2)}) copy-start(f32[8]{0:T(128)} %disp_ref.1) | copy-start | bytes 100
  1.7 5.0 %copy-start.1 = (f32[8]{0:T(128)S(1)}, f32[8]{0:T(128)}, u32[]{:S(2)}) copy-start(f32[8]{0:T(128)} %perm_ref.1) | copy-start | bytes 100
  1.7 35.3 %collective-permute-start.8 = (f32[8,2,64,128]{3,2,1,0:T(8,128)S(1)}, f32[8,2,64,128]{3,2,1,0:T(8,128)S(1)}, u32[]{:S(2)}, u32[]{:S(2)}) collective-permute-start(f32[8,2,64,128]{3,2,1,0:T(8,128)S(1)} %cut.5), channel_id=1, source_target_pairs={{0,24},{8,16},{16,8},{24,0},{1,25},{9,17},{17,9},{25,1},{2,26},{10... | collective-permute-start | bytes 1572872 | tf_op jit(solution)/shard_map/ppermute | solution.py:423
  6.2 21.2 %collective-permute-start.10 = (f32[8,2,64,128]{3,2,1,0:T(8,128)}, f32[8,2,64,128]{3,2,1,0:T(8,128)S(1)}, u32[]{:S(2)}, u32[]{:S(2)}) collective-permute-start(f32[8,2,64,128]{3,2,1,0:T(8,128)} %get-tuple-element.76), channel_id=1, source_target_pairs={{0,8},{8,0},{16,24},{24,16},{1,9},{9,1},{17,25},{25,17},{2,10},{10... | collective-permute-start | bytes 1572872 | tf_op jit(solution)/shard_map/ppermute | solution.py:423
  6.4 30.6 %collective-permute-start.9 = (f32[8,2,64,128]{3,2,1,0:T(8,128)}, f32[8,2,64,128]{3,2,1,0:T(8,128)}, u32[]{:S(2)}, u32[]{:S(2)}) collective-permute-start(f32[8,2,64,128]{3,2,1,0:T(8,128)} %get-tuple-element.75), channel_id=1, source_target_pairs={{0,16},{8,24},{16,0},{24,8},{1,17},{9,25},{17,1},{25,9},{2,18},{10... | collective-permute-start | bytes 1572872 | tf_op jit(solution)/shard_map/ppermute | solution.py:423
  9.5 12.9 %collective-permute-start = (f32[17,64,128]{2,1,0:T(8,128)}, f32[17,64,128]{2,1,0:T(8,128)S(1)}, u32[]{:S(2)}, u32[]{:S(2)}) collective-permute-start(f32[17,64,128]{2,1,0:T(8,128)} %get-tuple-element.80), channel_id=1, source_target_pairs={{0,1},{1,2},{2,3},{3,4},{4,5},{5,6},{6,7},{8,9},{9,10},{10,11},{11... | collective-permute-start | bytes 1671176 | tf_op jit(solution)/shard_map/ppermute | solution.py:432
  14.1 8.3 %collective-permute-start.1 = (f32[8,64,128]{2,1,0:T(8,128)}, f32[8,64,128]{2,1,0:T(8,128)S(1)}, u32[]{:S(2)}, u32[]{:S(2)}) collective-permute-start(f32[8,64,128]{2,1,0:T(8,128)} %get-tuple-element.81), channel_id=1, source_target_pairs={{1,0},{2,1},{3,2},{4,3},{5,4},{6,5},{7,6},{9,8},{10,9},{11,10},{12... | collective-permute-start | bytes 786440 | tf_op jit(solution)/shard_map/ppermute | solution.py:436
  25.0 17.3 %collective-permute-start.2 = (f32[8,2,64,128]{3,2,1,0:T(8,128)}, f32[8,2,64,128]{3,2,1,0:T(8,128)}, u32[]{:S(2)}, u32[]{:S(2)}) collective-permute-start(f32[8,2,64,128]{3,2,1,0:T(8,128)} %get-tuple-element.83), channel_id=1, source_target_pairs={{0,24},{8,16},{16,8},{24,0},{1,25},{9,17},{17,9},{25,1},{2,26},{10... | collective-permute-start | bytes 1572872 | tf_op jit(solution)/shard_map/ppermute | solution.py:423
  27.2 24.2 %collective-permute-start.3 = (f32[8,2,64,128]{3,2,1,0:T(8,128)}, f32[8,2,64,128]{3,2,1,0:T(8,128)}, u32[]{:S(2)}, u32[]{:S(2)}) collective-permute-start(f32[8,2,64,128]{3,2,1,0:T(8,128)} %get-tuple-element.84), channel_id=1, source_target_pairs={{0,16},{8,24},{16,0},{24,8},{1,17},{9,25},{17,1},{25,9},{2,18},{10... | collective-permute-start | bytes 1572872 | tf_op jit(solution)/shard_map/ppermute | solution.py:423
  27.4 24.0 %collective-permute-start.4 = (f32[8,2,64,128]{3,2,1,0:T(8,128)}, f32[8,2,64,128]{3,2,1,0:T(8,128)}, u32[]{:S(2)}, u32[]{:S(2)}) collective-permute-start(f32[8,2,64,128]{3,2,1,0:T(8,128)} %get-tuple-element.85), channel_id=1, source_target_pairs={{0,8},{8,0},{16,24},{24,16},{1,9},{9,1},{17,25},{25,17},{2,10},{10... | collective-permute-start | bytes 1572872 | tf_op jit(solution)/shard_map/ppermute | solution.py:423
  40.3 22.1 %collective-permute-start.11 = (f32[8,2,64,128]{3,2,1,0:T(8,128)S(1)}, f32[8,2,64,128]{3,2,1,0:T(8,128)S(1)}, u32[]{:S(2)}, u32[]{:S(2)}) collective-permute-start(f32[8,2,64,128]{3,2,1,0:T(8,128)S(1)} %get-tuple-element.98), channel_id=1, source_target_pairs={{0,24},{8,16},{16,8},{24,0},{1,25},{9,17},{17,9},{25,1},{2,26},{10... | collective-permute-start | bytes 1572872 | tf_op jit(solution)/shard_map/ppermute | solution.py:423
  42.1 35.3 %collective-permute-start.12 = (f32[8,2,64,128]{3,2,1,0:T(8,128)S(1)}, f32[8,2,64,128]{3,2,1,0:T(8,128)S(1)}, u32[]{:S(2)}, u32[]{:S(2)}) collective-permute-start(f32[8,2,64,128]{3,2,1,0:T(8,128)S(1)} %get-tuple-element.103), channel_id=1, source_target_pairs={{0,16},{8,24},{16,0},{24,8},{1,17},{9,25},{17,1},{25,9},{2,18},{10... | collective-permute-start | bytes 1572872 | tf_op jit(solution)/shard_map/ppermute | solution.py:423
  42.3 35.0 %collective-permute-start.13 = (f32[8,2,64,128]{3,2,1,0:T(8,128)S(1)}, f32[8,2,64,128]{3,2,1,0:T(8,128)S(1)}, u32[]{:S(2)}, u32[]{:S(2)}) collective-permute-start(f32[8,2,64,128]{3,2,1,0:T(8,128)S(1)} %get-tuple-element.104), channel_id=1, source_target_pairs={{0,8},{8,0},{16,24},{24,16},{1,9},{9,1},{17,25},{25,17},{2,10},{10... | collective-permute-start | bytes 1572872 | tf_op jit(solution)/shard_map/ppermute | solution.py:423
  54.8 30.2 %collective-permute-start.5 = (f32[8,2,64,128]{3,2,1,0:T(8,128)S(1)}, f32[8,2,64,128]{3,2,1,0:T(8,128)S(1)}, u32[]{:S(2)}, u32[]{:S(2)}) collective-permute-start(f32[8,2,64,128]{3,2,1,0:T(8,128)S(1)} %get-tuple-element.87), channel_id=1, source_target_pairs={{0,24},{8,16},{16,8},{24,0},{1,25},{9,17},{17,9},{25,1},{2,26},{10... | collective-permute-start | bytes 1572872 | tf_op jit(solution)/shard_map/ppermute | solution.py:423
  56.1 40.1 %collective-permute-start.6 = (f32[8,2,64,128]{3,2,1,0:T(8,128)S(1)}, f32[8,2,64,128]{3,2,1,0:T(8,128)S(1)}, u32[]{:S(2)}, u32[]{:S(2)}) collective-permute-start(f32[8,2,64,128]{3,2,1,0:T(8,128)S(1)} %get-tuple-element.88), channel_id=1, source_target_pairs={{0,16},{8,24},{16,0},{24,8},{1,17},{9,25},{17,1},{25,9},{2,18},{10... | collective-permute-start | bytes 1572872 | tf_op jit(solution)/shard_map/ppermute | solution.py:423
  62.5 36.1 %collective-permute-start.7 = (f32[8,2,64,128]{3,2,1,0:T(8,128)S(1)}, f32[8,2,64,128]{3,2,1,0:T(8,128)S(1)}, u32[]{:S(2)}, u32[]{:S(2)}) collective-permute-start(f32[8,2,64,128]{3,2,1,0:T(8,128)S(1)} %get-tuple-element.89), channel_id=1, source_target_pairs={{0,8},{8,0},{16,24},{24,16},{1,9},{9,1},{17,25},{25,17},{2,10},{10... | collective-permute-start | bytes 1572872 | tf_op jit(solution)/shard_map/ppermute | solution.py:423
  82.9 26.1 %collective-permute-start.21 = (f32[8,2,64,128]{3,2,1,0:T(8,128)S(1)}, f32[8,2,64,128]{3,2,1,0:T(8,128)S(1)}, u32[]{:S(2)}, u32[]{:S(2)}) collective-permute-start(f32[8,2,64,128]{3,2,1,0:T(8,128)S(1)} %get-tuple-element.120), channel_id=1, source_target_pairs={{0,24},{8,16},{16,8},{24,0},{1,25},{9,17},{17,9},{25,1},{2,26},{10... | collective-permute-start | bytes 1572872 | tf_op jit(solution)/shard_map/ppermute | solution.py:423
  84.1 34.5 %collective-permute-start.22 = (f32[8,2,64,128]{3,2,1,0:T(8,128)S(1)}, f32[8,2,64,128]{3,2,1,0:T(8,128)S(1)}, u32[]{:S(2)}, u32[]{:S(2)}) collective-permute-start(f32[8,2,64,128]{3,2,1,0:T(8,128)S(1)} %get-tuple-element.121), channel_id=1, source_target_pairs={{0,16},{8,24},{16,0},{24,8},{1,17},{9,25},{17,1},{25,9},{2,18},{10... | collective-permute-start | bytes 1572872 | tf_op jit(solution)/shard_map/ppermute | solution.py:423
  85.0 34.9 %collective-permute-start.23 = (f32[8,2,64,128]{3,2,1,0:T(8,128)S(1)}, f32[8,2,64,128]{3,2,1,0:T(8,128)S(1)}, u32[]{:S(2)}, u32[]{:S(2)}) collective-permute-start(f32[8,2,64,128]{3,2,1,0:T(8,128)S(1)} %get-tuple-element.122), channel_id=1, source_target_pairs={{0,8},{8,0},{16,24},{24,16},{1,9},{9,1},{17,25},{25,17},{2,10},{10... | collective-permute-start | bytes 1572872 | tf_op jit(solution)/shard_map/ppermute | solution.py:423
  96.2 11.0 %collective-permute-start.18 = (f32[8,64,128]{2,1,0:T(8,128)S(1)}, f32[8,64,128]{2,1,0:T(8,128)S(1)}, u32[]{:S(2)}, u32[]{:S(2)}) collective-permute-start(f32[8,64,128]{2,1,0:T(8,128)S(1)} %get-tuple-element.114), channel_id=1, source_target_pairs={{1,0},{2,1},{3,2},{4,3},{5,4},{6,5},{7,6},{9,8},{10,9},{11,10},{12... | collective-permute-start | bytes 786440 | tf_op jit(solution)/shard_map/ppermute | solution.py:436
  104.1 15.8 %collective-permute-start.17 = (f32[8,64,128]{2,1,0:T(8,128)S(1)}, f32[8,64,128]{2,1,0:T(8,128)S(1)}, u32[]{:S(2)}, u32[]{:S(2)}) collective-permute-start(f32[8,64,128]{2,1,0:T(8,128)S(1)} %get-tuple-element.113), channel_id=1, source_target_pairs={{0,1},{1,2},{2,3},{3,4},{4,5},{5,6},{6,7},{8,9},{9,10},{10,11},{11... | collective-permute-start | bytes 786440 | tf_op jit(solution)/shard_map/ppermute | solution.py:432
  107.2 22.8 %collective-permute-start.14 = (f32[8,2,64,128]{3,2,1,0:T(8,128)S(1)}, f32[8,2,64,128]{3,2,1,0:T(8,128)S(1)}, u32[]{:S(2)}, u32[]{:S(2)}) collective-permute-start(f32[8,2,64,128]{3,2,1,0:T(8,128)S(1)} %get-tuple-element.109), channel_id=1, source_target_pairs={{0,24},{8,16},{16,8},{24,0},{1,25},{9,17},{17,9},{25,1},{2,26},{10... | collective-permute-start | bytes 1572872 | tf_op jit(solution)/shard_map/ppermute | solution.py:423
  109.0 32.2 %collective-permute-start.15 = (f32[8,2,64,128]{3,2,1,0:T(8,128)S(1)}, f32[8,2,64,128]{3,2,1,0:T(8,128)S(1)}, u32[]{:S(2)}, u32[]{:S(2)}) collective-permute-start(f32[8,2,64,128]{3,2,1,0:T(8,128)S(1)} %get-tuple-element.110), channel_id=1, source_target_pairs={{0,16},{8,24},{16,0},{24,8},{1,17},{9,25},{17,1},{25,9},{2,18},{10... | collective-permute-start | bytes 1572872 | tf_op jit(solution)/shard_map/ppermute | solution.py:423
  118.7 22.7 %collective-permute-start.16 = (f32[8,2,64,128]{3,2,1,0:T(8,128)S(1)}, f32[8,2,64,128]{3,2,1,0:T(8,128)S(1)}, u32[]{:S(2)}, u32[]{:S(2)}) collective-permute-start(f32[8,2,64,128]{3,2,1,0:T(8,128)S(1)} %get-tuple-element.111), channel_id=1, source_target_pairs={{0,8},{8,0},{16,24},{24,16},{1,9},{9,1},{17,25},{25,17},{2,10},{10... | collective-permute-start | bytes 1572872 | tf_op jit(solution)/shard_map/ppermute | solution.py:423
  123.1 29.5 %collective-permute-start.24 = (f32[8,2,64,128]{3,2,1,0:T(8,128)S(1)}, f32[8,2,64,128]{3,2,1,0:T(8,128)S(1)}, u32[]{:S(2)}, u32[]{:S(2)}) collective-permute-start(f32[8,2,64,128]{3,2,1,0:T(8,128)S(1)} %get-tuple-element.126), channel_id=1, source_target_pairs={{0,24},{8,16},{16,8},{24,0},{1,25},{9,17},{17,9},{25,1},{2,26},{10... | collective-permute-start | bytes 1572872 | tf_op jit(solution)/shard_map/ppermute | solution.py:423
  124.4 41.5 %collective-permute-start.25 = (f32[8,2,64,128]{3,2,1,0:T(8,128)S(1)}, f32[8,2,64,128]{3,2,1,0:T(8,128)S(1)}, u32[]{:S(2)}, u32[]{:S(2)}) collective-permute-start(f32[8,2,64,128]{3,2,1,0:T(8,128)S(1)} %get-tuple-element.136), channel_id=1, source_target_pairs={{0,16},{8,24},{16,0},{24,8},{1,17},{9,25},{17,1},{25,9},{2,18},{10... | collective-permute-start | bytes 1572872 | tf_op jit(solution)/shard_map/ppermute | solution.py:423
  130.0 35.9 %collective-permute-start.26 = (f32[8,2,64,128]{3,2,1,0:T(8,128)S(1)}, f32[8,2,64,128]{3,2,1,0:T(8,128)S(1)}, u32[]{:S(2)}, u32[]{:S(2)}) collective-permute-start(f32[8,2,64,128]{3,2,1,0:T(8,128)S(1)} %get-tuple-element.137), channel_id=1, source_target_pairs={{0,8},{8,0},{16,24},{24,16},{1,9},{9,1},{17,25},{25,17},{2,10},{10... | collective-permute-start | bytes 1572872 | tf_op jit(solution)/shard_map/ppermute | solution.py:423
  144.5 30.5 %collective-permute-start.27 = (f32[8,2,64,128]{3,2,1,0:T(8,128)S(1)}, f32[8,2,64,128]{3,2,1,0:T(8,128)S(1)}, u32[]{:S(2)}, u32[]{:S(2)}) collective-permute-start(f32[8,2,64,128]{3,2,1,0:T(8,128)S(1)} %get-tuple-element.142), channel_id=1, source_target_pairs={{0,24},{8,16},{16,8},{24,0},{1,25},{9,17},{17,9},{25,1},{2,26},{10... | collective-permute-start | bytes 1572872 | tf_op jit(solution)/shard_map/ppermute | solution.py:423
  145.8 40.3 %collective-permute-start.19 = (f32[8,2,64,128]{3,2,1,0:T(8,128)S(1)}, f32[8,2,64,128]{3,2,1,0:T(8,128)S(1)}, u32[]{:S(2)}, u32[]{:S(2)}) collective-permute-start(f32[8,2,64,128]{3,2,1,0:T(8,128)S(1)} %get-tuple-element.118), channel_id=1, source_target_pairs={{0,16},{8,24},{16,0},{24,8},{1,17},{9,25},{17,1},{25,9},{2,18},{10... | collective-permute-start | bytes 1572872 | tf_op jit(solution)/shard_map/ppermute | solution.py:423
  152.5 33.8 %collective-permute-start.20 = (f32[8,2,64,128]{3,2,1,0:T(8,128)S(1)}, f32[8,2,64,128]{3,2,1,0:T(8,128)S(1)}, u32[]{:S(2)}, u32[]{:S(2)}) collective-permute-start(f32[8,2,64,128]{3,2,1,0:T(8,128)S(1)} %get-tuple-element.119), channel_id=1, source_target_pairs={{0,8},{8,0},{16,24},{24,16},{1,9},{9,1},{17,25},{25,17},{2,10},{10... | collective-permute-start | bytes 1572872 | tf_op jit(solution)/shard_map/ppermute | solution.py:423
